TPU v7x, 32 devices: a whole 2x2x4 slice. The times are simulated.
32 devices in a mesh: parts: 2 (over y), patch: 4 (over z), grp: 2 (over x), col: 2 (over core).
Axes of the slice: x: 2, y: 2, z: 4, core: 2. Of those that a mesh axis runs over, the one named last changes fastest.
Arguments:
- query_vectors: bfloat16 [2048, 1024], P(('parts', 'patch', 'grp'), 'col'), parts along dimension 0, may hold values from -180 to 180
- key_vectors: bfloat16 [2048, 1024], P(('parts', 'patch', 'grp'), 'col'), parts along dimension 0, may hold values from -6 to 6
- value_vectors: bfloat16 [2048, 1024], P(('parts', 'patch', 'grp'), 'col'), parts along dimension 0, may hold values from -6 to 6
- residual: bfloat16 [2048, 1024], P(('parts', 'patch', 'grp'), 'col'), parts along dimension 0, may hold values from -6 to 6
- neighbor_ids: int32 [16, 2], P(('parts', 'patch', 'grp')), parts along dimension 0, may hold values from 0 to 1, as said below
- neighbor_count: int32 [16], P(('parts', 'patch', 'grp')), parts along dimension 0, may hold values from 1 to 2
- output_weight: bfloat16 [1024, 1024], P('col'), may hold values from -0.1875 to 0.1875
- norm_gain: float32 [1024], P('col'), may hold values from 0.25 to 1.75
- up_weight: bfloat16 [1024, 4096], P(None, ('grp', 'col')), may hold values from -0.1875 to 0.1875
- down_weight: bfloat16 [4096, 1024], P(('grp', 'col')), may hold values from -0.09375 to 0.09375
- cotangent: bfloat16 [2048, 1024], P(('parts', 'patch', 'grp'), 'col'), parts along dimension 0, may hold values from -6 to 6
Outputs:
- layer_out: bfloat16 [2048, 1024], P(('parts', 'patch', 'grp'), 'col'), parts along dimension 0
- up_grad: float32 [2048, 4096], P('parts', ('grp', 'col')), parts along dimension 0
- down_grad: float32 [8192, 1024], P(('parts', 'grp', 'col')), parts along dimension 0
There are 2 independent parts, one for each index of `parts`. A program takes and returns all parts, laid end to end along the dimension named above; an argument that names none is the same for every part. Nothing has to cross between parts.
Inputs may be any that keep to these rules, and one draw needn't show every extreme that they name: `neighbor_ids`: entry 0 of row b is b % 2; the other entries of a row are distinct other indices of the group; entries past neighbor_count[b] are valid indices but unused.
All inputs are finite; a program needn't handle non-finite values.
Results may differ from a plain program's by a relative error of at most 0.012.
Values may be sent and summed in bfloat16 or wider, within the bound.
No kernel may reach another device: no remote copies, remote signals or barrier semaphores. Data moves between devices by JAX's collectives and lax.ppermute only.
A program may use at most 64 MiB of HBM per device.

v0:
```python
import jax
import jax.numpy as jnp
from jax import lax
from jax.sharding import PartitionSpec as P

HEAD = 64
D = 1024
BLK = 128


def spread_rows(part_rows):
    stacked = lax.all_gather(part_rows[None], ("grp", "col"), axis=0, tiled=True)
    grp_count = lax.axis_size("grp")
    col_count = lax.axis_size("col")
    row_count = part_rows.shape[0]
    half_width = part_rows.shape[1]
    arranged = stacked.reshape(grp_count, col_count, row_count, half_width).transpose(0, 2, 1, 3)
    return arranged.reshape(grp_count * row_count, col_count * half_width)


def shards(
    query_vectors,
    key_vectors,
    value_vectors,
    residual,
    neighbor_ids,
    neighbor_count,
    output_weight,
    norm_gain,
    up_weight,
    down_weight,
    cotangent,
):
    key_all, value_all = (
        lax.all_gather(key_vectors, "grp", axis=0, tiled=True),
        lax.all_gather(value_vectors, "grp", axis=0, tiled=True),
    )
    row_count = query_vectors.shape[0]
    local_heads = query_vectors.shape[1] // HEAD
    group_count = key_all.shape[0] // BLK
    column_ids = jnp.arange(group_count, dtype=jnp.int32)
    slot_ids = jnp.arange(neighbor_ids.shape[1], dtype=jnp.int32)
    listed = (neighbor_ids[:, :, None] == column_ids[None, None, :]) & (
        slot_ids[None, :, None] < neighbor_count[:, None, None]
    )
    allowed = jnp.any(listed, axis=1)
    token_mask = jnp.repeat(jnp.repeat(allowed, BLK, axis=0), BLK, axis=1)
    query_heads = query_vectors.reshape(row_count, local_heads, HEAD)
    key_heads = key_all.reshape(-1, local_heads, HEAD)
    value_heads = value_all.reshape(-1, local_heads, HEAD)
    scores = jnp.einsum(
        "qhd,khd->hqk", query_heads, key_heads, preferred_element_type=jnp.float32
    ) * HEAD ** (-0.5)
    scores = jnp.where(token_mask[None], scores, -1e30)
    largest = jnp.max(scores, axis=2, keepdims=True)
    weights = jnp.exp(scores - largest)
    probs = (weights / jnp.sum(weights, axis=2, keepdims=True)).astype(jnp.bfloat16)
    attended = jnp.einsum("hqk,khd->qhd", probs, value_heads, preferred_element_type=jnp.float32)
    attended = attended.astype(jnp.bfloat16).reshape(row_count, -1)
    projected = jnp.dot(attended, output_weight, preferred_element_type=jnp.float32)
    stream = residual.astype(jnp.float32) + lax.psum_scatter(
        projected.astype(jnp.bfloat16), "col", scatter_dimension=1, tiled=True
    ).astype(jnp.float32)
    first_sum, second_sum = lax.psum(
        (jnp.sum(stream, axis=1), jnp.sum(stream * stream, axis=1)), "col"
    )
    center = first_sum[:, None] / D
    shifted = stream - center
    spread_sq = second_sum[:, None] / D - center * center
    normed = (shifted * lax.rsqrt(spread_sq + 1e-05) * norm_gain[None, :]).astype(jnp.bfloat16)
    normed_rows = spread_rows(normed)
    pre = jnp.dot(normed_rows, up_weight, preferred_element_type=jnp.float32)
    hidden = jax.nn.gelu(pre).astype(jnp.bfloat16)
    grp_count = lax.axis_size("grp")
    col_count = lax.axis_size("col")
    partial_out = jnp.dot(hidden, down_weight, preferred_element_type=jnp.float32)
    half_width = partial_out.shape[1] // col_count
    partial_out = partial_out.reshape(grp_count, row_count, col_count, half_width).transpose(
        0, 2, 1, 3
    )
    partial_out = partial_out.reshape(grp_count * col_count * row_count, half_width)
    ff_out = lax.psum_scatter(
        partial_out.astype(jnp.bfloat16), ("grp", "col"), scatter_dimension=0, tiled=True
    ).astype(jnp.float32)
    layer_out = (stream + ff_out).astype(jnp.bfloat16)
    back_rows = spread_rows(cotangent)
    back_hidden = lax.dot_general(
        back_rows, down_weight, (((1,), (1,)), ((), ())), preferred_element_type=jnp.float32
    )
    _, gelu_back = jax.vjp(jax.nn.gelu, pre)
    back_pre = gelu_back(back_hidden)[0].astype(jnp.bfloat16)
    up_local = lax.dot_general(
        normed_rows, back_pre, (((0,), (0,)), ((), ())), preferred_element_type=jnp.float32
    )
    down_local = lax.dot_general(
        hidden, back_rows, (((0,), (0,)), ((), ())), preferred_element_type=jnp.float32
    )
    up_grad, down_grad = (
        lax.psum(up_local.astype(jnp.bfloat16), "patch").astype(jnp.float32),
        lax.psum(down_local.astype(jnp.bfloat16), "patch").astype(jnp.float32),
    )
    return (layer_out, up_grad, down_grad)


def solution(mesh):
    return jax.shard_map(
        shards,
        mesh=mesh,
        in_specs=(
            P(("parts", "patch", "grp"), "col"),
            P(("parts", "patch", "grp"), "col"),
            P(("parts", "patch", "grp"), "col"),
            P(("parts", "patch", "grp"), "col"),
            P(("parts", "patch", "grp"), None),
            P(("parts", "patch", "grp")),
            P("col", None),
            P("col"),
            P(None, ("grp", "col")),
            P(("grp", "col"), None),
            P(("parts", "patch", "grp"), "col"),
        ),
        out_specs=(
            P(("parts", "patch", "grp"), "col"),
            P("parts", ("grp", "col")),
            P(("parts", "grp", "col"), None),
        ),
        check_vma=False,
    )
```

profile of v0, /device:TPU:0, one launch (start us, length us, event | category | flops | bytes accessed | tf_op | source)
XLA Modules:
  0.0 253.6 jit_solution(1963257339254852949)
XLA Ops:
  7.2 0.0 copy-start
  7.2 0.0 reduce-scatter.3.cloned.1.call-start
  8.0 0.7 and_reduce_fusion
  8.8 0.1 broadcast_bitcast_fusion
  8.8 1.0 copy.24
  9.9 0.0 copy-start.8
  9.9 7.5 %all_gather.12 = bf16[256,512]{1,0:T(8,128)(2,1)S(1)} all-gather(bf16[128,512]{1,0:T(8,128)(2,1)} %param.12), channel_id=1, replica_groups=mesh['parts'=2,'patch'=4,'grp'=2,'col'=2] {'grp'}, dimensions={0}, use_global_device_ids=true | all-gather | bytes 393216 | tf_op jit(solution)/shard_map/all_gather | solution.py:35
  17.4 0.1 copy.25
  17.5 0.6 fusion.28
  18.2 1.3 fusion.3
  19.5 0.0 copy-done.8
  19.5 5.6 %all_gather.13 = bf16[256,512]{1,0:T(8,128)(2,1)S(1)} all-gather(bf16[128,512]{1,0:T(8,128)(2,1)S(1)} %copy-done.8), channel_id=1, replica_groups=mesh['parts'=2,'patch'=4,'grp'=2,'col'=2] {'grp'}, dimensions={0}, use_global_device_ids=true | all-gather | bytes 393216 | tf_op jit(solution)/shard_map/all_gather | solution.py:36
  25.1 0.1 copy.26
  25.3 0.0 copy-start.7
  25.3 0.0 copy-start.3
  25.3 0.0 copy-start.10
  25.3 4.2 %convolution_convert_fusion.4 = bf16[8,128,64]{1,2,0:T(8,128)(2,1)} fusion(bf16[256,8,64]{0,2,1:T(8,128)(2,1)S(1)} %bitcast.52, f32[8,128]{1,0:T(8,128)S(1)} %fusion.28, f32[8,128,256]{2,1,0:T(8,128)} %fusion.3), kind=kOutput, calls=%fused_computation.11 | convolution fusion | flops 34407680 | bytes 1445888 | tf_op jit(solution)/shard_map/hqk,khd->qhd/dot_general | solution.py:58
  29.5 0.0 copy-done.7
  29.5 1.9 convolution_convert_fusion.3
  31.5 0.0 reduce-scatter.3.cloned.1.call-update
  31.5 0.0 reduce-scatter.5.cloned.1.call-start
  31.5 9.2 %reduce-scatter.3.cloned.1.call-done = bf16[128,512]{1,0:T(8,128)(2,1)} async-done(((bf16[128,1024]{1,0:T(8,128)(2,1)}), bf16[128,512]{1,0:T(8,128)(2,1)}) %reduce-scatter.3.cloned.1.call-update) | async-done | bytes 131088 | tf_op jit(solution)/shard_map/reduce_scatter | solution.py:61
  40.8 1.0 fusion.18
  41.8 2.5 all-reduce
  44.3 0.0 copy-done.10
  44.3 1.2 multiply_convert_fusion.1
  45.5 7.4 %all-gather = bf16[512,512]{1,0:T(8,128)(2,1)S(1)} all-gather(bf16[128,512]{1,0:T(8,128)(2,1)S(1)} %multiply_convert_fusion.1), channel_id=2, replica_groups=mesh['parts'=2,'patch'=4,'grp'=2,'col'=2] {'grp','col'}, dimensions={0}, use_global_device_ids=true | all-gather | bytes 655360 | tf_op jit(solution)/shard_map/all_gather | solution.py:12
  52.9 0.5 copy.27
  53.4 0.1 copy.30
  53.5 0.0 copy-done.2
  53.5 0.7 fusion.31
  54.2 1.0 copy-done.5
  55.2 1.6 convolution_convert_fusion.2
  56.8 1.5 convert_element_type.66
  58.3 0.9 copy.28
  59.1 0.0 reduce-scatter.5.cloned.1.call-update
  59.1 0.0 all-reduce.4.cloned.1.call-start
  59.2 7.4 %all-gather.1 = bf16[512,512]{1,0:T(8,128)(2,1)S(1)} all-gather(bf16[128,512]{1,0:T(8,128)(2,1)S(1)} %copy-done.9), channel_id=3, replica_groups=mesh['parts'=2,'patch'=4,'grp'=2,'col'=2] {'grp','col'}, dimensions={0}, use_global_device_ids=true | all-gather | bytes 655360 | tf_op jit(solution)/shard_map/all_gather | solution.py:12
  66.6 0.5 copy.29
  67.2 0.1 copy.31
  67.3 2.3 convolution_convert_fusion
  69.5 4.4 %convolution_convert_fusion.1 = bf16[1024,1024]{1,0:T(8,128)(2,1)} fusion(bf16[256,1024]{1,0:T(8,128)(2,1)S(1)} %bitcast.40, f32[256,1024]{1,0:T(8,128)} %copy-done.5, bf16[256,1024]{1,0:T(8,128)(2,1)S(1)} %bitcast.49, bf16[1024,1024]{1,0:T(8,128)(2,1)S(1)} %copy-done), kind=kOutput, calls=%fused_computation.2 | convolution fusion | flops 1080033280 | bytes 6291456 | tf_op jit(solution)/shard_map/dot_general | solution.py:92
  73.9 0.0 all-reduce.4.cloned.1.call-update
  74.0 8.1 %reduce-scatter.5.cloned.1.call-done = bf16[128,512]{1,0:T(8,128)(2,1)} async-done(((bf16[512,512]{1,0:T(8,128)(2,1)}), bf16[128,512]{1,0:T(8,128)(2,1)}) %reduce-scatter.5.cloned.1.call-update) | async-done | bytes 131088 | tf_op jit(solution)/shard_map/reduce_scatter | solution.py:82
  82.0 1.6 add_convert_fusion
  83.7 156.7 %all-reduce.4.cloned.1.call-done = (bf16[1024,1024]{1,0:T(8,128)(2,1)}, bf16[1024,1024]{1,0:T(8,128)(2,1)}) async-done(((bf16[1024,1024]{1,0:T(8,128)(2,1)}, bf16[1024,1024]{1,0:T(8,128)(2,1)}), (bf16[1024,1024]{1,0:T(8,128)(2,1)}, bf16[1024,1024]{1,0:T(8,128)(2,1)})) %all-reduce.4.cloned.1.call-update) | async-done | bytes 4194320 | tf_op jit(solution)/shard_map/psum | solution.py:99
  240.4 4.2 %convert_element_type.73 = f32[1024,1024]{1,0:T(8,128)} convert(bf16[1024,1024]{1,0:T(8,128)(2,1)} %get-tuple-element.7) | non-fusion elementwise | flops 1048576 | bytes 6291456 | tf_op jit(solution)/shard_map/convert_element_type | solution.py:99
  244.6 2.5 convert_element_type.75
  (14 shorter events, 0.0 us)
Async XLA Ops:
  7.2 48.0 %copy-start = (bf16[1024,1024]{1,0:T(8,128)(2,1)S(1)}, bf16[1024,1024]{1,0:T(8,128)(2,1)}, u32[]{:S(2)}) copy-start(bf16[1024,1024]{1,0:T(8,128)(2,1)} %param.20) | copy-start | bytes 6291460
  7.2 33.6 %reduce-scatter.3.cloned.1.call-start = ((), (), s32[]{:S(2)}) async-start(), calls=%async_computation.2 | async-start | bytes 393216 | tf_op jit(solution)/shard_map/reduce_scatter | solution.py:61
  9.9 9.6 %copy-start.8 = (bf16[128,512]{1,0:T(8,128)(2,1)S(1)}, bf16[128,512]{1,0:T(8,128)(2,1)}, u32[]{:S(2)}) copy-start(bf16[128,512]{1,0:T(8,128)(2,1)} %param.13) | copy-start | bytes 393220
  25.3 4.3 %copy-start.7 = (bf16[512,1024]{1,0:T(8,128)(2,1)S(1)}, bf16[512,1024]{1,0:T(8,128)(2,1)}, u32[]{:S(2)}) copy-start(bf16[512,1024]{1,0:T(8,128)(2,1)} %param.17) | copy-start | bytes 3145732
  25.3 15.5 %copy-start.3 = (bf16[128,512]{1,0:T(8,128)(2,1)S(1)}, bf16[128,512]{1,0:T(8,128)(2,1)}, u32[]{:S(2)}) copy-start(bf16[128,512]{1,0:T(8,128)(2,1)} %param.14) | copy-start | bytes 393220
  25.3 19.0 %copy-start.10 = (f32[512]{0:T(512)S(1)}, f32[512]{0:T(512)}, u32[]{:S(2)}) copy-start(f32[512]{0:T(512)} %param.18) | copy-start | bytes 6148
  31.5 50.5 %reduce-scatter.5.cloned.1.call-start = ((), (), s32[]{:S(2)}) async-start(), calls=%async_computation.3 | async-start | bytes 655360 | tf_op jit(solution)/shard_map/reduce_scatter | solution.py:82
  44.3 9.2 %copy-start.2 = (bf16[1024,1024]{1,0:T(8,128)(2,1)S(1)}, bf16[1024,1024]{1,0:T(8,128)(2,1)}, u32[]{:S(2)}) copy-start(bf16[1024,1024]{1,0:T(8,128)(2,1)} %param.19) | copy-start | bytes 6291460
  54.2 1.0 copy-start.5
  56.8 2.4 copy-start.9
  59.1 181.3 %all-reduce.4.cloned.1.call-start = ((), (), s32[]{:S(2)}) async-start(), calls=%async_computation.4 | async-start | bytes 8388608 | tf_op jit(solution)/shard_map/psum | solution.py:99
  59.2 8.1 %copy-start.6 = (f32[256,1024]{1,0:T(8,128)S(1)}, f32[256,1024]{1,0:T(8,128)}, u32[]{:S(2)}) copy-start(f32[256,1024]{1,0:T(8,128)} %copy-done.5) | copy-start | bytes 3145732
  73.9 8.1 %copy-start.4 = (bf16[128,512]{1,0:T(8,128)(2,1)S(1)}, bf16[128,512]{1,0:T(8,128)(2,1)}, u32[]{:S(2)}) copy-start(bf16[128,512]{1,0:T(8,128)(2,1)} %reduce-scatter.3.cloned.1.call-done) | copy-start | bytes 393220
  240.4 4.2 %copy-start.1 = (bf16[1024,1024]{1,0:T(8,128)(2,1)S(1)}, bf16[1024,1024]{1,0:T(8,128)(2,1)}, u32[]{:S(2)}) copy-start(bf16[1024,1024]{1,0:T(8,128)(2,1)} %get-tuple-element.8) | copy-start | bytes 6291460
Sparse Core Ops, SparseCore 0:
  31.6 9.1 reduce-scatter.2
  59.3 22.7 reduce-scatter.4
  85.0 155.3 all-reduce.3
where the time goes:
time: 254 us
  waiting for transfers between devices  174 us (69%)
  blocking collectives  30.4 us (12%)
  matrix products  17.1 us (7%)
  between operations  14.7 us (6%)
  other arithmetic  11.3 us (4%)
  local copies, waits for them, and re-layouts  5.93 us (2%)
    psum x1, waiting for transfers between devices, shards(): lax.psum(up_local.astype(jnp.bfloat16), 'patch').astype(jnp.float32)  157 us
    all_gather x2, blocking collectives, spread_rows(): lax.all_gather(part_rows[None], ('grp', 'col'), axis=0, tiled=True)  14.8 us
    reduce_scatter x1, waiting for transfers between devices, shards(): lax.psum_scatter(projected.astype(jnp.bfloat16), 'col', scatter_dimension...  9.24 us
    reduce_scatter x1, waiting for transfers between devices, shards(): lax.psum_scatter(partial_out.astype(jnp.bfloat16), ('grp', 'col'), scatte...  8.08 us
    all_gather x1, blocking collectives, shards(): lax.all_gather(key_vectors, 'grp', axis=0, tiled=True)  7.5 us
    all_gather x1, blocking collectives, shards(): lax.all_gather(value_vectors, 'grp', axis=0, tiled=True)  5.63 us
  transfers between devices with their start and end apart: 3, of which 3 were waited for; matrix products, arithmetic and copies ran while one was open for 4% of the time, Pallas kernels for 0%

commit v1 on v0

--- a/solution.py
+++ b/solution.py
@@ -102,9 +102,158 @@
     return (layer_out, up_grad, down_grad)
 
 
+def shift(x, axis, k):
+    n = lax.axis_size(axis)
+    return lax.ppermute(x, axis, [(i, (i + k) % n) for i in range(n)])
+
+
+def spread(piece):
+    chunks = []
+    held = piece
+    for s in range(lax.axis_size("patch")):
+        if s:
+            held = shift(held, "patch", 1)
+        chunks.append([held] + [shift(held, "grp", k) for k in range(1, lax.axis_size("grp"))])
+    return chunks
+
+
+def join(pieces, dim):
+    n = len(pieces)
+    me = lax.axis_index("col")
+    size = pieces[0].shape[dim]
+    shape = list(pieces[0].shape)
+    shape[dim] = size * n
+    whole = jnp.zeros(shape, pieces[0].dtype)
+    for j, piece in enumerate(pieces):
+        start = [0] * len(shape)
+        start[dim] = (me - j + n) % n * size
+        whole = lax.dynamic_update_slice(whole, piece, start)
+    return whole
+
+
+def over_cores(piece, dim):
+    return join([piece] + [shift(piece, "col", j) for j in range(1, lax.axis_size("col"))], dim)
+
+
+def gather_plan(
+    query_vectors,
+    key_vectors,
+    value_vectors,
+    residual,
+    neighbor_ids,
+    neighbor_count,
+    output_weight,
+    norm_gain,
+    up_weight,
+    down_weight,
+    cotangent,
+):
+    cores = lax.axis_size("col")
+    grps = lax.axis_size("grp")
+    me = lax.axis_index("col")
+    row_count = query_vectors.shape[0]
+    half = query_vectors.shape[1]
+    keys = [key_vectors] + [shift(key_vectors, "grp", k) for k in range(1, grps)]
+    values = [value_vectors] + [shift(value_vectors, "grp", k) for k in range(1, grps)]
+    cot_chunks = spread(cotangent)
+    out_weight = over_cores(output_weight, 0)
+    res_rows = over_cores(residual, 1)
+    gain = over_cores(norm_gain, 0)
+
+    local_heads = half // HEAD
+    own = lax.axis_index("grp")
+    slot_ids = jnp.arange(neighbor_ids.shape[1], dtype=jnp.int32)
+    query_heads = query_vectors.reshape(row_count, local_heads, HEAD)
+    scores = []
+    for k in range(grps):
+        seen = jnp.any((neighbor_ids[0] == (own - k + grps) % grps) & (slot_ids < neighbor_count[0]))
+        part = jnp.einsum(
+            "qhd,khd->hqk",
+            query_heads,
+            keys[k].reshape(row_count, local_heads, HEAD),
+            preferred_element_type=jnp.float32,
+        ) * HEAD ** (-0.5)
+        scores.append(jnp.where(seen, part, -1e30))
+    scores = jnp.concatenate(scores, axis=2)
+    largest = jnp.max(scores, axis=2, keepdims=True)
+    weights = jnp.exp(scores - largest)
+    probs = (weights / jnp.sum(weights, axis=2, keepdims=True)).astype(jnp.bfloat16)
+    value_heads = jnp.concatenate(values, axis=0).reshape(-1, local_heads, HEAD)
+    attended = jnp.einsum("hqk,khd->qhd", probs, value_heads, preferred_element_type=jnp.float32)
+    attended = over_cores(attended.astype(jnp.bfloat16).reshape(row_count, -1), 1)
+    stream = res_rows.astype(jnp.float32) + jnp.dot(
+        attended, out_weight, preferred_element_type=jnp.float32
+    )
+    center = jnp.mean(stream, axis=1, keepdims=True)
+    shifted = stream - center
+    spread_sq = jnp.mean(shifted * shifted, axis=1, keepdims=True)
+    normed = (shifted * lax.rsqrt(spread_sq + 1e-05) * gain[None, :]).astype(jnp.bfloat16)
+    own_stream = lax.dynamic_slice(stream, (0, me * half), (row_count, half))
+
+    share = row_count // cores
+    norm_chunks = spread(lax.dynamic_slice(normed, (me * share, 0), (share, normed.shape[1])))
+
+    rows, backs, hiddens, back_pres = [], [], [], []
+    layer_out = None
+    for s, (norm_pieces, cot_pieces) in enumerate(zip(norm_chunks, cot_chunks)):
+        normed_rows = jnp.concatenate(
+            [normed if s == 0 and k == 0 else over_cores(p, 0) for k, p in enumerate(norm_pieces)], 0
+        )
+        back_rows = over_cores(jnp.concatenate(cot_pieces, 0), 1)
+        pre = jnp.dot(normed_rows, up_weight, preferred_element_type=jnp.float32)
+        hidden = jax.nn.gelu(pre).astype(jnp.bfloat16)
+        if s == 0:
+            partial_out = jnp.dot(hidden, down_weight, preferred_element_type=jnp.float32)
+            partial_out = partial_out.astype(jnp.bfloat16)
+            layer_out = own_stream
+            for k in range(grps):
+                for j in range(cores):
+                    piece = lax.dynamic_slice(
+                        partial_out, (k * row_count, (me - j + cores) % cores * half), (row_count, half)
+                    )
+                    if k or j:
+                        piece = lax.ppermute(
+                            piece,
+                            ("grp", "col"),
+                            [
+                                (a * cores + b, (a - k) % grps * cores + (b - j) % cores)
+                                for a in range(grps)
+                                for b in range(cores)
+                            ],
+                        )
+                    layer_out = layer_out + piece.astype(jnp.float32)
+            layer_out = layer_out.astype(jnp.bfloat16)
+        back_hidden = lax.dot_general(
+            back_rows, down_weight, (((1,), (1,)), ((), ())), preferred_element_type=jnp.float32
+        )
+        _, gelu_back = jax.vjp(jax.nn.gelu, pre)
+        back_pres.append(gelu_back(back_hidden)[0].astype(jnp.bfloat16))
+        rows.append(normed_rows)
+        backs.append(back_rows)
+        hiddens.append(hidden)
+    rows, backs, hiddens, back_pres = (
+        jnp.concatenate(a, 0) for a in (rows, backs, hiddens, back_pres)
+    )
+    up_grad = lax.dot_general(
+        rows, back_pres, (((0,), (0,)), ((), ())), preferred_element_type=jnp.float32
+    )
+    down_grad = lax.dot_general(
+        hiddens, backs, (((0,), (0,)), ((), ())), preferred_element_type=jnp.float32
+    )
+    return (layer_out, up_grad, down_grad)
+
+
+def layer(*args):
+    query_vectors, up_weight = args[0], args[8]
+    tokens = query_vectors.shape[0] * lax.axis_size("grp") * lax.axis_size("patch")
+    if tokens <= 2 * up_weight.shape[1]:
+        return gather_plan(*args)
+    return shards(*args)
+
+
 def solution(mesh):
     return jax.shard_map(
-        shards,
+        layer,
         mesh=mesh,
         in_specs=(
             P(("parts", "patch", "grp"), "col"),

time: 254 us -> 96.3 us (0.38)
  waiting for transfers between devices: 174 us -> 30.4 us
  blocking collectives: 30.4 us -> 0 us
  starting transfers between devices: 0.12 us -> 21.9 us
  between operations: 14.7 us -> 2.13 us
  local copies, waits for them, and re-layouts: 5.93 us -> 14.3 us
  other arithmetic: 11.3 us -> 3.65 us
  matrix products: 17.1 us -> 23.5 us
    psum x1 -> x0, waiting for transfers between devices: 157 us -> none  [shards(): lax.psum(up_local.astype(jnp.bfloat16), 'patch').astype(jnp.float32)]
    ppermute x0 -> x34, waiting for transfers between devices: none -> 30.4 us  [the longest x31 30.4 us: shift(): return lax.ppermute(x, axis, [(i, (i + k) % n) for i in range(n)])]
    all_gather x4 -> x0, blocking collectives: 27.9 us -> none  [the longest x2 14.8 us: spread_rows(): lax.all_gather(part_rows[None], ('grp', 'col'), axis=0, tiled=True)]
    ppermute x0 -> x34, starting transfers between devices: none -> 21.9 us  [the longest x31 20 us: shift(): return lax.ppermute(x, axis, [(i, (i + k) % n) for i in range(n)])]
    reduce_scatter x2 -> x0, waiting for transfers between devices: 17.3 us -> none  [the longest x1 9.24 us: shards(): lax.psum_scatter(projected.astype(jnp.bfloat16), 'col', scatter_dimension...]
    convert_element_type x4 -> x1, other arithmetic: 9.47 us -> 0.74 us  [gather_plan(): layer_out = layer_out.astype(jnp.bfloat16)]
    dot_general x7 -> x15, matrix products: 16.5 us -> 23.5 us  [the longest x4 5.6 us: gather_plan(): pre = jnp.dot(normed_rows, up_weight, preferred_element_type=jnp.float32)]
    dynamic_update_slice x0 -> x30, local copies, waits for them, and re-layouts: none -> 6.16 us  [join(): whole = lax.dynamic_update_slice(whole, piece, start)]
  transfers between devices with their start and end apart: 3 -> 34, of which waited for: 3 -> 12; matrix products, arithmetic and copies ran while one was open for 4% -> 28% of each run, Pallas kernels for 0% -> 0%
where the time goes in v1:
time: 96.3 us; the launch traced here: 95.9 us
  waiting for transfers between devices  30.4 us (32%)
  matrix products  23.5 us (24%)
  starting transfers between devices  21.9 us (23%)
  local copies, waits for them, and re-layouts  14.3 us (15%)
  other arithmetic  3.65 us (4%)
  between operations  2.13 us (2%)
    ppermute x31, waiting for transfers between devices, shift(): return lax.ppermute(x, axis, [(i, (i + k) % n) for i in range(n)])  30.4 us
    ppermute x31, starting transfers between devices, shift(): return lax.ppermute(x, axis, [(i, (i + k) % n) for i in range(n)])  20 us
    dynamic_update_slice x30, local copies, waits for them, and re-layouts, join(): whole = lax.dynamic_update_slice(whole, piece, start)  6.16 us
    dot_general x4, matrix products, gather_plan(): pre = jnp.dot(normed_rows, up_weight, preferred_element_type=jnp.float32)  5.6 us
    dot_general x1, matrix products, gather_plan(): lax.dot_general(hiddens, backs, (((0,), (0,)), ((), ())), preferred_eleme...  4.4 us
    dot_general x1, matrix products, gather_plan(): lax.dot_general(rows, back_pres, (((0,), (0,)), ((), ())), preferred_elem...  4.4 us
    unnamed x22, local copies, waits for them, and re-layouts  4.11 us
    dot_general x4, matrix products, gather_plan(): lax.dot_general(back_rows, down_weight, (((1,), (1,)), ((), ())), preferr...  3.19 us
  transfers between devices with their start and end apart: 34, of which 12 were waited for; matrix products, arithmetic and copies ran while one was open for 28% of the time, Pallas kernels for 0%

profile of v1, /device:TPU:0, one launch (start us, length us, event | category | flops | bytes accessed | tf_op | source)
XLA Modules:
  0.0 95.9 jit_solution(8924259061333275357)
XLA Ops:
  0.6 3.0 %collective-permute-start.23 = (bf16[128,512]{1,0:T(8,128)(2,1)}, bf16[128,512]{1,0:T(8,128)(2,1)S(1)}, u32[]{:S(2)}, u32[]{:S(2)}) collective-permute-start(bf16[128,512]{1,0:T(8,128)(2,1)} %param.21), channel_id=1, source_target_pairs={{0,2},{2,0},{1,3},{3,1},{4,6},{6,4},{5,7},{7,5},{8,10},{10,8},{9,1... | collective-permute-start | bytes 393224 | tf_op jit(solution)/shard_map/ppermute | solution.py:107
  4.2 1.9 %collective-permute-start.2 = (bf16[128,512]{1,0:T(8,128)(2,1)}, bf16[128,512]{1,0:T(8,128)(2,1)}, u32[]{:S(2)}, u32[]{:S(2)}) collective-permute-start(bf16[128,512]{1,0:T(8,128)(2,1)} %param.12), channel_id=1, source_target_pairs={{0,2},{2,0},{1,3},{3,1},{4,6},{6,4},{5,7},{7,5},{8,10},{10,8},{9,1... | collective-permute-start | bytes 393224 | tf_op jit(solution)/shard_map/ppermute | solution.py:107
  6.2 1.1 %copy.24 = bf16[128,512]{0,1:T(8,128)(2,1)S(1)} copy(bf16[128,512]{1,0:T(8,128)(2,1)} %param.12) | data formatting | bytes 262144 | tf_op args[1]
  7.3 1.0 %copy.23 = bf16[128,512]{0,1:T(8,128)(2,1)S(1)} copy(bf16[128,512]{1,0:T(8,128)(2,1)} %param.11) | data formatting | bytes 262144 | tf_op args[0]
  9.0 1.4 %fusion.72 = (pred[]{:T(512)}, pred[]{:T(512)}) fusion(s32[1,2]{1,0:T(1,128)} %param.15, s32[]{:T(128)} %bitcast.38, s32[]{:T(128)S(6)} %select_n.149, s32[]{:T(128)S(6)} %select_n.152), kind=kLoop, calls=%fused_computation.143 | loop fusion | flops 12 | bytes 22 | tf_op jit(solution)/shard_map/reduce_or | solution.py:169
  10.4 0.9 fusion.81
  11.3 1.6 %broadcast_in_dim.8 = bf16[1024,1024]{1,0:T(8,128)(2,1)} broadcast(bf16[]{:T(256)} %constant.127.clone.1), dimensions={} | broadcast | bytes 2097154 | tf_op jit(solution)/shard_map/broadcast_in_dim | solution.py:126
  12.9 1.0 %constant_dynamic-update-slice_fusion.39 = bf16[1024,1024]{1,0:T(8,128)(2,1)} fusion(bf16[1024,1024]{1,0:T(8,128)(2,1)} %broadcast_in_dim.8, bf16[512,1024]{1,0:T(8,128)(2,1)S(1)} %copy-done.2, s32[]{:T(128)S(6)} %select_n.146), kind=kLoop, calls=%fused_computation.135 | loop fusion | bytes 2097156 | tf_op jit(solution)/shard_map/dynamic_update_slice | solution.py:130
  13.9 0.9 constant_dynamic-update-slice_fusion.9
  15.5 1.6 %collective-permute-start.25 = (bf16[128,512]{1,0:T(8,128)(2,1)}, bf16[128,512]{1,0:T(8,128)(2,1)}, u32[]{:S(2)}, u32[]{:S(2)}) collective-permute-start(bf16[128,512]{1,0:T(8,128)(2,1)} %param.21), channel_id=1, source_target_pairs={{0,4},{4,8},{8,12},{12,0},{1,5},{5,9},{9,13},{13,1},{2,6},{6,10},{... | collective-permute-start | bytes 393224 | tf_op jit(solution)/shard_map/ppermute | solution.py:107
  17.4 1.0 %pad_maximum_fusion = bf16[256,512]{1,0:T(8,128)(2,1)S(1)} fusion(bf16[128,512]{1,0:T(8,128)(2,1)} %collective-permute-done.1, bf16[128,512]{1,0:T(8,128)(2,1)} %param.13), kind=kLoop, calls=%fused_computation.92 | loop fusion | flops 524288 | bytes 524288 | tf_op jit(solution)/shard_map/concatenate | solution.py:181
  18.4 0.8 copy.22
  19.2 1.0 %copy.25 = bf16[128,512]{0,1:T(8,128)(2,1)S(1)} copy(bf16[128,512]{1,0:T(8,128)(2,1)} %collective-permute-done.2) | data formatting | bytes 262144 | tf_op jit(solution)/shard_map/ppermute | solution.py:107
  20.2 0.8 fusion.82
  21.2 1.3 %convolution_convert_fusion.1 = bf16[8,64,128]{2,1,0:T(8,128)(2,1)S(1)} fusion(bf16[256,8,64]{0,2,1:T(8,128)(2,1)} %bitcast.43, f32[8,128,128]{1,2,0:T(8,128)S(1)} %get-tuple-element.23, f32[8,128,128]{1,2,0:T(8,128)S(1)} %get-tuple-element.21, f32[8,128]{1,0:T(8,128)S(1)} %fusion.54, f32[8,128]{1,0:T(8,128)S(1)} %reduce_max.22), kind=kOutput, calls=%fused_computation.36 | convolution fusion | flops 34668544 | bytes 1449984 | tf_op jit(solution)/shard_map/hqk,khd->qhd/dot_general | solution.py:182
  24.1 0.9 constant_dynamic-update-slice_fusion.11
  25.0 1.4 %collective-permute-start.28 = (bf16[128,512]{1,0:T(8,128)(2,1)}, bf16[128,512]{1,0:T(8,128)(2,1)S(1)}, u32[]{:S(2)}, u32[]{:S(2)}) collective-permute-start(bf16[128,512]{1,0:T(8,128)(2,1)} %collective-permute-done.25), channel_id=1, source_target_pairs={{0,4},{4,8},{8,12},{12,0},{1,5},{5,9},{9,13},{13,1},{2,6},{6,10},{... | collective-permute-start | bytes 393224 | tf_op jit(solution)/shard_map/ppermute | solution.py:107
  26.4 0.9 constant_dynamic-update-slice_fusion.42
  27.3 1.7 %collective-permute-done.26 = bf16[128,512]{1,0:T(8,128)(2,1)S(1)} collective-permute-done((bf16[128,512]{1,0:T(8,128)(2,1)}, bf16[128,512]{1,0:T(8,128)(2,1)S(1)}, u32[]{:S(2)}, u32[]{:S(2)}) %collective-permute-start.26) | collective-permute-done | bytes 131104 | tf_op jit(solution)/shard_map/ppermute | solution.py:107
  29.2 3.0 %collective-permute-done.28 = bf16[128,512]{1,0:T(8,128)(2,1)S(1)} collective-permute-done((bf16[128,512]{1,0:T(8,128)(2,1)}, bf16[128,512]{1,0:T(8,128)(2,1)S(1)}, u32[]{:S(2)}, u32[]{:S(2)}) %collective-permute-start.28) | collective-permute-done | bytes 131104 | tf_op jit(solution)/shard_map/ppermute | solution.py:107
  32.2 1.6 %collective-permute-start.29 = (bf16[128,512]{1,0:T(8,128)(2,1)S(1)}, bf16[128,512]{1,0:T(8,128)(2,1)S(1)}, u32[]{:S(2)}, u32[]{:S(2)}) collective-permute-start(bf16[128,512]{1,0:T(8,128)(2,1)S(1)} %collective-permute-done.28), channel_id=1, source_target_pairs={{0,2},{2,0},{1,3},{3,1},{4,6},{6,4},{5,7},{7,5},{8,10},{10,8},{9,1... | collective-permute-start | bytes 393224 | tf_op jit(solution)/shard_map/ppermute | solution.py:107
  33.8 3.4 %collective-permute-done.29 = bf16[128,512]{1,0:T(8,128)(2,1)S(1)} collective-permute-done((bf16[128,512]{1,0:T(8,128)(2,1)S(1)}, bf16[128,512]{1,0:T(8,128)(2,1)S(1)}, u32[]{:S(2)}, u32[]{:S(2)}) %collective-permute-start.29) | collective-permute-done | bytes 131104 | tf_op jit(solution)/shard_map/ppermute | solution.py:107
  37.3 1.0 %constant_dynamic-update-slice_fusion.21 = bf16[256,1024]{1,0:T(8,128)(2,1)S(1)} fusion(bf16[256,1024]{1,0:T(8,128)(2,1)S(1)} %constant_dynamic-update-slice_fusion.22, bf16[256,512]{1,0:T(8,128)(2,1)} %collective-permute-done.24, s32[]{:T(128)S(6)} %select_n.148), kind=kLoop, calls=%fused_computation.115 | loop fusion | bytes 524292 | tf_op jit(solution)/shard_map/dynamic_update_slice | solution.py:130
  38.3 0.8 fusion.83
  39.1 1.6 %collective-permute-start.32 = (bf16[128,512]{1,0:T(8,128)(2,1)S(1)}, bf16[128,512]{1,0:T(8,128)(2,1)S(1)}, u32[]{:S(2)}, u32[]{:S(2)}) collective-permute-start(bf16[128,512]{1,0:T(8,128)(2,1)S(1)} %collective-permute-done.31), channel_id=1, source_target_pairs={{0,2},{2,0},{1,3},{3,1},{4,6},{6,4},{5,7},{7,5},{8,10},{10,8},{9,1... | collective-permute-start | bytes 393224 | tf_op jit(solution)/shard_map/ppermute | solution.py:107
  40.8 4.3 %collective-permute-done.32 = bf16[128,512]{1,0:T(8,128)(2,1)S(1)} collective-permute-done((bf16[128,512]{1,0:T(8,128)(2,1)S(1)}, bf16[128,512]{1,0:T(8,128)(2,1)S(1)}, u32[]{:S(2)}, u32[]{:S(2)}) %collective-permute-start.32) | collective-permute-done | bytes 131104 | tf_op jit(solution)/shard_map/ppermute | solution.py:107
  45.3 0.8 fusion.84
  46.2 0.8 fusion.85
  47.0 2.3 %constant_dynamic-update-slice_fusion.38 = bf16[1024,1024]{1,0:T(8,128)(2,1)} fusion(bf16[1024,1024]{1,0:T(8,128)(2,1)} %constant_dynamic-update-slice_fusion.39, bf16[512,1024]{1,0:T(8,128)(2,1)} %collective-permute-done.4, s32[]{:T(128)S(6)} %select_n.148), kind=kLoop, calls=%fused_computation.134 | loop fusion | bytes 2097156 | tf_op jit(solution)/shard_map/dynamic_update_slice | solution.py:130
  49.3 2.1 %fusion.80 = (f32[128]{0:T(128)S(1)}, f32[128,1024]{1,0:T(8,128)S(1)}) fusion(bf16[128,1024]{1,0:T(8,128)(2,1)S(1)} %constant_dynamic-update-slice_fusion.42, bf16[128,1024]{1,0:T(8,128)(2,1)S(1)} %constant_dynamic-update-slice_fusion.40, bf16[1024,1024]{1,0:T(8,128)(2,1)} %constant_dynamic-update-slice_fusion.38), kind=kOutput, calls=%fused_computation.155 | convolution fusion | flops 268828544 | bytes 3146240 | tf_op jit(solution)/shard_map/dot_general | solution.py:184
  51.8 1.6 %collective-permute-start.6 = (bf16[64,1024]{1,0:T(8,128)(2,1)S(1)}, bf16[64,1024]{1,0:T(8,128)(2,1)S(1)}, u32[]{:S(2)}, u32[]{:S(2)}) collective-permute-start(bf16[64,1024]{1,0:T(8,128)(2,1)S(1)} %constant_dynamic-slice_fusion.1), channel_id=1, source_target_pairs={{0,2},{2,0},{1,3},{3,1},{4,6},{6,4},{5,7},{7,5},{8,10},{10,8},{9,1... | collective-permute-start | bytes 393224 | tf_op jit(solution)/shard_map/ppermute | solution.py:107
  53.4 1.3 %collective-permute-start.11 = (bf16[64,1024]{1,0:T(8,128)(2,1)S(1)}, bf16[64,1024]{1,0:T(8,128)(2,1)S(1)}, u32[]{:S(2)}, u32[]{:S(2)}) collective-permute-start(bf16[64,1024]{1,0:T(8,128)(2,1)S(1)} %constant_dynamic-slice_fusion.1), channel_id=1, source_target_pairs={{0,4},{4,8},{8,12},{12,0},{1,5},{5,9},{9,13},{13,1},{2,6},{6,10},{... | collective-permute-start | bytes 393224 | tf_op jit(solution)/shard_map/ppermute | solution.py:107
  55.5 5.5 %collective-permute-done.11 = bf16[64,1024]{1,0:T(8,128)(2,1)S(1)} collective-permute-done((bf16[64,1024]{1,0:T(8,128)(2,1)S(1)}, bf16[64,1024]{1,0:T(8,128)(2,1)S(1)}, u32[]{:S(2)}, u32[]{:S(2)}) %collective-permute-start.11) | collective-permute-done | bytes 131104 | tf_op jit(solution)/shard_map/ppermute | solution.py:107
  62.0 1.0 %collective-permute-done.7 = bf16[64,1024]{1,0:T(8,128)(2,1)S(1)} collective-permute-done((bf16[64,1024]{1,0:T(8,128)(2,1)S(1)}, bf16[64,1024]{1,0:T(8,128)(2,1)S(1)}, u32[]{:S(2)}, u32[]{:S(2)}) %collective-permute-start.7) | collective-permute-done | bytes 131104 | tf_op jit(solution)/shard_map/ppermute | solution.py:107
  63.0 1.4 %fusion.31 = (bf16[256,1024]{1,0:T(8,128)(2,1)S(1)}, bf16[256,1024]{1,0:T(8,128)(2,1)S(1)}) fusion(f32[256,1024]{1,0:T(8,128)S(1)} %fusion.83, bf16[1024,1024]{1,0:T(8,128)(2,1)S(1)} %copy-done, bf16[128,1024]{1,0:T(8,128)(2,1)S(1)} %constant_dynamic-update-slice_fusion.36, bf16[128,1024]{1,0:T(8,128)(2,1)S(1)} %get-tuple-element.6), kind=kOutput, calls=%fused_computation.43 | convolution fusion | flops 543686656 | bytes 4718592 | tf_op jit(solution)/shard_map/dot_general | solution.py:203
  65.2 1.4 %collective-permute-start.10 = (bf16[128,512]{1,0:T(8,128)(2,1)S(1)}, bf16[128,512]{1,0:T(8,128)(2,1)S(1)}, u32[]{:S(2)}, u32[]{:S(2)}) collective-permute-start(bf16[128,512]{1,0:T(8,128)(2,1)S(1)} %get-tuple-element.18), channel_id=1, source_target_pairs={{0,3},{1,2},{2,1},{3,0},{4,7},{5,6},{6,5},{7,4},{8,11},{9,10},{10,... | collective-permute-start | bytes 393224 | tf_op jit(solution)/shard_map/ppermute | solution.py:215
  67.2 1.9 %collective-permute-done.15 = bf16[64,1024]{1,0:T(8,128)(2,1)S(1)} collective-permute-done((bf16[64,1024]{1,0:T(8,128)(2,1)S(1)}, bf16[64,1024]{1,0:T(8,128)(2,1)S(1)}, u32[]{:S(2)}, u32[]{:S(2)}) %collective-permute-start.15) | collective-permute-done | bytes 131104 | tf_op jit(solution)/shard_map/ppermute | solution.py:107
  69.1 1.6 %collective-permute-start.17 = (bf16[64,1024]{1,0:T(8,128)(2,1)S(1)}, bf16[64,1024]{1,0:T(8,128)(2,1)S(1)}, u32[]{:S(2)}, u32[]{:S(2)}) collective-permute-start(bf16[64,1024]{1,0:T(8,128)(2,1)S(1)} %collective-permute-done.15), channel_id=1, source_target_pairs={{0,2},{2,0},{1,3},{3,1},{4,6},{6,4},{5,7},{7,5},{8,10},{10,8},{9,1... | collective-permute-start | bytes 393224 | tf_op jit(solution)/shard_map/ppermute | solution.py:107
  71.0 1.4 %multiply_convert_fusion.2 = (bf16[256,1024]{1,0:T(8,128)(2,1)S(1)}, bf16[256,1024]{1,0:T(8,128)(2,1)S(1)}) fusion(f32[256,1024]{1,0:T(8,128)S(1)} %fusion.84, bf16[1024,1024]{1,0:T(8,128)(2,1)S(1)} %copy-done, bf16[128,1024]{1,0:T(8,128)(2,1)S(1)} %constant_dynamic-update-slice_fusion.31, bf16[128,1024]{1,0:T(8,128)(2,1)S(1)} %constant_dynamic-update-slice_fusion.33), kind=kOutput, calls=%fused_computation.69 | convolution fusion | flops 543686656 | bytes 4718592 | tf_op jit(solution)/shard_map/dot_general | solution.py:203
  72.4 4.2 %collective-permute-done.17 = bf16[64,1024]{1,0:T(8,128)(2,1)S(1)} collective-permute-done((bf16[64,1024]{1,0:T(8,128)(2,1)S(1)}, bf16[64,1024]{1,0:T(8,128)(2,1)S(1)}, u32[]{:S(2)}, u32[]{:S(2)}) %collective-permute-start.17) | collective-permute-done | bytes 131104 | tf_op jit(solution)/shard_map/ppermute | solution.py:107
  77.3 1.1 %collective-permute-done.19 = bf16[64,1024]{1,0:T(8,128)(2,1)S(1)} collective-permute-done((bf16[64,1024]{1,0:T(8,128)(2,1)S(1)}, bf16[64,1024]{1,0:T(8,128)(2,1)S(1)}, u32[]{:S(2)}, u32[]{:S(2)}) %collective-permute-start.19) | collective-permute-done | bytes 131104 | tf_op jit(solution)/shard_map/ppermute | solution.py:107
  78.4 0.8 collective-permute-start.21
  80.2 1.4 %multiply_convert_fusion.1 = (bf16[256,1024]{1,0:T(8,128)(2,1)S(1)}, bf16[256,1024]{1,0:T(8,128)(2,1)S(1)}) fusion(f32[256,1024]{1,0:T(8,128)S(1)} %fusion.85, bf16[1024,1024]{1,0:T(8,128)(2,1)S(1)} %copy-done, bf16[128,1024]{1,0:T(8,128)(2,1)S(1)} %constant_dynamic-update-slice_fusion.27, bf16[128,1024]{1,0:T(8,128)(2,1)S(1)} %constant_dynamic-update-slice_fusion.29), kind=kOutput, calls=%fused_computation.68 | convolution fusion | flops 543686656 | bytes 4718592 | tf_op jit(solution)/shard_map/dot_general | solution.py:203
  81.6 2.8 %collective-permute-done.21 = bf16[64,1024]{1,0:T(8,128)(2,1)S(1)} collective-permute-done((bf16[64,1024]{1,0:T(8,128)(2,1)S(1)}, bf16[64,1024]{1,0:T(8,128)(2,1)S(1)}, u32[]{:S(2)}, u32[]{:S(2)}) %collective-permute-start.21) | collective-permute-done | bytes 131104 | tf_op jit(solution)/shard_map/ppermute | solution.py:107
  84.5 1.2 %collective-permute-done.22 = bf16[64,1024]{1,0:T(8,128)(2,1)S(1)} collective-permute-done((bf16[64,1024]{1,0:T(8,128)(2,1)S(1)}, bf16[64,1024]{1,0:T(8,128)(2,1)S(1)}, u32[]{:S(2)}, u32[]{:S(2)}) %collective-permute-start.22) | collective-permute-done | bytes 131104 | tf_op jit(solution)/shard_map/ppermute | solution.py:107
  85.7 1.4 %multiply_convert_fusion = (bf16[256,1024]{1,0:T(8,128)(2,1)S(1)}, bf16[256,1024]{1,0:T(8,128)(2,1)S(1)}) fusion(f32[256,1024]{1,0:T(8,128)S(1)} %fusion.86, bf16[1024,1024]{1,0:T(8,128)(2,1)S(1)} %copy-done, bf16[128,1024]{1,0:T(8,128)(2,1)S(1)} %constant_dynamic-update-slice_fusion.23, bf16[128,1024]{1,0:T(8,128)(2,1)S(1)} %constant_dynamic-update-slice_fusion.25), kind=kOutput, calls=%fused_computation.67 | convolution fusion | flops 543686656 | bytes 4718592 | tf_op jit(solution)/shard_map/dot_general | solution.py:203
  87.1 4.4 %fusion.8 = f32[1024,1024]{1,0:T(8,128)} fusion(bf16[256,1024]{1,0:T(8,128)(2,1)S(1)} %get-tuple-element.13, bf16[256,1024]{1,0:T(8,128)(2,1)S(1)} %get-tuple-element.11, bf16[256,1024]{1,0:T(8,128)(2,1)S(1)} %get-tuple-element.9, bf16[256,1024]{1,0:T(8,128)(2,1)S(1)} %get-tuple-element.16, bf16[256,1024]{1,0:T(8,128)(2,1)S(1)} %constant_dynamic-update-slice_fusion.35, ...), kind=kOutput, calls=%fused_computation.8 | convolution fusion | flops 2164260864 | bytes 8388608 | tf_op jit(solution)/shard_map/dot_general | solution.py:240
  91.5 4.4 %fusion = f32[1024,1024]{1,0:T(8,128)} fusion(bf16[1024,1024]{1,0:T(8,128)(2,1)S(1)} %constant_dynamic-update-slice_fusion, bf16[256,1024]{1,0:T(8,128)(2,1)S(1)} %get-tuple-element.14, bf16[256,1024]{1,0:T(8,128)(2,1)S(1)} %get-tuple-element.12, bf16[256,1024]{1,0:T(8,128)(2,1)S(1)} %get-tuple-element.10, bf16[256,1024]{1,0:T(8,128)(2,1)S(1)} %get-tuple-element.15), kind=kOutput, calls=%fused_computation | convolution fusion | flops 2155872256 | bytes 8388608 | tf_op jit(solution)/shard_map/dot_general | solution.py:237
  (121 shorter events, 9.1 us)
Async XLA Ops:
  0.6 62.4 %copy-start = (bf16[1024,1024]{1,0:T(8,128)(2,1)S(1)}, bf16[1024,1024]{1,0:T(8,128)(2,1)}, u32[]{:S(2)}) copy-start(bf16[1024,1024]{1,0:T(8,128)(2,1)} %param.19) | copy-start | bytes 6291460
  0.6 14.9 %collective-permute-start.23 = (bf16[128,512]{1,0:T(8,128)(2,1)}, bf16[128,512]{1,0:T(8,128)(2,1)S(1)}, u32[]{:S(2)}, u32[]{:S(2)}) collective-permute-start(bf16[128,512]{1,0:T(8,128)(2,1)} %param.21), channel_id=1, source_target_pairs={{0,2},{2,0},{1,3},{3,1},{4,6},{6,4},{5,7},{7,5},{8,10},{10,8},{9,1... | collective-permute-start | bytes 393224 | tf_op jit(solution)/shard_map/ppermute | solution.py:107
  3.6 11.6 %collective-permute-start.5 = (f32[512]{0:T(512)}, f32[512]{0:T(512)S(1)}, u32[]{:S(2)}, u32[]{:S(2)}) collective-permute-start(f32[512]{0:T(512)} %param.18), channel_id=1, source_target_pairs={{0,1},{1,0},{2,3},{3,2},{4,5},{5,4},{6,7},{7,6},{8,9},{9,8},{10,11... | collective-permute-start | bytes 6152 | tf_op jit(solution)/shard_map/ppermute | solution.py:107
  3.7 21.4 %collective-permute-start = (bf16[128,512]{1,0:T(8,128)(2,1)}, bf16[128,512]{1,0:T(8,128)(2,1)}, u32[]{:S(2)}, u32[]{:S(2)}) collective-permute-start(bf16[128,512]{1,0:T(8,128)(2,1)} %param.14), channel_id=1, source_target_pairs={{0,1},{1,0},{2,3},{3,2},{4,5},{5,4},{6,7},{7,6},{8,9},{9,8},{10,11... | collective-permute-start | bytes 393224 | tf_op jit(solution)/shard_map/ppermute | solution.py:107
  4.2 13.0 %collective-permute-start.1 = (bf16[128,512]{1,0:T(8,128)(2,1)}, bf16[128,512]{1,0:T(8,128)(2,1)}, u32[]{:S(2)}, u32[]{:S(2)}) collective-permute-start(bf16[128,512]{1,0:T(8,128)(2,1)} %param.13), channel_id=1, source_target_pairs={{0,2},{2,0},{1,3},{3,1},{4,6},{6,4},{5,7},{7,5},{8,10},{10,8},{9,1... | collective-permute-start | bytes 393224 | tf_op jit(solution)/shard_map/ppermute | solution.py:107
  4.2 15.0 %collective-permute-start.2 = (bf16[128,512]{1,0:T(8,128)(2,1)}, bf16[128,512]{1,0:T(8,128)(2,1)}, u32[]{:S(2)}, u32[]{:S(2)}) collective-permute-start(bf16[128,512]{1,0:T(8,128)(2,1)} %param.12), channel_id=1, source_target_pairs={{0,2},{2,0},{1,3},{3,1},{4,6},{6,4},{5,7},{7,5},{8,10},{10,8},{9,1... | collective-permute-start | bytes 393224 | tf_op jit(solution)/shard_map/ppermute | solution.py:107
  9.0 3.9 %copy-start.2 = (bf16[512,1024]{1,0:T(8,128)(2,1)S(1)}, bf16[512,1024]{1,0:T(8,128)(2,1)}, u32[]{:S(2)}) copy-start(bf16[512,1024]{1,0:T(8,128)(2,1)} %param.17) | copy-start | bytes 3145732
  11.3 3.6 %copy-start.3 = (bf16[128,512]{1,0:T(8,128)(2,1)S(1)}, bf16[128,512]{1,0:T(8,128)(2,1)}, u32[]{:S(2)}) copy-start(bf16[128,512]{1,0:T(8,128)(2,1)} %param.14) | copy-start | bytes 393220
  11.3 3.7 %copy-start.4 = (f32[512]{0:T(512)S(1)}, f32[512]{0:T(512)}, u32[]{:S(2)}) copy-start(f32[512]{0:T(512)} %param.18) | copy-start | bytes 6148
  15.2 31.8 %collective-permute-start.4 = (bf16[512,1024]{1,0:T(8,128)(2,1)}, bf16[512,1024]{1,0:T(8,128)(2,1)}, u32[]{:S(2)}, u32[]{:S(2)}) collective-permute-start(bf16[512,1024]{1,0:T(8,128)(2,1)} %param.17), channel_id=1, source_target_pairs={{0,1},{1,0},{2,3},{3,2},{4,5},{5,4},{6,7},{7,6},{8,9},{9,8},{10,11... | collective-permute-start | bytes 3145736 | tf_op jit(solution)/shard_map/ppermute | solution.py:107
  15.5 8.0 %collective-permute-start.25 = (bf16[128,512]{1,0:T(8,128)(2,1)}, bf16[128,512]{1,0:T(8,128)(2,1)}, u32[]{:S(2)}, u32[]{:S(2)}) collective-permute-start(bf16[128,512]{1,0:T(8,128)(2,1)} %param.21), channel_id=1, source_target_pairs={{0,4},{4,8},{8,12},{12,0},{1,5},{5,9},{9,13},{13,1},{2,6},{6,10},{... | collective-permute-start | bytes 393224 | tf_op jit(solution)/shard_map/ppermute | solution.py:107
  17.1 20.1 %collective-permute-start.24 = (bf16[256,512]{1,0:T(8,128)(2,1)S(1)}, bf16[256,512]{1,0:T(8,128)(2,1)}, u32[]{:S(2)}, u32[]{:S(2)}) collective-permute-start(bf16[256,512]{1,0:T(8,128)(2,1)S(1)} %constant_dynamic-update-slice_fusion.8), channel_id=1, source_target_pairs={{0,1},{1,0},{2,3},{3,2},{4,5},{5,4},{6,7},{7,6},{8,9},{9,8},{10,11... | collective-permute-start | bytes 786440 | tf_op jit(solution)/shard_map/ppermute | solution.py:107
  22.7 15.5 %copy-start.1 = (bf16[1024,1024]{1,0:T(8,128)(2,1)S(1)}, bf16[1024,1024]{1,0:T(8,128)(2,1)}, u32[]{:S(2)}) copy-start(bf16[1024,1024]{1,0:T(8,128)(2,1)} %param.20) | copy-start | bytes 6291460
  22.8 9.4 %collective-permute-start.3 = (bf16[128,512]{1,0:T(8,128)(2,1)S(1)}, bf16[128,512]{1,0:T(8,128)(2,1)S(1)}, u32[]{:S(2)}, u32[]{:S(2)}) collective-permute-start(bf16[128,512]{1,0:T(8,128)(2,1)S(1)} %copy.27), channel_id=1, source_target_pairs={{0,1},{1,0},{2,3},{3,2},{4,5},{5,4},{6,7},{7,6},{8,9},{9,8},{10,11... | collective-permute-start | bytes 393224 | tf_op jit(solution)/shard_map/ppermute | solution.py:107
  23.5 5.5 %collective-permute-start.26 = (bf16[128,512]{1,0:T(8,128)(2,1)}, bf16[128,512]{1,0:T(8,128)(2,1)S(1)}, u32[]{:S(2)}, u32[]{:S(2)}) collective-permute-start(bf16[128,512]{1,0:T(8,128)(2,1)} %collective-permute-done.25), channel_id=1, source_target_pairs={{0,2},{2,0},{1,3},{3,1},{4,6},{6,4},{5,7},{7,5},{8,10},{10,8},{9,1... | collective-permute-start | bytes 393224 | tf_op jit(solution)/shard_map/ppermute | solution.py:107
  25.0 7.1 %collective-permute-start.28 = (bf16[128,512]{1,0:T(8,128)(2,1)}, bf16[128,512]{1,0:T(8,128)(2,1)S(1)}, u32[]{:S(2)}, u32[]{:S(2)}) collective-permute-start(bf16[128,512]{1,0:T(8,128)(2,1)} %collective-permute-done.25), channel_id=1, source_target_pairs={{0,4},{4,8},{8,12},{12,0},{1,5},{5,9},{9,13},{13,1},{2,6},{6,10},{... | collective-permute-start | bytes 393224 | tf_op jit(solution)/shard_map/ppermute | solution.py:107
  29.1 16.2 %collective-permute-start.27 = (bf16[256,512]{1,0:T(8,128)(2,1)S(1)}, bf16[256,512]{1,0:T(8,128)(2,1)S(1)}, u32[]{:S(2)}, u32[]{:S(2)}) collective-permute-start(bf16[256,512]{1,0:T(8,128)(2,1)S(1)} %constant_dynamic-update-slice_fusion.10), channel_id=1, source_target_pairs={{0,1},{1,0},{2,3},{3,2},{4,5},{5,4},{6,7},{7,6},{8,9},{9,8},{10,11... | collective-permute-start | bytes 786440 | tf_op jit(solution)/shard_map/ppermute | solution.py:107
  32.1 7.0 %collective-permute-start.31 = (bf16[128,512]{1,0:T(8,128)(2,1)S(1)}, bf16[128,512]{1,0:T(8,128)(2,1)S(1)}, u32[]{:S(2)}, u32[]{:S(2)}) collective-permute-start(bf16[128,512]{1,0:T(8,128)(2,1)S(1)} %collective-permute-done.28), channel_id=1, source_target_pairs={{0,4},{4,8},{8,12},{12,0},{1,5},{5,9},{9,13},{13,1},{2,6},{6,10},{... | collective-permute-start | bytes 393224 | tf_op jit(solution)/shard_map/ppermute | solution.py:107
  32.2 5.0 %collective-permute-start.29 = (bf16[128,512]{1,0:T(8,128)(2,1)S(1)}, bf16[128,512]{1,0:T(8,128)(2,1)S(1)}, u32[]{:S(2)}, u32[]{:S(2)}) collective-permute-start(bf16[128,512]{1,0:T(8,128)(2,1)S(1)} %collective-permute-done.28), channel_id=1, source_target_pairs={{0,2},{2,0},{1,3},{3,1},{4,6},{6,4},{5,7},{7,5},{8,10},{10,8},{9,1... | collective-permute-start | bytes 393224 | tf_op jit(solution)/shard_map/ppermute | solution.py:107
  37.2 8.9 %collective-permute-start.30 = (bf16[256,512]{1,0:T(8,128)(2,1)S(1)}, bf16[256,512]{1,0:T(8,128)(2,1)S(1)}, u32[]{:S(2)}, u32[]{:S(2)}) collective-permute-start(bf16[256,512]{1,0:T(8,128)(2,1)S(1)} %constant_dynamic-update-slice_fusion.12), channel_id=1, source_target_pairs={{0,1},{1,0},{2,3},{3,2},{4,5},{5,4},{6,7},{7,6},{8,9},{9,8},{10,11... | collective-permute-start | bytes 786440 | tf_op jit(solution)/shard_map/ppermute | solution.py:107
  39.1 6.0 %collective-permute-start.32 = (bf16[128,512]{1,0:T(8,128)(2,1)S(1)}, bf16[128,512]{1,0:T(8,128)(2,1)S(1)}, u32[]{:S(2)}, u32[]{:S(2)}) collective-permute-start(bf16[128,512]{1,0:T(8,128)(2,1)S(1)} %collective-permute-done.31), channel_id=1, source_target_pairs={{0,2},{2,0},{1,3},{3,1},{4,6},{6,4},{5,7},{7,5},{8,10},{10,8},{9,1... | collective-permute-start | bytes 393224 | tf_op jit(solution)/shard_map/ppermute | solution.py:107
  45.1 1.9 %collective-permute-start.33 = (bf16[256,512]{1,0:T(8,128)(2,1)S(1)}, bf16[256,512]{1,0:T(8,128)(2,1)S(1)}, u32[]{:S(2)}, u32[]{:S(2)}) collective-permute-start(bf16[256,512]{1,0:T(8,128)(2,1)S(1)} %constant_dynamic-update-slice_fusion.14), channel_id=1, source_target_pairs={{0,1},{1,0},{2,3},{3,2},{4,5},{5,4},{6,7},{7,6},{8,9},{9,8},{10,11... | collective-permute-start | bytes 786440 | tf_op jit(solution)/shard_map/ppermute | solution.py:107
  51.8 9.8 %collective-permute-start.6 = (bf16[64,1024]{1,0:T(8,128)(2,1)S(1)}, bf16[64,1024]{1,0:T(8,128)(2,1)S(1)}, u32[]{:S(2)}, u32[]{:S(2)}) collective-permute-start(bf16[64,1024]{1,0:T(8,128)(2,1)S(1)} %constant_dynamic-slice_fusion.1), channel_id=1, source_target_pairs={{0,2},{2,0},{1,3},{3,1},{4,6},{6,4},{5,7},{7,5},{8,10},{10,8},{9,1... | collective-permute-start | bytes 393224 | tf_op jit(solution)/shard_map/ppermute | solution.py:107
  53.4 7.7 %collective-permute-start.11 = (bf16[64,1024]{1,0:T(8,128)(2,1)S(1)}, bf16[64,1024]{1,0:T(8,128)(2,1)S(1)}, u32[]{:S(2)}, u32[]{:S(2)}) collective-permute-start(bf16[64,1024]{1,0:T(8,128)(2,1)S(1)} %constant_dynamic-slice_fusion.1), channel_id=1, source_target_pairs={{0,4},{4,8},{8,12},{12,0},{1,5},{5,9},{9,13},{13,1},{2,6},{6,10},{... | collective-permute-start | bytes 393224 | tf_op jit(solution)/shard_map/ppermute | solution.py:107
  61.1 8.0 %collective-permute-start.12 = (bf16[64,1024]{1,0:T(8,128)(2,1)S(1)}, bf16[64,1024]{1,0:T(8,128)(2,1)S(1)}, u32[]{:S(2)}, u32[]{:S(2)}) collective-permute-start(bf16[64,1024]{1,0:T(8,128)(2,1)S(1)} %collective-permute-done.11), channel_id=1, source_target_pairs={{0,1},{1,0},{2,3},{3,2},{4,5},{5,4},{6,7},{7,6},{8,9},{9,8},{10,11... | collective-permute-start | bytes 393224 | tf_op jit(solution)/shard_map/ppermute | solution.py:107
  61.1 6.0 %collective-permute-start.13 = (bf16[64,1024]{1,0:T(8,128)(2,1)S(1)}, bf16[64,1024]{1,0:T(8,128)(2,1)S(1)}, u32[]{:S(2)}, u32[]{:S(2)}) collective-permute-start(bf16[64,1024]{1,0:T(8,128)(2,1)S(1)} %collective-permute-done.11), channel_id=1, source_target_pairs={{0,2},{2,0},{1,3},{3,1},{4,6},{6,4},{5,7},{7,5},{8,10},{10,8},{9,1... | collective-permute-start | bytes 393224 | tf_op jit(solution)/shard_map/ppermute | solution.py:107
  61.6 7.4 %collective-permute-start.15 = (bf16[64,1024]{1,0:T(8,128)(2,1)S(1)}, bf16[64,1024]{1,0:T(8,128)(2,1)S(1)}, u32[]{:S(2)}, u32[]{:S(2)}) collective-permute-start(bf16[64,1024]{1,0:T(8,128)(2,1)S(1)} %collective-permute-done.11), channel_id=1, source_target_pairs={{0,4},{4,8},{8,12},{12,0},{1,5},{5,9},{9,13},{13,1},{2,6},{6,10},{... | collective-permute-start | bytes 393224 | tf_op jit(solution)/shard_map/ppermute | solution.py:107
  61.6 1.3 %collective-permute-start.7 = (bf16[64,1024]{1,0:T(8,128)(2,1)S(1)}, bf16[64,1024]{1,0:T(8,128)(2,1)S(1)}, u32[]{:S(2)}, u32[]{:S(2)}) collective-permute-start(bf16[64,1024]{1,0:T(8,128)(2,1)S(1)} %collective-permute-done.6), channel_id=1, source_target_pairs={{0,1},{1,0},{2,3},{3,2},{4,5},{5,4},{6,7},{7,6},{8,9},{9,8},{10,11... | collective-permute-start | bytes 393224 | tf_op jit(solution)/shard_map/ppermute | solution.py:107
  65.2 11.5 %collective-permute-start.10 = (bf16[128,512]{1,0:T(8,128)(2,1)S(1)}, bf16[128,512]{1,0:T(8,128)(2,1)S(1)}, u32[]{:S(2)}, u32[]{:S(2)}) collective-permute-start(bf16[128,512]{1,0:T(8,128)(2,1)S(1)} %get-tuple-element.18), channel_id=1, source_target_pairs={{0,3},{1,2},{2,1},{3,0},{4,7},{5,6},{6,5},{7,4},{8,11},{9,10},{10,... | collective-permute-start | bytes 393224 | tf_op jit(solution)/shard_map/ppermute | solution.py:215
  66.6 11.8 %collective-permute-start.9 = (bf16[128,512]{1,0:T(8,128)(2,1)S(1)}, bf16[128,512]{1,0:T(8,128)(2,1)S(1)}, u32[]{:S(2)}, u32[]{:S(2)}) collective-permute-start(bf16[128,512]{1,0:T(8,128)(2,1)S(1)} %get-tuple-element.19), channel_id=1, source_target_pairs={{0,2},{1,3},{2,0},{3,1},{4,6},{5,7},{6,4},{7,5},{8,10},{9,11},{10,... | collective-permute-start | bytes 393224 | tf_op jit(solution)/shard_map/ppermute | solution.py:215
  67.1 12.1 %collective-permute-start.8 = (bf16[128,512]{1,0:T(8,128)(2,1)S(1)}, bf16[128,512]{1,0:T(8,128)(2,1)S(1)}, u32[]{:S(2)}, u32[]{:S(2)}) collective-permute-start(bf16[128,512]{1,0:T(8,128)(2,1)S(1)} %get-tuple-element.17), channel_id=1, source_target_pairs={{0,1},{1,0},{2,3},{3,2},{4,5},{5,4},{6,7},{7,6},{8,9},{9,8},{10,11... | collective-permute-start | bytes 393224 | tf_op jit(solution)/shard_map/ppermute | solution.py:215
  69.0 1.7 %collective-permute-start.14 = (bf16[64,1024]{1,0:T(8,128)(2,1)S(1)}, bf16[64,1024]{1,0:T(8,128)(2,1)S(1)}, u32[]{:S(2)}, u32[]{:S(2)}) collective-permute-start(bf16[64,1024]{1,0:T(8,128)(2,1)S(1)} %collective-permute-done.13), channel_id=1, source_target_pairs={{0,1},{1,0},{2,3},{3,2},{4,5},{5,4},{6,7},{7,6},{8,9},{9,8},{10,11... | collective-permute-start | bytes 393224 | tf_op jit(solution)/shard_map/ppermute | solution.py:107
  69.1 7.5 %collective-permute-start.17 = (bf16[64,1024]{1,0:T(8,128)(2,1)S(1)}, bf16[64,1024]{1,0:T(8,128)(2,1)S(1)}, u32[]{:S(2)}, u32[]{:S(2)}) collective-permute-start(bf16[64,1024]{1,0:T(8,128)(2,1)S(1)} %collective-permute-done.15), channel_id=1, source_target_pairs={{0,2},{2,0},{1,3},{3,1},{4,6},{6,4},{5,7},{7,5},{8,10},{10,8},{9,1... | collective-permute-start | bytes 393224 | tf_op jit(solution)/shard_map/ppermute | solution.py:107
  70.8 7.7 %collective-permute-start.19 = (bf16[64,1024]{1,0:T(8,128)(2,1)S(1)}, bf16[64,1024]{1,0:T(8,128)(2,1)S(1)}, u32[]{:S(2)}, u32[]{:S(2)}) collective-permute-start(bf16[64,1024]{1,0:T(8,128)(2,1)S(1)} %collective-permute-done.15), channel_id=1, source_target_pairs={{0,4},{4,8},{8,12},{12,0},{1,5},{5,9},{9,13},{13,1},{2,6},{6,10},{... | collective-permute-start | bytes 393224 | tf_op jit(solution)/shard_map/ppermute | solution.py:107
  76.7 3.4 %collective-permute-start.16 = (bf16[64,1024]{1,0:T(8,128)(2,1)S(1)}, bf16[64,1024]{1,0:T(8,128)(2,1)S(1)}, u32[]{:S(2)}, u32[]{:S(2)}) collective-permute-start(bf16[64,1024]{1,0:T(8,128)(2,1)S(1)} %collective-permute-done.15), channel_id=1, source_target_pairs={{0,1},{1,0},{2,3},{3,2},{4,5},{5,4},{6,7},{7,6},{8,9},{9,8},{10,11... | collective-permute-start | bytes 393224 | tf_op jit(solution)/shard_map/ppermute | solution.py:107
  76.7 3.4 %collective-permute-start.18 = (bf16[64,1024]{1,0:T(8,128)(2,1)S(1)}, bf16[64,1024]{1,0:T(8,128)(2,1)S(1)}, u32[]{:S(2)}, u32[]{:S(2)}) collective-permute-start(bf16[64,1024]{1,0:T(8,128)(2,1)S(1)} %collective-permute-done.17), channel_id=1, source_target_pairs={{0,1},{1,0},{2,3},{3,2},{4,5},{5,4},{6,7},{7,6},{8,9},{9,8},{10,11... | collective-permute-start | bytes 393224 | tf_op jit(solution)/shard_map/ppermute | solution.py:107
  78.4 6.0 %collective-permute-start.20 = (bf16[64,1024]{1,0:T(8,128)(2,1)S(1)}, bf16[64,1024]{1,0:T(8,128)(2,1)S(1)}, u32[]{:S(2)}, u32[]{:S(2)}) collective-permute-start(bf16[64,1024]{1,0:T(8,128)(2,1)S(1)} %collective-permute-done.19), channel_id=1, source_target_pairs={{0,1},{1,0},{2,3},{3,2},{4,5},{5,4},{6,7},{7,6},{8,9},{9,8},{10,11... | collective-permute-start | bytes 393224 | tf_op jit(solution)/shard_map/ppermute | solution.py:107
  78.4 5.9 %collective-permute-start.21 = (bf16[64,1024]{1,0:T(8,128)(2,1)S(1)}, bf16[64,1024]{1,0:T(8,128)(2,1)S(1)}, u32[]{:S(2)}, u32[]{:S(2)}) collective-permute-start(bf16[64,1024]{1,0:T(8,128)(2,1)S(1)} %collective-permute-done.19), channel_id=1, source_target_pairs={{0,2},{2,0},{1,3},{3,1},{4,6},{6,4},{5,7},{7,5},{8,10},{10,8},{9,1... | collective-permute-start | bytes 393224 | tf_op jit(solution)/shard_map/ppermute | solution.py:107
  84.3 1.3 %collective-permute-start.22 = (bf16[64,1024]{1,0:T(8,128)(2,1)S(1)}, bf16[64,1024]{1,0:T(8,128)(2,1)S(1)}, u32[]{:S(2)}, u32[]{:S(2)}) collective-permute-start(bf16[64,1024]{1,0:T(8,128)(2,1)S(1)} %collective-permute-done.21), channel_id=1, source_target_pairs={{0,1},{1,0},{2,3},{3,2},{4,5},{5,4},{6,7},{7,6},{8,9},{9,8},{10,11... | collective-permute-start | bytes 393224 | tf_op jit(solution)/shard_map/ppermute | solution.py:107

commit v2 on v1

--- a/solution.py
+++ b/solution.py
@@ -1,6 +1,8 @@
 import jax
 import jax.numpy as jnp
 from jax import lax
+from jax.experimental import pallas as pl
+from jax.experimental.pallas import tpu as pltpu
 from jax.sharding import PartitionSpec as P
 
 HEAD = 64
@@ -107,14 +109,90 @@
     return lax.ppermute(x, axis, [(i, (i + k) % n) for i in range(n)])
 
 
-def spread(piece):
-    chunks = []
-    held = piece
-    for s in range(lax.axis_size("patch")):
-        if s:
-            held = shift(held, "patch", 1)
-        chunks.append([held] + [shift(held, "grp", k) for k in range(1, lax.axis_size("grp"))])
-    return chunks
+def after(x, *others):
+    return lax.optimization_barrier((x,) + others)[0]
+
+
+def others(x, axis):
+    return [shift(x, axis, k) for k in range(1, lax.axis_size(axis))]
+
+
+def attend(seen_ref, query_ref, *refs):
+    grps = seen_ref.shape[0]
+    keys, values, out_ref = refs[:grps], refs[grps : 2 * grps], refs[2 * grps]
+    lane = lax.broadcasted_iota(jnp.int32, (BLK, 2 * HEAD), 1)
+    nt = (((1,), (1,)), ((), ()))
+    for pair in range(query_ref.shape[1] // (2 * HEAD)):
+        cols = pl.ds(pair * 2 * HEAD, 2 * HEAD)
+        query = query_ref[:, cols]
+        found = []
+        for head in range(2):
+            one = jnp.where((lane < HEAD) == (head == 0), query, jnp.zeros_like(query))
+            scores = []
+            for k in range(grps):
+                part = lax.dot_general(
+                    one, keys[k][:, cols], nt, preferred_element_type=jnp.float32
+                ) * HEAD ** (-0.5)
+                scores.append(jnp.where(seen_ref[k] > 0, part, -1e30))
+            largest = scores[0]
+            for part in scores[1:]:
+                largest = jnp.maximum(largest, part)
+            largest = jnp.max(largest, axis=1, keepdims=True)
+            weights = [jnp.exp(part - largest) for part in scores]
+            total = weights[0]
+            for part in weights[1:]:
+                total = total + part
+            total = jnp.sum(total, axis=1, keepdims=True)
+            result = 0.0
+            for k in range(grps):
+                probs = (weights[k] / total).astype(jnp.bfloat16)
+                result = result + jnp.dot(
+                    probs, values[k][:, cols], preferred_element_type=jnp.float32
+                )
+            found.append(result)
+        out_ref[:, cols] = jnp.where(lane < HEAD, found[0], found[1]).astype(jnp.bfloat16)
+
+
+def project(me_ref, gain_ref, *refs):
+    cores = (len(refs) - 3) // 3
+    attended, weights, residuals = refs[:cores], refs[cores : 2 * cores], refs[2 * cores : 3 * cores]
+    stream_ref, normed_ref, full = refs[3 * cores :]
+    half = stream_ref.shape[1]
+    me = me_ref[0]
+    total = jnp.dot(attended[0][...], weights[0][...], preferred_element_type=jnp.float32)
+    for j in range(1, cores):
+        total = total + jnp.dot(
+            attended[j][...], weights[j][...], preferred_element_type=jnp.float32
+        )
+    full[...] = total
+    parts = []
+    for j in range(cores):
+        cols = pl.ds(pl.multiple_of(lax.rem(me - j + cores, cores) * half, half), half)
+        parts.append(full[:, cols] + residuals[j][...].astype(jnp.float32))
+    width = half * cores
+    center = sum(jnp.sum(part, axis=1, keepdims=True) for part in parts) / width
+    spread_sq = sum(
+        jnp.sum((part - center) * (part - center), axis=1, keepdims=True) for part in parts
+    ) / width
+    stream_ref[...] = parts[0]
+    normed_ref[...] = (
+        (parts[0] - center) * lax.rsqrt(spread_sq + 1e-05) * gain_ref[...]
+    ).astype(jnp.bfloat16)
+
+
+def call(kernel, out_shape, smem, args, flops, scratch=()):
+    moved = sum(a.size * a.dtype.itemsize for a in args) + sum(
+        o.size * o.dtype.itemsize for o in jax.tree.leaves(out_shape)
+    )
+    return pl.pallas_call(
+        kernel,
+        out_shape=out_shape,
+        in_specs=[pl.BlockSpec(memory_space=pltpu.SMEM)] * smem
+        + [pl.BlockSpec(memory_space=pltpu.VMEM)] * (len(args) - smem),
+        scratch_shapes=scratch,
+        cost_estimate=pl.CostEstimate(flops=flops, bytes_accessed=moved, transcendentals=0),
+        compiler_params=pltpu.CompilerParams(vmem_limit_bytes=24 * 2**20),
+    )(*args)
 
 
 def join(pieces, dim):
@@ -132,7 +210,7 @@
 
 
 def over_cores(piece, dim):
-    return join([piece] + [shift(piece, "col", j) for j in range(1, lax.axis_size("col"))], dim)
+    return join([piece] + others(piece, "col"), dim)
 
 
 def gather_plan(
@@ -150,66 +228,66 @@
 ):
     cores = lax.axis_size("col")
     grps = lax.axis_size("grp")
+    patches = lax.axis_size("patch")
     me = lax.axis_index("col")
-    row_count = query_vectors.shape[0]
-    half = query_vectors.shape[1]
-    keys = [key_vectors] + [shift(key_vectors, "grp", k) for k in range(1, grps)]
-    values = [value_vectors] + [shift(value_vectors, "grp", k) for k in range(1, grps)]
-    cot_chunks = spread(cotangent)
-    out_weight = over_cores(output_weight, 0)
-    res_rows = over_cores(residual, 1)
-    gain = over_cores(norm_gain, 0)
-
-    local_heads = half // HEAD
+    rows, half = query_vectors.shape
+    width = half * cores
+
+    keys = [key_vectors] + others(key_vectors, "grp")
+    values = [value_vectors] + others(value_vectors, "grp")
+    cots = [cotangent, shift(cotangent, "patch", 1)]
+    weights = [output_weight] + others(output_weight, "col")
+    residuals = [residual] + others(residual, "col")
+
     own = lax.axis_index("grp")
-    slot_ids = jnp.arange(neighbor_ids.shape[1], dtype=jnp.int32)
-    query_heads = query_vectors.reshape(row_count, local_heads, HEAD)
-    scores = []
-    for k in range(grps):
-        seen = jnp.any((neighbor_ids[0] == (own - k + grps) % grps) & (slot_ids < neighbor_count[0]))
-        part = jnp.einsum(
-            "qhd,khd->hqk",
-            query_heads,
-            keys[k].reshape(row_count, local_heads, HEAD),
-            preferred_element_type=jnp.float32,
-        ) * HEAD ** (-0.5)
-        scores.append(jnp.where(seen, part, -1e30))
-    scores = jnp.concatenate(scores, axis=2)
-    largest = jnp.max(scores, axis=2, keepdims=True)
-    weights = jnp.exp(scores - largest)
-    probs = (weights / jnp.sum(weights, axis=2, keepdims=True)).astype(jnp.bfloat16)
-    value_heads = jnp.concatenate(values, axis=0).reshape(-1, local_heads, HEAD)
-    attended = jnp.einsum("hqk,khd->qhd", probs, value_heads, preferred_element_type=jnp.float32)
-    attended = over_cores(attended.astype(jnp.bfloat16).reshape(row_count, -1), 1)
-    stream = res_rows.astype(jnp.float32) + jnp.dot(
-        attended, out_weight, preferred_element_type=jnp.float32
-    )
-    center = jnp.mean(stream, axis=1, keepdims=True)
-    shifted = stream - center
-    spread_sq = jnp.mean(shifted * shifted, axis=1, keepdims=True)
-    normed = (shifted * lax.rsqrt(spread_sq + 1e-05) * gain[None, :]).astype(jnp.bfloat16)
-    own_stream = lax.dynamic_slice(stream, (0, me * half), (row_count, half))
-
-    share = row_count // cores
-    norm_chunks = spread(lax.dynamic_slice(normed, (me * share, 0), (share, normed.shape[1])))
-
-    rows, backs, hiddens, back_pres = [], [], [], []
+    source = (own - jnp.arange(grps, dtype=jnp.int32) + grps) % grps
+    slots = jnp.arange(neighbor_ids.shape[1], dtype=jnp.int32) < neighbor_count[0]
+    seen = jnp.any((neighbor_ids[0][None] == source[:, None]) & slots[None], axis=1)
+    attended = call(
+        attend,
+        jax.ShapeDtypeStruct((rows, half), jnp.bfloat16),
+        1,
+        [seen.astype(jnp.int32), query_vectors] + keys + values,
+        4 * rows * rows * grps * width,
+    )
+    attended_all = [attended] + others(attended, "col")
+    cots.append(shift(after(cots[1], attended), "patch", 1))
+    stream, normed = call(
+        project,
+        (
+            jax.ShapeDtypeStruct((rows, half), jnp.float32),
+            jax.ShapeDtypeStruct((rows, half), jnp.bfloat16),
+        ),
+        1,
+        [me[None], norm_gain[None]] + attended_all + weights + residuals,
+        2 * rows * width * width,
+        [pltpu.VMEM((rows, width), jnp.float32)],
+    )
+    cots[0], cots[1], cots[2] = (after(c, normed) for c in cots)
+    for s in range(3, patches):
+        cots.append(shift(cots[s - 1], "patch", 1))
+
+    norms = [normed]
+    for s in range(1, patches):
+        norms.append(shift(norms[-1], "patch", 1))
+
+    saved = []
     layer_out = None
-    for s, (norm_pieces, cot_pieces) in enumerate(zip(norm_chunks, cot_chunks)):
-        normed_rows = jnp.concatenate(
-            [normed if s == 0 and k == 0 else over_cores(p, 0) for k, p in enumerate(norm_pieces)], 0
-        )
+    for s in range(patches):
+        norm_pieces = [norms[s]] + others(norms[s], "grp")
+        cot_pieces = [cots[s]] + others(cots[s], "grp")
+        normed_rows = jnp.concatenate([over_cores(p, 1) for p in norm_pieces], 0)
         back_rows = over_cores(jnp.concatenate(cot_pieces, 0), 1)
         pre = jnp.dot(normed_rows, up_weight, preferred_element_type=jnp.float32)
         hidden = jax.nn.gelu(pre).astype(jnp.bfloat16)
         if s == 0:
             partial_out = jnp.dot(hidden, down_weight, preferred_element_type=jnp.float32)
             partial_out = partial_out.astype(jnp.bfloat16)
-            layer_out = own_stream
+            layer_out = stream
             for k in range(grps):
                 for j in range(cores):
                     piece = lax.dynamic_slice(
-                        partial_out, (k * row_count, (me - j + cores) % cores * half), (row_count, half)
+                        partial_out, (k * rows, (me - j + cores) % cores * half), (rows, half)
                     )
                     if k or j:
                         piece = lax.ppermute(
@@ -227,18 +305,14 @@
             back_rows, down_weight, (((1,), (1,)), ((), ())), preferred_element_type=jnp.float32
         )
         _, gelu_back = jax.vjp(jax.nn.gelu, pre)
-        back_pres.append(gelu_back(back_hidden)[0].astype(jnp.bfloat16))
-        rows.append(normed_rows)
-        backs.append(back_rows)
-        hiddens.append(hidden)
-    rows, backs, hiddens, back_pres = (
-        jnp.concatenate(a, 0) for a in (rows, backs, hiddens, back_pres)
-    )
+        back_pre = gelu_back(back_hidden)[0].astype(jnp.bfloat16)
+        saved.append((normed_rows, back_rows, hidden, back_pre))
+    all_normed, all_back, all_hidden, all_pre = (jnp.concatenate(a, 0) for a in zip(*saved))
     up_grad = lax.dot_general(
-        rows, back_pres, (((0,), (0,)), ((), ())), preferred_element_type=jnp.float32
+        all_normed, all_pre, (((0,), (0,)), ((), ())), preferred_element_type=jnp.float32
     )
     down_grad = lax.dot_general(
-        hiddens, backs, (((0,), (0,)), ((), ())), preferred_element_type=jnp.float32
+        all_hidden, all_back, (((0,), (0,)), ((), ())), preferred_element_type=jnp.float32
     )
     return (layer_out, up_grad, down_grad)
 

time: 96.3 us -> 88.7 us (0.921)
  matrix products: 23.5 us -> 18.3 us
  local copies, waits for them, and re-layouts: 14.3 us -> 10 us
  starting transfers between devices: 21.9 us -> 26.1 us
  Pallas kernels: 0 us -> 4.14 us
  waiting for transfers between devices: 30.4 us -> 26.3 us
  other arithmetic: 3.65 us -> 1.61 us
    ppermute x31, waiting for transfers between devices: 30.4 us -> 22.4 us  [shift(): return lax.ppermute(x, axis, [(i, (i + k) % n) for i in range(n)])]
    dynamic_update_slice x30 -> x24, local copies, waits for them, and re-layouts: 6.16 us -> 0.45 us  [join(): whole = lax.dynamic_update_slice(whole, piece, start)]
    dot_general x6 -> x2, matrix products: 14 us -> 8.79 us  [the longest x1 4.4 us: gather_plan(): lax.dot_general(all_hidden, all_back, (((0,), (0,)), ((), ())), preferred...]
    unnamed x22 -> x33, local copies, waits for them, and re-layouts: 4.11 us -> 9.11 us
    pallas_call x0 -> x2, Pallas kernels: none -> 4.14 us  [call(): pl.pallas_call(kernel, out_shape=out_shape, in_specs=[pl.BlockSpec(memory...]
    ppermute x3, waiting for transfers between devices: 0.01 us -> 3.9 us  [gather_plan(): lax.ppermute(piece, ('grp', 'col'), [(a * cores + b, (a - k) % grps * cor...]
    ppermute x31, starting transfers between devices: 20 us -> 23.7 us  [shift(): return lax.ppermute(x, axis, [(i, (i + k) % n) for i in range(n)])]
    broadcast_in_dim x1 -> x0, local copies, waits for them, and re-layouts: 1.58 us -> none  [join(): whole = jnp.zeros(shape, pieces[0].dtype)]
  transfers between devices with their start and end apart: 34 -> 34, of which waited for: 12 -> 15; matrix products, arithmetic and copies ran while one was open for 28% -> 14% of each run, Pallas kernels for 0% -> 5%
where the time goes in v2:
time: 88.7 us; the launch traced here: 88.4 us
  waiting for transfers between devices  26.3 us (30%)
  starting transfers between devices  26.1 us (29%)
  matrix products  18.3 us (21%)
  local copies, waits for them, and re-layouts  10 us (11%)
  Pallas kernels  4.14 us (5%)
  between operations  1.95 us (2%)
  other arithmetic  1.61 us (2%)
    ppermute x31, starting transfers between devices, shift(): return lax.ppermute(x, axis, [(i, (i + k) % n) for i in range(n)])  23.7 us
    ppermute x31, waiting for transfers between devices, shift(): return lax.ppermute(x, axis, [(i, (i + k) % n) for i in range(n)])  22.4 us
    unnamed x33, local copies, waits for them, and re-layouts  9.11 us
    dot_general x4, matrix products, gather_plan(): pre = jnp.dot(normed_rows, up_weight, preferred_element_type=jnp.float32)  5.58 us
    dot_general x1, matrix products, gather_plan(): lax.dot_general(all_hidden, all_back, (((0,), (0,)), ((), ())), preferred...  4.4 us
    dot_general x1, matrix products, gather_plan(): lax.dot_general(all_normed, all_pre, (((0,), (0,)), ((), ())), preferred_...  4.4 us
    pallas_call x2, Pallas kernels, call(): pl.pallas_call(kernel, out_shape=out_shape, in_specs=[pl.BlockSpec(memory...  4.14 us
    ppermute x3, waiting for transfers between devices, gather_plan(): lax.ppermute(piece, ('grp', 'col'), [(a * cores + b, (a - k) % grps * cor...  3.9 us
  transfers between devices with their start and end apart: 34, of which 15 were waited for; matrix products, arithmetic and copies ran while one was open for 14% of the time, Pallas kernels for 5%

profile of v2, /device:TPU:0, one launch (start us, length us, event | category | flops | bytes accessed | tf_op | source)
XLA Modules:
  0.0 88.4 jit_solution(11957238486156018885)
XLA Ops:
  1.2 2.6 %collective-permute-start = (bf16[128,512]{1,0:T(8,128)(2,1)}, bf16[128,512]{1,0:T(8,128)(2,1)S(1)}, u32[]{:S(2)}, u32[]{:S(2)}) collective-permute-start(bf16[128,512]{1,0:T(8,128)(2,1)} %refs_0_.1), channel_id=1, source_target_pairs={{0,2},{2,0},{1,3},{3,1},{4,6},{6,4},{5,7},{7,5},{8,10},{10,8},{9,1... | collective-permute-start | bytes 393224 | tf_op jit(solution)/shard_map/ppermute | solution.py:109
  3.9 1.9 %collective-permute-start.25 = (bf16[128,512]{1,0:T(8,128)(2,1)}, bf16[128,512]{1,0:T(8,128)(2,1)}, u32[]{:S(2)}, u32[]{:S(2)}) collective-permute-start(bf16[128,512]{1,0:T(8,128)(2,1)} %param.21), channel_id=1, source_target_pairs={{0,4},{4,8},{8,12},{12,0},{1,5},{5,9},{9,13},{13,1},{2,6},{6,10},{... | collective-permute-start | bytes 393224 | tf_op jit(solution)/shard_map/ppermute | solution.py:109
  6.5 0.8 and_reduce_fusion
  7.4 0.9 %collective-permute-done.refs_1_ = bf16[128,512]{1,0:T(8,128)(2,1)S(1)} collective-permute-done((bf16[128,512]{1,0:T(8,128)(2,1)}, bf16[128,512]{1,0:T(8,128)(2,1)S(1)}, u32[]{:S(2)}, u32[]{:S(2)}) %collective-permute-start) | collective-permute-done | bytes 131104 | tf_op jit(solution)/shard_map/ppermute | solution.py:109
  8.3 2.5 %collective-permute-done.1.refs_3_ = bf16[128,512]{1,0:T(8,128)(2,1)S(1)} collective-permute-done((bf16[128,512]{1,0:T(8,128)(2,1)}, bf16[128,512]{1,0:T(8,128)(2,1)S(1)}, u32[]{:S(2)}, u32[]{:S(2)}) %collective-permute-start.1) | collective-permute-done | bytes 131104 | tf_op jit(solution)/shard_map/ppermute | solution.py:109
  11.5 0.9 %copy-done.3 = bf16[128,512]{1,0:T(8,128)(2,1)S(1)} copy-done((bf16[128,512]{1,0:T(8,128)(2,1)S(1)}, bf16[128,512]{1,0:T(8,128)(2,1)}, u32[]{:S(2)}) %copy-start.3) | copy-done | bytes 131096
  12.4 0.9 %copy-done.4 = bf16[128,512]{1,0:T(8,128)(2,1)S(1)} copy-done((bf16[128,512]{1,0:T(8,128)(2,1)S(1)}, bf16[128,512]{1,0:T(8,128)(2,1)}, u32[]{:S(2)}) %copy-start.4) | copy-done | bytes 131096
  13.3 0.9 %copy-done.5 = bf16[128,512]{1,0:T(8,128)(2,1)S(1)} copy-done((bf16[128,512]{1,0:T(8,128)(2,1)S(1)}, bf16[128,512]{1,0:T(8,128)(2,1)}, u32[]{:S(2)}) %copy-start.5) | copy-done | bytes 131096
  14.2 0.9 %copy-done.7 = bf16[128,512]{1,0:T(8,128)(2,1)S(1)} copy-done((bf16[128,512]{1,0:T(8,128)(2,1)S(1)}, bf16[128,512]{1,0:T(8,128)(2,1)}, u32[]{:S(2)}) %copy-start.7) | copy-done | bytes 131096
  15.1 3.4 %shard_map.130.refs_0_ = bf16[128,512]{1,0:T(8,128)(2,1)S(1)} custom-call(s32[2]{0:T(128)S(1)} %convert_element_type.45.seen_ref, bf16[128,512]{1,0:T(8,128)(2,1)S(1)} %copy-done.3, bf16[128,512]{1,0:T(8,128)(2,1)S(1)} %copy-done.4, bf16[128,512]{1,0:T(8,128)(2,1)S(1)} %collective-permute-done.refs_1_, bf16[128,512]{1,0:T(8,128)(2,1)S(1)} %copy-done.5, ...), custom_call_target="tpu_custom_call" | custom-call | flops 134217728 | bytes 786440 | tf_op jit(solution)/shard_map/pallas_call | solution.py:187
  18.6 1.9 %collective-permute-start.28 = (bf16[128,512]{1,0:T(8,128)(2,1)}, bf16[128,512]{1,0:T(8,128)(2,1)}, u32[]{:S(2)}, u32[]{:S(2)}) collective-permute-start(bf16[128,512]{1,0:T(8,128)(2,1)} %collective-permute-done.25), channel_id=1, source_target_pairs={{0,4},{4,8},{8,12},{12,0},{1,5},{5,9},{9,13},{13,1},{2,6},{6,10},{... | collective-permute-start | bytes 393224 | tf_op jit(solution)/shard_map/ppermute | solution.py:109
  20.5 1.2 %copy-done.1 = bf16[512,1024]{1,0:T(8,128)(2,1)S(1)} copy-done((bf16[512,1024]{1,0:T(8,128)(2,1)S(1)}, bf16[512,1024]{1,0:T(8,128)(2,1)}, u32[]{:S(2)}) %copy-start.1) | copy-done | bytes 1048600
  21.8 0.9 %copy-done.2 = bf16[128,512]{1,0:T(8,128)(2,1)S(1)} copy-done((bf16[128,512]{1,0:T(8,128)(2,1)S(1)}, bf16[128,512]{1,0:T(8,128)(2,1)}, u32[]{:S(2)}) %copy-start.2) | copy-done | bytes 131096
  24.1 2.9 %collective-permute-done.28 = bf16[128,512]{1,0:T(8,128)(2,1)} collective-permute-done((bf16[128,512]{1,0:T(8,128)(2,1)}, bf16[128,512]{1,0:T(8,128)(2,1)}, u32[]{:S(2)}, u32[]{:S(2)}) %collective-permute-start.28) | collective-permute-done | bytes 131104 | tf_op jit(solution)/shard_map/ppermute | solution.py:109
  27.0 1.5 %collective-permute-start.29 = (bf16[128,512]{1,0:T(8,128)(2,1)}, bf16[128,512]{1,0:T(8,128)(2,1)S(1)}, u32[]{:S(2)}, u32[]{:S(2)}) collective-permute-start(bf16[128,512]{1,0:T(8,128)(2,1)} %collective-permute-done.28), channel_id=1, source_target_pairs={{0,2},{2,0},{1,3},{3,1},{4,6},{6,4},{5,7},{7,5},{8,10},{10,8},{9,1... | collective-permute-start | bytes 393224 | tf_op jit(solution)/shard_map/ppermute | solution.py:109
  28.5 1.3 %collective-permute-start.11 = (bf16[128,512]{1,0:T(8,128)(2,1)S(1)}, bf16[128,512]{1,0:T(8,128)(2,1)S(1)}, u32[]{:S(2)}, u32[]{:S(2)}) collective-permute-start(bf16[128,512]{1,0:T(8,128)(2,1)S(1)} %get-tuple-element.10), channel_id=1, source_target_pairs={{0,4},{4,8},{8,12},{12,0},{1,5},{5,9},{9,13},{13,1},{2,6},{6,10},{... | collective-permute-start | bytes 393224 | tf_op jit(solution)/shard_map/ppermute | solution.py:109
  30.3 1.6 %collective-permute-start.26 = (bf16[128,512]{1,0:T(8,128)(2,1)}, bf16[128,512]{1,0:T(8,128)(2,1)S(1)}, u32[]{:S(2)}, u32[]{:S(2)}) collective-permute-start(bf16[128,512]{1,0:T(8,128)(2,1)} %collective-permute-done.25), channel_id=1, source_target_pairs={{0,2},{2,0},{1,3},{3,1},{4,6},{6,4},{5,7},{7,5},{8,10},{10,8},{9,1... | collective-permute-start | bytes 393224 | tf_op jit(solution)/shard_map/ppermute | solution.py:109
  31.9 0.9 %constant_dynamic-update-slice_fusion.11 = bf16[256,512]{1,0:T(8,128)(2,1)S(1)} fusion(bf16[128,512]{1,0:T(8,128)(2,1)} %collective-permute-done.25), kind=kLoop, calls=%fused_computation.92 | loop fusion | bytes 262144
  32.8 0.9 %constant_dynamic-update-slice_fusion.13 = bf16[256,512]{1,0:T(8,128)(2,1)S(1)} fusion(bf16[128,512]{1,0:T(8,128)(2,1)} %collective-permute-done.28), kind=kLoop, calls=%fused_computation.94 | loop fusion | bytes 262144
  33.8 1.6 %collective-permute-done.31 = bf16[128,512]{1,0:T(8,128)(2,1)S(1)} collective-permute-done((bf16[128,512]{1,0:T(8,128)(2,1)}, bf16[128,512]{1,0:T(8,128)(2,1)S(1)}, u32[]{:S(2)}, u32[]{:S(2)}) %collective-permute-start.31) | collective-permute-done | bytes 131104 | tf_op jit(solution)/shard_map/ppermute | solution.py:109
  35.4 1.5 %collective-permute-start.6 = (bf16[128,512]{1,0:T(8,128)(2,1)S(1)}, bf16[128,512]{1,0:T(8,128)(2,1)S(1)}, u32[]{:S(2)}, u32[]{:S(2)}) collective-permute-start(bf16[128,512]{1,0:T(8,128)(2,1)S(1)} %get-tuple-element.10), channel_id=1, source_target_pairs={{0,2},{2,0},{1,3},{3,1},{4,6},{6,4},{5,7},{7,5},{8,10},{10,8},{9,1... | collective-permute-start | bytes 393224 | tf_op jit(solution)/shard_map/ppermute | solution.py:109
  37.6 1.6 %collective-permute-done.26 = bf16[128,512]{1,0:T(8,128)(2,1)S(1)} collective-permute-done((bf16[128,512]{1,0:T(8,128)(2,1)}, bf16[128,512]{1,0:T(8,128)(2,1)S(1)}, u32[]{:S(2)}, u32[]{:S(2)}) %collective-permute-start.26) | collective-permute-done | bytes 131104 | tf_op jit(solution)/shard_map/ppermute | solution.py:109
  40.0 0.8 collective-permute-done.6
  40.9 1.3 %collective-permute-start.32 = (bf16[128,512]{1,0:T(8,128)(2,1)S(1)}, bf16[128,512]{1,0:T(8,128)(2,1)S(1)}, u32[]{:S(2)}, u32[]{:S(2)}) collective-permute-start(bf16[128,512]{1,0:T(8,128)(2,1)S(1)} %collective-permute-done.31), channel_id=1, source_target_pairs={{0,2},{2,0},{1,3},{3,1},{4,6},{6,4},{5,7},{7,5},{8,10},{10,8},{9,1... | collective-permute-start | bytes 393224 | tf_op jit(solution)/shard_map/ppermute | solution.py:109
  42.4 1.0 %collective-permute-start.15 = (bf16[128,512]{1,0:T(8,128)(2,1)S(1)}, bf16[128,512]{1,0:T(8,128)(2,1)S(1)}, u32[]{:S(2)}, u32[]{:S(2)}) collective-permute-start(bf16[128,512]{1,0:T(8,128)(2,1)S(1)} %collective-permute-done.11), channel_id=1, source_target_pairs={{0,4},{4,8},{8,12},{12,0},{1,5},{5,9},{9,13},{13,1},{2,6},{6,10},{... | collective-permute-start | bytes 393224 | tf_op jit(solution)/shard_map/ppermute | solution.py:109
  43.4 2.4 %collective-permute-done.32 = bf16[128,512]{1,0:T(8,128)(2,1)S(1)} collective-permute-done((bf16[128,512]{1,0:T(8,128)(2,1)S(1)}, bf16[128,512]{1,0:T(8,128)(2,1)S(1)}, u32[]{:S(2)}, u32[]{:S(2)}) %collective-permute-start.32) | collective-permute-done | bytes 131104 | tf_op jit(solution)/shard_map/ppermute | solution.py:109
  45.9 1.2 %collective-permute-done.7 = bf16[128,512]{1,0:T(8,128)(2,1)S(1)} collective-permute-done((bf16[128,512]{1,0:T(8,128)(2,1)S(1)}, bf16[128,512]{1,0:T(8,128)(2,1)S(1)}, u32[]{:S(2)}, u32[]{:S(2)}) %collective-permute-start.7) | collective-permute-done | bytes 131104 | tf_op jit(solution)/shard_map/ppermute | solution.py:109
  47.4 1.2 %collective-permute-done.12 = bf16[128,512]{1,0:T(8,128)(2,1)S(1)} collective-permute-done((bf16[128,512]{1,0:T(8,128)(2,1)S(1)}, bf16[128,512]{1,0:T(8,128)(2,1)S(1)}, u32[]{:S(2)}, u32[]{:S(2)}) %collective-permute-start.12) | collective-permute-done | bytes 131104 | tf_op jit(solution)/shard_map/ppermute | solution.py:109
  48.5 1.3 %collective-permute-start.13 = (bf16[128,512]{1,0:T(8,128)(2,1)S(1)}, bf16[128,512]{1,0:T(8,128)(2,1)S(1)}, u32[]{:S(2)}, u32[]{:S(2)}) collective-permute-start(bf16[128,512]{1,0:T(8,128)(2,1)S(1)} %collective-permute-done.11), channel_id=1, source_target_pairs={{0,2},{2,0},{1,3},{3,1},{4,6},{6,4},{5,7},{7,5},{8,10},{10,8},{9,1... | collective-permute-start | bytes 393224 | tf_op jit(solution)/shard_map/ppermute | solution.py:109
  49.9 1.2 %collective-permute-start.19 = (bf16[128,512]{1,0:T(8,128)(2,1)S(1)}, bf16[128,512]{1,0:T(8,128)(2,1)S(1)}, u32[]{:S(2)}, u32[]{:S(2)}) collective-permute-start(bf16[128,512]{1,0:T(8,128)(2,1)S(1)} %collective-permute-done.15), channel_id=1, source_target_pairs={{0,4},{4,8},{8,12},{12,0},{1,5},{5,9},{9,13},{13,1},{2,6},{6,10},{... | collective-permute-start | bytes 393224 | tf_op jit(solution)/shard_map/ppermute | solution.py:109
  51.2 2.9 %collective-permute-done.13 = bf16[128,512]{1,0:T(8,128)(2,1)S(1)} collective-permute-done((bf16[128,512]{1,0:T(8,128)(2,1)S(1)}, bf16[128,512]{1,0:T(8,128)(2,1)S(1)}, u32[]{:S(2)}, u32[]{:S(2)}) %collective-permute-start.13) | collective-permute-done | bytes 131104 | tf_op jit(solution)/shard_map/ppermute | solution.py:109
  54.1 1.3 %collective-permute-start.17 = (bf16[128,512]{1,0:T(8,128)(2,1)S(1)}, bf16[128,512]{1,0:T(8,128)(2,1)S(1)}, u32[]{:S(2)}, u32[]{:S(2)}) collective-permute-start(bf16[128,512]{1,0:T(8,128)(2,1)S(1)} %collective-permute-done.15), channel_id=1, source_target_pairs={{0,2},{2,0},{1,3},{3,1},{4,6},{6,4},{5,7},{7,5},{8,10},{10,8},{9,1... | collective-permute-start | bytes 393224 | tf_op jit(solution)/shard_map/ppermute | solution.py:109
  55.5 1.8 %collective-permute-done.19 = bf16[128,512]{1,0:T(8,128)(2,1)S(1)} collective-permute-done((bf16[128,512]{1,0:T(8,128)(2,1)S(1)}, bf16[128,512]{1,0:T(8,128)(2,1)S(1)}, u32[]{:S(2)}, u32[]{:S(2)}) %collective-permute-start.19) | collective-permute-done | bytes 131104 | tf_op jit(solution)/shard_map/ppermute | solution.py:109
  57.3 1.7 %collective-permute-done.17 = bf16[128,512]{1,0:T(8,128)(2,1)S(1)} collective-permute-done((bf16[128,512]{1,0:T(8,128)(2,1)S(1)}, bf16[128,512]{1,0:T(8,128)(2,1)S(1)}, u32[]{:S(2)}, u32[]{:S(2)}) %collective-permute-start.17) | collective-permute-done | bytes 131104 | tf_op jit(solution)/shard_map/ppermute | solution.py:109
  60.4 1.3 %collective-permute-start.21 = (bf16[128,512]{1,0:T(8,128)(2,1)S(1)}, bf16[128,512]{1,0:T(8,128)(2,1)S(1)}, u32[]{:S(2)}, u32[]{:S(2)}) collective-permute-start(bf16[128,512]{1,0:T(8,128)(2,1)S(1)} %collective-permute-done.19), channel_id=1, source_target_pairs={{0,2},{2,0},{1,3},{3,1},{4,6},{6,4},{5,7},{7,5},{8,10},{10,8},{9,1... | collective-permute-start | bytes 393224 | tf_op jit(solution)/shard_map/ppermute | solution.py:109
  62.0 0.8 fusion.74
  63.4 0.8 fusion.75
  64.2 1.4 %fusion.29 = (bf16[256,1024]{1,0:T(8,128)(2,1)S(1)}, bf16[256,1024]{1,0:T(8,128)(2,1)S(1)}) fusion(f32[256,1024]{1,0:T(8,128)S(1)} %fusion.74, bf16[1024,1024]{1,0:T(8,128)(2,1)S(1)} %copy-done, bf16[128,1024]{1,0:T(8,128)(2,1)S(1)} %constant_dynamic-update-slice_fusion.36, bf16[128,1024]{1,0:T(8,128)(2,1)S(1)} %constant_dynamic-update-slice_fusion.38), kind=kOutput, calls=%fused_computation.38 | convolution fusion | flops 543686656 | bytes 4718592 | tf_op jit(solution)/shard_map/dot_general | solution.py:281
  65.6 1.4 %multiply_convert_fusion.2 = (bf16[256,1024]{1,0:T(8,128)(2,1)S(1)}, bf16[256,1024]{1,0:T(8,128)(2,1)S(1)}) fusion(f32[256,1024]{1,0:T(8,128)S(1)} %fusion.75, bf16[1024,1024]{1,0:T(8,128)(2,1)S(1)} %copy-done, bf16[128,1024]{1,0:T(8,128)(2,1)S(1)} %constant_dynamic-update-slice_fusion.32, bf16[128,1024]{1,0:T(8,128)(2,1)S(1)} %constant_dynamic-update-slice_fusion.34), kind=kOutput, calls=%fused_computation.62 | convolution fusion | flops 543686656 | bytes 4718592 | tf_op jit(solution)/shard_map/dot_general | solution.py:281
  67.9 0.8 fusion.76
  68.7 0.8 collective-permute-start.10
  69.6 1.4 %multiply_convert_fusion.1 = (bf16[256,1024]{1,0:T(8,128)(2,1)S(1)}, bf16[256,1024]{1,0:T(8,128)(2,1)S(1)}) fusion(f32[256,1024]{1,0:T(8,128)S(1)} %fusion.76, bf16[1024,1024]{1,0:T(8,128)(2,1)S(1)} %copy-done, bf16[128,1024]{1,0:T(8,128)(2,1)S(1)} %constant_dynamic-update-slice_fusion.28, bf16[128,1024]{1,0:T(8,128)(2,1)S(1)} %constant_dynamic-update-slice_fusion.30), kind=kOutput, calls=%fused_computation.61 | convolution fusion | flops 543686656 | bytes 4718592 | tf_op jit(solution)/shard_map/dot_general | solution.py:281
  71.0 1.4 %collective-permute-start.9 = (bf16[128,512]{1,0:T(8,128)(2,1)S(1)}, bf16[128,512]{1,0:T(8,128)(2,1)S(1)}, u32[]{:S(2)}, u32[]{:S(2)}) collective-permute-start(bf16[128,512]{1,0:T(8,128)(2,1)S(1)} %get-tuple-element.25), channel_id=1, source_target_pairs={{0,2},{1,3},{2,0},{3,1},{4,6},{5,7},{6,4},{7,5},{8,10},{9,11},{10,... | collective-permute-start | bytes 393224 | tf_op jit(solution)/shard_map/ppermute | solution.py:293
  72.7 0.8 fusion.77
  73.9 3.4 %collective-permute-done.9 = bf16[128,512]{1,0:T(8,128)(2,1)S(1)} collective-permute-done((bf16[128,512]{1,0:T(8,128)(2,1)S(1)}, bf16[128,512]{1,0:T(8,128)(2,1)S(1)}, u32[]{:S(2)}, u32[]{:S(2)}) %collective-permute-start.9) | collective-permute-done | bytes 131104 | tf_op jit(solution)/shard_map/ppermute | solution.py:293
  78.1 1.4 %multiply_convert_fusion = (bf16[256,1024]{1,0:T(8,128)(2,1)S(1)}, bf16[256,1024]{1,0:T(8,128)(2,1)S(1)}) fusion(f32[256,1024]{1,0:T(8,128)S(1)} %fusion.77, bf16[1024,1024]{1,0:T(8,128)(2,1)S(1)} %copy-done, bf16[128,1024]{1,0:T(8,128)(2,1)S(1)} %constant_dynamic-update-slice_fusion.24, bf16[128,1024]{1,0:T(8,128)(2,1)S(1)} %constant_dynamic-update-slice_fusion.26), kind=kOutput, calls=%fused_computation.60 | convolution fusion | flops 543686656 | bytes 4718592 | tf_op jit(solution)/shard_map/dot_general | solution.py:281
  79.6 4.4 %fusion.8 = f32[1024,1024]{1,0:T(8,128)} fusion(bf16[256,1024]{1,0:T(8,128)(2,1)S(1)} %get-tuple-element.19, bf16[256,1024]{1,0:T(8,128)(2,1)S(1)} %get-tuple-element.17, bf16[256,1024]{1,0:T(8,128)(2,1)S(1)} %get-tuple-element.15, bf16[256,1024]{1,0:T(8,128)(2,1)S(1)} %get-tuple-element.22, bf16[256,1024]{1,0:T(8,128)(2,1)S(1)} %constant_dynamic-update-slice_fusion.16, ...), kind=kOutput, calls=%fused_computation.8 | convolution fusion | flops 2164260864 | bytes 8388608 | tf_op jit(solution)/shard_map/dot_general | solution.py:314
  84.0 4.4 %fusion = f32[1024,1024]{1,0:T(8,128)} fusion(bf16[1024,1024]{1,0:T(8,128)(2,1)S(1)} %constant_dynamic-update-slice_fusion, bf16[256,1024]{1,0:T(8,128)(2,1)S(1)} %get-tuple-element.20, bf16[256,1024]{1,0:T(8,128)(2,1)S(1)} %get-tuple-element.18, bf16[256,1024]{1,0:T(8,128)(2,1)S(1)} %get-tuple-element.16, bf16[256,1024]{1,0:T(8,128)(2,1)S(1)} %get-tuple-element.21), kind=kOutput, calls=%fused_computation | convolution fusion | flops 2155872256 | bytes 8388608 | tf_op jit(solution)/shard_map/dot_general | solution.py:311
  (113 shorter events, 9.9 us)
Async XLA Ops:
  0.6 63.5 %copy-start = (bf16[1024,1024]{1,0:T(8,128)(2,1)S(1)}, bf16[1024,1024]{1,0:T(8,128)(2,1)}, u32[]{:S(2)}) copy-start(bf16[1024,1024]{1,0:T(8,128)(2,1)} %param.19) | copy-start | bytes 6291460
  0.6 19.9 %collective-permute-start.3 = (bf16[512,1024]{1,0:T(8,128)(2,1)}, bf16[512,1024]{1,0:T(8,128)(2,1)S(1)}, u32[]{:S(2)}, u32[]{:S(2)}) collective-permute-start(bf16[512,1024]{1,0:T(8,128)(2,1)} %refs_2_.3), channel_id=1, source_target_pairs={{0,1},{1,0},{2,3},{3,2},{4,5},{5,4},{6,7},{7,6},{8,9},{9,8},{10,11... | collective-permute-start | bytes 3145736 | tf_op jit(solution)/shard_map/ppermute | solution.py:109
  1.2 7.1 %collective-permute-start = (bf16[128,512]{1,0:T(8,128)(2,1)}, bf16[128,512]{1,0:T(8,128)(2,1)S(1)}, u32[]{:S(2)}, u32[]{:S(2)}) collective-permute-start(bf16[128,512]{1,0:T(8,128)(2,1)} %refs_0_.1), channel_id=1, source_target_pairs={{0,2},{2,0},{1,3},{3,1},{4,6},{6,4},{5,7},{7,5},{8,10},{10,8},{9,1... | collective-permute-start | bytes 393224 | tf_op jit(solution)/shard_map/ppermute | solution.py:109
  3.7 7.1 %collective-permute-start.1 = (bf16[128,512]{1,0:T(8,128)(2,1)}, bf16[128,512]{1,0:T(8,128)(2,1)S(1)}, u32[]{:S(2)}, u32[]{:S(2)}) collective-permute-start(bf16[128,512]{1,0:T(8,128)(2,1)} %refs_2_.2), channel_id=1, source_target_pairs={{0,2},{2,0},{1,3},{3,1},{4,6},{6,4},{5,7},{7,5},{8,10},{10,8},{9,1... | collective-permute-start | bytes 393224 | tf_op jit(solution)/shard_map/ppermute | solution.py:109
  3.8 16.7 %collective-permute-start.4 = (bf16[128,512]{1,0:T(8,128)(2,1)}, bf16[128,512]{1,0:T(8,128)(2,1)S(1)}, u32[]{:S(2)}, u32[]{:S(2)}) collective-permute-start(bf16[128,512]{1,0:T(8,128)(2,1)} %refs_4_.1), channel_id=1, source_target_pairs={{0,1},{1,0},{2,3},{3,2},{4,5},{5,4},{6,7},{7,6},{8,9},{9,8},{10,11... | collective-permute-start | bytes 393224 | tf_op jit(solution)/shard_map/ppermute | solution.py:109
  3.9 14.7 %collective-permute-start.25 = (bf16[128,512]{1,0:T(8,128)(2,1)}, bf16[128,512]{1,0:T(8,128)(2,1)}, u32[]{:S(2)}, u32[]{:S(2)}) collective-permute-start(bf16[128,512]{1,0:T(8,128)(2,1)} %param.21), channel_id=1, source_target_pairs={{0,4},{4,8},{8,12},{12,0},{1,5},{5,9},{9,13},{13,1},{2,6},{6,10},{... | collective-permute-start | bytes 393224 | tf_op jit(solution)/shard_map/ppermute | solution.py:109
  10.8 0.7 copy-start.6
  11.5 0.9 %copy-start.3 = (bf16[128,512]{1,0:T(8,128)(2,1)S(1)}, bf16[128,512]{1,0:T(8,128)(2,1)}, u32[]{:S(2)}) copy-start(bf16[128,512]{1,0:T(8,128)(2,1)} %query_ref.1) | copy-start | bytes 393220
  12.4 0.9 %copy-start.4 = (bf16[128,512]{1,0:T(8,128)(2,1)S(1)}, bf16[128,512]{1,0:T(8,128)(2,1)}, u32[]{:S(2)}) copy-start(bf16[128,512]{1,0:T(8,128)(2,1)} %refs_0_.1) | copy-start | bytes 393220
  13.3 0.9 %copy-start.5 = (bf16[128,512]{1,0:T(8,128)(2,1)S(1)}, bf16[128,512]{1,0:T(8,128)(2,1)}, u32[]{:S(2)}) copy-start(bf16[128,512]{1,0:T(8,128)(2,1)} %refs_2_.2) | copy-start | bytes 393220
  14.2 0.9 %copy-start.7 = (bf16[128,512]{1,0:T(8,128)(2,1)S(1)}, bf16[128,512]{1,0:T(8,128)(2,1)}, u32[]{:S(2)}) copy-start(bf16[128,512]{1,0:T(8,128)(2,1)} %copy-done.6) | copy-start | bytes 393220
  18.5 2.0 %collective-permute-start.2 = (bf16[128,512]{1,0:T(8,128)(2,1)S(1)}, bf16[128,512]{1,0:T(8,128)(2,1)S(1)}, u32[]{:S(2)}, u32[]{:S(2)}) collective-permute-start(bf16[128,512]{1,0:T(8,128)(2,1)S(1)} %shard_map.130.refs_0_), channel_id=1, source_target_pairs={{0,1},{1,0},{2,3},{3,2},{4,5},{5,4},{6,7},{7,6},{8,9},{9,8},{10,11... | collective-permute-start | bytes 393224 | tf_op jit(solution)/shard_map/ppermute | solution.py:109
  18.6 8.3 %collective-permute-start.28 = (bf16[128,512]{1,0:T(8,128)(2,1)}, bf16[128,512]{1,0:T(8,128)(2,1)}, u32[]{:S(2)}, u32[]{:S(2)}) collective-permute-start(bf16[128,512]{1,0:T(8,128)(2,1)} %collective-permute-done.25), channel_id=1, source_target_pairs={{0,4},{4,8},{8,12},{12,0},{1,5},{5,9},{9,13},{13,1},{2,6},{6,10},{... | collective-permute-start | bytes 393224 | tf_op jit(solution)/shard_map/ppermute | solution.py:109
  20.5 1.2 %copy-start.1 = (bf16[512,1024]{1,0:T(8,128)(2,1)S(1)}, bf16[512,1024]{1,0:T(8,128)(2,1)}, u32[]{:S(2)}) copy-start(bf16[512,1024]{1,0:T(8,128)(2,1)} %refs_2_.3) | copy-start | bytes 3145732
  21.8 0.9 %copy-start.2 = (bf16[128,512]{1,0:T(8,128)(2,1)S(1)}, bf16[128,512]{1,0:T(8,128)(2,1)}, u32[]{:S(2)}) copy-start(bf16[128,512]{1,0:T(8,128)(2,1)} %refs_4_.1) | copy-start | bytes 393220
  22.7 0.7 copy-start.8
  23.4 6.4 %copy-start.10 = (bf16[128,512]{1,0:T(8,128)(2,1)S(1)}, bf16[128,512]{1,0:T(8,128)(2,1)}, u32[]{:S(2)}) copy-start(bf16[128,512]{1,0:T(8,128)(2,1)} %param.21) | copy-start | bytes 393220
  27.0 8.4 %collective-permute-start.31 = (bf16[128,512]{1,0:T(8,128)(2,1)}, bf16[128,512]{1,0:T(8,128)(2,1)S(1)}, u32[]{:S(2)}, u32[]{:S(2)}) collective-permute-start(bf16[128,512]{1,0:T(8,128)(2,1)} %collective-permute-done.28), channel_id=1, source_target_pairs={{0,4},{4,8},{8,12},{12,0},{1,5},{5,9},{9,13},{13,1},{2,6},{6,10},{... | collective-permute-start | bytes 393224 | tf_op jit(solution)/shard_map/ppermute | solution.py:109
  27.0 9.9 %collective-permute-start.29 = (bf16[128,512]{1,0:T(8,128)(2,1)}, bf16[128,512]{1,0:T(8,128)(2,1)S(1)}, u32[]{:S(2)}, u32[]{:S(2)}) collective-permute-start(bf16[128,512]{1,0:T(8,128)(2,1)} %collective-permute-done.28), channel_id=1, source_target_pairs={{0,2},{2,0},{1,3},{3,1},{4,6},{6,4},{5,7},{7,5},{8,10},{10,8},{9,1... | collective-permute-start | bytes 393224 | tf_op jit(solution)/shard_map/ppermute | solution.py:109
  28.5 10.8 %collective-permute-start.11 = (bf16[128,512]{1,0:T(8,128)(2,1)S(1)}, bf16[128,512]{1,0:T(8,128)(2,1)S(1)}, u32[]{:S(2)}, u32[]{:S(2)}) collective-permute-start(bf16[128,512]{1,0:T(8,128)(2,1)S(1)} %get-tuple-element.10), channel_id=1, source_target_pairs={{0,4},{4,8},{8,12},{12,0},{1,5},{5,9},{9,13},{13,1},{2,6},{6,10},{... | collective-permute-start | bytes 393224 | tf_op jit(solution)/shard_map/ppermute | solution.py:109
  29.8 7.2 %collective-permute-start.23 = (bf16[128,512]{1,0:T(8,128)(2,1)S(1)}, bf16[128,512]{1,0:T(8,128)(2,1)S(1)}, u32[]{:S(2)}, u32[]{:S(2)}) collective-permute-start(bf16[128,512]{1,0:T(8,128)(2,1)S(1)} %copy-done.10), channel_id=1, source_target_pairs={{0,2},{2,0},{1,3},{3,1},{4,6},{6,4},{5,7},{7,5},{8,10},{10,8},{9,1... | collective-permute-start | bytes 393224 | tf_op jit(solution)/shard_map/ppermute | solution.py:109
  30.3 8.9 %collective-permute-start.26 = (bf16[128,512]{1,0:T(8,128)(2,1)}, bf16[128,512]{1,0:T(8,128)(2,1)S(1)}, u32[]{:S(2)}, u32[]{:S(2)}) collective-permute-start(bf16[128,512]{1,0:T(8,128)(2,1)} %collective-permute-done.25), channel_id=1, source_target_pairs={{0,2},{2,0},{1,3},{3,1},{4,6},{6,4},{5,7},{7,5},{8,10},{10,8},{9,1... | collective-permute-start | bytes 393224 | tf_op jit(solution)/shard_map/ppermute | solution.py:109
  35.4 5.5 %collective-permute-start.6 = (bf16[128,512]{1,0:T(8,128)(2,1)S(1)}, bf16[128,512]{1,0:T(8,128)(2,1)S(1)}, u32[]{:S(2)}, u32[]{:S(2)}) collective-permute-start(bf16[128,512]{1,0:T(8,128)(2,1)S(1)} %get-tuple-element.10), channel_id=1, source_target_pairs={{0,2},{2,0},{1,3},{3,1},{4,6},{6,4},{5,7},{7,5},{8,10},{10,8},{9,1... | collective-permute-start | bytes 393224 | tf_op jit(solution)/shard_map/ppermute | solution.py:109
  36.9 5.5 %collective-permute-start.5 = (bf16[128,512]{1,0:T(8,128)(2,1)S(1)}, bf16[128,512]{1,0:T(8,128)(2,1)S(1)}, u32[]{:S(2)}, u32[]{:S(2)}) collective-permute-start(bf16[128,512]{1,0:T(8,128)(2,1)S(1)} %get-tuple-element.10), channel_id=1, source_target_pairs={{0,1},{1,0},{2,3},{3,2},{4,5},{5,4},{6,7},{7,6},{8,9},{9,8},{10,11... | collective-permute-start | bytes 393224 | tf_op jit(solution)/shard_map/ppermute | solution.py:109
  37.0 30.8 %collective-permute-start.30 = (bf16[256,512]{1,0:T(8,128)(2,1)S(1)}, bf16[256,512]{1,0:T(8,128)(2,1)S(1)}, u32[]{:S(2)}, u32[]{:S(2)}) collective-permute-start(bf16[256,512]{1,0:T(8,128)(2,1)S(1)} %constant_dynamic-update-slice_fusion.12), channel_id=1, source_target_pairs={{0,1},{1,0},{2,3},{3,2},{4,5},{5,4},{6,7},{7,6},{8,9},{9,8},{10,11... | collective-permute-start | bytes 786440 | tf_op jit(solution)/shard_map/ppermute | solution.py:109
  39.2 22.6 %collective-permute-start.24 = (bf16[256,512]{1,0:T(8,128)(2,1)S(1)}, bf16[256,512]{1,0:T(8,128)(2,1)S(1)}, u32[]{:S(2)}, u32[]{:S(2)}) collective-permute-start(bf16[256,512]{1,0:T(8,128)(2,1)S(1)} %constant_dynamic-update-slice_fusion.8), channel_id=1, source_target_pairs={{0,1},{1,0},{2,3},{3,2},{4,5},{5,4},{6,7},{7,6},{8,9},{9,8},{10,11... | collective-permute-start | bytes 786440 | tf_op jit(solution)/shard_map/ppermute | solution.py:109
  39.3 23.5 %collective-permute-start.27 = (bf16[256,512]{1,0:T(8,128)(2,1)S(1)}, bf16[256,512]{1,0:T(8,128)(2,1)S(1)}, u32[]{:S(2)}, u32[]{:S(2)}) collective-permute-start(bf16[256,512]{1,0:T(8,128)(2,1)S(1)} %constant_dynamic-update-slice_fusion.10), channel_id=1, source_target_pairs={{0,1},{1,0},{2,3},{3,2},{4,5},{5,4},{6,7},{7,6},{8,9},{9,8},{10,11... | collective-permute-start | bytes 786440 | tf_op jit(solution)/shard_map/ppermute | solution.py:109
  40.9 5.0 %collective-permute-start.32 = (bf16[128,512]{1,0:T(8,128)(2,1)S(1)}, bf16[128,512]{1,0:T(8,128)(2,1)S(1)}, u32[]{:S(2)}, u32[]{:S(2)}) collective-permute-start(bf16[128,512]{1,0:T(8,128)(2,1)S(1)} %collective-permute-done.31), channel_id=1, source_target_pairs={{0,2},{2,0},{1,3},{3,1},{4,6},{6,4},{5,7},{7,5},{8,10},{10,8},{9,1... | collective-permute-start | bytes 393224 | tf_op jit(solution)/shard_map/ppermute | solution.py:109
  42.4 7.6 %collective-permute-start.15 = (bf16[128,512]{1,0:T(8,128)(2,1)S(1)}, bf16[128,512]{1,0:T(8,128)(2,1)S(1)}, u32[]{:S(2)}, u32[]{:S(2)}) collective-permute-start(bf16[128,512]{1,0:T(8,128)(2,1)S(1)} %collective-permute-done.11), channel_id=1, source_target_pairs={{0,4},{4,8},{8,12},{12,0},{1,5},{5,9},{9,13},{13,1},{2,6},{6,10},{... | collective-permute-start | bytes 393224 | tf_op jit(solution)/shard_map/ppermute | solution.py:109
  45.8 1.3 %collective-permute-start.7 = (bf16[128,512]{1,0:T(8,128)(2,1)S(1)}, bf16[128,512]{1,0:T(8,128)(2,1)S(1)}, u32[]{:S(2)}, u32[]{:S(2)}) collective-permute-start(bf16[128,512]{1,0:T(8,128)(2,1)S(1)} %collective-permute-done.6), channel_id=1, source_target_pairs={{0,1},{1,0},{2,3},{3,2},{4,5},{5,4},{6,7},{7,6},{8,9},{9,8},{10,11... | collective-permute-start | bytes 393224 | tf_op jit(solution)/shard_map/ppermute | solution.py:109
  47.2 1.3 %collective-permute-start.12 = (bf16[128,512]{1,0:T(8,128)(2,1)S(1)}, bf16[128,512]{1,0:T(8,128)(2,1)S(1)}, u32[]{:S(2)}, u32[]{:S(2)}) collective-permute-start(bf16[128,512]{1,0:T(8,128)(2,1)S(1)} %collective-permute-done.11), channel_id=1, source_target_pairs={{0,1},{1,0},{2,3},{3,2},{4,5},{5,4},{6,7},{7,6},{8,9},{9,8},{10,11... | collective-permute-start | bytes 393224 | tf_op jit(solution)/shard_map/ppermute | solution.py:109
  48.5 5.6 %collective-permute-start.13 = (bf16[128,512]{1,0:T(8,128)(2,1)S(1)}, bf16[128,512]{1,0:T(8,128)(2,1)S(1)}, u32[]{:S(2)}, u32[]{:S(2)}) collective-permute-start(bf16[128,512]{1,0:T(8,128)(2,1)S(1)} %collective-permute-done.11), channel_id=1, source_target_pairs={{0,2},{2,0},{1,3},{3,1},{4,6},{6,4},{5,7},{7,5},{8,10},{10,8},{9,1... | collective-permute-start | bytes 393224 | tf_op jit(solution)/shard_map/ppermute | solution.py:109
  49.9 12.0 %copy-start.9 = (bf16[1024,1024]{1,0:T(8,128)(2,1)S(1)}, bf16[1024,1024]{1,0:T(8,128)(2,1)}, u32[]{:S(2)}) copy-start(bf16[1024,1024]{1,0:T(8,128)(2,1)} %param.20) | copy-start | bytes 6291460
  49.9 7.3 %collective-permute-start.19 = (bf16[128,512]{1,0:T(8,128)(2,1)S(1)}, bf16[128,512]{1,0:T(8,128)(2,1)S(1)}, u32[]{:S(2)}, u32[]{:S(2)}) collective-permute-start(bf16[128,512]{1,0:T(8,128)(2,1)S(1)} %collective-permute-done.15), channel_id=1, source_target_pairs={{0,4},{4,8},{8,12},{12,0},{1,5},{5,9},{9,13},{13,1},{2,6},{6,10},{... | collective-permute-start | bytes 393224 | tf_op jit(solution)/shard_map/ppermute | solution.py:109
  54.1 5.0 %collective-permute-start.17 = (bf16[128,512]{1,0:T(8,128)(2,1)S(1)}, bf16[128,512]{1,0:T(8,128)(2,1)S(1)}, u32[]{:S(2)}, u32[]{:S(2)}) collective-permute-start(bf16[128,512]{1,0:T(8,128)(2,1)S(1)} %collective-permute-done.15), channel_id=1, source_target_pairs={{0,2},{2,0},{1,3},{3,1},{4,6},{6,4},{5,7},{7,5},{8,10},{10,8},{9,1... | collective-permute-start | bytes 393224 | tf_op jit(solution)/shard_map/ppermute | solution.py:109
  57.2 1.9 %collective-permute-start.16 = (bf16[128,512]{1,0:T(8,128)(2,1)S(1)}, bf16[128,512]{1,0:T(8,128)(2,1)S(1)}, u32[]{:S(2)}, u32[]{:S(2)}) collective-permute-start(bf16[128,512]{1,0:T(8,128)(2,1)S(1)} %collective-permute-done.15), channel_id=1, source_target_pairs={{0,1},{1,0},{2,3},{3,2},{4,5},{5,4},{6,7},{7,6},{8,9},{9,8},{10,11... | collective-permute-start | bytes 393224 | tf_op jit(solution)/shard_map/ppermute | solution.py:109
  59.0 1.3 %collective-permute-start.14 = (bf16[128,512]{1,0:T(8,128)(2,1)S(1)}, bf16[128,512]{1,0:T(8,128)(2,1)S(1)}, u32[]{:S(2)}, u32[]{:S(2)}) collective-permute-start(bf16[128,512]{1,0:T(8,128)(2,1)S(1)} %collective-permute-done.13), channel_id=1, source_target_pairs={{0,1},{1,0},{2,3},{3,2},{4,5},{5,4},{6,7},{7,6},{8,9},{9,8},{10,11... | collective-permute-start | bytes 393224 | tf_op jit(solution)/shard_map/ppermute | solution.py:109
  59.1 13.5 %collective-permute-start.33 = (bf16[256,512]{1,0:T(8,128)(2,1)S(1)}, bf16[256,512]{1,0:T(8,128)(2,1)S(1)}, u32[]{:S(2)}, u32[]{:S(2)}) collective-permute-start(bf16[256,512]{1,0:T(8,128)(2,1)S(1)} %constant_dynamic-update-slice_fusion.14), channel_id=1, source_target_pairs={{0,1},{1,0},{2,3},{3,2},{4,5},{5,4},{6,7},{7,6},{8,9},{9,8},{10,11... | collective-permute-start | bytes 786440 | tf_op jit(solution)/shard_map/ppermute | solution.py:109
  60.4 10.6 %collective-permute-start.21 = (bf16[128,512]{1,0:T(8,128)(2,1)S(1)}, bf16[128,512]{1,0:T(8,128)(2,1)S(1)}, u32[]{:S(2)}, u32[]{:S(2)}) collective-permute-start(bf16[128,512]{1,0:T(8,128)(2,1)S(1)} %collective-permute-done.19), channel_id=1, source_target_pairs={{0,2},{2,0},{1,3},{3,1},{4,6},{6,4},{5,7},{7,5},{8,10},{10,8},{9,1... | collective-permute-start | bytes 393224 | tf_op jit(solution)/shard_map/ppermute | solution.py:109
  61.8 10.6 %collective-permute-start.20 = (bf16[128,512]{1,0:T(8,128)(2,1)S(1)}, bf16[128,512]{1,0:T(8,128)(2,1)S(1)}, u32[]{:S(2)}, u32[]{:S(2)}) collective-permute-start(bf16[128,512]{1,0:T(8,128)(2,1)S(1)} %collective-permute-done.19), channel_id=1, source_target_pairs={{0,1},{1,0},{2,3},{3,2},{4,5},{5,4},{6,7},{7,6},{8,9},{9,8},{10,11... | collective-permute-start | bytes 393224 | tf_op jit(solution)/shard_map/ppermute | solution.py:109
  62.8 5.9 %collective-permute-start.18 = (bf16[128,512]{1,0:T(8,128)(2,1)S(1)}, bf16[128,512]{1,0:T(8,128)(2,1)S(1)}, u32[]{:S(2)}, u32[]{:S(2)}) collective-permute-start(bf16[128,512]{1,0:T(8,128)(2,1)S(1)} %collective-permute-done.17), channel_id=1, source_target_pairs={{0,1},{1,0},{2,3},{3,2},{4,5},{5,4},{6,7},{7,6},{8,9},{9,8},{10,11... | collective-permute-start | bytes 393224 | tf_op jit(solution)/shard_map/ppermute | solution.py:109
  67.8 5.7 %collective-permute-start.8 = (bf16[128,512]{1,0:T(8,128)(2,1)S(1)}, bf16[128,512]{1,0:T(8,128)(2,1)S(1)}, u32[]{:S(2)}, u32[]{:S(2)}) collective-permute-start(bf16[128,512]{1,0:T(8,128)(2,1)S(1)} %get-tuple-element.23), channel_id=1, source_target_pairs={{0,1},{1,0},{2,3},{3,2},{4,5},{5,4},{6,7},{7,6},{8,9},{9,8},{10,11... | collective-permute-start | bytes 393224 | tf_op jit(solution)/shard_map/ppermute | solution.py:293
  68.7 5.2 %collective-permute-start.10 = (bf16[128,512]{1,0:T(8,128)(2,1)S(1)}, bf16[128,512]{1,0:T(8,128)(2,1)S(1)}, u32[]{:S(2)}, u32[]{:S(2)}) collective-permute-start(bf16[128,512]{1,0:T(8,128)(2,1)S(1)} %get-tuple-element.24), channel_id=1, source_target_pairs={{0,3},{1,2},{2,1},{3,0},{4,7},{5,6},{6,5},{7,4},{8,11},{9,10},{10,... | collective-permute-start | bytes 393224 | tf_op jit(solution)/shard_map/ppermute | solution.py:293
  71.0 6.4 %collective-permute-start.9 = (bf16[128,512]{1,0:T(8,128)(2,1)S(1)}, bf16[128,512]{1,0:T(8,128)(2,1)S(1)}, u32[]{:S(2)}, u32[]{:S(2)}) collective-permute-start(bf16[128,512]{1,0:T(8,128)(2,1)S(1)} %get-tuple-element.25), channel_id=1, source_target_pairs={{0,2},{1,3},{2,0},{3,1},{4,6},{5,7},{6,4},{7,5},{8,10},{9,11},{10,... | collective-permute-start | bytes 393224 | tf_op jit(solution)/shard_map/ppermute | solution.py:293
  72.5 5.7 %collective-permute-start.22 = (bf16[128,512]{1,0:T(8,128)(2,1)S(1)}, bf16[128,512]{1,0:T(8,128)(2,1)S(1)}, u32[]{:S(2)}, u32[]{:S(2)}) collective-permute-start(bf16[128,512]{1,0:T(8,128)(2,1)S(1)} %collective-permute-done.21), channel_id=1, source_target_pairs={{0,1},{1,0},{2,3},{3,2},{4,5},{5,4},{6,7},{7,6},{8,9},{9,8},{10,11... | collective-permute-start | bytes 393224 | tf_op jit(solution)/shard_map/ppermute | solution.py:109

commit v3 on v2

--- a/solution.py
+++ b/solution.py
@@ -1,3 +1,5 @@
+import functools
+
 import jax
 import jax.numpy as jnp
 from jax import lax
@@ -114,26 +116,67 @@
 
 
 def others(x, axis):
-    return [shift(x, axis, k) for k in range(1, lax.axis_size(axis))]
-
-
-def attend(seen_ref, query_ref, *refs):
+    n = lax.axis_size(axis)
+    if n & (n - 1):
+        return [shift(x, axis, k) for k in range(1, n)]
+    return [lax.ppermute(x, axis, [(i, i ^ k) for i in range(n)]) for k in range(1, n)]
+
+
+def member(axis, k):
+    n = lax.axis_size(axis)
+    me = lax.axis_index(axis)
+    return (me - k + n) % n if n & (n - 1) else me ^ k
+
+
+def one_head(query, lane, head):
+    return jnp.where((lane < HEAD) == (head == 0), query, jnp.zeros_like(query))
+
+
+def pair_scores(query, key):
+    return lax.dot_general(
+        query, key, (((1,), (1,)), ((), ())), preferred_element_type=jnp.float32
+    ) * HEAD ** (-0.5)
+
+
+def stage(count, *refs):
+    sources, targets, score_ref, sems = refs[:count], refs[count : 2 * count], refs[-2], refs[-1]
+    copies = [
+        pltpu.make_async_copy(source, target, sems.at[i])
+        for i, (source, target) in enumerate(zip(sources, targets))
+    ]
+    for copy in copies:
+        copy.start()
+    copies[0].wait()
+    copies[1].wait()
+    query_ref, key_ref = targets[:2]
+    rows = query_ref.shape[0]
+    lane = lax.broadcasted_iota(jnp.int32, (rows, 2 * HEAD), 1)
+    for pair in range(query_ref.shape[1] // (2 * HEAD)):
+        cols = pl.ds(pair * 2 * HEAD, 2 * HEAD)
+        query, key = query_ref[:, cols], key_ref[:, cols]
+        for head in range(2):
+            score_ref[2 * pair + head] = pair_scores(one_head(query, lane, head), key)
+    for copy in copies[2:]:
+        copy.wait()
+
+
+def attend(seen_ref, score_ref, query_ref, *refs):
     grps = seen_ref.shape[0]
-    keys, values, out_ref = refs[:grps], refs[grps : 2 * grps], refs[2 * grps]
-    lane = lax.broadcasted_iota(jnp.int32, (BLK, 2 * HEAD), 1)
-    nt = (((1,), (1,)), ((), ()))
+    keys, values, out_ref = refs[: grps - 1], refs[grps - 1 : 2 * grps - 1], refs[2 * grps - 1]
+    rows = query_ref.shape[0]
+    lane = lax.broadcasted_iota(jnp.int32, (rows, 2 * HEAD), 1)
     for pair in range(query_ref.shape[1] // (2 * HEAD)):
         cols = pl.ds(pair * 2 * HEAD, 2 * HEAD)
         query = query_ref[:, cols]
         found = []
         for head in range(2):
-            one = jnp.where((lane < HEAD) == (head == 0), query, jnp.zeros_like(query))
-            scores = []
-            for k in range(grps):
-                part = lax.dot_general(
-                    one, keys[k][:, cols], nt, preferred_element_type=jnp.float32
-                ) * HEAD ** (-0.5)
-                scores.append(jnp.where(seen_ref[k] > 0, part, -1e30))
+            one = one_head(query, lane, head)
+            scores = [score_ref[2 * pair + head]] + [
+                pair_scores(one, keys[k][:, cols]) for k in range(grps - 1)
+            ]
+            scores = [
+                jnp.where(seen_ref[k] > 0, part, -1e30) for k, part in enumerate(scores)
+            ]
             largest = scores[0]
             for part in scores[1:]:
                 largest = jnp.maximum(largest, part)
@@ -153,12 +196,11 @@
         out_ref[:, cols] = jnp.where(lane < HEAD, found[0], found[1]).astype(jnp.bfloat16)
 
 
-def project(me_ref, gain_ref, *refs):
+def project(place_ref, gain_ref, *refs):
     cores = (len(refs) - 3) // 3
     attended, weights, residuals = refs[:cores], refs[cores : 2 * cores], refs[2 * cores : 3 * cores]
     stream_ref, normed_ref, full = refs[3 * cores :]
     half = stream_ref.shape[1]
-    me = me_ref[0]
     total = jnp.dot(attended[0][...], weights[0][...], preferred_element_type=jnp.float32)
     for j in range(1, cores):
         total = total + jnp.dot(
@@ -167,7 +209,7 @@
     full[...] = total
     parts = []
     for j in range(cores):
-        cols = pl.ds(pl.multiple_of(lax.rem(me - j + cores, cores) * half, half), half)
+        cols = pl.ds(pl.multiple_of(place_ref[j] * half, half), half)
         parts.append(full[:, cols] + residuals[j][...].astype(jnp.float32))
     width = half * cores
     center = sum(jnp.sum(part, axis=1, keepdims=True) for part in parts) / width
@@ -197,20 +239,32 @@
 
 def join(pieces, dim):
     n = len(pieces)
-    me = lax.axis_index("col")
     size = pieces[0].shape[dim]
     shape = list(pieces[0].shape)
     shape[dim] = size * n
     whole = jnp.zeros(shape, pieces[0].dtype)
     for j, piece in enumerate(pieces):
         start = [0] * len(shape)
-        start[dim] = (me - j + n) % n * size
+        start[dim] = member("col", j) * size
         whole = lax.dynamic_update_slice(whole, piece, start)
     return whole
 
 
 def over_cores(piece, dim):
     return join([piece] + others(piece, "col"), dim)
+
+
+def send_back(piece, k, j):
+    if not (k or j):
+        return piece
+    grps, cores = lax.axis_size("grp"), lax.axis_size("col")
+    pairs = []
+    for a in range(grps):
+        for b in range(cores):
+            to_grp = (a - k) % grps if grps & (grps - 1) else a ^ k
+            to_core = (b - j) % cores if cores & (cores - 1) else b ^ j
+            pairs.append((a * cores + b, to_grp * cores + to_core))
+    return lax.ppermute(piece, ("grp", "col"), pairs)
 
 
 def gather_plan(
@@ -229,29 +283,43 @@
     cores = lax.axis_size("col")
     grps = lax.axis_size("grp")
     patches = lax.axis_size("patch")
-    me = lax.axis_index("col")
     rows, half = query_vectors.shape
     width = half * cores
 
-    keys = [key_vectors] + others(key_vectors, "grp")
-    values = [value_vectors] + others(value_vectors, "grp")
-    cots = [cotangent, shift(cotangent, "patch", 1)]
-    weights = [output_weight] + others(output_weight, "col")
-    residuals = [residual] + others(residual, "col")
-
-    own = lax.axis_index("grp")
-    source = (own - jnp.arange(grps, dtype=jnp.int32) + grps) % grps
+    key_others = others(key_vectors, "grp")
+    value_others = others(value_vectors, "grp")
+    cot_others = others(cotangent, "grp")
+    weight_others = others(output_weight, "col")
+    residual_others = others(residual, "col")
+
+    source = jnp.stack([member("grp", k) for k in range(grps)])
     slots = jnp.arange(neighbor_ids.shape[1], dtype=jnp.int32) < neighbor_count[0]
     seen = jnp.any((neighbor_ids[0][None] == source[:, None]) & slots[None], axis=1)
+    held = [query_vectors, key_vectors, value_vectors, output_weight, residual, norm_gain[None], cotangent]
+    heads = half // HEAD
+    *held, scores = pl.pallas_call(
+        functools.partial(stage, len(held)),
+        out_shape=[jax.ShapeDtypeStruct(a.shape, a.dtype) for a in held]
+        + [jax.ShapeDtypeStruct((heads, rows, rows), jnp.float32)],
+        in_specs=[pl.BlockSpec(memory_space=pl.ANY)] * len(held),
+        out_specs=[pl.BlockSpec(memory_space=pltpu.VMEM)] * (len(held) + 1),
+        scratch_shapes=[pltpu.SemaphoreType.DMA((len(held),))],
+        cost_estimate=pl.CostEstimate(
+            flops=2 * rows * rows * width, bytes_accessed=4 * 2**20, transcendentals=0
+        ),
+        compiler_params=pltpu.CompilerParams(vmem_limit_bytes=24 * 2**20),
+    )(*held)
+    query, _, value, weight, residual, gain, cot = held
     attended = call(
         attend,
         jax.ShapeDtypeStruct((rows, half), jnp.bfloat16),
         1,
-        [seen.astype(jnp.int32), query_vectors] + keys + values,
+        [seen.astype(jnp.int32), scores, query] + key_others + [value] + value_others,
         4 * rows * rows * grps * width,
     )
-    attended_all = [attended] + others(attended, "col")
-    cots.append(shift(after(cots[1], attended), "patch", 1))
+    attended_others = others(attended, "col")
+    cots = [jnp.concatenate([cot] + [after(c, attended) for c in cot_others], 0)]
+    cots += others(cots[0], "patch")
     stream, normed = call(
         project,
         (
@@ -259,25 +327,23 @@
             jax.ShapeDtypeStruct((rows, half), jnp.bfloat16),
         ),
         1,
-        [me[None], norm_gain[None]] + attended_all + weights + residuals,
+        [jnp.stack([member("col", j) for j in range(cores)]), gain, attended]
+        + attended_others
+        + [weight]
+        + weight_others
+        + [residual]
+        + residual_others,
         2 * rows * width * width,
         [pltpu.VMEM((rows, width), jnp.float32)],
     )
-    cots[0], cots[1], cots[2] = (after(c, normed) for c in cots)
-    for s in range(3, patches):
-        cots.append(shift(cots[s - 1], "patch", 1))
-
-    norms = [normed]
-    for s in range(1, patches):
-        norms.append(shift(norms[-1], "patch", 1))
+    norms = [jnp.concatenate([normed] + others(normed, "grp"), 0)]
+    norms += others(norms[0], "patch")
 
     saved = []
     layer_out = None
     for s in range(patches):
-        norm_pieces = [norms[s]] + others(norms[s], "grp")
-        cot_pieces = [cots[s]] + others(cots[s], "grp")
-        normed_rows = jnp.concatenate([over_cores(p, 1) for p in norm_pieces], 0)
-        back_rows = over_cores(jnp.concatenate(cot_pieces, 0), 1)
+        normed_rows = over_cores(norms[s], 1)
+        back_rows = over_cores(cots[s], 1)
         pre = jnp.dot(normed_rows, up_weight, preferred_element_type=jnp.float32)
         hidden = jax.nn.gelu(pre).astype(jnp.bfloat16)
         if s == 0:
@@ -287,19 +353,9 @@
             for k in range(grps):
                 for j in range(cores):
                     piece = lax.dynamic_slice(
-                        partial_out, (k * rows, (me - j + cores) % cores * half), (rows, half)
+                        partial_out, (k * rows, member("col", j) * half), (rows, half)
                     )
-                    if k or j:
-                        piece = lax.ppermute(
-                            piece,
-                            ("grp", "col"),
-                            [
-                                (a * cores + b, (a - k) % grps * cores + (b - j) % cores)
-                                for a in range(grps)
-                                for b in range(cores)
-                            ],
-                        )
-                    layer_out = layer_out + piece.astype(jnp.float32)
+                    layer_out = layer_out + send_back(piece, k, j).astype(jnp.float32)
             layer_out = layer_out.astype(jnp.bfloat16)
         back_hidden = lax.dot_general(
             back_rows, down_weight, (((1,), (1,)), ((), ())), preferred_element_type=jnp.float32

time: 88.7 us -> 100 us (1.13)
  waiting for transfers between devices: 26.3 us -> 40.5 us
  starting transfers between devices: 26.1 us -> 17.8 us
  local copies, waits for them, and re-layouts: 10 us -> 12.6 us
  matrix products: 18.3 us -> 20 us
  Pallas kernels: 4.14 us -> 5.53 us
    ppermute x34 -> x24, waiting for transfers between devices: 26.3 us -> 40.5 us  [the longest x21 40.4 us: others(): lax.ppermute(x, axis, [(i, i ^ k) for i in range(n)])]
    ppermute x34 -> x24, starting transfers between devices: 26.1 us -> 17.8 us  [the longest x21 16.6 us: others(): lax.ppermute(x, axis, [(i, i ^ k) for i in range(n)])]
    pallas_call x0 -> x1, Pallas kernels: none -> 2.18 us  [gather_plan(): pl.pallas_call(functools.partial(stage, len(held)), out_shape=[jax.ShapeD...]
    dynamic_update_slice x24 -> x16, local copies, waits for them, and re-layouts: 0.45 us -> 2.31 us  [join(): whole = lax.dynamic_update_slice(whole, piece, start)]
    concatenate x5 -> x2, local copies, waits for them, and re-layouts: 0.06 us -> 1.58 us  [the longest x1 1.57 us: gather_plan(): jnp.concatenate([cot] + [after(c, attended) for c in cot_others], 0)]
    dot_general x4, matrix products: 3.2 us -> 4.62 us  [gather_plan(): lax.dot_general(back_rows, down_weight, (((1,), (1,)), ((), ())), preferr...]
    unnamed x33 -> x28, local copies, waits for them, and re-layouts: 9.11 us -> 8.27 us
  transfers between devices with their start and end apart: 34 -> 24, of which waited for: 15 -> 8; matrix products, arithmetic and copies ran while one was open for 14% -> 15% of each run, Pallas kernels for 5% -> 6%
where the time goes in v3:
time: 100 us; the launch traced here: 99.9 us
  waiting for transfers between devices  40.5 us (40%)
  matrix products  20 us (20%)
  starting transfers between devices  17.8 us (18%)
  local copies, waits for them, and re-layouts  12.6 us (13%)
  Pallas kernels  5.53 us (6%)
  between operations  1.78 us (2%)
  other arithmetic  1.75 us (2%)
    ppermute x21, waiting for transfers between devices, others(): lax.ppermute(x, axis, [(i, i ^ k) for i in range(n)])  40.4 us
    ppermute x21, starting transfers between devices, others(): lax.ppermute(x, axis, [(i, i ^ k) for i in range(n)])  16.6 us
    unnamed x28, local copies, waits for them, and re-layouts  8.27 us
    dot_general x4, matrix products, gather_plan(): pre = jnp.dot(normed_rows, up_weight, preferred_element_type=jnp.float32)  5.58 us
    dot_general x1, matrix products, gather_plan(): lax.dot_general(all_hidden, all_back, (((0,), (0,)), ((), ())), preferred...  4.64 us
    dot_general x4, matrix products, gather_plan(): lax.dot_general(back_rows, down_weight, (((1,), (1,)), ((), ())), preferr...  4.62 us
    dot_general x1, matrix products, gather_plan(): lax.dot_general(all_normed, all_pre, (((0,), (0,)), ((), ())), preferred_...  4.44 us
    pallas_call x2, Pallas kernels, call(): pl.pallas_call(kernel, out_shape=out_shape, in_specs=[pl.BlockSpec(memory...  3.36 us
  transfers between devices with their start and end apart: 24, of which 8 were waited for; matrix products, arithmetic and copies ran while one was open for 15% of the time, Pallas kernels for 6%

profile of v3, /device:TPU:0, one launch (start us, length us, event | category | flops | bytes accessed | tf_op | source)
XLA Modules:
  0.0 99.9 jit_solution(599430552589247126)
XLA Ops:
  0.6 3.0 %collective-permute-start = (bf16[128,512]{1,0:T(8,128)(2,1)}, bf16[128,512]{1,0:T(8,128)(2,1)S(1)}, u32[]{:S(2)}, u32[]{:S(2)}) collective-permute-start(bf16[128,512]{1,0:T(8,128)(2,1)} %refs_1_.1), channel_id=1, source_target_pairs={{0,2},{2,0},{1,3},{3,1},{4,6},{6,4},{5,7},{7,5},{8,10},{10,8},{9,1... | collective-permute-start | bytes 393224 | tf_op jit(solution)/shard_map/ppermute | solution.py:122
  3.7 1.9 %collective-permute-start.16 = (bf16[128,512]{1,0:T(8,128)(2,1)}, bf16[128,512]{1,0:T(8,128)(2,1)}, u32[]{:S(2)}, u32[]{:S(2)}) collective-permute-start(bf16[128,512]{1,0:T(8,128)(2,1)} %refs_6_.1), channel_id=1, source_target_pairs={{0,2},{2,0},{1,3},{3,1},{4,6},{6,4},{5,7},{7,5},{8,10},{10,8},{9,1... | collective-permute-start | bytes 393224 | tf_op jit(solution)/shard_map/ppermute | solution.py:122
  6.4 0.8 and_reduce_fusion
  7.3 1.2 %copy-done.1 = bf16[512,1024]{1,0:T(8,128)(2,1)S(1)} copy-done((bf16[512,1024]{1,0:T(8,128)(2,1)S(1)}, bf16[512,1024]{1,0:T(8,128)(2,1)}, u32[]{:S(2)}) %copy-start.1) | copy-done | bytes 1048600
  8.5 0.9 copy-done.7
  9.4 0.9 copy-done.8
  10.3 0.9 copy-done.9
  11.2 0.9 copy-done.10
  12.1 0.7 copy-done.11
  12.8 2.2 %shard_map.130 = (bf16[128,512]{1,0:T(8,128)(2,1)S(1)}, bf16[128,512]{1,0:T(8,128)(2,1)}, bf16[128,512]{1,0:T(8,128)(2,1)S(1)}, bf16[512,1024]{1,0:T(8,128)(2,1)...) custom-call(bf16[128,512]{1,0:T(8,128)(2,1)S(1)} %copy-done.7, ...), custom_call_target="tpu_custom_call" | custom-call | flops 33554432 | bytes 4194304 | tf_op jit(solution)/shard_map/pallas_call | solution.py:300
  15.0 0.7 constant_dynamic-update-slice_fusion.3
  15.7 0.7 copy-done.5
  16.4 0.9 copy-done.6
  17.3 1.4 %shard_map.131.refs_0_ = bf16[128,512]{1,0:T(8,128)(2,1)S(1)} custom-call(s32[2]{0:T(128)S(1)} %convert_element_type.45.seen_ref, f32[8,128,128]{2,1,0:T(8,128)S(1)} %get-tuple-element.14.score_ref, bf16[128,512]{1,0:T(8,128)(2,1)S(1)} %get-tuple-element.15.query_ref, bf16[128,512]{1,0:T(8,128)(2,1)S(1)} %collective-permute-done.refs_0_, ...), custom_call_target="tpu_custom_call" | custom-call | flops 134217728 | bytes 1179656 | tf_op jit(solution)/shard_map/pallas_call | solution.py:229
  18.7 1.6 %constant_dynamic-update-slice_fusion.2 = bf16[256,512]{1,0:T(8,128)(2,1)} fusion(bf16[256,512]{1,0:T(8,128)(2,1)} %constant_dynamic-update-slice_fusion.3, bf16[128,512]{1,0:T(8,128)(2,1)} %collective-permute-done.16), kind=kLoop, calls=%fused_computation.74 | loop fusion | bytes 262144 | tf_op jit(solution)/shard_map/concatenate | solution.py:321
  20.3 0.5 collective-permute-start.4
  20.9 3.6 %collective-permute-start.22 = (bf16[256,512]{1,0:T(8,128)(2,1)}, bf16[256,512]{1,0:T(8,128)(2,1)S(1)}, u32[]{:S(2)}, u32[]{:S(2)}) collective-permute-start(bf16[256,512]{1,0:T(8,128)(2,1)} %constant_dynamic-update-slice_fusion.2), channel_id=1, source_target_pairs={{0,12},{4,8},{8,4},{12,0},{1,13},{5,9},{9,5},{13,1},{2,14},{6,10},... | collective-permute-start | bytes 786440 | tf_op jit(solution)/shard_map/ppermute | solution.py:122
  24.6 1.0 constant_dynamic-update-slice_fusion.11
  25.6 0.9 collective-permute-start.18
  26.4 1.0 constant_dynamic-update-slice_fusion.10
  27.4 2.4 %fusion.60 = f32[256,1024]{1,0:T(8,128)S(1)} fusion(bf16[256,1024]{1,0:T(8,128)(2,1)S(1)} %constant_dynamic-update-slice_fusion.10, bf16[1024,1024]{1,0:T(8,128)(2,1)} %param.20), kind=kOutput, calls=%fused_computation.101 | convolution fusion | flops 536870912 | bytes 3670016 | tf_op jit(solution)/shard_map/dot_general | solution.py:360
  29.8 17.8 %collective-permute-done.20 = bf16[256,512]{1,0:T(8,128)(2,1)S(1)} collective-permute-done((bf16[256,512]{1,0:T(8,128)(2,1)}, bf16[256,512]{1,0:T(8,128)(2,1)S(1)}, u32[]{:S(2)}, u32[]{:S(2)}) %collective-permute-start.20) | collective-permute-done | bytes 262176 | tf_op jit(solution)/shard_map/ppermute | solution.py:122
  47.8 0.6 collective-permute-start.19
  48.6 0.6 collective-permute-done.21
  49.4 0.2 collective-permute-done.19
  49.6 0.7 fusion.61
  50.4 0.7 fusion.62
  51.1 0.4 copy-done.4
  51.6 2.0 %shard_map.132 = (f32[128,512]{1,0:T(8,128)S(1)}, bf16[128,512]{1,0:T(8,128)(2,1)S(1)}) custom-call(s32[2]{0:T(128)S(1)} %pad_add_fusion.place_ref, f32[1,512]{1,0:T(1,128)S(1)} %get-tuple-element.13.gain_ref, bf16[128,512]{1,0:T(8,128)(2,1)S(1)} %shard_map.131.refs_0_, bf16[128,512]{1,0:T(8,128)(2,1)S(1)} %collective-permute-done.2.refs_1_, ...), custom_call_target="tpu_custom_call" | custom-call | flops 268435456 | bytes 3016712 | tf_op jit(solution)/shard_map/pallas_call | solution.py:229
  53.6 0.6 collective-permute-start.5
  54.2 5.1 %collective-permute-done.5 = bf16[128,512]{1,0:T(8,128)(2,1)S(1)} collective-permute-done((bf16[128,512]{1,0:T(8,128)(2,1)S(1)}, bf16[128,512]{1,0:T(8,128)(2,1)S(1)}, u32[]{:S(2)}, u32[]{:S(2)}) %collective-permute-start.5) | collective-permute-done | bytes 131104 | tf_op jit(solution)/shard_map/ppermute | solution.py:122
  59.4 0.7 fusion.63
  60.2 2.5 %collective-permute-start.14 = (bf16[256,512]{1,0:T(8,128)(2,1)S(1)}, bf16[256,512]{1,0:T(8,128)(2,1)S(1)}, u32[]{:S(2)}, u32[]{:S(2)}) collective-permute-start(bf16[256,512]{1,0:T(8,128)(2,1)S(1)} %constant_dynamic-update-slice_fusion), channel_id=1, source_target_pairs={{0,12},{4,8},{8,4},{12,0},{1,13},{5,9},{9,5},{13,1},{2,14},{6,10},... | collective-permute-start | bytes 786440 | tf_op jit(solution)/shard_map/ppermute | solution.py:122
  62.7 1.9 %collective-permute-start.10 = (bf16[256,512]{1,0:T(8,128)(2,1)S(1)}, bf16[256,512]{1,0:T(8,128)(2,1)S(1)}, u32[]{:S(2)}, u32[]{:S(2)}) collective-permute-start(bf16[256,512]{1,0:T(8,128)(2,1)S(1)} %constant_dynamic-update-slice_fusion), channel_id=1, source_target_pairs={{0,4},{4,0},{8,12},{12,8},{1,5},{5,1},{9,13},{13,9},{2,6},{6,2},{1... | collective-permute-start | bytes 786440 | tf_op jit(solution)/shard_map/ppermute | solution.py:122
  64.8 1.4 %fusion.36 = (bf16[256,1024]{1,0:T(8,128)(2,1)S(1)}, bf16[256,1024]{1,0:T(8,128)(2,1)S(1)}) fusion(f32[256,1024]{1,0:T(8,128)S(1)} %fusion.60, bf16[256,1024]{1,0:T(8,128)(2,1)S(1)} %constant_dynamic-update-slice_fusion.18, bf16[1024,1024]{1,0:T(8,128)(2,1)S(1)} %copy-done), kind=kOutput, calls=%fused_computation.45 | convolution fusion | flops 542638080 | bytes 4718592 | tf_op jit(solution)/shard_map/dot_general | solution.py:347
  66.2 0.7 convolution_convert_fusion
  67.0 0.7 collective-permute-start.9
  67.7 3.6 %collective-permute-done.14 = bf16[256,512]{1,0:T(8,128)(2,1)S(1)} collective-permute-done((bf16[256,512]{1,0:T(8,128)(2,1)S(1)}, bf16[256,512]{1,0:T(8,128)(2,1)S(1)}, u32[]{:S(2)}, u32[]{:S(2)}) %collective-permute-start.14) | collective-permute-done | bytes 262176 | tf_op jit(solution)/shard_map/ppermute | solution.py:122
  71.3 0.5 collective-permute-start.8
  71.9 8.4 %collective-permute-done.10 = bf16[256,512]{1,0:T(8,128)(2,1)S(1)} collective-permute-done((bf16[256,512]{1,0:T(8,128)(2,1)S(1)}, bf16[256,512]{1,0:T(8,128)(2,1)S(1)}, u32[]{:S(2)}, u32[]{:S(2)}) %collective-permute-start.10) | collective-permute-done | bytes 262176 | tf_op jit(solution)/shard_map/ppermute | solution.py:122
  80.4 4.6 %collective-permute-done.12 = bf16[256,512]{1,0:T(8,128)(2,1)S(1)} collective-permute-done((bf16[256,512]{1,0:T(8,128)(2,1)S(1)}, bf16[256,512]{1,0:T(8,128)(2,1)S(1)}, u32[]{:S(2)}, u32[]{:S(2)}) %collective-permute-start.12) | collective-permute-done | bytes 262176 | tf_op jit(solution)/shard_map/ppermute | solution.py:122
  85.1 0.6 collective-permute-start.13
  85.7 0.8 add_convert_fusion
  86.6 1.4 %multiply_convert_fusion.2 = (bf16[256,1024]{1,0:T(8,128)(2,1)S(1)}, bf16[256,1024]{1,0:T(8,128)(2,1)S(1)}) fusion(f32[256,1024]{1,0:T(8,128)S(1)} %fusion.61, bf16[256,1024]{1,0:T(8,128)(2,1)S(1)} %constant_dynamic-update-slice_fusion.16, bf16[1024,1024]{1,0:T(8,128)(2,1)S(1)} %copy-done), kind=kOutput, calls=%fused_computation.69 | convolution fusion | flops 542638080 | bytes 4718592 | tf_op jit(solution)/shard_map/dot_general | solution.py:347
  88.0 1.4 %multiply_convert_fusion.1 = (bf16[256,1024]{1,0:T(8,128)(2,1)S(1)}, bf16[256,1024]{1,0:T(8,128)(2,1)S(1)}) fusion(f32[256,1024]{1,0:T(8,128)S(1)} %fusion.62, bf16[256,1024]{1,0:T(8,128)(2,1)S(1)} %constant_dynamic-update-slice_fusion.14, bf16[1024,1024]{1,0:T(8,128)(2,1)S(1)} %copy-done), kind=kOutput, calls=%fused_computation.68 | convolution fusion | flops 542638080 | bytes 4718592 | tf_op jit(solution)/shard_map/dot_general | solution.py:347
  89.4 1.4 %multiply_convert_fusion = (bf16[256,1024]{1,0:T(8,128)(2,1)S(1)}, bf16[256,1024]{1,0:T(8,128)(2,1)S(1)}) fusion(f32[256,1024]{1,0:T(8,128)S(1)} %fusion.63, bf16[256,1024]{1,0:T(8,128)(2,1)S(1)} %constant_dynamic-update-slice_fusion.12, bf16[1024,1024]{1,0:T(8,128)(2,1)S(1)} %copy-done), kind=kOutput, calls=%fused_computation.67 | convolution fusion | flops 542638080 | bytes 4718592 | tf_op jit(solution)/shard_map/dot_general | solution.py:347
  90.8 4.6 %fusion.15 = f32[1024,1024]{1,0:T(8,128)} fusion(bf16[256,1024]{1,0:T(8,128)(2,1)S(1)} %get-tuple-element.27, bf16[256,1024]{1,0:T(8,128)(2,1)S(1)} %get-tuple-element.25, bf16[256,1024]{1,0:T(8,128)(2,1)S(1)} %get-tuple-element.23, bf16[256,1024]{1,0:T(8,128)(2,1)S(1)} %get-tuple-element.30, bf16[256,1024]{1,0:T(8,128)(2,1)S(1)} %constant_dynamic-update-slice_fusion.4, ...), kind=kOutput, calls=%fused_computation.15 | convolution fusion | flops 2164260864 | bytes 8388608 | tf_op jit(solution)/shard_map/dot_general | solution.py:370
  95.5 4.4 %fusion = f32[1024,1024]{1,0:T(8,128)} fusion(bf16[256,1024]{1,0:T(8,128)(2,1)S(1)} %constant_dynamic-update-slice_fusion.12, bf16[256,1024]{1,0:T(8,128)(2,1)S(1)} %constant_dynamic-update-slice_fusion.14, bf16[256,1024]{1,0:T(8,128)(2,1)S(1)} %constant_dynamic-update-slice_fusion.16, bf16[256,1024]{1,0:T(8,128)(2,1)S(1)} %constant_dynamic-update-slice_fusion.18, ...), kind=kOutput, calls=%fused_computation | convolution fusion | flops 2164260864 | bytes 8388608 | tf_op jit(solution)/shard_map/dot_general | solution.py:367
  (75 shorter events, 1.7 us)
Async XLA Ops:
  0.6 64.1 %copy-start = (bf16[1024,1024]{1,0:T(8,128)(2,1)S(1)}, bf16[1024,1024]{1,0:T(8,128)(2,1)}, u32[]{:S(2)}) copy-start(bf16[1024,1024]{1,0:T(8,128)(2,1)} %param.19) | copy-start | bytes 6291460
  0.6 15.1 %collective-permute-start = (bf16[128,512]{1,0:T(8,128)(2,1)}, bf16[128,512]{1,0:T(8,128)(2,1)S(1)}, u32[]{:S(2)}, u32[]{:S(2)}) collective-permute-start(bf16[128,512]{1,0:T(8,128)(2,1)} %refs_1_.1), channel_id=1, source_target_pairs={{0,2},{2,0},{1,3},{3,1},{4,6},{6,4},{5,7},{7,5},{8,10},{10,8},{9,1... | collective-permute-start | bytes 393224 | tf_op jit(solution)/shard_map/ppermute | solution.py:122
  3.6 12.1 %collective-permute-start.1 = (bf16[128,512]{1,0:T(8,128)(2,1)}, bf16[128,512]{1,0:T(8,128)(2,1)S(1)}, u32[]{:S(2)}, u32[]{:S(2)}) collective-permute-start(bf16[128,512]{1,0:T(8,128)(2,1)} %refs_2_.1), channel_id=1, source_target_pairs={{0,2},{2,0},{1,3},{3,1},{4,6},{6,4},{5,7},{7,5},{8,10},{10,8},{9,1... | collective-permute-start | bytes 393224 | tf_op jit(solution)/shard_map/ppermute | solution.py:122
  3.7 14.9 %collective-permute-start.16 = (bf16[128,512]{1,0:T(8,128)(2,1)}, bf16[128,512]{1,0:T(8,128)(2,1)}, u32[]{:S(2)}, u32[]{:S(2)}) collective-permute-start(bf16[128,512]{1,0:T(8,128)(2,1)} %refs_6_.1), channel_id=1, source_target_pairs={{0,2},{2,0},{1,3},{3,1},{4,6},{6,4},{5,7},{7,5},{8,10},{10,8},{9,1... | collective-permute-start | bytes 393224 | tf_op jit(solution)/shard_map/ppermute | solution.py:122
  7.3 1.2 %copy-start.1 = (bf16[512,1024]{1,0:T(8,128)(2,1)S(1)}, bf16[512,1024]{1,0:T(8,128)(2,1)}, u32[]{:S(2)}) copy-start(bf16[512,1024]{1,0:T(8,128)(2,1)} %refs_3_.1) | copy-start | bytes 3145732
  8.5 0.9 copy-start.7
  9.4 0.9 copy-start.8
  10.3 0.9 copy-start.9
  11.2 0.9 copy-start.10
  12.1 0.7 copy-start.11
  12.8 8.0 %copy-start.2 = (bf16[512,1024]{1,0:T(8,128)(2,1)S(1)}, bf16[512,1024]{1,0:T(8,128)(2,1)}, u32[]{:S(2)}) copy-start(bf16[512,1024]{1,0:T(8,128)(2,1)} %refs_3_.1) | copy-start | bytes 3145732
  15.0 5.3 %copy-start.3 = (bf16[512,1024]{1,0:T(8,128)(2,1)}, bf16[512,1024]{1,0:T(8,128)(2,1)S(1)}, u32[]{:S(2)}) copy-start(bf16[512,1024]{1,0:T(8,128)(2,1)S(1)} %get-tuple-element.17.refs_2_) | copy-start | bytes 3145732
  15.7 0.7 copy-start.5
  16.4 0.9 copy-start.6
  20.3 5.3 %collective-permute-start.17 = (bf16[256,512]{1,0:T(8,128)(2,1)}, bf16[256,512]{1,0:T(8,128)(2,1)}, u32[]{:S(2)}, u32[]{:S(2)}) collective-permute-start(bf16[256,512]{1,0:T(8,128)(2,1)} %constant_dynamic-update-slice_fusion.2), channel_id=1, source_target_pairs={{0,1},{1,0},{2,3},{3,2},{4,5},{5,4},{6,7},{7,6},{8,9},{9,8},{10,11... | collective-permute-start | bytes 786440 | tf_op jit(solution)/shard_map/ppermute | solution.py:122
  20.3 30.9 %collective-permute-start.4 = (bf16[128,512]{1,0:T(8,128)(2,1)}, bf16[128,512]{1,0:T(8,128)(2,1)S(1)}, u32[]{:S(2)}, u32[]{:S(2)}) collective-permute-start(bf16[128,512]{1,0:T(8,128)(2,1)} %refs_4_.1), channel_id=1, source_target_pairs={{0,1},{1,0},{2,3},{3,2},{4,5},{5,4},{6,7},{7,6},{8,9},{9,8},{10,11... | collective-permute-start | bytes 393224 | tf_op jit(solution)/shard_map/ppermute | solution.py:122
  20.8 30.4 %collective-permute-start.3 = (bf16[512,1024]{1,0:T(8,128)(2,1)S(1)}, bf16[512,1024]{1,0:T(8,128)(2,1)}, u32[]{:S(2)}, u32[]{:S(2)}) collective-permute-start(bf16[512,1024]{1,0:T(8,128)(2,1)S(1)} %copy-done.2), channel_id=1, source_target_pairs={{0,1},{1,0},{2,3},{3,2},{4,5},{5,4},{6,7},{7,6},{8,9},{9,8},{10,11... | collective-permute-start | bytes 3145736 | tf_op jit(solution)/shard_map/ppermute | solution.py:122
  20.9 27.5 %collective-permute-start.22 = (bf16[256,512]{1,0:T(8,128)(2,1)}, bf16[256,512]{1,0:T(8,128)(2,1)S(1)}, u32[]{:S(2)}, u32[]{:S(2)}) collective-permute-start(bf16[256,512]{1,0:T(8,128)(2,1)} %constant_dynamic-update-slice_fusion.2), channel_id=1, source_target_pairs={{0,12},{4,8},{8,4},{12,0},{1,13},{5,9},{9,5},{13,1},{2,14},{6,10},... | collective-permute-start | bytes 786440 | tf_op jit(solution)/shard_map/ppermute | solution.py:122
  24.5 23.1 %collective-permute-start.20 = (bf16[256,512]{1,0:T(8,128)(2,1)}, bf16[256,512]{1,0:T(8,128)(2,1)S(1)}, u32[]{:S(2)}, u32[]{:S(2)}) collective-permute-start(bf16[256,512]{1,0:T(8,128)(2,1)} %constant_dynamic-update-slice_fusion.2), channel_id=1, source_target_pairs={{0,8},{4,12},{8,0},{12,4},{1,9},{5,13},{9,1},{13,5},{2,10},{6,14},... | collective-permute-start | bytes 786440 | tf_op jit(solution)/shard_map/ppermute | solution.py:122
  25.6 22.2 %collective-permute-start.18 = (bf16[256,512]{1,0:T(8,128)(2,1)}, bf16[256,512]{1,0:T(8,128)(2,1)S(1)}, u32[]{:S(2)}, u32[]{:S(2)}) collective-permute-start(bf16[256,512]{1,0:T(8,128)(2,1)} %constant_dynamic-update-slice_fusion.2), channel_id=1, source_target_pairs={{0,4},{4,0},{8,12},{12,8},{1,5},{5,1},{9,13},{13,9},{2,6},{6,2},{1... | collective-permute-start | bytes 786440 | tf_op jit(solution)/shard_map/ppermute | solution.py:122
  29.8 19.8 %copy-start.12 = (bf16[1024,1024]{1,0:T(8,128)(2,1)S(1)}, bf16[1024,1024]{1,0:T(8,128)(2,1)}, u32[]{:S(2)}) copy-start(bf16[1024,1024]{1,0:T(8,128)(2,1)} %param.20) | copy-start | bytes 6291460
  47.6 1.5 %collective-permute-start.21 = (bf16[256,512]{1,0:T(8,128)(2,1)S(1)}, bf16[256,512]{1,0:T(8,128)(2,1)S(1)}, u32[]{:S(2)}, u32[]{:S(2)}) collective-permute-start(bf16[256,512]{1,0:T(8,128)(2,1)S(1)} %collective-permute-done.20), channel_id=1, source_target_pairs={{0,1},{1,0},{2,3},{3,2},{4,5},{5,4},{6,7},{7,6},{8,9},{9,8},{10,11... | collective-permute-start | bytes 786440 | tf_op jit(solution)/shard_map/ppermute | solution.py:122
  47.8 1.8 %collective-permute-start.19 = (bf16[256,512]{1,0:T(8,128)(2,1)S(1)}, bf16[256,512]{1,0:T(8,128)(2,1)S(1)}, u32[]{:S(2)}, u32[]{:S(2)}) collective-permute-start(bf16[256,512]{1,0:T(8,128)(2,1)S(1)} %collective-permute-done.18), channel_id=1, source_target_pairs={{0,1},{1,0},{2,3},{3,2},{4,5},{5,4},{6,7},{7,6},{8,9},{9,8},{10,11... | collective-permute-start | bytes 786440 | tf_op jit(solution)/shard_map/ppermute | solution.py:122
  48.4 2.7 %collective-permute-start.2 = (bf16[128,512]{1,0:T(8,128)(2,1)S(1)}, bf16[128,512]{1,0:T(8,128)(2,1)S(1)}, u32[]{:S(2)}, u32[]{:S(2)}) collective-permute-start(bf16[128,512]{1,0:T(8,128)(2,1)S(1)} %shard_map.131.refs_0_), channel_id=1, source_target_pairs={{0,1},{1,0},{2,3},{3,2},{4,5},{5,4},{6,7},{7,6},{8,9},{9,8},{10,11... | collective-permute-start | bytes 393224 | tf_op jit(solution)/shard_map/ppermute | solution.py:122
  49.2 5.0 %collective-permute-start.23 = (bf16[256,512]{1,0:T(8,128)(2,1)S(1)}, bf16[256,512]{1,0:T(8,128)(2,1)S(1)}, u32[]{:S(2)}, u32[]{:S(2)}) collective-permute-start(bf16[256,512]{1,0:T(8,128)(2,1)S(1)} %collective-permute-done.22), channel_id=1, source_target_pairs={{0,1},{1,0},{2,3},{3,2},{4,5},{5,4},{6,7},{7,6},{8,9},{9,8},{10,11... | collective-permute-start | bytes 786440 | tf_op jit(solution)/shard_map/ppermute | solution.py:122
  50.3 1.2 %copy-start.4 = (bf16[512,1024]{1,0:T(8,128)(2,1)S(1)}, bf16[512,1024]{1,0:T(8,128)(2,1)}, u32[]{:S(2)}) copy-start(bf16[512,1024]{1,0:T(8,128)(2,1)} %copy-done.3) | copy-start | bytes 3145732
  53.6 5.8 %collective-permute-start.5 = (bf16[128,512]{1,0:T(8,128)(2,1)S(1)}, bf16[128,512]{1,0:T(8,128)(2,1)S(1)}, u32[]{:S(2)}, u32[]{:S(2)}) collective-permute-start(bf16[128,512]{1,0:T(8,128)(2,1)S(1)} %get-tuple-element.20), channel_id=1, source_target_pairs={{0,2},{2,0},{1,3},{3,1},{4,6},{6,4},{5,7},{7,5},{8,10},{10,8},{9,1... | collective-permute-start | bytes 393224 | tf_op jit(solution)/shard_map/ppermute | solution.py:122
  59.3 5.4 %collective-permute-start.6 = (bf16[256,512]{1,0:T(8,128)(2,1)S(1)}, bf16[256,512]{1,0:T(8,128)(2,1)S(1)}, u32[]{:S(2)}, u32[]{:S(2)}) collective-permute-start(bf16[256,512]{1,0:T(8,128)(2,1)S(1)} %constant_dynamic-update-slice_fusion), channel_id=1, source_target_pairs={{0,1},{1,0},{2,3},{3,2},{4,5},{5,4},{6,7},{7,6},{8,9},{9,8},{10,11... | collective-permute-start | bytes 786440 | tf_op jit(solution)/shard_map/ppermute | solution.py:122
  60.2 11.1 %collective-permute-start.14 = (bf16[256,512]{1,0:T(8,128)(2,1)S(1)}, bf16[256,512]{1,0:T(8,128)(2,1)S(1)}, u32[]{:S(2)}, u32[]{:S(2)}) collective-permute-start(bf16[256,512]{1,0:T(8,128)(2,1)S(1)} %constant_dynamic-update-slice_fusion), channel_id=1, source_target_pairs={{0,12},{4,8},{8,4},{12,0},{1,13},{5,9},{9,5},{13,1},{2,14},{6,10},... | collective-permute-start | bytes 786440 | tf_op jit(solution)/shard_map/ppermute | solution.py:122
  62.7 22.3 %collective-permute-start.12 = (bf16[256,512]{1,0:T(8,128)(2,1)S(1)}, bf16[256,512]{1,0:T(8,128)(2,1)S(1)}, u32[]{:S(2)}, u32[]{:S(2)}) collective-permute-start(bf16[256,512]{1,0:T(8,128)(2,1)S(1)} %constant_dynamic-update-slice_fusion), channel_id=1, source_target_pairs={{0,8},{4,12},{8,0},{12,4},{1,9},{5,13},{9,1},{13,5},{2,10},{6,14},... | collective-permute-start | bytes 786440 | tf_op jit(solution)/shard_map/ppermute | solution.py:122
  62.7 17.5 %collective-permute-start.10 = (bf16[256,512]{1,0:T(8,128)(2,1)S(1)}, bf16[256,512]{1,0:T(8,128)(2,1)S(1)}, u32[]{:S(2)}, u32[]{:S(2)}) collective-permute-start(bf16[256,512]{1,0:T(8,128)(2,1)S(1)} %constant_dynamic-update-slice_fusion), channel_id=1, source_target_pairs={{0,4},{4,0},{8,12},{12,8},{1,5},{5,1},{9,13},{13,9},{2,6},{6,2},{1... | collective-permute-start | bytes 786440 | tf_op jit(solution)/shard_map/ppermute | solution.py:122
  66.9 18.1 %collective-permute-start.7 = (bf16[128,512]{1,0:T(8,128)(2,1)S(1)}, bf16[128,512]{1,0:T(8,128)(2,1)S(1)}, u32[]{:S(2)}, u32[]{:S(2)}) collective-permute-start(bf16[128,512]{1,0:T(8,128)(2,1)S(1)} %get-tuple-element.31), channel_id=1, source_target_pairs={{0,1},{1,0},{2,3},{3,2},{4,5},{5,4},{6,7},{7,6},{8,9},{9,8},{10,11... | collective-permute-start | bytes 393224 | tf_op jit(solution)/shard_map/ppermute | solution.py:267
  67.0 18.6 %collective-permute-start.9 = (bf16[128,512]{1,0:T(8,128)(2,1)S(1)}, bf16[128,512]{1,0:T(8,128)(2,1)S(1)}, u32[]{:S(2)}, u32[]{:S(2)}) collective-permute-start(bf16[128,512]{1,0:T(8,128)(2,1)S(1)} %get-tuple-element.32), channel_id=1, source_target_pairs={{0,3},{1,2},{2,1},{3,0},{4,7},{5,6},{6,5},{7,4},{8,11},{9,10},{10,... | collective-permute-start | bytes 393224 | tf_op jit(solution)/shard_map/ppermute | solution.py:267
  71.3 14.4 %collective-permute-start.8 = (bf16[128,512]{1,0:T(8,128)(2,1)S(1)}, bf16[128,512]{1,0:T(8,128)(2,1)S(1)}, u32[]{:S(2)}, u32[]{:S(2)}) collective-permute-start(bf16[128,512]{1,0:T(8,128)(2,1)S(1)} %get-tuple-element.33), channel_id=1, source_target_pairs={{0,2},{1,3},{2,0},{3,1},{4,6},{5,7},{6,4},{7,5},{8,10},{9,11},{10,... | collective-permute-start | bytes 393224 | tf_op jit(solution)/shard_map/ppermute | solution.py:267
  80.3 9.1 %collective-permute-start.15 = (bf16[256,512]{1,0:T(8,128)(2,1)S(1)}, bf16[256,512]{1,0:T(8,128)(2,1)S(1)}, u32[]{:S(2)}, u32[]{:S(2)}) collective-permute-start(bf16[256,512]{1,0:T(8,128)(2,1)S(1)} %collective-permute-done.14), channel_id=1, source_target_pairs={{0,1},{1,0},{2,3},{3,2},{4,5},{5,4},{6,7},{7,6},{8,9},{9,8},{10,11... | collective-permute-start | bytes 786440 | tf_op jit(solution)/shard_map/ppermute | solution.py:122
  85.0 1.5 %collective-permute-start.11 = (bf16[256,512]{1,0:T(8,128)(2,1)S(1)}, bf16[256,512]{1,0:T(8,128)(2,1)S(1)}, u32[]{:S(2)}, u32[]{:S(2)}) collective-permute-start(bf16[256,512]{1,0:T(8,128)(2,1)S(1)} %collective-permute-done.10), channel_id=1, source_target_pairs={{0,1},{1,0},{2,3},{3,2},{4,5},{5,4},{6,7},{7,6},{8,9},{9,8},{10,11... | collective-permute-start | bytes 786440 | tf_op jit(solution)/shard_map/ppermute | solution.py:122
  85.1 2.9 %collective-permute-start.13 = (bf16[256,512]{1,0:T(8,128)(2,1)S(1)}, bf16[256,512]{1,0:T(8,128)(2,1)S(1)}, u32[]{:S(2)}, u32[]{:S(2)}) collective-permute-start(bf16[256,512]{1,0:T(8,128)(2,1)S(1)} %collective-permute-done.12), channel_id=1, source_target_pairs={{0,1},{1,0},{2,3},{3,2},{4,5},{5,4},{6,7},{7,6},{8,9},{9,8},{10,11... | collective-permute-start | bytes 786440 | tf_op jit(solution)/shard_map/ppermute | solution.py:122

commit v4 on v3

--- a/solution.py
+++ b/solution.py
@@ -105,6 +105,9 @@
     )
     return (layer_out, up_grad, down_grad)
 
+GAIN_ROWS = 16
+STAGE_LIMIT = 56 * 2**20
+
 
 def shift(x, axis, k):
     n = lax.axis_size(axis)
@@ -138,20 +141,42 @@
     ) * HEAD ** (-0.5)
 
 
-def stage(count, *refs):
-    sources, targets, score_ref, sems = refs[:count], refs[count : 2 * count], refs[-2], refs[-1]
+def stage(place_ref, gain_ref, query_src, key_src, value_src, weight_src, residual_src, *refs):
+    cores = place_ref.shape[0]
+    cots = refs[:cores]
+    query_ref, key_ref, value_ref, weight_ref, packed_ref, cot_ref, score_ref, sems = refs[cores:]
+    rows, half = query_ref.shape
+    pairs = [
+        (query_src, query_ref),
+        (key_src, key_ref),
+        (value_src, value_ref),
+        (weight_src, weight_ref),
+        (residual_src, packed_ref.at[pl.ds(0, rows)]),
+    ]
+    for j, source in enumerate(cots):
+        cols = pl.ds(pl.multiple_of(place_ref[j] * half, half), half)
+        pairs.append((source, cot_ref.at[:, cols]))
     copies = [
-        pltpu.make_async_copy(source, target, sems.at[i])
-        for i, (source, target) in enumerate(zip(sources, targets))
+        pltpu.make_async_copy(source, target, sems.at[i]) for i, (source, target) in enumerate(pairs)
     ]
     for copy in copies:
         copy.start()
+    gain = gain_ref[...]
+    high = gain.astype(jnp.bfloat16)
+    rest = gain - high.astype(jnp.float32)
+    middle = rest.astype(jnp.bfloat16)
+    low = rest - middle.astype(jnp.float32)
+    row = lax.broadcasted_iota(jnp.int32, (GAIN_ROWS, half), 0)
+    parts = jnp.where(
+        row == 0,
+        high.astype(jnp.float32),
+        jnp.where(row == 1, middle.astype(jnp.float32), jnp.where(row == 2, low, 0.0)),
+    )
+    packed_ref[pl.ds(rows, GAIN_ROWS), :] = parts.astype(jnp.bfloat16)
     copies[0].wait()
     copies[1].wait()
-    query_ref, key_ref = targets[:2]
-    rows = query_ref.shape[0]
     lane = lax.broadcasted_iota(jnp.int32, (rows, 2 * HEAD), 1)
-    for pair in range(query_ref.shape[1] // (2 * HEAD)):
+    for pair in range(half // (2 * HEAD)):
         cols = pl.ds(pair * 2 * HEAD, 2 * HEAD)
         query, key = query_ref[:, cols], key_ref[:, cols]
         for head in range(2):
@@ -196,30 +221,31 @@
         out_ref[:, cols] = jnp.where(lane < HEAD, found[0], found[1]).astype(jnp.bfloat16)
 
 
-def project(place_ref, gain_ref, *refs):
-    cores = (len(refs) - 3) // 3
-    attended, weights, residuals = refs[:cores], refs[cores : 2 * cores], refs[2 * cores : 3 * cores]
-    stream_ref, normed_ref, full = refs[3 * cores :]
-    half = stream_ref.shape[1]
+def project(place_ref, *refs):
+    cores = place_ref.shape[0]
+    attended, weights, packed = refs[:cores], refs[cores : 2 * cores], refs[2 * cores : 3 * cores]
+    stream_ref, normed_ref, full, gain = refs[3 * cores :]
+    rows, half = stream_ref.shape
+    width = half * cores
     total = jnp.dot(attended[0][...], weights[0][...], preferred_element_type=jnp.float32)
     for j in range(1, cores):
         total = total + jnp.dot(
             attended[j][...], weights[j][...], preferred_element_type=jnp.float32
         )
     full[...] = total
-    parts = []
     for j in range(cores):
         cols = pl.ds(pl.multiple_of(place_ref[j] * half, half), half)
-        parts.append(full[:, cols] + residuals[j][...].astype(jnp.float32))
-    width = half * cores
-    center = sum(jnp.sum(part, axis=1, keepdims=True) for part in parts) / width
-    spread_sq = sum(
-        jnp.sum((part - center) * (part - center), axis=1, keepdims=True) for part in parts
-    ) / width
-    stream_ref[...] = parts[0]
-    normed_ref[...] = (
-        (parts[0] - center) * lax.rsqrt(spread_sq + 1e-05) * gain_ref[...]
-    ).astype(jnp.bfloat16)
+        part = full[:, cols] + packed[j][pl.ds(0, rows), :].astype(jnp.float32)
+        full[:, cols] = part
+        if j == 0:
+            stream_ref[...] = part
+        gains = packed[j][pl.ds(rows, GAIN_ROWS), :].astype(jnp.float32)
+        gain[0:1, cols] = (gains[1:2] + gains[2:3]) + gains[0:1]
+    stream = full[...]
+    center = jnp.sum(stream, axis=1, keepdims=True) / width
+    shifted = stream - center
+    spread_sq = jnp.sum(shifted * shifted, axis=1, keepdims=True) / width
+    normed_ref[...] = (shifted * lax.rsqrt(spread_sq + 1e-05) * gain[0:1, :]).astype(jnp.bfloat16)
 
 
 def call(kernel, out_shape, smem, args, flops, scratch=()):
@@ -237,34 +263,24 @@
     )(*args)
 
 
-def join(pieces, dim):
-    n = len(pieces)
-    size = pieces[0].shape[dim]
-    shape = list(pieces[0].shape)
-    shape[dim] = size * n
-    whole = jnp.zeros(shape, pieces[0].dtype)
-    for j, piece in enumerate(pieces):
-        start = [0] * len(shape)
-        start[dim] = member("col", j) * size
-        whole = lax.dynamic_update_slice(whole, piece, start)
-    return whole
-
-
-def over_cores(piece, dim):
-    return join([piece] + others(piece, "col"), dim)
-
-
-def send_back(piece, k, j):
-    if not (k or j):
-        return piece
-    grps, cores = lax.axis_size("grp"), lax.axis_size("col")
+def send(x, routes):
+    patches, grps, cores = (lax.axis_size(a) for a in ("patch", "grp", "col"))
     pairs = []
-    for a in range(grps):
-        for b in range(cores):
-            to_grp = (a - k) % grps if grps & (grps - 1) else a ^ k
-            to_core = (b - j) % cores if cores & (cores - 1) else b ^ j
-            pairs.append((a * cores + b, to_grp * cores + to_core))
-    return lax.ppermute(piece, ("grp", "col"), pairs)
+    for p in range(patches):
+        for g in range(grps):
+            for c, route in enumerate(routes):
+                if route is not None:
+                    to = ((p ^ route[0]) * grps + (g ^ route[1])) * cores + c
+                    pairs.append(((p * grps + g) * cores + c, to))
+    return lax.ppermute(x, ("patch", "grp", "col"), pairs)
+
+
+def swap(x):
+    return lax.ppermute(x, "col", [(0, 1), (1, 0)])
+
+
+def hand_over(x):
+    return lax.ppermute(x, "col", [(0, 1)])
 
 
 def gather_plan(
@@ -282,34 +298,55 @@
 ):
     cores = lax.axis_size("col")
     grps = lax.axis_size("grp")
-    patches = lax.axis_size("patch")
     rows, half = query_vectors.shape
     width = half * cores
 
     key_others = others(key_vectors, "grp")
     value_others = others(value_vectors, "grp")
-    cot_others = others(cotangent, "grp")
+    cot_others = others(cotangent, "col")
     weight_others = others(output_weight, "col")
-    residual_others = others(residual, "col")
 
     source = jnp.stack([member("grp", k) for k in range(grps)])
     slots = jnp.arange(neighbor_ids.shape[1], dtype=jnp.int32) < neighbor_count[0]
     seen = jnp.any((neighbor_ids[0][None] == source[:, None]) & slots[None], axis=1)
-    held = [query_vectors, key_vectors, value_vectors, output_weight, residual, norm_gain[None], cotangent]
+    place = jnp.stack([member("col", j) for j in range(cores)])
     heads = half // HEAD
-    *held, scores = pl.pallas_call(
-        functools.partial(stage, len(held)),
-        out_shape=[jax.ShapeDtypeStruct(a.shape, a.dtype) for a in held]
-        + [jax.ShapeDtypeStruct((heads, rows, rows), jnp.float32)],
-        in_specs=[pl.BlockSpec(memory_space=pl.ANY)] * len(held),
-        out_specs=[pl.BlockSpec(memory_space=pltpu.VMEM)] * (len(held) + 1),
-        scratch_shapes=[pltpu.SemaphoreType.DMA((len(held),))],
+    bf16 = jnp.bfloat16
+    query, _, value, weight, packed, cot, scores = pl.pallas_call(
+        stage,
+        out_shape=[jax.ShapeDtypeStruct((rows, half), bf16)] * 3
+        + [
+            jax.ShapeDtypeStruct(output_weight.shape, bf16),
+            jax.ShapeDtypeStruct((rows + GAIN_ROWS, half), bf16),
+            jax.ShapeDtypeStruct((rows, width), bf16),
+            jax.ShapeDtypeStruct((heads, rows, rows), jnp.float32),
+        ],
+        in_specs=[
+            pl.BlockSpec(memory_space=pltpu.SMEM),
+            pl.BlockSpec((1, half), lambda i: (0, 0)),
+        ]
+        + [pl.BlockSpec(memory_space=pl.ANY)] * (5 + cores),
+        out_specs=[pl.BlockSpec(memory_space=pltpu.VMEM)] * 7,
+        grid=(1,),
+        scratch_shapes=[pltpu.SemaphoreType.DMA((5 + cores,))],
         cost_estimate=pl.CostEstimate(
             flops=2 * rows * rows * width, bytes_accessed=4 * 2**20, transcendentals=0
         ),
-        compiler_params=pltpu.CompilerParams(vmem_limit_bytes=24 * 2**20),
-    )(*held)
-    query, _, value, weight, residual, gain, cot = held
+        compiler_params=pltpu.CompilerParams(vmem_limit_bytes=STAGE_LIMIT),
+    )(
+        place,
+        norm_gain[None],
+        query_vectors,
+        key_vectors,
+        value_vectors,
+        output_weight,
+        residual,
+        cotangent,
+        *cot_others,
+    )
+    packed_others = others(packed, "col")
+    cot12 = send(cot, [(1, 0), (2, 0)])
+    cot3x = send(cot, [(3, 0), (0, 1)])
     attended = call(
         attend,
         jax.ShapeDtypeStruct((rows, half), jnp.bfloat16),
@@ -318,50 +355,63 @@
         4 * rows * rows * grps * width,
     )
     attended_others = others(attended, "col")
-    cots = [jnp.concatenate([cot] + [after(c, attended) for c in cot_others], 0)]
-    cots += others(cots[0], "patch")
     stream, normed = call(
         project,
         (
             jax.ShapeDtypeStruct((rows, half), jnp.float32),
-            jax.ShapeDtypeStruct((rows, half), jnp.bfloat16),
+            jax.ShapeDtypeStruct((rows, width), bf16),
         ),
         1,
-        [jnp.stack([member("col", j) for j in range(cores)]), gain, attended]
+        [place, attended]
         + attended_others
         + [weight]
         + weight_others
-        + [residual]
-        + residual_others,
+        + [packed]
+        + packed_others,
         2 * rows * width * width,
-        [pltpu.VMEM((rows, width), jnp.float32)],
-    )
-    norms = [jnp.concatenate([normed] + others(normed, "grp"), 0)]
-    norms += others(norms[0], "patch")
+        [pltpu.VMEM((rows, width), jnp.float32), pltpu.VMEM((8, width), jnp.float32)],
+    )
+    first = lax.axis_index("col") == 0
+
+    def passed_on(own, by12, by3x):
+        swap12, swap3x = swap(by12), swap(by3x)
+        over12 = send(by12, [(0, 1), (0, 1)])
+        over3 = send(by3x, [(0, 1), None])
+        group = jnp.concatenate([own, jnp.where(first, swap3x, by3x)], 0)
+        third = jnp.concatenate(
+            [jnp.where(first, by3x, swap3x), jnp.where(first, over3, hand_over(over3))], 0
+        )
+        return [
+            group,
+            jnp.concatenate([by12, swap12], 0),
+            jnp.concatenate([over12, swap(over12)], 0),
+            third,
+        ]
+
+    norm12 = send(normed, [(1, 0), (2, 0)])
+    norm3x = send(normed, [(3, 0), (0, 1)])
+    cots = passed_on(cot, after(cot12, normed), after(cot3x, normed))
+    norms = passed_on(normed, norm12, norm3x)
 
     saved = []
     layer_out = None
-    for s in range(patches):
-        normed_rows = over_cores(norms[s], 1)
-        back_rows = over_cores(cots[s], 1)
+    for s, (normed_rows, back_rows) in enumerate(zip(norms, cots)):
         pre = jnp.dot(normed_rows, up_weight, preferred_element_type=jnp.float32)
-        hidden = jax.nn.gelu(pre).astype(jnp.bfloat16)
+        hidden = jax.nn.gelu(pre).astype(bf16)
         if s == 0:
             partial_out = jnp.dot(hidden, down_weight, preferred_element_type=jnp.float32)
-            partial_out = partial_out.astype(jnp.bfloat16)
-            layer_out = stream
-            for k in range(grps):
-                for j in range(cores):
-                    piece = lax.dynamic_slice(
-                        partial_out, (k * rows, member("col", j) * half), (rows, half)
-                    )
-                    layer_out = layer_out + send_back(piece, k, j).astype(jnp.float32)
-            layer_out = layer_out.astype(jnp.bfloat16)
+            partial_out = partial_out.astype(bf16)
+            mine, theirs = (
+                lax.dynamic_slice(partial_out, (0, place[j] * half), (2 * rows, half)) for j in (0, 1)
+            )
+            both = mine.astype(jnp.float32) + swap(theirs).astype(jnp.float32)
+            rest = lax.ppermute(both[rows:].astype(bf16), "grp", [(0, 1), (1, 0)])
+            layer_out = (stream + both[:rows] + rest.astype(jnp.float32)).astype(bf16)
         back_hidden = lax.dot_general(
             back_rows, down_weight, (((1,), (1,)), ((), ())), preferred_element_type=jnp.float32
         )
         _, gelu_back = jax.vjp(jax.nn.gelu, pre)
-        back_pre = gelu_back(back_hidden)[0].astype(jnp.bfloat16)
+        back_pre = gelu_back(back_hidden)[0].astype(bf16)
         saved.append((normed_rows, back_rows, hidden, back_pre))
     all_normed, all_back, all_hidden, all_pre = (jnp.concatenate(a, 0) for a in zip(*saved))
     up_grad = lax.dot_general(
@@ -375,8 +425,9 @@
 
 def layer(*args):
     query_vectors, up_weight = args[0], args[8]
-    tokens = query_vectors.shape[0] * lax.axis_size("grp") * lax.axis_size("patch")
-    if tokens <= 2 * up_weight.shape[1]:
+    patches, grps, cores = (lax.axis_size(a) for a in ("patch", "grp", "col"))
+    tokens = query_vectors.shape[0] * grps * patches
+    if (patches, grps, cores) == (4, 2, 2) and tokens <= 2 * up_weight.shape[1]:
         return gather_plan(*args)
     return shards(*args)
 

time: 100 us -> 75.5 us (0.76); the launches traced: 99.9 us -> 74.2 us
  waiting for transfers between devices: 40.5 us -> 6.81 us
  starting transfers between devices: 17.8 us -> 25.6 us
  local copies, waits for them, and re-layouts: 12.6 us -> 8.74 us
  other arithmetic: 1.75 us -> 3.76 us
  Pallas kernels: 5.53 us -> 7.02 us
    ppermute x21 -> x6, waiting for transfers between devices: 40.4 us -> 1.27 us  [others(): lax.ppermute(x, axis, [(i, i ^ k) for i in range(n)])]
    ppermute x3 -> x18, starting transfers between devices: 1.26 us -> 21.9 us  [the longest x8 14.5 us: send(): return lax.ppermute(x, ('patch', 'grp', 'col'), pairs)]
    ppermute x21 -> x6, starting transfers between devices: 16.6 us -> 3.69 us  [others(): lax.ppermute(x, axis, [(i, i ^ k) for i in range(n)])]
    ppermute x3 -> x18, waiting for transfers between devices: 0.01 us -> 5.54 us  [the longest x8 5.52 us: send(): return lax.ppermute(x, ('patch', 'grp', 'col'), pairs)]
    dynamic_update_slice x16 -> x0, local copies, waits for them, and re-layouts: 2.31 us -> none  [join(): whole = lax.dynamic_update_slice(whole, piece, start)]
    concatenate x2 -> x0, local copies, waits for them, and re-layouts: 1.58 us -> none  [the longest x1 1.57 us: gather_plan(): jnp.concatenate([cot] + [after(c, attended) for c in cot_others], 0)]
    dot_general x4, matrix products: 4.62 us -> 6.11 us  [gather_plan(): lax.dot_general(back_rows, down_weight, (((1,), (1,)), ((), ())), preferr...]
    pallas_call x1, Pallas kernels: 2.18 us -> 3.65 us  [gather_plan(): pl.pallas_call(stage, out_shape=[jax.ShapeDtypeStruct((rows, half), bf16)...]
  transfers between devices with their start and end apart: 24 -> 24, of which waited for: 8 -> 3; matrix products, arithmetic and copies ran while one was open for 15% -> 36% of each run, Pallas kernels for 6% -> 9%
where the time goes in v4:
time: 75.5 us; the launch traced here: 74.2 us
  starting transfers between devices  25.6 us (34%)
  matrix products  20.5 us (27%)
  local copies, waits for them, and re-layouts  8.74 us (12%)
  Pallas kernels  7.02 us (9%)
  waiting for transfers between devices  6.81 us (9%)
  other arithmetic  3.76 us (5%)
  between operations  1.75 us (2%)
    ppermute x8, starting transfers between devices, send(): return lax.ppermute(x, ('patch', 'grp', 'col'), pairs)  14.5 us
    unnamed x30, local copies, waits for them, and re-layouts  8.69 us
    dot_general x4, matrix products, gather_plan(): lax.dot_general(back_rows, down_weight, (((1,), (1,)), ((), ())), preferr...  6.11 us
    ppermute x8, waiting for transfers between devices, send(): return lax.ppermute(x, ('patch', 'grp', 'col'), pairs)  5.52 us
    dot_general x4, matrix products, gather_plan(): pre = jnp.dot(normed_rows, up_weight, preferred_element_type=jnp.float32)  4.82 us
    ppermute x2, starting transfers between devices, hand_over(): return lax.ppermute(x, 'col', [(0, 1)])  4.57 us
    dot_general x1, matrix products, gather_plan(): lax.dot_general(all_normed, all_pre, (((0,), (0,)), ((), ())), preferred_...  4.45 us
    dot_general x1, matrix products, gather_plan(): lax.dot_general(all_hidden, all_back, (((0,), (0,)), ((), ())), preferred...  4.45 us
  transfers between devices with their start and end apart: 24, of which 3 were waited for; matrix products, arithmetic and copies ran while one was open for 36% of the time, Pallas kernels for 9%

profile of v4, /device:TPU:0, one launch (start us, length us, event | category | flops | bytes accessed | tf_op | source)
XLA Modules:
  0.0 74.2 jit_solution(1836232832386830682)
XLA Ops:
  0.6 0.5 collective-permute-start.4
  1.2 0.1 collective-permute-start
  1.2 2.9 %collective-permute-start.1 = (bf16[128,512]{1,0:T(8,128)(2,1)}, bf16[128,512]{1,0:T(8,128)(2,1)S(1)}, u32[]{:S(2)}, u32[]{:S(2)}) collective-permute-start(bf16[128,512]{1,0:T(8,128)(2,1)} %key_src.1), channel_id=1, source_target_pairs={{0,2},{2,0},{1,3},{3,1},{4,6},{6,4},{5,7},{7,5},{8,10},{10,8},{9,1... | collective-permute-start | bytes 393224 | tf_op jit(solution)/shard_map/ppermute | solution.py:125
  4.9 0.7 pad_add_fusion.place_ref
  5.6 0.7 copy-done.8
  6.2 3.6 %shard_map.130 = (bf16[128,512]{1,0:T(8,128)(2,1)}, bf16[128,512]{1,0:T(8,128)(2,1)}, bf16[128,512]{1,0:T(8,128)(2,1)}, bf16[512,1024]{1,0:T(8,128)(2,1)}, bf16[...) custom-call(s32[2]{0:T(128)} %pad_add_fusion.place_ref, f32[1,512]{1,0:T(1,128)} %bitcast.20, ...), custom_call_target="tpu_custom_call" | custom-call | flops 33554432 | bytes 4194304 | tf_op jit(solution)/shard_map/pallas_call | solution.py:315
  10.0 4.2 %collective-permute-start.16 = (bf16[128,1024]{1,0:T(8,128)(2,1)}, bf16[128,1024]{1,0:T(8,128)(2,1)}, u32[]{:S(2)}, u32[]{:S(2)}) collective-permute-start(bf16[128,1024]{1,0:T(8,128)(2,1)} %get-tuple-element.20), channel_id=1, source_target_pairs={{0,12},{1,3},{2,14},{3,1},{4,8},{5,7},{6,10},{7,5},{8,4},{9,11},{1... | collective-permute-start | bytes 786440 | tf_op jit(solution)/shard_map/ppermute | solution.py:275
  14.2 0.8 %and_reduce_fusion = pred[2]{0:T(512)(128)(4,1)S(1)} fusion(pred[2]{0:T(512)(128)(4,1)S(1)} %iota_compare_fusion, s32[2]{0:T(128)} %bitcast.21, s32[2]{0:T(128)S(1)} %pad_add_fusion.1), kind=kLoop, calls=%fused_computation.116 | loop fusion | flops 10 | bytes 20 | tf_op jit(solution)/shard_map/reduce_or | solution.py:311
  15.0 1.0 %copy-done.2 = f32[8,128,128]{2,1,0:T(8,128)S(1)} copy-done((f32[8,128,128]{2,1,0:T(8,128)S(1)}, f32[8,128,128]{2,1,0:T(8,128)}, u32[]{:S(2)}) %copy-start.2) | copy-done | bytes 524312
  16.1 0.9 %copy-done.4 = bf16[128,512]{1,0:T(8,128)(2,1)S(1)} copy-done((bf16[128,512]{1,0:T(8,128)(2,1)S(1)}, bf16[128,512]{1,0:T(8,128)(2,1)}, u32[]{:S(2)}) %copy-start.4) | copy-done | bytes 131096
  17.0 0.9 %copy-done.5 = bf16[128,512]{1,0:T(8,128)(2,1)S(1)} copy-done((bf16[128,512]{1,0:T(8,128)(2,1)S(1)}, bf16[128,512]{1,0:T(8,128)(2,1)}, u32[]{:S(2)}) %copy-start.5) | copy-done | bytes 131096
  17.9 1.4 %shard_map.131.refs_0_ = bf16[128,512]{1,0:T(8,128)(2,1)S(1)} custom-call(s32[2]{0:T(128)S(1)} %convert_element_type.43.seen_ref, f32[8,128,128]{2,1,0:T(8,128)S(1)} %copy-done.2, bf16[128,512]{1,0:T(8,128)(2,1)S(1)} %copy-done.4, bf16[128,512]{1,0:T(8,128)(2,1)S(1)} %collective-permute-done.1.refs_0_, bf16[128,512]{1,0:T(8,128)(2,1)S(1)} %copy-done.5, ...), custom_call_target="tpu_custom_call" | custom-call | flops 134217728 | bytes 1179656 | tf_op jit(solution)/shard_map/pallas_call | solution.py:255
  19.4 1.3 %collective-permute-done.3.refs_1_ = bf16[128,512]{1,0:T(8,128)(2,1)S(1)} collective-permute-done((bf16[128,512]{1,0:T(8,128)(2,1)S(1)}, bf16[128,512]{1,0:T(8,128)(2,1)S(1)}, u32[]{:S(2)}, u32[]{:S(2)}) %collective-permute-start.3) | collective-permute-done | bytes 131104 | tf_op jit(solution)/shard_map/ppermute | solution.py:125
  20.7 1.2 %copy-done.1 = bf16[512,1024]{1,0:T(8,128)(2,1)S(1)} copy-done((bf16[512,1024]{1,0:T(8,128)(2,1)S(1)}, bf16[512,1024]{1,0:T(8,128)(2,1)}, u32[]{:S(2)}) %copy-start.1) | copy-done | bytes 1048600
  21.9 0.9 %copy-done.3 = bf16[144,512]{1,0:T(8,128)(2,1)S(1)} copy-done((bf16[144,512]{1,0:T(8,128)(2,1)S(1)}, bf16[144,512]{1,0:T(8,128)(2,1)}, u32[]{:S(2)}) %copy-start.3) | copy-done | bytes 147480
  22.8 2.0 %shard_map.132 = (f32[128,512]{1,0:T(8,128)S(1)}, bf16[128,1024]{1,0:T(8,128)(2,1)}) custom-call(s32[2]{0:T(128)S(1)} %copy-done.6, bf16[128,512]{1,0:T(8,128)(2,1)S(1)} %shard_map.131.refs_0_, bf16[128,512]{1,0:T(8,128)(2,1)S(1)} %collective-permute-done.3.refs_1_, bf16[512,1024]{1,0:T(8,128)(2,1)S(1)} %copy-done.1, ...), custom_call_target="tpu_custom_call" | custom-call | flops 268435456 | bytes 3178504 | tf_op jit(solution)/shard_map/pallas_call | solution.py:255
  24.8 1.3 %collective-permute-start.6 = (bf16[128,1024]{1,0:T(8,128)(2,1)}, bf16[128,1024]{1,0:T(8,128)(2,1)S(1)}, u32[]{:S(2)}, u32[]{:S(2)}) collective-permute-start(bf16[128,1024]{1,0:T(8,128)(2,1)} %get-tuple-element.19), channel_id=1, source_target_pairs={{0,12},{1,3},{2,14},{3,1},{4,8},{5,7},{6,10},{7,5},{8,4},{9,11},{1... | collective-permute-start | bytes 786440 | tf_op jit(solution)/shard_map/ppermute | solution.py:275
  26.2 1.0 %constant_dynamic-update-slice_fusion.15 = bf16[1024,1024]{1,0:T(8,128)(2,1)S(1)} fusion(bf16[128,1024]{1,0:T(8,128)(2,1)} %get-tuple-element.20), kind=kLoop, calls=%fused_computation.115 | loop fusion | bytes 524288
  27.1 0.1 collective-permute-start.10
  27.3 1.6 %collective-permute-done.18 = bf16[128,1024]{1,0:T(8,128)(2,1)} collective-permute-done((bf16[128,1024]{1,0:T(8,128)(2,1)}, bf16[128,1024]{1,0:T(8,128)(2,1)}, u32[]{:S(2)}, u32[]{:S(2)}) %collective-permute-start.18) | collective-permute-done | bytes 262176 | tf_op jit(solution)/shard_map/ppermute | solution.py:275
  28.9 1.5 %collective-permute-start.20 = (bf16[128,1024]{1,0:T(8,128)(2,1)}, bf16[128,1024]{1,0:T(8,128)(2,1)S(1)}, u32[]{:S(2)}, u32[]{:S(2)}) collective-permute-start(bf16[128,1024]{1,0:T(8,128)(2,1)} %collective-permute-done.18), channel_id=1, source_target_pairs={{0,2},{1,3},{2,0},{3,1},{4,6},{5,7},{6,4},{7,5},{8,10},{9,11},{10,... | collective-permute-start | bytes 786440 | tf_op jit(solution)/shard_map/ppermute | solution.py:275
  30.4 1.0 %constant_dynamic-update-slice_fusion.7 = bf16[1024,1024]{1,0:T(8,128)(2,1)S(1)} fusion(bf16[128,1024]{1,0:T(8,128)(2,1)} %get-tuple-element.19), kind=kLoop, calls=%fused_computation.107 | loop fusion | bytes 524288
  31.4 3.9 %collective-permute-done.6 = bf16[128,1024]{1,0:T(8,128)(2,1)S(1)} collective-permute-done((bf16[128,1024]{1,0:T(8,128)(2,1)}, bf16[128,1024]{1,0:T(8,128)(2,1)S(1)}, u32[]{:S(2)}, u32[]{:S(2)}) %collective-permute-start.6) | collective-permute-done | bytes 262176 | tf_op jit(solution)/shard_map/ppermute | solution.py:275
  35.3 3.4 %collective-permute-start.22 = (bf16[128,1024]{1,0:T(8,128)(2,1)}, bf16[128,1024]{1,0:T(8,128)(2,1)S(1)}, u32[]{:S(2)}, u32[]{:S(2)}) collective-permute-start(bf16[128,1024]{1,0:T(8,128)(2,1)} %collective-permute-done.16), channel_id=1, source_target_pairs={{0,2},{2,0},{4,6},{6,4},{8,10},{10,8},{12,14},{14,12},{16,18},{18,... | collective-permute-start | bytes 786440 | tf_op jit(solution)/shard_map/ppermute | solution.py:275
  38.7 0.1 constant_dynamic-update-slice_fusion.14
  38.8 1.0 %constant_dynamic-update-slice_fusion.13 = bf16[1024,1024]{1,0:T(8,128)(2,1)S(1)} fusion(bf16[1024,1024]{1,0:T(8,128)(2,1)S(1)} %get-tuple-element.27, bf16[128,1024]{1,0:T(8,128)(2,1)} %collective-permute-done.18), kind=kLoop, calls=%fused_computation.113 | loop fusion | bytes 524288
  39.8 1.5 %collective-permute-start.11 = (bf16[128,1024]{1,0:T(8,128)(2,1)S(1)}, bf16[128,1024]{1,0:T(8,128)(2,1)S(1)}, u32[]{:S(2)}, u32[]{:S(2)}) collective-permute-start(bf16[128,1024]{1,0:T(8,128)(2,1)S(1)} %collective-permute-done.10), channel_id=1, source_target_pairs={{0,1},{1,0},{2,3},{3,2},{4,5},{5,4},{6,7},{7,6},{8,9},{9,8},{10,11... | collective-permute-start | bytes 786440 | tf_op jit(solution)/shard_map/ppermute | solution.py:279
  41.3 0.5 collective-permute-start.12
  41.9 3.4 %collective-permute-start.14 = (bf16[128,1024]{1,0:T(8,128)(2,1)S(1)}, bf16[128,1024]{1,0:T(8,128)(2,1)S(1)}, u32[]{:S(2)}, u32[]{:S(2)}) collective-permute-start(bf16[128,1024]{1,0:T(8,128)(2,1)S(1)} %collective-permute-done.6), channel_id=1, source_target_pairs={{0,2},{2,0},{4,6},{6,4},{8,10},{10,8},{12,14},{14,12},{16,18},{18,... | collective-permute-start | bytes 786440 | tf_op jit(solution)/shard_map/ppermute | solution.py:275
  45.4 2.4 %collective-permute-start.23 = (bf16[128,1024]{1,0:T(8,128)(2,1)S(1)}, bf16[128,1024]{1,0:T(8,128)(2,1)S(1)}, u32[]{:S(2)}, u32[]{:S(2)}) collective-permute-start(bf16[128,1024]{1,0:T(8,128)(2,1)S(1)} %collective-permute-done.22), channel_id=1, source_target_pairs={{0,1},{2,3},{4,5},{6,7},{8,9},{10,11},{12,13},{14,15},{16,17},{18,... | collective-permute-start | bytes 786440 | tf_op jit(solution)/shard_map/ppermute | solution.py:283
  47.9 2.0 %multiply_convert_fusion.3 = (bf16[256,1024]{1,0:T(8,128)(2,1)S(1)}, f32[256,1024]{1,0:T(8,128)S(1)}) fusion(bf16[1024,1024]{1,0:T(8,128)(2,1)S(1)} %copy-done, bf16[128,1024]{1,0:T(8,128)(2,1)S(1)} %get-tuple-element.34, bf16[128,1024]{1,0:T(8,128)(2,1)} %get-tuple-element.19), kind=kOutput, calls=%fused_computation.56 | convolution fusion | flops 540278784 | bytes 4194304 | tf_op jit(solution)/shard_map/dot_general | solution.py:399
  50.0 1.3 %fusion.22 = bf16[256,1024]{1,0:T(8,128)(2,1)S(1)} fusion(f32[256,1024]{1,0:T(8,128)S(1)} %get-tuple-element.36, bf16[1024,1024]{1,0:T(8,128)(2,1)S(1)} %copy-done.9, bf16[128,1024]{1,0:T(8,128)(2,1)S(1)} %get-tuple-element.28, bf16[128,1024]{1,0:T(8,128)(2,1)S(1)} %copy-done.7), kind=kOutput, calls=%fused_computation.31 | convolution fusion | flops 543162368 | bytes 4194304 | tf_op jit(solution)/shard_map/dot_general | solution.py:410
  51.3 0.7 convolution_convert_fusion
  52.2 0.5 collective-permute-start.13
  52.7 2.2 %collective-permute-start.15 = (bf16[128,1024]{1,0:T(8,128)(2,1)S(1)}, bf16[128,1024]{1,0:T(8,128)(2,1)S(1)}, u32[]{:S(2)}, u32[]{:S(2)}) collective-permute-start(bf16[128,1024]{1,0:T(8,128)(2,1)S(1)} %collective-permute-done.14), channel_id=1, source_target_pairs={{0,1},{2,3},{4,5},{6,7},{8,9},{10,11},{12,13},{14,15},{16,17},{18,... | collective-permute-start | bytes 786440 | tf_op jit(solution)/shard_map/ppermute | solution.py:283
  54.8 0.9 %multiply_convert_fusion.2 = (bf16[256,1024]{1,0:T(8,128)(2,1)S(1)}, f32[256,1024]{1,0:T(8,128)S(1)}) fusion(bf16[1024,1024]{1,0:T(8,128)(2,1)S(1)} %copy-done, bf16[128,1024]{1,0:T(8,128)(2,1)S(1)} %collective-permute-done.11, bf16[128,1024]{1,0:T(8,128)(2,1)S(1)} %collective-permute-done.10), kind=kOutput, calls=%fused_computation.55 | convolution fusion | flops 540278784 | bytes 4194304 | tf_op jit(solution)/shard_map/dot_general | solution.py:399
  55.8 2.2 %fusion.29 = bf16[256,1024]{1,0:T(8,128)(2,1)S(1)} fusion(f32[256,1024]{1,0:T(8,128)S(1)} %get-tuple-element.42, bf16[1024,1024]{1,0:T(8,128)(2,1)S(1)} %copy-done.9, bf16[128,1024]{1,0:T(8,128)(2,1)S(1)} %collective-permute-done.19, bf16[128,1024]{1,0:T(8,128)(2,1)} %collective-permute-done.18), kind=kOutput, calls=%fused_computation.38 | convolution fusion | flops 543162368 | bytes 4194304 | tf_op jit(solution)/shard_map/dot_general | solution.py:410
  58.1 1.0 %constant_dynamic-update-slice_fusion.9 = (bf16[1024,1024]{1,0:T(8,128)(2,1)S(1)}, bf16[128,1024]{1,0:T(8,128)(2,1)S(1)}) fusion(bf16[1024,1024]{1,0:T(8,128)(2,1)S(1)} %constant_dynamic-update-slice_fusion.10, bf16[128,1024]{1,0:T(8,128)(2,1)} %collective-permute-done.16, bf16[128,1024]{1,0:T(8,128)(2,1)S(1)} %collective-permute-done.17, pred[]{:T(512)S(6)} %eq.22), kind=kLoop, calls=%fused_computation.109 | loop fusion | flops 131072 | bytes 1048577
  59.1 0.1 constant_dynamic-update-slice_fusion.8
  59.3 0.1 convert_add_fusion
  59.4 0.6 collective-permute-start.9
  60.2 0.9 %multiply_convert_fusion = (bf16[256,1024]{1,0:T(8,128)(2,1)S(1)}, f32[256,1024]{1,0:T(8,128)S(1)}) fusion(bf16[1024,1024]{1,0:T(8,128)(2,1)S(1)} %copy-done, bf16[128,1024]{1,0:T(8,128)(2,1)S(1)} %get-tuple-element.30, bf16[128,1024]{1,0:T(8,128)(2,1)S(1)} %get-tuple-element.32), kind=kOutput, calls=%fused_computation.53 | convolution fusion | flops 540278784 | bytes 4194304 | tf_op jit(solution)/shard_map/dot_general | solution.py:399
  61.1 1.3 %fusion.43 = bf16[256,1024]{1,0:T(8,128)(2,1)S(1)} fusion(f32[256,1024]{1,0:T(8,128)S(1)} %get-tuple-element.38, bf16[1024,1024]{1,0:T(8,128)(2,1)S(1)} %copy-done.9, bf16[128,1024]{1,0:T(8,128)(2,1)S(1)} %get-tuple-element.24, bf16[128,1024]{1,0:T(8,128)(2,1)S(1)} %get-tuple-element.26), kind=kOutput, calls=%fused_computation.52 | convolution fusion | flops 543162368 | bytes 4194304 | tf_op jit(solution)/shard_map/dot_general | solution.py:410
  62.4 0.9 %multiply_convert_fusion.1 = (bf16[256,1024]{1,0:T(8,128)(2,1)S(1)}, f32[256,1024]{1,0:T(8,128)S(1)}) fusion(bf16[1024,1024]{1,0:T(8,128)(2,1)S(1)} %copy-done, bf16[128,1024]{1,0:T(8,128)(2,1)S(1)} %collective-permute-done.13, bf16[128,1024]{1,0:T(8,128)(2,1)S(1)} %collective-permute-done.12), kind=kOutput, calls=%fused_computation.54 | convolution fusion | flops 540278784 | bytes 4194304 | tf_op jit(solution)/shard_map/dot_general | solution.py:399
  63.3 4.4 %fusion.8 = f32[1024,1024]{1,0:T(8,128)} fusion(bf16[1024,1024]{1,0:T(8,128)(2,1)S(1)} %get-tuple-element.23, bf16[256,1024]{1,0:T(8,128)(2,1)S(1)} %get-tuple-element.37, bf16[256,1024]{1,0:T(8,128)(2,1)S(1)} %get-tuple-element.39, bf16[256,1024]{1,0:T(8,128)(2,1)S(1)} %get-tuple-element.41, bf16[256,1024]{1,0:T(8,128)(2,1)S(1)} %get-tuple-element.35), kind=kOutput, calls=%fused_computation.8 | convolution fusion | flops 2155872256 | bytes 8388608 | tf_op jit(solution)/shard_map/dot_general | solution.py:420
  67.8 1.3 %fusion.36 = bf16[256,1024]{1,0:T(8,128)(2,1)S(1)} fusion(f32[256,1024]{1,0:T(8,128)S(1)} %get-tuple-element.40, bf16[1024,1024]{1,0:T(8,128)(2,1)S(1)} %copy-done.9, bf16[128,1024]{1,0:T(8,128)(2,1)S(1)} %collective-permute-done.21, bf16[128,1024]{1,0:T(8,128)(2,1)S(1)} %collective-permute-done.20), kind=kOutput, calls=%fused_computation.45 | convolution fusion | flops 543162368 | bytes 4194304 | tf_op jit(solution)/shard_map/dot_general | solution.py:410
  69.1 4.4 %fusion = f32[1024,1024]{1,0:T(8,128)} fusion(bf16[1024,1024]{1,0:T(8,128)(2,1)S(1)} %get-tuple-element.29, bf16[256,1024]{1,0:T(8,128)(2,1)S(1)} %fusion.43, bf16[256,1024]{1,0:T(8,128)(2,1)S(1)} %fusion.36, bf16[256,1024]{1,0:T(8,128)(2,1)S(1)} %fusion.29, bf16[256,1024]{1,0:T(8,128)(2,1)S(1)} %fusion.22), kind=kOutput, calls=%fused_computation | convolution fusion | flops 2155872256 | bytes 8388608 | tf_op jit(solution)/shard_map/dot_general | solution.py:417
  73.5 0.7 fusion.85
  (59 shorter events, 1.1 us)
Async XLA Ops:
  0.6 47.3 %copy-start = (bf16[1024,1024]{1,0:T(8,128)(2,1)S(1)}, bf16[1024,1024]{1,0:T(8,128)(2,1)}, u32[]{:S(2)}) copy-start(bf16[1024,1024]{1,0:T(8,128)(2,1)} %param.19) | copy-start | bytes 6291460
  0.6 20.0 %collective-permute-start.4 = (bf16[512,1024]{1,0:T(8,128)(2,1)}, bf16[512,1024]{1,0:T(8,128)(2,1)S(1)}, u32[]{:S(2)}, u32[]{:S(2)}) collective-permute-start(bf16[512,1024]{1,0:T(8,128)(2,1)} %weight_src.1), channel_id=1, source_target_pairs={{0,1},{1,0},{2,3},{3,2},{4,5},{5,4},{6,7},{7,6},{8,9},{9,8},{10,11... | collective-permute-start | bytes 3145736 | tf_op jit(solution)/shard_map/ppermute | solution.py:125
  1.2 4.4 %collective-permute-start = (bf16[128,512]{1,0:T(8,128)(2,1)}, bf16[128,512]{1,0:T(8,128)(2,1)S(1)}, u32[]{:S(2)}, u32[]{:S(2)}) collective-permute-start(bf16[128,512]{1,0:T(8,128)(2,1)} %refs_0_.1), channel_id=1, source_target_pairs={{0,1},{1,0},{2,3},{3,2},{4,5},{5,4},{6,7},{7,6},{8,9},{9,8},{10,11... | collective-permute-start | bytes 393224 | tf_op jit(solution)/shard_map/ppermute | solution.py:125
  1.2 13.8 %collective-permute-start.1 = (bf16[128,512]{1,0:T(8,128)(2,1)}, bf16[128,512]{1,0:T(8,128)(2,1)S(1)}, u32[]{:S(2)}, u32[]{:S(2)}) collective-permute-start(bf16[128,512]{1,0:T(8,128)(2,1)} %key_src.1), channel_id=1, source_target_pairs={{0,2},{2,0},{1,3},{3,1},{4,6},{6,4},{5,7},{7,5},{8,10},{10,8},{9,1... | collective-permute-start | bytes 393224 | tf_op jit(solution)/shard_map/ppermute | solution.py:125
  4.2 10.8 %collective-permute-start.2 = (bf16[128,512]{1,0:T(8,128)(2,1)}, bf16[128,512]{1,0:T(8,128)(2,1)S(1)}, u32[]{:S(2)}, u32[]{:S(2)}) collective-permute-start(bf16[128,512]{1,0:T(8,128)(2,1)} %value_src.1), channel_id=1, source_target_pairs={{0,2},{2,0},{1,3},{3,1},{4,6},{6,4},{5,7},{7,5},{8,10},{10,8},{9,1... | collective-permute-start | bytes 393224 | tf_op jit(solution)/shard_map/ppermute | solution.py:125
  5.5 15.2 %copy-start.6 = (s32[2]{0:T(128)S(1)}, s32[2]{0:T(128)}, u32[]{:S(2)}) copy-start(s32[2]{0:T(128)} %pad_add_fusion.place_ref) | copy-start | bytes 28
  5.6 0.7 copy-start.8
  9.9 10.8 %collective-permute-start.5 = (bf16[144,512]{1,0:T(8,128)(2,1)}, bf16[144,512]{1,0:T(8,128)(2,1)S(1)}, u32[]{:S(2)}, u32[]{:S(2)}) collective-permute-start(bf16[144,512]{1,0:T(8,128)(2,1)} %get-tuple-element.17.refs_4_), channel_id=1, source_target_pairs={{0,1},{1,0},{2,3},{3,2},{4,5},{5,4},{6,7},{7,6},{8,9},{9,8},{10,11... | collective-permute-start | bytes 442376 | tf_op jit(solution)/shard_map/ppermute | solution.py:125
  10.0 16.1 %collective-permute-start.16 = (bf16[128,1024]{1,0:T(8,128)(2,1)}, bf16[128,1024]{1,0:T(8,128)(2,1)}, u32[]{:S(2)}, u32[]{:S(2)}) collective-permute-start(bf16[128,1024]{1,0:T(8,128)(2,1)} %get-tuple-element.20), channel_id=1, source_target_pairs={{0,12},{1,3},{2,14},{3,1},{4,8},{5,7},{6,10},{7,5},{8,4},{9,11},{1... | collective-permute-start | bytes 786440 | tf_op jit(solution)/shard_map/ppermute | solution.py:275
  15.0 1.0 %copy-start.2 = (f32[8,128,128]{2,1,0:T(8,128)S(1)}, f32[8,128,128]{2,1,0:T(8,128)}, u32[]{:S(2)}) copy-start(f32[8,128,128]{2,1,0:T(8,128)} %get-tuple-element.13.score_ref) | copy-start | bytes 1572868
  16.1 0.9 %copy-start.4 = (bf16[128,512]{1,0:T(8,128)(2,1)S(1)}, bf16[128,512]{1,0:T(8,128)(2,1)}, u32[]{:S(2)}) copy-start(bf16[128,512]{1,0:T(8,128)(2,1)} %get-tuple-element.14.query_ref) | copy-start | bytes 393220
  17.0 0.9 %copy-start.5 = (bf16[128,512]{1,0:T(8,128)(2,1)S(1)}, bf16[128,512]{1,0:T(8,128)(2,1)}, u32[]{:S(2)}) copy-start(bf16[128,512]{1,0:T(8,128)(2,1)} %get-tuple-element.15.refs_1_) | copy-start | bytes 393220
  19.3 1.4 %collective-permute-start.3 = (bf16[128,512]{1,0:T(8,128)(2,1)S(1)}, bf16[128,512]{1,0:T(8,128)(2,1)S(1)}, u32[]{:S(2)}, u32[]{:S(2)}) collective-permute-start(bf16[128,512]{1,0:T(8,128)(2,1)S(1)} %shard_map.131.refs_0_), channel_id=1, source_target_pairs={{0,1},{1,0},{2,3},{3,2},{4,5},{5,4},{6,7},{7,6},{8,9},{9,8},{10,11... | collective-permute-start | bytes 393224 | tf_op jit(solution)/shard_map/ppermute | solution.py:125
  19.3 9.6 %collective-permute-start.18 = (bf16[128,1024]{1,0:T(8,128)(2,1)}, bf16[128,1024]{1,0:T(8,128)(2,1)}, u32[]{:S(2)}, u32[]{:S(2)}) collective-permute-start(bf16[128,1024]{1,0:T(8,128)(2,1)} %get-tuple-element.20), channel_id=1, source_target_pairs={{0,4},{1,9},{2,6},{3,11},{4,0},{5,13},{6,2},{7,15},{8,12},{9,1},{1... | collective-permute-start | bytes 786440 | tf_op jit(solution)/shard_map/ppermute | solution.py:275
  20.7 1.2 %copy-start.1 = (bf16[512,1024]{1,0:T(8,128)(2,1)S(1)}, bf16[512,1024]{1,0:T(8,128)(2,1)}, u32[]{:S(2)}) copy-start(bf16[512,1024]{1,0:T(8,128)(2,1)} %get-tuple-element.16.refs_2_) | copy-start | bytes 3145732
  21.9 0.9 %copy-start.3 = (bf16[144,512]{1,0:T(8,128)(2,1)S(1)}, bf16[144,512]{1,0:T(8,128)(2,1)}, u32[]{:S(2)}) copy-start(bf16[144,512]{1,0:T(8,128)(2,1)} %get-tuple-element.17.refs_4_) | copy-start | bytes 442372
  24.8 10.4 %collective-permute-start.6 = (bf16[128,1024]{1,0:T(8,128)(2,1)}, bf16[128,1024]{1,0:T(8,128)(2,1)S(1)}, u32[]{:S(2)}, u32[]{:S(2)}) collective-permute-start(bf16[128,1024]{1,0:T(8,128)(2,1)} %get-tuple-element.19), channel_id=1, source_target_pairs={{0,12},{1,3},{2,14},{3,1},{4,8},{5,7},{6,10},{7,5},{8,4},{9,11},{1... | collective-permute-start | bytes 786440 | tf_op jit(solution)/shard_map/ppermute | solution.py:275
  26.1 12.6 %collective-permute-start.17 = (bf16[128,1024]{1,0:T(8,128)(2,1)}, bf16[128,1024]{1,0:T(8,128)(2,1)S(1)}, u32[]{:S(2)}, u32[]{:S(2)}) collective-permute-start(bf16[128,1024]{1,0:T(8,128)(2,1)} %collective-permute-done.16), channel_id=1, source_target_pairs={{0,1},{1,0},{2,3},{3,2},{4,5},{5,4},{6,7},{7,6},{8,9},{9,8},{10,11... | collective-permute-start | bytes 786440 | tf_op jit(solution)/shard_map/ppermute | solution.py:279
  27.1 12.7 %collective-permute-start.10 = (bf16[128,1024]{1,0:T(8,128)(2,1)}, bf16[128,1024]{1,0:T(8,128)(2,1)S(1)}, u32[]{:S(2)}, u32[]{:S(2)}) collective-permute-start(bf16[128,1024]{1,0:T(8,128)(2,1)} %get-tuple-element.19), channel_id=1, source_target_pairs={{0,4},{1,9},{2,6},{3,11},{4,0},{5,13},{6,2},{7,15},{8,12},{9,1},{1... | collective-permute-start | bytes 786440 | tf_op jit(solution)/shard_map/ppermute | solution.py:275
  28.9 12.4 %collective-permute-start.19 = (bf16[128,1024]{1,0:T(8,128)(2,1)}, bf16[128,1024]{1,0:T(8,128)(2,1)S(1)}, u32[]{:S(2)}, u32[]{:S(2)}) collective-permute-start(bf16[128,1024]{1,0:T(8,128)(2,1)} %collective-permute-done.18), channel_id=1, source_target_pairs={{0,1},{1,0},{2,3},{3,2},{4,5},{5,4},{6,7},{7,6},{8,9},{9,8},{10,11... | collective-permute-start | bytes 786440 | tf_op jit(solution)/shard_map/ppermute | solution.py:279
  28.9 13.0 %collective-permute-start.20 = (bf16[128,1024]{1,0:T(8,128)(2,1)}, bf16[128,1024]{1,0:T(8,128)(2,1)S(1)}, u32[]{:S(2)}, u32[]{:S(2)}) collective-permute-start(bf16[128,1024]{1,0:T(8,128)(2,1)} %collective-permute-done.18), channel_id=1, source_target_pairs={{0,2},{1,3},{2,0},{3,1},{4,6},{5,7},{6,4},{7,5},{8,10},{9,11},{10,... | collective-permute-start | bytes 786440 | tf_op jit(solution)/shard_map/ppermute | solution.py:275
  35.3 10.1 %collective-permute-start.22 = (bf16[128,1024]{1,0:T(8,128)(2,1)}, bf16[128,1024]{1,0:T(8,128)(2,1)S(1)}, u32[]{:S(2)}, u32[]{:S(2)}) collective-permute-start(bf16[128,1024]{1,0:T(8,128)(2,1)} %collective-permute-done.16), channel_id=1, source_target_pairs={{0,2},{2,0},{4,6},{6,4},{8,10},{10,8},{12,14},{14,12},{16,18},{18,... | collective-permute-start | bytes 786440 | tf_op jit(solution)/shard_map/ppermute | solution.py:275
  38.7 6.7 %collective-permute-start.7 = (bf16[128,1024]{1,0:T(8,128)(2,1)S(1)}, bf16[128,1024]{1,0:T(8,128)(2,1)S(1)}, u32[]{:S(2)}, u32[]{:S(2)}) collective-permute-start(bf16[128,1024]{1,0:T(8,128)(2,1)S(1)} %collective-permute-done.6), channel_id=1, source_target_pairs={{0,1},{1,0},{2,3},{3,2},{4,5},{5,4},{6,7},{7,6},{8,9},{9,8},{10,11... | collective-permute-start | bytes 786440 | tf_op jit(solution)/shard_map/ppermute | solution.py:279
  39.8 12.3 %collective-permute-start.11 = (bf16[128,1024]{1,0:T(8,128)(2,1)S(1)}, bf16[128,1024]{1,0:T(8,128)(2,1)S(1)}, u32[]{:S(2)}, u32[]{:S(2)}) collective-permute-start(bf16[128,1024]{1,0:T(8,128)(2,1)S(1)} %collective-permute-done.10), channel_id=1, source_target_pairs={{0,1},{1,0},{2,3},{3,2},{4,5},{5,4},{6,7},{7,6},{8,9},{9,8},{10,11... | collective-permute-start | bytes 786440 | tf_op jit(solution)/shard_map/ppermute | solution.py:279
  41.3 10.9 %collective-permute-start.12 = (bf16[128,1024]{1,0:T(8,128)(2,1)S(1)}, bf16[128,1024]{1,0:T(8,128)(2,1)S(1)}, u32[]{:S(2)}, u32[]{:S(2)}) collective-permute-start(bf16[128,1024]{1,0:T(8,128)(2,1)S(1)} %collective-permute-done.10), channel_id=1, source_target_pairs={{0,2},{1,3},{2,0},{3,1},{4,6},{5,7},{6,4},{7,5},{8,10},{9,11},{10,... | collective-permute-start | bytes 786440 | tf_op jit(solution)/shard_map/ppermute | solution.py:275
  41.9 10.8 %collective-permute-start.14 = (bf16[128,1024]{1,0:T(8,128)(2,1)S(1)}, bf16[128,1024]{1,0:T(8,128)(2,1)S(1)}, u32[]{:S(2)}, u32[]{:S(2)}) collective-permute-start(bf16[128,1024]{1,0:T(8,128)(2,1)S(1)} %collective-permute-done.6), channel_id=1, source_target_pairs={{0,2},{2,0},{4,6},{6,4},{8,10},{10,8},{12,14},{14,12},{16,18},{18,... | collective-permute-start | bytes 786440 | tf_op jit(solution)/shard_map/ppermute | solution.py:275
  45.3 12.7 %collective-permute-start.21 = (bf16[128,1024]{1,0:T(8,128)(2,1)S(1)}, bf16[128,1024]{1,0:T(8,128)(2,1)S(1)}, u32[]{:S(2)}, u32[]{:S(2)}) collective-permute-start(bf16[128,1024]{1,0:T(8,128)(2,1)S(1)} %collective-permute-done.20), channel_id=1, source_target_pairs={{0,1},{1,0},{2,3},{3,2},{4,5},{5,4},{6,7},{7,6},{8,9},{9,8},{10,11... | collective-permute-start | bytes 786440 | tf_op jit(solution)/shard_map/ppermute | solution.py:279
  45.4 13.7 %collective-permute-start.23 = (bf16[128,1024]{1,0:T(8,128)(2,1)S(1)}, bf16[128,1024]{1,0:T(8,128)(2,1)S(1)}, u32[]{:S(2)}, u32[]{:S(2)}) collective-permute-start(bf16[128,1024]{1,0:T(8,128)(2,1)S(1)} %collective-permute-done.22), channel_id=1, source_target_pairs={{0,1},{2,3},{4,5},{6,7},{8,9},{10,11},{12,13},{14,15},{16,17},{18,... | collective-permute-start | bytes 786440 | tf_op jit(solution)/shard_map/ppermute | solution.py:283
  47.9 2.1 %copy-start.7 = (bf16[128,1024]{1,0:T(8,128)(2,1)S(1)}, bf16[128,1024]{1,0:T(8,128)(2,1)}, u32[]{:S(2)}) copy-start(bf16[128,1024]{1,0:T(8,128)(2,1)} %get-tuple-element.20) | copy-start | bytes 786436
  47.9 2.1 %copy-start.9 = (bf16[1024,1024]{1,0:T(8,128)(2,1)S(1)}, bf16[1024,1024]{1,0:T(8,128)(2,1)}, u32[]{:S(2)}) copy-start(bf16[1024,1024]{1,0:T(8,128)(2,1)} %param.20) | copy-start | bytes 6291460
  52.1 7.2 %collective-permute-start.8 = (bf16[256,512]{1,0:T(8,128)(2,1)S(1)}, bf16[256,512]{1,0:T(8,128)(2,1)S(1)}, u32[]{:S(2)}, u32[]{:S(2)}) collective-permute-start(bf16[256,512]{1,0:T(8,128)(2,1)S(1)} %constant_dynamic-slice_fusion), channel_id=1, source_target_pairs={{0,1},{1,0},{2,3},{3,2},{4,5},{5,4},{6,7},{7,6},{8,9},{9,8},{10,11... | collective-permute-start | bytes 786440 | tf_op jit(solution)/shard_map/ppermute | solution.py:279
  52.2 7.8 %collective-permute-start.13 = (bf16[128,1024]{1,0:T(8,128)(2,1)S(1)}, bf16[128,1024]{1,0:T(8,128)(2,1)S(1)}, u32[]{:S(2)}, u32[]{:S(2)}) collective-permute-start(bf16[128,1024]{1,0:T(8,128)(2,1)S(1)} %collective-permute-done.12), channel_id=1, source_target_pairs={{0,1},{1,0},{2,3},{3,2},{4,5},{5,4},{6,7},{7,6},{8,9},{9,8},{10,11... | collective-permute-start | bytes 786440 | tf_op jit(solution)/shard_map/ppermute | solution.py:279
  52.7 7.4 %collective-permute-start.15 = (bf16[128,1024]{1,0:T(8,128)(2,1)S(1)}, bf16[128,1024]{1,0:T(8,128)(2,1)S(1)}, u32[]{:S(2)}, u32[]{:S(2)}) collective-permute-start(bf16[128,1024]{1,0:T(8,128)(2,1)S(1)} %collective-permute-done.14), channel_id=1, source_target_pairs={{0,1},{2,3},{4,5},{6,7},{8,9},{10,11},{12,13},{14,15},{16,17},{18,... | collective-permute-start | bytes 786440 | tf_op jit(solution)/shard_map/ppermute | solution.py:283
  59.4 14.1 %collective-permute-start.9 = (bf16[128,512]{1,0:T(8,128)(2,1)S(1)}, bf16[128,512]{1,0:T(8,128)(2,1)S(1)}, u32[]{:S(2)}, u32[]{:S(2)}) collective-permute-start(bf16[128,512]{1,0:T(8,128)(2,1)S(1)} %slice.17), channel_id=1, source_target_pairs={{0,2},{2,0},{1,3},{3,1},{4,6},{6,4},{5,7},{7,5},{8,10},{10,8},{9,1... | collective-permute-start | bytes 393224 | tf_op jit(solution)/shard_map/ppermute | solution.py:408

commit v5 on v0

--- a/solution.py
+++ b/solution.py
@@ -1,6 +1,10 @@
+import functools
+
 import jax
 import jax.numpy as jnp
 from jax import lax
+from jax.experimental import pallas as pl
+from jax.experimental.pallas import tpu as pltpu
 from jax.sharding import PartitionSpec as P
 
 HEAD = 64
@@ -102,9 +106,372 @@
     return (layer_out, up_grad, down_grad)
 
 
+GAIN_ROWS = 16
+TILE = 256
+OWN_LIMIT = 56 * 2**20
+
+
+def shift(x, axis, k):
+    n = lax.axis_size(axis)
+    return lax.ppermute(x, axis, [(i, (i + k) % n) for i in range(n)])
+
+
+def after(x, *others):
+    return lax.optimization_barrier((x,) + others)[0]
+
+
+def others(x, axis):
+    n = lax.axis_size(axis)
+    if n & (n - 1):
+        return [shift(x, axis, k) for k in range(1, n)]
+    return [lax.ppermute(x, axis, [(i, i ^ k) for i in range(n)]) for k in range(1, n)]
+
+
+def member(axis, k):
+    n = lax.axis_size(axis)
+    me = lax.axis_index(axis)
+    return (me - k + n) % n if n & (n - 1) else me ^ k
+
+
+def one_head(query, lane, head):
+    return jnp.where((lane < HEAD) == (head == 0), query, jnp.zeros_like(query))
+
+
+def pair_scores(query, key):
+    return lax.dot_general(
+        query, key, (((1,), (1,)), ((), ())), preferred_element_type=jnp.float32
+    ) * HEAD ** (-0.5)
+
+
+def core_columns(j, half):
+    return pl.ds(pl.multiple_of(member("col", j) * half, half), half)
+
+
+def join_cores(weight_ref, *refs):
+    parts, (kept_ref, out_ref) = refs[:-2], refs[-2:]
+    half = parts[0].shape[1]
+    for j, part in enumerate(parts):
+        out_ref[:, core_columns(j, half)] = part[...]
+    kept_ref[...] = weight_ref[...]
+
+
+def attend(grps, ids_ref, count_ref, gain_ref, residual_ref, query_ref, *refs):
+    seen = []
+    for k in range(grps):
+        listed = [
+            (ids_ref[0, m] == member("grp", k)) & (m < count_ref[0]) for m in range(ids_ref.shape[1])
+        ]
+        seen.append(functools.reduce(jnp.logical_or, listed))
+    keys, values, (out_ref, score_ref) = refs[:grps], refs[grps : 2 * grps], refs[2 * grps :]
+    rows, half = query_ref.shape
+    heads = half // HEAD
+    lane = lax.broadcasted_iota(jnp.int32, (rows, 2 * HEAD), 1)
+    for head in range(heads):
+        cols = pl.ds(head // 2 * 2 * HEAD, 2 * HEAD)
+        query = one_head(query_ref[:, cols], lane, head % 2)
+        for k in range(grps):
+            part = pair_scores(query, keys[k][:, cols])
+            score_ref[head * grps + k] = jnp.where(seen[k], part, -1e30)
+    for pair in range(heads // 2):
+        cols = pl.ds(pair * 2 * HEAD, 2 * HEAD)
+        value = [ref[:, cols] for ref in values]
+        found = []
+        for head in (2 * pair, 2 * pair + 1):
+            scores = [score_ref[head * grps + k] for k in range(grps)]
+            largest = scores[0]
+            for part in scores[1:]:
+                largest = jnp.maximum(largest, part)
+            largest = jnp.max(largest, axis=1, keepdims=True)
+            weights = [jnp.exp(part - largest) for part in scores]
+            total = weights[0]
+            for part in weights[1:]:
+                total = total + part
+            total = jnp.sum(total, axis=1, keepdims=True)
+            result = 0.0
+            for k in range(grps):
+                probs = (weights[k] / total).astype(jnp.bfloat16)
+                result = result + jnp.dot(probs, value[k], preferred_element_type=jnp.float32)
+            found.append(result)
+        out_ref[pl.ds(0, rows), cols] = jnp.where(lane < HEAD, found[0], found[1]).astype(
+            jnp.bfloat16
+        )
+    gain = gain_ref[...]
+    high = gain.astype(jnp.bfloat16).astype(jnp.float32)
+    middle = (gain - high).astype(jnp.bfloat16).astype(jnp.float32)
+    low = gain - high - middle
+    row = lax.broadcasted_iota(jnp.int32, (GAIN_ROWS, half), 0)
+    parts = jnp.where(
+        row == 0, high, jnp.where(row == 1, middle, jnp.where(row == 2, low, 0.0))
+    )
+    out_ref[pl.ds(rows, GAIN_ROWS), :] = parts.astype(jnp.bfloat16)
+    out_ref[pl.ds(rows + GAIN_ROWS, rows), :] = residual_ref[...]
+
+
+def project(cores, *refs):
+    packs, weights, (stream_ref, normed_ref, full, gain) = refs[:cores], refs[cores:-4], refs[-4:]
+    rows, half = stream_ref.shape
+    width = half * cores
+    full[...] = sum(
+        jnp.dot(pack[pl.ds(0, rows), :], weight[...], preferred_element_type=jnp.float32)
+        for pack, weight in zip(packs, weights)
+    )
+    for j, pack in enumerate(packs):
+        cols = core_columns(j, half)
+        part = full[:, cols] + pack[pl.ds(rows + GAIN_ROWS, rows), :].astype(jnp.float32)
+        full[:, cols] = part
+        if j == 0:
+            stream_ref[...] = part
+        gains = pack[pl.ds(rows, GAIN_ROWS), :].astype(jnp.float32)
+        gain[0:1, cols] = (gains[1:2] + gains[2:3]) + gains[0:1]
+    stream = full[...]
+    center = jnp.sum(stream, axis=1, keepdims=True) / width
+    shifted = stream - center
+    spread_sq = jnp.sum(shifted * shifted, axis=1, keepdims=True) / width
+    normed_ref[...] = (shifted * lax.rsqrt(spread_sq + 1e-05) * gain[0:1, :]).astype(jnp.bfloat16)
+
+
+def add_products(*refs):
+    pairs, (up_ref, down_ref) = refs[:-2], refs[-2:]
+    count = len(pairs) // 4
+    for start in range(0, up_ref.shape[0], TILE):
+        tile = pl.ds(start, TILE)
+        for k, out_ref in ((0, up_ref), (2, down_ref)):
+            out_ref[tile, :] = sum(
+                lax.dot_general(
+                    pairs[4 * i + k][:, tile],
+                    pairs[4 * i + k + 1][...],
+                    (((0,), (0,)), ((), ())),
+                    preferred_element_type=jnp.float32,
+                )
+                for i in range(count)
+            )
+
+
+def finish_products(*refs):
+    up_sum, down_sum = refs[:2]
+    up_ref, down_ref, buffer, sems = refs[-4:]
+    pairs = refs[2:-4]
+    count = len(pairs) // 4
+    copies = []
+    for start in range(0, up_ref.shape[0], TILE):
+        tile = pl.ds(start, TILE)
+        for k, sum_ref, out_ref in ((0, up_sum, up_ref), (2, down_sum, down_ref)):
+            slot = len(copies) % buffer.shape[0]
+            if len(copies) >= buffer.shape[0]:
+                copies[-buffer.shape[0]].wait()
+            buffer[slot] = sum_ref[tile, :] + sum(
+                lax.dot_general(
+                    pairs[4 * i + k][:, tile],
+                    pairs[4 * i + k + 1][...],
+                    (((0,), (0,)), ((), ())),
+                    preferred_element_type=jnp.float32,
+                )
+                for i in range(count)
+            )
+            copies.append(
+                pltpu.make_async_copy(buffer.at[slot], out_ref.at[tile], sems.at[slot])
+            )
+            copies[-1].start()
+    for copy in copies[-buffer.shape[0] :]:
+        copy.wait()
+
+
+def call(kernel, out_shape, smem, args, flops, scratch=(), limit=16 * 2**20):
+    moved = sum(a.size * a.dtype.itemsize for a in args) + sum(
+        o.size * o.dtype.itemsize for o in jax.tree.leaves(out_shape)
+    )
+    return pl.pallas_call(
+        kernel,
+        out_shape=out_shape,
+        in_specs=[pl.BlockSpec(memory_space=pltpu.SMEM)] * smem
+        + [pl.BlockSpec(memory_space=pltpu.VMEM)] * (len(args) - smem),
+        scratch_shapes=scratch,
+        cost_estimate=pl.CostEstimate(flops=flops, bytes_accessed=moved, transcendentals=0),
+        compiler_params=pltpu.CompilerParams(vmem_limit_bytes=limit),
+    )(*args)
+
+
+def send(x, routes):
+    patches, grps, cores = (lax.axis_size(a) for a in ("patch", "grp", "col"))
+    pairs = []
+    for p in range(patches):
+        for g in range(grps):
+            for c, route in enumerate(routes):
+                if route is not None:
+                    to = ((p ^ route[0]) * grps + (g ^ route[1])) * cores + c
+                    pairs.append(((p * grps + g) * cores + c, to))
+    return lax.ppermute(x, ("patch", "grp", "col"), pairs)
+
+
+def swap(x):
+    return lax.ppermute(x, "col", [(0, 1), (1, 0)])
+
+
+def hand_over(x):
+    return lax.ppermute(x, "col", [(0, 1)])
+
+
+def gather_plan(
+    query_vectors,
+    key_vectors,
+    value_vectors,
+    residual,
+    neighbor_ids,
+    neighbor_count,
+    output_weight,
+    norm_gain,
+    up_weight,
+    down_weight,
+    cotangent,
+):
+    cores = lax.axis_size("col")
+    grps = lax.axis_size("grp")
+    rows, half = query_vectors.shape
+    width = half * cores
+
+    bf16 = jnp.bfloat16
+    cot_parts = [cotangent] + others(cotangent, "col")
+    keys = [key_vectors] + others(key_vectors, "grp")
+    values = [value_vectors] + others(value_vectors, "grp")
+    weights = [output_weight] + others(output_weight, "col")
+    weights[0], cot = call(
+        join_cores,
+        (
+            jax.ShapeDtypeStruct(output_weight.shape, bf16),
+            jax.ShapeDtypeStruct((rows, width), bf16),
+        ),
+        0,
+        [output_weight] + cot_parts,
+        0,
+    )
+    cot12 = send(cot, [(1, 0), (2, 0)])
+    cot3x = send(cot, [(3, 0), (0, 1)])
+
+    packed = call(
+        functools.partial(attend, grps),
+        jax.ShapeDtypeStruct((2 * rows + GAIN_ROWS, half), bf16),
+        2,
+        [neighbor_ids, neighbor_count, norm_gain[None], residual, after(query_vectors, cot)]
+        + keys
+        + values,
+        4 * rows * rows * grps * width,
+        [pltpu.VMEM((half // HEAD * grps, rows, rows), jnp.float32)],
+        OWN_LIMIT,
+    )
+    stream, normed = call(
+        functools.partial(project, cores),
+        (
+            jax.ShapeDtypeStruct((rows, half), jnp.float32),
+            jax.ShapeDtypeStruct((rows, width), bf16),
+        ),
+        0,
+        [packed] + others(packed, "col") + weights,
+        2 * rows * width * width,
+        [pltpu.VMEM((rows, width), jnp.float32), pltpu.VMEM((8, width), jnp.float32)],
+    )
+    first = lax.axis_index("col") == 0
+
+    def pairs_of(own, by12, by3x, swapped, over12, over3, swapped_over):
+        swap12, swap3x = swapped[:rows], swapped[rows:]
+        return [
+            jnp.concatenate([own, jnp.where(first, swap3x, by3x)], 0),
+            jnp.concatenate([by12, swap12], 0),
+            jnp.concatenate([over12, swapped_over[:rows]], 0),
+            jnp.concatenate(
+                [jnp.where(first, by3x, swap3x), jnp.where(first, over3, swapped_over[rows:])], 0
+            ),
+        ]
+
+    def forward(by12, by3x):
+        return send(by12, [(0, 1), (0, 1)]), send(by3x, [(0, 1), None])
+
+    norm12 = send(normed, [(1, 0), (2, 0)])
+    norm3x = send(normed, [(3, 0), (0, 1)])
+    own_pre = jnp.dot(normed, up_weight, preferred_element_type=jnp.float32)
+    cot12, cot3x = after(cot12, own_pre), after(cot3x, norm12)
+    over12, over3 = forward(cot12, cot3x)
+    late = swap(jnp.concatenate([cot3x, over12], 0))
+    cots = pairs_of(
+        cot,
+        cot12,
+        cot3x,
+        jnp.concatenate([swap(cot12), late[:rows]], 0),
+        over12,
+        over3,
+        jnp.concatenate([late[rows:], hand_over(over3)], 0),
+    )
+    over12, over3 = forward(norm12, norm3x)
+    norms = pairs_of(
+        normed,
+        norm12,
+        norm3x,
+        jnp.concatenate([swap(norm12), swap(norm3x)], 0),
+        over12,
+        over3,
+        jnp.concatenate([swap(over12), hand_over(over3)], 0),
+    )
+
+    saved = []
+    layer_out = None
+    for s, (normed_rows, back_rows) in enumerate(zip(norms, cots)):
+        if s == 0:
+            pre = jnp.dot(normed_rows[rows:], up_weight, preferred_element_type=jnp.float32)
+            pre = jnp.concatenate([own_pre, pre], 0)
+        else:
+            pre = jnp.dot(normed_rows, up_weight, preferred_element_type=jnp.float32)
+        hidden = jax.nn.gelu(pre).astype(bf16)
+        if s == 0:
+            partial_out = jnp.dot(hidden, down_weight, preferred_element_type=jnp.float32)
+            partial_out = partial_out.astype(bf16)
+            mine, theirs = (
+                lax.dynamic_slice(partial_out, (0, member("col", j) * half), (2 * rows, half)) for j in (0, 1)
+            )
+            both = mine.astype(jnp.float32) + swap(theirs).astype(jnp.float32)
+            rest = lax.ppermute(both[rows:].astype(bf16), "grp", [(0, 1), (1, 0)])
+            layer_out = (stream + both[:rows] + rest.astype(jnp.float32)).astype(bf16)
+        back_hidden = lax.dot_general(
+            back_rows, down_weight, (((1,), (1,)), ((), ())), preferred_element_type=jnp.float32
+        )
+        _, gelu_back = jax.vjp(jax.nn.gelu, pre)
+        back_pre = gelu_back(back_hidden)[0].astype(bf16)
+        saved.append([normed_rows, back_pre, hidden, back_rows])
+    panel = up_weight.shape[1]
+    grads = (
+        jax.ShapeDtypeStruct((width, panel), jnp.float32),
+        jax.ShapeDtypeStruct((panel, width), jnp.float32),
+    )
+    early, last = saved[0] + saved[1], saved[2] + saved[3]
+    flops = 8 * 2 * rows * panel * width
+    sums = call(add_products, grads, 0, early, flops)
+    up_grad, down_grad = pl.pallas_call(
+        finish_products,
+        out_shape=grads,
+        in_specs=[pl.BlockSpec(memory_space=pltpu.VMEM)] * (2 + len(last)),
+        out_specs=[pl.BlockSpec(memory_space=pl.ANY)] * 2,
+        scratch_shapes=[
+            pltpu.VMEM((4, TILE, width), jnp.float32),
+            pltpu.SemaphoreType.DMA((4,)),
+        ],
+        cost_estimate=pl.CostEstimate(
+            flops=flops, bytes_accessed=16 * panel * width, transcendentals=0
+        ),
+        compiler_params=pltpu.CompilerParams(vmem_limit_bytes=16 * 2**20),
+    )(*sums, *last)
+    return (layer_out, up_grad, down_grad)
+
+
+def layer(*args):
+    query_vectors, up_weight = args[0], args[8]
+    patches, grps, cores = (lax.axis_size(a) for a in ("patch", "grp", "col"))
+    tokens = query_vectors.shape[0] * grps * patches
+    if (patches, grps, cores) == (4, 2, 2) and tokens <= 2 * up_weight.shape[1]:
+        return gather_plan(*args)
+    return shards(*args)
+
+
 def solution(mesh):
     return jax.shard_map(
-        shards,
+        layer,
         mesh=mesh,
         in_specs=(
             P(("parts", "patch", "grp"), "col"),

time: 254 us -> 75 us (0.30)
  waiting for transfers between devices: 174 us -> 7.92 us
  starting transfers between devices: 0.12 us -> 34 us
  blocking collectives: 30.4 us -> 0 us
  between operations: 14.7 us -> 1.69 us
  Pallas kernels: 0 us -> 10.3 us
  other arithmetic: 11.3 us -> 4.43 us
  matrix products: 17.1 us -> 10.3 us
    psum x1 -> x0, waiting for transfers between devices: 157 us -> none  [shards(): lax.psum(up_local.astype(jnp.bfloat16), 'patch').astype(jnp.float32)]
    ppermute x0 -> x22, starting transfers between devices: none -> 34 us  [the longest x8 17.3 us: send(): return lax.ppermute(x, ('patch', 'grp', 'col'), pairs)]
    all_gather x4 -> x0, blocking collectives: 27.9 us -> none  [the longest x2 14.8 us: spread_rows(): lax.all_gather(part_rows[None], ('grp', 'col'), axis=0, tiled=True)]
    reduce_scatter x2 -> x0, waiting for transfers between devices: 17.3 us -> none  [the longest x1 9.24 us: shards(): lax.psum_scatter(projected.astype(jnp.bfloat16), 'col', scatter_dimension...]
    pallas_call x0 -> x5, Pallas kernels: none -> 10.3 us  [the longest x4 5.98 us: call(): pl.pallas_call(kernel, out_shape=out_shape, in_specs=[pl.BlockSpec(memory...]
    convert_element_type x4 -> x2, other arithmetic: 9.47 us -> 1.04 us  [the longest x1 0.71 us: gather_plan(): layer_out = (stream + both[:rows] + rest.astype(jnp.float32)).astype(bf16)]
    ppermute x0 -> x22, waiting for transfers between devices: none -> 7.92 us  [the longest x5 3.84 us: others(): lax.ppermute(x, axis, [(i, i ^ k) for i in range(n)])]
    dot_general x7 -> x10, matrix products: 16.5 us -> 10.3 us  [the longest x4 5.48 us: gather_plan(): lax.dot_general(back_rows, down_weight, (((1,), (1,)), ((), ())), preferr...]
  transfers between devices with their start and end apart: 3 -> 22, of which waited for: 3 -> 6; matrix products, arithmetic and copies ran while one was open for 4% -> 22% of each run, Pallas kernels for 0% -> 14%
where the time goes in v5:
time: 75 us; the launch traced here: 74.5 us
  starting transfers between devices  34 us (45%)
  Pallas kernels  10.3 us (14%)
  matrix products  10.3 us (14%)
  waiting for transfers between devices  7.92 us (11%)
  local copies, waits for them, and re-layouts  5.83 us (8%)
  other arithmetic  4.43 us (6%)
  between operations  1.69 us (2%)
    ppermute x8, starting transfers between devices, send(): return lax.ppermute(x, ('patch', 'grp', 'col'), pairs)  17.3 us
    ppermute x6, starting transfers between devices, swap(): return lax.ppermute(x, 'col', [(0, 1), (1, 0)])  9.91 us
    pallas_call x4, Pallas kernels, call(): pl.pallas_call(kernel, out_shape=out_shape, in_specs=[pl.BlockSpec(memory...  5.98 us
    unnamed x17, local copies, waits for them, and re-layouts  5.73 us
    dot_general x4, matrix products, gather_plan(): lax.dot_general(back_rows, down_weight, (((1,), (1,)), ((), ())), preferr...  5.48 us
    pallas_call x1, Pallas kernels, gather_plan(): pl.pallas_call(finish_products, out_shape=grads, in_specs=[pl.BlockSpec(m...  4.3 us
    ppermute x5, waiting for transfers between devices, others(): lax.ppermute(x, axis, [(i, i ^ k) for i in range(n)])  3.84 us
    ppermute x5, starting transfers between devices, others(): lax.ppermute(x, axis, [(i, i ^ k) for i in range(n)])  3.55 us
  transfers between devices with their start and end apart: 22, of which 6 were waited for; matrix products, arithmetic and copies ran while one was open for 22% of the time, Pallas kernels for 14%

profile of v5, /device:TPU:0, one launch (start us, length us, event | category | flops | bytes accessed | tf_op | source)
XLA Modules:
  0.0 74.5 jit_solution(3656874579861977939)
XLA Ops:
  0.6 0.5 collective-permute-start.4
  1.2 2.9 %collective-permute-start.1 = (bf16[128,512]{1,0:T(8,128)(2,1)}, bf16[128,512]{1,0:T(8,128)(2,1)S(1)}, u32[]{:S(2)}, u32[]{:S(2)}) collective-permute-start(bf16[128,512]{1,0:T(8,128)(2,1)} %refs_0_.3), channel_id=1, source_target_pairs={{0,2},{2,0},{1,3},{3,1},{4,6},{6,4},{5,7},{7,5},{8,10},{10,8},{9,1... | collective-permute-start | bytes 393224 | tf_op jit(solution)/shard_map/ppermute | solution.py:127
  4.9 1.2 %copy-done.2 = bf16[512,1024]{1,0:T(8,128)(2,1)S(1)} copy-done((bf16[512,1024]{1,0:T(8,128)(2,1)S(1)}, bf16[512,1024]{1,0:T(8,128)(2,1)}, u32[]{:S(2)}) %copy-start.2) | copy-done | bytes 1048600
  6.1 0.9 %copy-done.3 = bf16[128,512]{1,0:T(8,128)(2,1)S(1)} copy-done((bf16[128,512]{1,0:T(8,128)(2,1)S(1)}, bf16[128,512]{1,0:T(8,128)(2,1)}, u32[]{:S(2)}) %copy-start.3) | copy-done | bytes 131096
  7.1 1.6 %collective-permute-done.1.refs_1_ = bf16[128,512]{1,0:T(8,128)(2,1)S(1)} collective-permute-done((bf16[128,512]{1,0:T(8,128)(2,1)}, bf16[128,512]{1,0:T(8,128)(2,1)S(1)}, u32[]{:S(2)}, u32[]{:S(2)}) %collective-permute-start.1) | collective-permute-done | bytes 131104 | tf_op jit(solution)/shard_map/ppermute | solution.py:127
  8.7 2.3 %collective-permute-done.2.refs_3_ = bf16[128,512]{1,0:T(8,128)(2,1)S(1)} collective-permute-done((bf16[128,512]{1,0:T(8,128)(2,1)}, bf16[128,512]{1,0:T(8,128)(2,1)S(1)}, u32[]{:S(2)}, u32[]{:S(2)}) %collective-permute-start.2) | collective-permute-done | bytes 131104 | tf_op jit(solution)/shard_map/ppermute | solution.py:127
  10.9 0.7 copy-done.6
  11.6 2.8 %shard_map.131.refs_0_ = bf16[272,512]{1,0:T(8,128)(2,1)} custom-call(s32[1,2]{1,0:T(1,128)} %ids_ref.1, s32[1]{0:T(128)S(6)} %copy.17.count_ref, f32[1,512]{1,0:T(1,128)} %bitcast.17, bf16[128,512]{1,0:T(8,128)(2,1)} %residual_ref.1, bf16[128,512]{1,0:T(8,128)(2,1)} %query_ref, bf16[128,512]{1,0:T(8,128)(2,1)} %refs_0_.3, bf16[128,512]{1,0:T(8,128)(2,1)} %copy-done.5, ...), custom_call_target="tpu_custom_call" | custom-call | flops 134217728 | bytes 1067020 | tf_op jit(solution)/shard_map/pallas_call | solution.py:283
  14.3 1.8 %collective-permute-start.11 = (bf16[128,1024]{1,0:T(8,128)(2,1)S(1)}, bf16[128,1024]{1,0:T(8,128)(2,1)}, u32[]{:S(2)}, u32[]{:S(2)}) collective-permute-start(bf16[128,1024]{1,0:T(8,128)(2,1)S(1)} %get-tuple-element.14), channel_id=1, source_target_pairs={{0,4},{1,9},{2,6},{3,11},{4,0},{5,13},{6,2},{7,15},{8,12},{9,1},{1... | collective-permute-start | bytes 786440 | tf_op jit(solution)/shard_map/ppermute | solution.py:303
  16.2 2.5 %collective-permute-start.9 = (bf16[128,1024]{1,0:T(8,128)(2,1)S(1)}, bf16[128,1024]{1,0:T(8,128)(2,1)}, u32[]{:S(2)}, u32[]{:S(2)}) collective-permute-start(bf16[128,1024]{1,0:T(8,128)(2,1)S(1)} %get-tuple-element.14), channel_id=1, source_target_pairs={{0,12},{1,3},{2,14},{3,1},{4,8},{5,7},{6,10},{7,5},{8,4},{9,11},{1... | collective-permute-start | bytes 786440 | tf_op jit(solution)/shard_map/ppermute | solution.py:303
  18.7 1.0 %copy-done.1 = bf16[272,512]{1,0:T(8,128)(2,1)S(1)} copy-done((bf16[272,512]{1,0:T(8,128)(2,1)S(1)}, bf16[272,512]{1,0:T(8,128)(2,1)}, u32[]{:S(2)}) %copy-start.1) | copy-done | bytes 278552
  19.6 0.7 %shard_map.132 = (f32[128,512]{1,0:T(8,128)S(1)}, bf16[128,1024]{1,0:T(8,128)(2,1)S(1)}) custom-call(bf16[272,512]{1,0:T(8,128)(2,1)S(1)} %copy-done.1, bf16[272,512]{1,0:T(8,128)(2,1)S(1)} %collective-permute-done.3.refs_1_, bf16[512,1024]{1,0:T(8,128)(2,1)S(1)} %get-tuple-element.16.refs_2_, bf16[512,1024]{1,0:T(8,128)(2,1)S(1)} %collective-permute-done.4.refs_3_), custom_call_target="tpu_custom_call" | custom-call | flops 268435456 | bytes 3178496 | tf_op jit(solution)/shard_map/pallas_call | solution.py:283
  20.4 0.7 %collective-permute-start.10 = (bf16[128,1024]{1,0:T(8,128)(2,1)S(1)}, bf16[128,1024]{1,0:T(8,128)(2,1)}, u32[]{:S(2)}, u32[]{:S(2)}) collective-permute-start(bf16[128,1024]{1,0:T(8,128)(2,1)S(1)} %get-tuple-element.18), channel_id=1, source_target_pairs={{0,4},{1,9},{2,6},{3,11},{4,0},{5,13},{6,2},{7,15},{8,12},{9,1},{1... | collective-permute-start | bytes 786440 | tf_op jit(solution)/shard_map/ppermute | solution.py:303
  21.1 0.4 fusion.34
  21.6 0.9 %collective-permute-done.11 = bf16[128,1024]{1,0:T(8,128)(2,1)} collective-permute-done((bf16[128,1024]{1,0:T(8,128)(2,1)S(1)}, bf16[128,1024]{1,0:T(8,128)(2,1)}, u32[]{:S(2)}, u32[]{:S(2)}) %collective-permute-start.11) | collective-permute-done | bytes 262176 | tf_op jit(solution)/shard_map/ppermute | solution.py:303
  22.5 1.8 %collective-permute-start.12 = (bf16[128,1024]{1,0:T(8,128)(2,1)}, bf16[128,1024]{1,0:T(8,128)(2,1)}, u32[]{:S(2)}, u32[]{:S(2)}) collective-permute-start(bf16[128,1024]{1,0:T(8,128)(2,1)} %collective-permute-done.11), channel_id=1, source_target_pairs={{0,2},{1,3},{2,0},{3,1},{4,6},{5,7},{6,4},{7,5},{8,10},{9,11},{10,... | collective-permute-start | bytes 786440 | tf_op jit(solution)/shard_map/ppermute | solution.py:303
  24.2 3.0 %collective-permute-start.5 = (bf16[128,1024]{1,0:T(8,128)(2,1)S(1)}, bf16[128,1024]{1,0:T(8,128)(2,1)S(1)}, u32[]{:S(2)}, u32[]{:S(2)}) collective-permute-start(bf16[128,1024]{1,0:T(8,128)(2,1)S(1)} %get-tuple-element.18), channel_id=1, source_target_pairs={{0,12},{1,3},{2,14},{3,1},{4,8},{5,7},{6,10},{7,5},{8,4},{9,11},{1... | collective-permute-start | bytes 786440 | tf_op jit(solution)/shard_map/ppermute | solution.py:303
  27.3 5.5 %collective-permute-start.15 = (bf16[128,1024]{1,0:T(8,128)(2,1)}, bf16[128,1024]{1,0:T(8,128)(2,1)S(1)}, u32[]{:S(2)}, u32[]{:S(2)}) collective-permute-start(bf16[128,1024]{1,0:T(8,128)(2,1)} %collective-permute-done.11), channel_id=1, source_target_pairs={{0,1},{1,0},{2,3},{3,2},{4,5},{5,4},{6,7},{7,6},{8,9},{9,8},{10,11... | collective-permute-start | bytes 786440 | tf_op jit(solution)/shard_map/ppermute | solution.py:307
  32.8 1.0 %constant_dynamic-update-slice_fusion.3 = bf16[256,1024]{1,0:T(8,128)(2,1)S(1)} fusion(bf16[128,1024]{1,0:T(8,128)(2,1)} %collective-permute-done.11), kind=kLoop, calls=%fused_computation.62 | loop fusion | bytes 524288
  33.8 3.5 %collective-permute-start.20 = (bf16[128,1024]{1,0:T(8,128)(2,1)}, bf16[128,1024]{1,0:T(8,128)(2,1)S(1)}, u32[]{:S(2)}, u32[]{:S(2)}) collective-permute-start(bf16[128,1024]{1,0:T(8,128)(2,1)} %collective-permute-done.9), channel_id=1, source_target_pairs={{0,2},{2,0},{4,6},{6,4},{8,10},{10,8},{12,14},{14,12},{16,18},{18,... | collective-permute-start | bytes 786440 | tf_op jit(solution)/shard_map/ppermute | solution.py:303
  37.4 1.1 %pad_maximum_fusion.2 = bf16[256,1024]{1,0:T(8,128)(2,1)S(1)} fusion(bf16[128,1024]{1,0:T(8,128)(2,1)} %collective-permute-done.12, bf16[128,1024]{1,0:T(8,128)(2,1)} %collective-permute-done.9), kind=kLoop, calls=%fused_computation.43 | loop fusion | flops 1048576 | bytes 1048576 | tf_op jit(solution)/shard_map/concatenate | solution.py:393
  38.4 3.2 %collective-permute-start.13 = (bf16[256,1024]{1,0:T(8,128)(2,1)S(1)}, bf16[256,1024]{1,0:T(8,128)(2,1)S(1)}, u32[]{:S(2)}, u32[]{:S(2)}) collective-permute-start(bf16[256,1024]{1,0:T(8,128)(2,1)S(1)} %pad_maximum_fusion.2), channel_id=1, source_target_pairs={{0,1},{1,0},{2,3},{3,2},{4,5},{5,4},{6,7},{7,6},{8,9},{9,8},{10,11... | collective-permute-start | bytes 1572872 | tf_op jit(solution)/shard_map/ppermute | solution.py:307
  41.6 1.6 %collective-permute-start.16 = (bf16[128,1024]{1,0:T(8,128)(2,1)}, bf16[128,1024]{1,0:T(8,128)(2,1)S(1)}, u32[]{:S(2)}, u32[]{:S(2)}) collective-permute-start(bf16[128,1024]{1,0:T(8,128)(2,1)} %collective-permute-done.10), channel_id=1, source_target_pairs={{0,2},{1,3},{2,0},{3,1},{4,6},{5,7},{6,4},{7,5},{8,10},{9,11},{10,... | collective-permute-start | bytes 786440 | tf_op jit(solution)/shard_map/ppermute | solution.py:303
  43.2 1.0 %constant_dynamic-update-slice_fusion.1 = bf16[256,1024]{1,0:T(8,128)(2,1)S(1)} fusion(bf16[128,1024]{1,0:T(8,128)(2,1)} %collective-permute-done.10), kind=kLoop, calls=%fused_computation.60 | loop fusion | bytes 524288
  44.3 0.5 collective-permute-start.6
  44.8 0.7 %fusion.36 = f32[256,1024]{1,0:T(8,128)S(1)} fusion(bf16[256,1024]{1,0:T(8,128)(2,1)S(1)} %constant_dynamic-update-slice_fusion.2.refs_7_, bf16[1024,1024]{1,0:T(8,128)(2,1)S(1)} %copy-done.4), kind=kOutput, calls=%fused_computation.72 | convolution fusion | flops 536870912 | bytes 3670016 | tf_op jit(solution)/shard_map/dot_general | solution.py:432
  45.6 0.6 collective-permute-done.6
  46.2 2.3 %collective-permute-start.18 = (bf16[128,1024]{1,0:T(8,128)(2,1)S(1)}, bf16[128,1024]{1,0:T(8,128)(2,1)S(1)}, u32[]{:S(2)}, u32[]{:S(2)}) collective-permute-start(bf16[128,1024]{1,0:T(8,128)(2,1)S(1)} %collective-permute-done.5), channel_id=1, source_target_pairs={{0,2},{2,0},{4,6},{6,4},{8,10},{10,8},{12,14},{14,12},{16,18},{18,... | collective-permute-start | bytes 786440 | tf_op jit(solution)/shard_map/ppermute | solution.py:303
  48.6 0.4 fusion.35
  49.0 0.3 multiply_convert_fusion.3.refs_2_
  49.4 0.7 convolution_convert_fusion
  50.3 1.4 %multiply_convert_fusion.2 = (bf16[256,1024]{1,0:T(8,128)(2,1)S(1)}, bf16[256,1024]{1,0:T(8,128)(2,1)S(1)}) fusion(f32[256,1024]{1,0:T(8,128)S(1)} %fusion.36, bf16[256,1024]{1,0:T(8,128)(2,1)S(1)} %constant_dynamic-update-slice_fusion.refs_4_, bf16[1024,1024]{1,0:T(8,128)(2,1)S(1)} %copy-done), kind=kOutput, calls=%fused_computation.40 | convolution fusion | flops 542638080 | bytes 4718592 | tf_op jit(solution)/shard_map/dot_general | solution.py:421
  51.7 0.6 collective-permute-start.17
  52.2 2.2 %collective-permute-done.18 = bf16[128,1024]{1,0:T(8,128)(2,1)S(1)} collective-permute-done((bf16[128,1024]{1,0:T(8,128)(2,1)S(1)}, bf16[128,1024]{1,0:T(8,128)(2,1)S(1)}, u32[]{:S(2)}, u32[]{:S(2)}) %collective-permute-start.18) | collective-permute-done | bytes 262176 | tf_op jit(solution)/shard_map/ppermute | solution.py:303
  54.5 1.3 %collective-permute-start.19 = (bf16[128,1024]{1,0:T(8,128)(2,1)S(1)}, bf16[128,1024]{1,0:T(8,128)(2,1)S(1)}, u32[]{:S(2)}, u32[]{:S(2)}) collective-permute-start(bf16[128,1024]{1,0:T(8,128)(2,1)S(1)} %collective-permute-done.18), channel_id=1, source_target_pairs={{0,1},{2,3},{4,5},{6,7},{8,9},{10,11},{12,13},{14,15},{16,17},{18,... | collective-permute-start | bytes 786440 | tf_op jit(solution)/shard_map/ppermute | solution.py:311
  55.8 1.5 %collective-permute-start.21 = (bf16[128,1024]{1,0:T(8,128)(2,1)S(1)}, bf16[128,1024]{1,0:T(8,128)(2,1)S(1)}, u32[]{:S(2)}, u32[]{:S(2)}) collective-permute-start(bf16[128,1024]{1,0:T(8,128)(2,1)S(1)} %collective-permute-done.20), channel_id=1, source_target_pairs={{0,1},{2,3},{4,5},{6,7},{8,9},{10,11},{12,13},{14,15},{16,17},{18,... | collective-permute-start | bytes 786440 | tf_op jit(solution)/shard_map/ppermute | solution.py:311
  57.5 0.5 collective-permute-start.8
  58.0 0.3 collective-permute-done.21
  58.3 0.9 %multiply_convert_fusion = (bf16[256,1024]{1,0:T(8,128)(2,1)S(1)}, f32[256,1024]{1,0:T(8,128)S(1)}) fusion(bf16[1024,1024]{1,0:T(8,128)(2,1)S(1)} %copy-done, bf16[128,1024]{1,0:T(8,128)(2,1)S(1)} %broadcast_select_fusion.2, bf16[128,1024]{1,0:T(8,128)(2,1)S(1)} %get-tuple-element.30), kind=kOutput, calls=%fused_computation.38 | convolution fusion | flops 540278784 | bytes 4194304 | tf_op jit(solution)/shard_map/dot_general | solution.py:421
  59.3 1.0 %broadcast_select_fusion.1 = (bf16[128,1024]{1,0:T(8,128)(2,1)S(1)}, bf16[128,1024]{1,0:T(8,128)(2,1)S(1)}, bf16[128,1024]{1,0:T(8,128)(2,1)S(1)}) fusion(bf16[128,1024]{1,0:T(8,128)(2,1)} %collective-permute-done.9, pred[]{:T(512)S(6)} %eq.3, bf16[256,1024]{1,0:T(8,128)(2,1)S(1)} %collective-permute-done.13), kind=kLoop, calls=%fused_computation.54 | loop fusion | flops 262144 | bytes 1572865 | tf_op jit(solution)/shard_map/jit(_where)/select_n | solution.py:381
  60.3 1.3 %fusion.27.refs_7_ = bf16[256,1024]{1,0:T(8,128)(2,1)S(1)} fusion(f32[256,1024]{1,0:T(8,128)S(1)} %get-tuple-element.35, bf16[1024,1024]{1,0:T(8,128)(2,1)S(1)} %copy-done.4, bf16[128,1024]{1,0:T(8,128)(2,1)S(1)} %broadcast_select_fusion, bf16[128,1024]{1,0:T(8,128)(2,1)S(1)} %get-tuple-element.27), kind=kOutput, calls=%fused_computation.36 | convolution fusion | flops 543162368 | bytes 4194304 | tf_op jit(solution)/shard_map/dot_general | solution.py:432
  61.5 1.2 %fusion.6.refs_1_ = bf16[256,1024]{1,0:T(8,128)(2,1)S(1)} fusion(f32[128,1024]{1,0:T(8,128)S(1)} %fusion.35, f32[128,1024]{1,0:T(8,128)S(1)} %fusion.34, bf16[1024,1024]{1,0:T(8,128)(2,1)S(1)} %copy-done.4, bf16[128,1024]{1,0:T(8,128)(2,1)S(1)} %get-tuple-element.28, bf16[128,1024]{1,0:T(8,128)(2,1)S(1)} %get-tuple-element.14), kind=kOutput, calls=%fused_computation.15 | convolution fusion | flops 543424512 | bytes 4194304 | tf_op jit(solution)/shard_map/dot_general | solution.py:432
  62.9 0.9 %multiply_convert_fusion.1 = (bf16[256,1024]{1,0:T(8,128)(2,1)S(1)}, f32[256,1024]{1,0:T(8,128)S(1)}) fusion(bf16[256,1024]{1,0:T(8,128)(2,1)S(1)} %constant_dynamic-update-slice_fusion.4.refs_2_, bf16[1024,1024]{1,0:T(8,128)(2,1)S(1)} %copy-done), kind=kOutput, calls=%fused_computation.39 | convolution fusion | flops 539230208 | bytes 4194304 | tf_op jit(solution)/shard_map/dot_general | solution.py:421
  63.9 2.4 %shard_map.133 = (f32[1024,1024]{1,0:T(8,128)S(1)}, f32[1024,1024]{1,0:T(8,128)S(1)}) custom-call(bf16[256,1024]{1,0:T(8,128)(2,1)S(1)} %pad_maximum_fusion.1.refs_0_, bf16[256,1024]{1,0:T(8,128)(2,1)S(1)} %fusion.6.refs_1_, bf16[256,1024]{1,0:T(8,128)(2,1)S(1)} %multiply_convert_fusion.3.refs_2_, bf16[256,1024]{1,0:T(8,128)(2,1)S(1)} %pad_maximum_fusion.3.refs_3_, ...), custom_call_target="tpu_custom_call" | custom-call | flops 2147483648 | bytes 12582912 | tf_op jit(solution)/shard_map/pallas_call | solution.py:283
  66.2 1.0 %pad_maximum_fusion.4.refs_5_ = bf16[256,1024]{1,0:T(8,128)(2,1)S(1)} fusion(bf16[128,1024]{1,0:T(8,128)(2,1)S(1)} %get-tuple-element.29, bf16[128,1024]{1,0:T(8,128)(2,1)} %collective-permute-done.12), kind=kLoop, calls=%fused_computation.45 | loop fusion | flops 1048576 | bytes 1048576 | tf_op jit(solution)/shard_map/concatenate | solution.py:379
  67.2 2.2 %fusion.20.refs_3_ = bf16[256,1024]{1,0:T(8,128)(2,1)S(1)} fusion(f32[256,1024]{1,0:T(8,128)S(1)} %get-tuple-element.33, bf16[1024,1024]{1,0:T(8,128)(2,1)S(1)} %copy-done.4, bf16[128,1024]{1,0:T(8,128)(2,1)S(1)} %get-tuple-element.29, bf16[128,1024]{1,0:T(8,128)(2,1)} %collective-permute-done.12), kind=kOutput, calls=%fused_computation.29 | convolution fusion | flops 543162368 | bytes 4194304 | tf_op jit(solution)/shard_map/dot_general | solution.py:432
  69.5 4.3 %shard_map.134 = (f32[1024,1024]{1,0:T(8,128)}, f32[1024,1024]{1,0:T(8,128)}) custom-call(f32[1024,1024]{1,0:T(8,128)S(1)} %get-tuple-element.21.refs_0_, f32[1024,1024]{1,0:T(8,128)S(1)} %get-tuple-element.22.refs_1_, bf16[256,1024]{1,0:T(8,128)(2,1)S(1)} %constant_dynamic-update-slice_fusion.4.refs_2_, bf16[256,1024]{1,0:T(8,128)(2,1)S(1)} %fusion.20.refs_3_, ...), custom_call_target="tpu_custom_call" | custom-call | flops 2147483648 | bytes 16777216 | tf_op jit(solution)/shard_map/pallas_call | solution.py:446
  73.8 0.7 fusion.29
  (46 shorter events, 0.9 us)
Async XLA Ops:
  0.6 20.5 %copy-start = (bf16[1024,1024]{1,0:T(8,128)(2,1)S(1)}, bf16[1024,1024]{1,0:T(8,128)(2,1)}, u32[]{:S(2)}) copy-start(bf16[1024,1024]{1,0:T(8,128)(2,1)} %param.19) | copy-start | bytes 6291460
  0.6 18.0 %collective-permute-start.4 = (bf16[512,1024]{1,0:T(8,128)(2,1)}, bf16[512,1024]{1,0:T(8,128)(2,1)S(1)}, u32[]{:S(2)}, u32[]{:S(2)}) collective-permute-start(bf16[512,1024]{1,0:T(8,128)(2,1)} %weight_ref.1), channel_id=1, source_target_pairs={{0,1},{1,0},{2,3},{3,2},{4,5},{5,4},{6,7},{7,6},{8,9},{9,8},{10,11... | collective-permute-start | bytes 3145736 | tf_op jit(solution)/shard_map/ppermute | solution.py:127
  1.2 3.7 %collective-permute-start = (bf16[128,512]{1,0:T(8,128)(2,1)}, bf16[128,512]{1,0:T(8,128)(2,1)S(1)}, u32[]{:S(2)}, u32[]{:S(2)}) collective-permute-start(bf16[128,512]{1,0:T(8,128)(2,1)} %refs_0_.2), channel_id=1, source_target_pairs={{0,1},{1,0},{2,3},{3,2},{4,5},{5,4},{6,7},{7,6},{8,9},{9,8},{10,11... | collective-permute-start | bytes 393224 | tf_op jit(solution)/shard_map/ppermute | solution.py:127
  1.2 7.4 %collective-permute-start.1 = (bf16[128,512]{1,0:T(8,128)(2,1)}, bf16[128,512]{1,0:T(8,128)(2,1)S(1)}, u32[]{:S(2)}, u32[]{:S(2)}) collective-permute-start(bf16[128,512]{1,0:T(8,128)(2,1)} %refs_0_.3), channel_id=1, source_target_pairs={{0,2},{2,0},{1,3},{3,1},{4,6},{6,4},{5,7},{7,5},{8,10},{10,8},{9,1... | collective-permute-start | bytes 393224 | tf_op jit(solution)/shard_map/ppermute | solution.py:127
  4.2 6.8 %collective-permute-start.2 = (bf16[128,512]{1,0:T(8,128)(2,1)}, bf16[128,512]{1,0:T(8,128)(2,1)S(1)}, u32[]{:S(2)}, u32[]{:S(2)}) collective-permute-start(bf16[128,512]{1,0:T(8,128)(2,1)} %refs_2_.1), channel_id=1, source_target_pairs={{0,2},{2,0},{1,3},{3,1},{4,6},{6,4},{5,7},{7,5},{8,10},{10,8},{9,1... | collective-permute-start | bytes 393224 | tf_op jit(solution)/shard_map/ppermute | solution.py:127
  4.9 1.2 %copy-start.2 = (bf16[512,1024]{1,0:T(8,128)(2,1)S(1)}, bf16[512,1024]{1,0:T(8,128)(2,1)}, u32[]{:S(2)}) copy-start(bf16[512,1024]{1,0:T(8,128)(2,1)} %weight_ref.1) | copy-start | bytes 3145732
  6.1 0.9 %copy-start.3 = (bf16[128,512]{1,0:T(8,128)(2,1)S(1)}, bf16[128,512]{1,0:T(8,128)(2,1)}, u32[]{:S(2)}) copy-start(bf16[128,512]{1,0:T(8,128)(2,1)} %refs_0_.2) | copy-start | bytes 393220
  8.7 2.3 %copy-start.5 = (bf16[128,512]{1,0:T(8,128)(2,1)}, bf16[128,512]{1,0:T(8,128)(2,1)S(1)}, u32[]{:S(2)}) copy-start(bf16[128,512]{1,0:T(8,128)(2,1)S(1)} %collective-permute-done.1.refs_1_) | copy-start | bytes 393220
  10.9 0.7 copy-start.6
  14.3 4.3 %collective-permute-start.3 = (bf16[272,512]{1,0:T(8,128)(2,1)}, bf16[272,512]{1,0:T(8,128)(2,1)S(1)}, u32[]{:S(2)}, u32[]{:S(2)}) collective-permute-start(bf16[272,512]{1,0:T(8,128)(2,1)} %shard_map.131.refs_0_), channel_id=1, source_target_pairs={{0,1},{1,0},{2,3},{3,2},{4,5},{5,4},{6,7},{7,6},{8,9},{9,8},{10,11... | collective-permute-start | bytes 835592 | tf_op jit(solution)/shard_map/ppermute | solution.py:127
  14.3 8.2 %collective-permute-start.11 = (bf16[128,1024]{1,0:T(8,128)(2,1)S(1)}, bf16[128,1024]{1,0:T(8,128)(2,1)}, u32[]{:S(2)}, u32[]{:S(2)}) collective-permute-start(bf16[128,1024]{1,0:T(8,128)(2,1)S(1)} %get-tuple-element.14), channel_id=1, source_target_pairs={{0,4},{1,9},{2,6},{3,11},{4,0},{5,13},{6,2},{7,15},{8,12},{9,1},{1... | collective-permute-start | bytes 786440 | tf_op jit(solution)/shard_map/ppermute | solution.py:303
  16.2 17.6 %collective-permute-start.9 = (bf16[128,1024]{1,0:T(8,128)(2,1)S(1)}, bf16[128,1024]{1,0:T(8,128)(2,1)}, u32[]{:S(2)}, u32[]{:S(2)}) collective-permute-start(bf16[128,1024]{1,0:T(8,128)(2,1)S(1)} %get-tuple-element.14), channel_id=1, source_target_pairs={{0,12},{1,3},{2,14},{3,1},{4,8},{5,7},{6,10},{7,5},{8,4},{9,11},{1... | collective-permute-start | bytes 786440 | tf_op jit(solution)/shard_map/ppermute | solution.py:303
  18.6 1.0 %copy-start.1 = (bf16[272,512]{1,0:T(8,128)(2,1)S(1)}, bf16[272,512]{1,0:T(8,128)(2,1)}, u32[]{:S(2)}) copy-start(bf16[272,512]{1,0:T(8,128)(2,1)} %shard_map.131.refs_0_) | copy-start | bytes 835588
  20.4 13.5 %collective-permute-start.10 = (bf16[128,1024]{1,0:T(8,128)(2,1)S(1)}, bf16[128,1024]{1,0:T(8,128)(2,1)}, u32[]{:S(2)}, u32[]{:S(2)}) collective-permute-start(bf16[128,1024]{1,0:T(8,128)(2,1)S(1)} %get-tuple-element.18), channel_id=1, source_target_pairs={{0,4},{1,9},{2,6},{3,11},{4,0},{5,13},{6,2},{7,15},{8,12},{9,1},{1... | collective-permute-start | bytes 786440 | tf_op jit(solution)/shard_map/ppermute | solution.py:303
  22.5 14.9 %collective-permute-start.12 = (bf16[128,1024]{1,0:T(8,128)(2,1)}, bf16[128,1024]{1,0:T(8,128)(2,1)}, u32[]{:S(2)}, u32[]{:S(2)}) collective-permute-start(bf16[128,1024]{1,0:T(8,128)(2,1)} %collective-permute-done.11), channel_id=1, source_target_pairs={{0,2},{1,3},{2,0},{3,1},{4,6},{5,7},{6,4},{7,5},{8,10},{9,11},{10,... | collective-permute-start | bytes 786440 | tf_op jit(solution)/shard_map/ppermute | solution.py:303
  24.2 20.6 %copy-start.4 = (bf16[1024,1024]{1,0:T(8,128)(2,1)S(1)}, bf16[1024,1024]{1,0:T(8,128)(2,1)}, u32[]{:S(2)}) copy-start(bf16[1024,1024]{1,0:T(8,128)(2,1)} %param.20) | copy-start | bytes 6291460
  24.2 20.0 %collective-permute-start.5 = (bf16[128,1024]{1,0:T(8,128)(2,1)S(1)}, bf16[128,1024]{1,0:T(8,128)(2,1)S(1)}, u32[]{:S(2)}, u32[]{:S(2)}) collective-permute-start(bf16[128,1024]{1,0:T(8,128)(2,1)S(1)} %get-tuple-element.18), channel_id=1, source_target_pairs={{0,12},{1,3},{2,14},{3,1},{4,8},{5,7},{6,10},{7,5},{8,4},{9,11},{1... | collective-permute-start | bytes 786440 | tf_op jit(solution)/shard_map/ppermute | solution.py:303
  27.3 17.0 %collective-permute-start.15 = (bf16[128,1024]{1,0:T(8,128)(2,1)}, bf16[128,1024]{1,0:T(8,128)(2,1)S(1)}, u32[]{:S(2)}, u32[]{:S(2)}) collective-permute-start(bf16[128,1024]{1,0:T(8,128)(2,1)} %collective-permute-done.11), channel_id=1, source_target_pairs={{0,1},{1,0},{2,3},{3,2},{4,5},{5,4},{6,7},{7,6},{8,9},{9,8},{10,11... | collective-permute-start | bytes 786440 | tf_op jit(solution)/shard_map/ppermute | solution.py:307
  33.8 22.0 %collective-permute-start.20 = (bf16[128,1024]{1,0:T(8,128)(2,1)}, bf16[128,1024]{1,0:T(8,128)(2,1)S(1)}, u32[]{:S(2)}, u32[]{:S(2)}) collective-permute-start(bf16[128,1024]{1,0:T(8,128)(2,1)} %collective-permute-done.9), channel_id=1, source_target_pairs={{0,2},{2,0},{4,6},{6,4},{8,10},{10,8},{12,14},{14,12},{16,18},{18,... | collective-permute-start | bytes 786440 | tf_op jit(solution)/shard_map/ppermute | solution.py:303
  38.4 20.8 %collective-permute-start.13 = (bf16[256,1024]{1,0:T(8,128)(2,1)S(1)}, bf16[256,1024]{1,0:T(8,128)(2,1)S(1)}, u32[]{:S(2)}, u32[]{:S(2)}) collective-permute-start(bf16[256,1024]{1,0:T(8,128)(2,1)S(1)} %pad_maximum_fusion.2), channel_id=1, source_target_pairs={{0,1},{1,0},{2,3},{3,2},{4,5},{5,4},{6,7},{7,6},{8,9},{9,8},{10,11... | collective-permute-start | bytes 1572872 | tf_op jit(solution)/shard_map/ppermute | solution.py:307
  41.6 10.0 %collective-permute-start.16 = (bf16[128,1024]{1,0:T(8,128)(2,1)}, bf16[128,1024]{1,0:T(8,128)(2,1)S(1)}, u32[]{:S(2)}, u32[]{:S(2)}) collective-permute-start(bf16[128,1024]{1,0:T(8,128)(2,1)} %collective-permute-done.10), channel_id=1, source_target_pairs={{0,2},{1,3},{2,0},{3,1},{4,6},{5,7},{6,4},{7,5},{8,10},{9,11},{10,... | collective-permute-start | bytes 786440 | tf_op jit(solution)/shard_map/ppermute | solution.py:303
  44.2 5.9 %collective-permute-start.14 = (bf16[128,1024]{1,0:T(8,128)(2,1)}, bf16[128,1024]{1,0:T(8,128)(2,1)S(1)}, u32[]{:S(2)}, u32[]{:S(2)}) collective-permute-start(bf16[128,1024]{1,0:T(8,128)(2,1)} %collective-permute-done.10), channel_id=1, source_target_pairs={{0,1},{1,0},{2,3},{3,2},{4,5},{5,4},{6,7},{7,6},{8,9},{9,8},{10,11... | collective-permute-start | bytes 786440 | tf_op jit(solution)/shard_map/ppermute | solution.py:307
  44.3 1.9 %collective-permute-start.6 = (bf16[128,1024]{1,0:T(8,128)(2,1)S(1)}, bf16[128,1024]{1,0:T(8,128)(2,1)S(1)}, u32[]{:S(2)}, u32[]{:S(2)}) collective-permute-start(bf16[128,1024]{1,0:T(8,128)(2,1)S(1)} %collective-permute-done.5), channel_id=1, source_target_pairs={{0,1},{1,0},{2,3},{3,2},{4,5},{5,4},{6,7},{7,6},{8,9},{9,8},{10,11... | collective-permute-start | bytes 786440 | tf_op jit(solution)/shard_map/ppermute | solution.py:307
  46.2 8.3 %collective-permute-start.18 = (bf16[128,1024]{1,0:T(8,128)(2,1)S(1)}, bf16[128,1024]{1,0:T(8,128)(2,1)S(1)}, u32[]{:S(2)}, u32[]{:S(2)}) collective-permute-start(bf16[128,1024]{1,0:T(8,128)(2,1)S(1)} %collective-permute-done.5), channel_id=1, source_target_pairs={{0,2},{2,0},{4,6},{6,4},{8,10},{10,8},{12,14},{14,12},{16,18},{18,... | collective-permute-start | bytes 786440 | tf_op jit(solution)/shard_map/ppermute | solution.py:303
  50.1 7.2 %collective-permute-start.7 = (bf16[256,512]{1,0:T(8,128)(2,1)S(1)}, bf16[256,512]{1,0:T(8,128)(2,1)S(1)}, u32[]{:S(2)}, u32[]{:S(2)}) collective-permute-start(bf16[256,512]{1,0:T(8,128)(2,1)S(1)} %constant_dynamic-slice_fusion), channel_id=1, source_target_pairs={{0,1},{1,0},{2,3},{3,2},{4,5},{5,4},{6,7},{7,6},{8,9},{9,8},{10,11... | collective-permute-start | bytes 786440 | tf_op jit(solution)/shard_map/ppermute | solution.py:307
  51.7 11.2 %collective-permute-start.17 = (bf16[128,1024]{1,0:T(8,128)(2,1)S(1)}, bf16[128,1024]{1,0:T(8,128)(2,1)S(1)}, u32[]{:S(2)}, u32[]{:S(2)}) collective-permute-start(bf16[128,1024]{1,0:T(8,128)(2,1)S(1)} %collective-permute-done.16), channel_id=1, source_target_pairs={{0,1},{1,0},{2,3},{3,2},{4,5},{5,4},{6,7},{7,6},{8,9},{9,8},{10,11... | collective-permute-start | bytes 786440 | tf_op jit(solution)/shard_map/ppermute | solution.py:307
  54.5 3.5 %collective-permute-start.19 = (bf16[128,1024]{1,0:T(8,128)(2,1)S(1)}, bf16[128,1024]{1,0:T(8,128)(2,1)S(1)}, u32[]{:S(2)}, u32[]{:S(2)}) collective-permute-start(bf16[128,1024]{1,0:T(8,128)(2,1)S(1)} %collective-permute-done.18), channel_id=1, source_target_pairs={{0,1},{2,3},{4,5},{6,7},{8,9},{10,11},{12,13},{14,15},{16,17},{18,... | collective-permute-start | bytes 786440 | tf_op jit(solution)/shard_map/ppermute | solution.py:311
  55.8 2.4 %collective-permute-start.21 = (bf16[128,1024]{1,0:T(8,128)(2,1)S(1)}, bf16[128,1024]{1,0:T(8,128)(2,1)S(1)}, u32[]{:S(2)}, u32[]{:S(2)}) collective-permute-start(bf16[128,1024]{1,0:T(8,128)(2,1)S(1)} %collective-permute-done.20), channel_id=1, source_target_pairs={{0,1},{2,3},{4,5},{6,7},{8,9},{10,11},{12,13},{14,15},{16,17},{18,... | collective-permute-start | bytes 786440 | tf_op jit(solution)/shard_map/ppermute | solution.py:311
  57.5 16.3 %collective-permute-start.8 = (bf16[128,512]{1,0:T(8,128)(2,1)S(1)}, bf16[128,512]{1,0:T(8,128)(2,1)S(1)}, u32[]{:S(2)}, u32[]{:S(2)}) collective-permute-start(bf16[128,512]{1,0:T(8,128)(2,1)S(1)} %slice.29), channel_id=1, source_target_pairs={{0,2},{2,0},{1,3},{3,1},{4,6},{6,4},{5,7},{7,5},{8,10},{10,8},{9,1... | collective-permute-start | bytes 393224 | tf_op jit(solution)/shard_map/ppermute | solution.py:430

commit v6 on v5

--- a/solution.py
+++ b/solution.py
@@ -108,6 +108,8 @@
 
 GAIN_ROWS = 16
 TILE = 256
+PANEL_TILE = 512
+ROOT, CUBIC = 0.7978845608028654, 0.044715
 OWN_LIMIT = 56 * 2**20
 
 
@@ -147,15 +149,62 @@
     return pl.ds(pl.multiple_of(member("col", j) * half, half), half)
 
 
-def join_cores(weight_ref, *refs):
-    parts, (kept_ref, out_ref) = refs[:-2], refs[-2:]
+def join_cores(*refs):
+    parts, out_ref = refs[:-1], refs[-1]
     half = parts[0].shape[1]
     for j, part in enumerate(parts):
         out_ref[:, core_columns(j, half)] = part[...]
-    kept_ref[...] = weight_ref[...]
-
-
-def attend(grps, ids_ref, count_ref, gain_ref, residual_ref, query_ref, *refs):
+
+
+def keep(*refs):
+    count = len(refs) // 2
+    for source, target in zip(refs[:count], refs[count:]):
+        target[...] = source[...]
+
+
+def gelu_and_slope(pre):
+    square = pre * pre
+    curve = jnp.tanh(ROOT * (pre + CUBIC * (square * pre)))
+    half = 0.5 * (1.0 + curve)
+    slope = half + 0.5 * pre * (1.0 - curve * curve) * (ROOT * (1.0 + 3.0 * CUBIC * square))
+    return pre * half, slope
+
+
+def feed_forward(choices, share, *refs):
+    count = 2 * sum(choices)
+    blocks, (up_ref, down_ref), outs = refs[:count], refs[count : count + 2], refs[count + 2 :]
+    rows_ref, back_pre_ref, hidden_ref, back_ref = outs[:4]
+    first = lax.axis_index("col") == 0
+    at = 0
+    for out_ref in (rows_ref, back_ref):
+        for i, width in enumerate(choices):
+            rows = blocks[at].shape[0]
+            block = blocks[at][...]
+            if width == 2:
+                block = jnp.where(first, block, blocks[at + 1][...])
+            out_ref[pl.ds(i * rows, rows), :] = block
+            at += width
+    rows, back = rows_ref[...], back_ref[...]
+    for start in range(0, up_ref.shape[1], PANEL_TILE):
+        tile = pl.ds(start, PANEL_TILE)
+        pre = jnp.dot(rows, up_ref[:, tile], preferred_element_type=jnp.float32)
+        back_hidden = lax.dot_general(
+            back, down_ref[tile, :], (((1,), (1,)), ((), ())), preferred_element_type=jnp.float32
+        )
+        hidden, slope = gelu_and_slope(pre)
+        hidden_ref[:, tile] = hidden.astype(jnp.bfloat16)
+        back_pre_ref[:, tile] = (back_hidden * slope).astype(jnp.bfloat16)
+    if share:
+        for j, out_ref in enumerate(outs[4:]):
+            part = jnp.dot(
+                hidden_ref[...],
+                down_ref[:, core_columns(j, out_ref.shape[1])],
+                preferred_element_type=jnp.float32,
+            )
+            out_ref[...] = part.astype(out_ref.dtype)
+
+
+def attend(grps, ids_ref, count_ref, gain_ref, query_ref, *refs):
     seen = []
     for k in range(grps):
         listed = [
@@ -204,11 +253,11 @@
         row == 0, high, jnp.where(row == 1, middle, jnp.where(row == 2, low, 0.0))
     )
     out_ref[pl.ds(rows, GAIN_ROWS), :] = parts.astype(jnp.bfloat16)
-    out_ref[pl.ds(rows + GAIN_ROWS, rows), :] = residual_ref[...]
 
 
 def project(cores, *refs):
-    packs, weights, (stream_ref, normed_ref, full, gain) = refs[:cores], refs[cores:-4], refs[-4:]
+    packs, weights, residuals = refs[:cores], refs[cores : 2 * cores], refs[2 * cores : 3 * cores]
+    stream_ref, normed_ref, full, gain = refs[3 * cores :]
     rows, half = stream_ref.shape
     width = half * cores
     full[...] = sum(
@@ -217,7 +266,7 @@
     )
     for j, pack in enumerate(packs):
         cols = core_columns(j, half)
-        part = full[:, cols] + pack[pl.ds(rows + GAIN_ROWS, rows), :].astype(jnp.float32)
+        part = full[:, cols] + residuals[j][...].astype(jnp.float32)
         full[:, cols] = part
         if j == 0:
             stream_ref[...] = part
@@ -276,17 +325,17 @@
         copy.wait()
 
 
-def call(kernel, out_shape, smem, args, flops, scratch=(), limit=16 * 2**20):
-    moved = sum(a.size * a.dtype.itemsize for a in args) + sum(
-        o.size * o.dtype.itemsize for o in jax.tree.leaves(out_shape)
-    )
+SMALL = pl.CostEstimate(flops=1, bytes_accessed=1, transcendentals=0)
+
+
+def call(kernel, out_shape, smem, args, scratch=(), limit=16 * 2**20):
     return pl.pallas_call(
         kernel,
         out_shape=out_shape,
         in_specs=[pl.BlockSpec(memory_space=pltpu.SMEM)] * smem
         + [pl.BlockSpec(memory_space=pltpu.VMEM)] * (len(args) - smem),
         scratch_shapes=scratch,
-        cost_estimate=pl.CostEstimate(flops=flops, bytes_accessed=moved, transcendentals=0),
+        cost_estimate=SMALL,
         compiler_params=pltpu.CompilerParams(vmem_limit_bytes=limit),
     )(*args)
 
@@ -331,30 +380,27 @@
 
     bf16 = jnp.bfloat16
     cot_parts = [cotangent] + others(cotangent, "col")
+    residuals = [residual] + others(residual, "col")
     keys = [key_vectors] + others(key_vectors, "grp")
     values = [value_vectors] + others(value_vectors, "grp")
     weights = [output_weight] + others(output_weight, "col")
-    weights[0], cot = call(
-        join_cores,
-        (
-            jax.ShapeDtypeStruct(output_weight.shape, bf16),
-            jax.ShapeDtypeStruct((rows, width), bf16),
-        ),
-        0,
-        [output_weight] + cot_parts,
-        0,
-    )
+    cot = call(join_cores, jax.ShapeDtypeStruct((rows, width), bf16), 0, cot_parts)
     cot12 = send(cot, [(1, 0), (2, 0)])
     cot3x = send(cot, [(3, 0), (0, 1)])
 
+    weights[0], residuals[0] = call(
+        keep,
+        [jax.ShapeDtypeStruct(a.shape, bf16) for a in (output_weight, residual)],
+        0,
+        [after(output_weight, cot), residual],
+    )
     packed = call(
         functools.partial(attend, grps),
-        jax.ShapeDtypeStruct((2 * rows + GAIN_ROWS, half), bf16),
+        jax.ShapeDtypeStruct((rows + GAIN_ROWS, half), bf16),
         2,
-        [neighbor_ids, neighbor_count, norm_gain[None], residual, after(query_vectors, cot)]
+        [neighbor_ids, neighbor_count, norm_gain[None], after(query_vectors, weights[0])]
         + keys
         + values,
-        4 * rows * rows * grps * width,
         [pltpu.VMEM((half // HEAD * grps, rows, rows), jnp.float32)],
         OWN_LIMIT,
     )
@@ -365,84 +411,55 @@
             jax.ShapeDtypeStruct((rows, width), bf16),
         ),
         0,
-        [packed] + others(packed, "col") + weights,
-        2 * rows * width * width,
+        [packed] + others(packed, "col") + [after(weights[0], cot12)] + weights[1:] + residuals,
         [pltpu.VMEM((rows, width), jnp.float32), pltpu.VMEM((8, width), jnp.float32)],
     )
-    first = lax.axis_index("col") == 0
-
-    def pairs_of(own, by12, by3x, swapped, over12, over3, swapped_over):
-        swap12, swap3x = swapped[:rows], swapped[rows:]
-        return [
-            jnp.concatenate([own, jnp.where(first, swap3x, by3x)], 0),
-            jnp.concatenate([by12, swap12], 0),
-            jnp.concatenate([over12, swapped_over[:rows]], 0),
-            jnp.concatenate(
-                [jnp.where(first, by3x, swap3x), jnp.where(first, over3, swapped_over[rows:])], 0
-            ),
-        ]
 
     def forward(by12, by3x):
         return send(by12, [(0, 1), (0, 1)]), send(by3x, [(0, 1), None])
 
     norm12 = send(normed, [(1, 0), (2, 0)])
     norm3x = send(normed, [(3, 0), (0, 1)])
-    own_pre = jnp.dot(normed, up_weight, preferred_element_type=jnp.float32)
-    cot12, cot3x = after(cot12, own_pre), after(cot3x, norm12)
-    over12, over3 = forward(cot12, cot3x)
-    late = swap(jnp.concatenate([cot3x, over12], 0))
-    cots = pairs_of(
-        cot,
-        cot12,
-        cot3x,
-        jnp.concatenate([swap(cot12), late[:rows]], 0),
-        over12,
-        over3,
-        jnp.concatenate([late[rows:], hand_over(over3)], 0),
+    cot12, cot3x = after(cot12, normed), after(cot3x, normed)
+    cot_over12, cot_over3 = forward(cot12, cot3x)
+    cot_swap12, cot_swap3x = swap(cot12), swap(cot3x)
+    cot_swap_over, cot_handed = swap(cot_over12), hand_over(cot_over3)
+    norm12, norm3x, *_ = lax.optimization_barrier(
+        (norm12, norm3x, cot_over12, cot_swap12)
     )
     over12, over3 = forward(norm12, norm3x)
-    norms = pairs_of(
-        normed,
-        norm12,
-        norm3x,
-        jnp.concatenate([swap(norm12), swap(norm3x)], 0),
-        over12,
-        over3,
-        jnp.concatenate([swap(over12), hand_over(over3)], 0),
-    )
-
-    saved = []
-    layer_out = None
-    for s, (normed_rows, back_rows) in enumerate(zip(norms, cots)):
-        if s == 0:
-            pre = jnp.dot(normed_rows[rows:], up_weight, preferred_element_type=jnp.float32)
-            pre = jnp.concatenate([own_pre, pre], 0)
-        else:
-            pre = jnp.dot(normed_rows, up_weight, preferred_element_type=jnp.float32)
-        hidden = jax.nn.gelu(pre).astype(bf16)
-        if s == 0:
-            partial_out = jnp.dot(hidden, down_weight, preferred_element_type=jnp.float32)
-            partial_out = partial_out.astype(bf16)
-            mine, theirs = (
-                lax.dynamic_slice(partial_out, (0, member("col", j) * half), (2 * rows, half)) for j in (0, 1)
-            )
-            both = mine.astype(jnp.float32) + swap(theirs).astype(jnp.float32)
-            rest = lax.ppermute(both[rows:].astype(bf16), "grp", [(0, 1), (1, 0)])
-            layer_out = (stream + both[:rows] + rest.astype(jnp.float32)).astype(bf16)
-        back_hidden = lax.dot_general(
-            back_rows, down_weight, (((1,), (1,)), ((), ())), preferred_element_type=jnp.float32
+    swap12, swap3x = swap(norm12), swap(norm3x)
+    swap_over, handed = swap(over12), hand_over(over3)
+
+    def pair(choices, blocks, shares=()):
+        made = jax.ShapeDtypeStruct((2 * rows, width), bf16)
+        return call(
+            functools.partial(feed_forward, choices, bool(shares)),
+            [made] * 4 + [jax.ShapeDtypeStruct((2 * rows, half), t) for t in shares],
+            0,
+            blocks + [up_weight, down_weight],
         )
-        _, gelu_back = jax.vjp(jax.nn.gelu, pre)
-        back_pre = gelu_back(back_hidden)[0].astype(bf16)
-        saved.append([normed_rows, back_pre, hidden, back_rows])
+
+    *group, mine, theirs = pair(
+        (1, 2), [normed, swap3x, norm3x, cot, cot_swap3x, cot3x], (jnp.float32, bf16)
+    )
+    near = pair((1, 1), [norm12, swap12, cot12, cot_swap12])
+    both = mine + swap(theirs).astype(jnp.float32)
+    rest = lax.ppermute(both[rows:].astype(bf16), "grp", [(0, 1), (1, 0)])
+    layer_out = (stream + both[:rows] + rest.astype(jnp.float32)).astype(bf16)
     panel = up_weight.shape[1]
     grads = (
         jax.ShapeDtypeStruct((width, panel), jnp.float32),
         jax.ShapeDtypeStruct((panel, width), jnp.float32),
     )
-    early, last = saved[0] + saved[1], saved[2] + saved[3]
-    flops = 8 * 2 * rows * panel * width
-    sums = call(add_products, grads, 0, early, flops)
+    sums = call(add_products, grads, 0, list(group) + list(near))
+    over = pair((1, 1), [over12, swap_over, cot_over12, cot_swap_over])
+    third = pair(
+        (2, 2),
+        [after(norm3x, sums[0]), swap3x, over3, handed]
+        + [cot3x, cot_swap3x, cot_over3, cot_handed],
+    )
+    last = list(over) + list(third)
     up_grad, down_grad = pl.pallas_call(
         finish_products,
         out_shape=grads,
@@ -452,9 +469,7 @@
             pltpu.VMEM((4, TILE, width), jnp.float32),
             pltpu.SemaphoreType.DMA((4,)),
         ],
-        cost_estimate=pl.CostEstimate(
-            flops=flops, bytes_accessed=16 * panel * width, transcendentals=0
-        ),
+        cost_estimate=SMALL,
         compiler_params=pltpu.CompilerParams(vmem_limit_bytes=16 * 2**20),
     )(*sums, *last)
     return (layer_out, up_grad, down_grad)

time: 75 us -> 69.4 us (0.925)
  matrix products: 10.3 us -> 0 us
  waiting for transfers between devices: 7.92 us -> 16.5 us
  Pallas kernels: 10.3 us -> 17.8 us
  starting transfers between devices: 34 us -> 28.7 us
  other arithmetic: 4.43 us -> 0.78 us
  local copies, waits for them, and re-layouts: 5.83 us -> 3.71 us
    ppermute x8, waiting for transfers between devices: 3.19 us -> 16.2 us  [send(): return lax.ppermute(x, ('patch', 'grp', 'col'), pairs)]
    dot_general x10 -> x0, matrix products: 10.3 us -> none  [the longest x4 5.48 us: gather_plan(): lax.dot_general(back_rows, down_weight, (((1,), (1,)), ((), ())), preferr...]
    ppermute x6 -> x7, starting transfers between devices: 9.91 us -> 2.33 us  [swap(): return lax.ppermute(x, 'col', [(0, 1), (1, 0)])]
    pallas_call x4 -> x9, Pallas kernels: 5.98 us -> 13.5 us  [call(): pl.pallas_call(kernel, out_shape=out_shape, in_specs=[pl.BlockSpec(memory...]
    ppermute x5 -> x6, waiting for transfers between devices: 3.84 us -> 0.25 us  [others(): lax.ppermute(x, axis, [(i, i ^ k) for i in range(n)])]
    concatenate x6 -> x0, other arithmetic: 2.2 us -> none  [the longest x1 1.07 us: gather_plan(): late = swap(jnp.concatenate([cot3x, over12], 0))]
    unnamed x17 -> x14, local copies, waits for them, and re-layouts: 5.73 us -> 3.69 us
    select_n x4 -> x0, other arithmetic: 1.11 us -> none  [the longest x2 1.05 us: pairs_of(): jnp.where(first, by3x, swap3x)]
  transfers between devices with their start and end apart: 22 -> 24, of which waited for: 6 -> 5; matrix products, arithmetic and copies ran while one was open for 22% -> 0% of each run, Pallas kernels for 14% -> 26%
where the time goes in v6:
time: 69.4 us; the launch traced here: 69.1 us
  starting transfers between devices  28.7 us (41%)
  Pallas kernels  17.8 us (26%)
  waiting for transfers between devices  16.5 us (24%)
  local copies, waits for them, and re-layouts  3.71 us (5%)
  between operations  1.57 us (2%)
  other arithmetic  0.78 us (1%)
    ppermute x8, starting transfers between devices, send(): return lax.ppermute(x, ('patch', 'grp', 'col'), pairs)  16.8 us
    ppermute x8, waiting for transfers between devices, send(): return lax.ppermute(x, ('patch', 'grp', 'col'), pairs)  16.2 us
    pallas_call x9, Pallas kernels, call(): pl.pallas_call(kernel, out_shape=out_shape, in_specs=[pl.BlockSpec(memory...  13.5 us
    pallas_call x1, Pallas kernels, gather_plan(): pl.pallas_call(finish_products, out_shape=grads, in_specs=[pl.BlockSpec(m...  4.31 us
    ppermute x6, starting transfers between devices, others(): lax.ppermute(x, axis, [(i, i ^ k) for i in range(n)])  4.21 us
    ppermute x2, starting transfers between devices, hand_over(): return lax.ppermute(x, 'col', [(0, 1)])  3.87 us
    unnamed x14, local copies, waits for them, and re-layouts  3.69 us
    ppermute x7, starting transfers between devices, swap(): return lax.ppermute(x, 'col', [(0, 1), (1, 0)])  2.33 us
  transfers between devices with their start and end apart: 24, of which 5 were waited for; matrix products, arithmetic and copies ran while one was open for 0% of the time, Pallas kernels for 26%

profile of v6, /device:TPU:0, one launch (start us, length us, event | category | flops | bytes accessed | tf_op | source)
XLA Modules:
  0.0 69.1 jit_solution(16838099896343317160)
XLA Ops:
  0.7 0.5 collective-permute-start.5
  1.2 0.1 collective-permute-start
  1.2 2.9 %collective-permute-start.1 = (bf16[128,512]{1,0:T(8,128)(2,1)}, bf16[128,512]{1,0:T(8,128)(2,1)S(1)}, u32[]{:S(2)}, u32[]{:S(2)}) collective-permute-start(bf16[128,512]{1,0:T(8,128)(2,1)} %refs_0_.4), channel_id=1, source_target_pairs={{0,2},{2,0},{1,3},{3,1},{4,6},{6,4},{5,7},{7,5},{8,10},{10,8},{9,1... | collective-permute-start | bytes 393224 | tf_op jit(solution)/shard_map/ppermute | solution.py:129
  4.2 0.0 collective-permute-start.2
  4.2 0.0 collective-permute-done.refs_1_
  4.2 0.9 %copy-done.4 = bf16[128,512]{1,0:T(8,128)(2,1)S(1)} copy-done((bf16[128,512]{1,0:T(8,128)(2,1)S(1)}, bf16[128,512]{1,0:T(8,128)(2,1)}, u32[]{:S(2)}) %copy-start.4) | copy-done | bytes 131096
  5.1 2.7 %collective-permute-start.4 = (bf16[128,1024]{1,0:T(8,128)(2,1)S(1)}, bf16[128,1024]{1,0:T(8,128)(2,1)S(1)}, u32[]{:S(2)}, u32[]{:S(2)}) collective-permute-start(bf16[128,1024]{1,0:T(8,128)(2,1)S(1)} %shard_map.130.refs_3_), channel_id=1, source_target_pairs={{0,4},{1,9},{2,6},{3,11},{4,0},{5,13},{6,2},{7,15},{8,12},{9,1},{1... | collective-permute-start | bytes 786440 | tf_op jit(solution)/shard_map/ppermute | solution.py:352
  8.4 0.0 copy-start.2
  8.5 1.2 %copy-done.2 = bf16[512,1024]{1,0:T(8,128)(2,1)S(1)} copy-done((bf16[512,1024]{1,0:T(8,128)(2,1)S(1)}, bf16[512,1024]{1,0:T(8,128)(2,1)}, u32[]{:S(2)}) %copy-start.2) | copy-done | bytes 1048600
  9.7 1.0 %shard_map.131 = (bf16[512,1024]{1,0:T(8,128)(2,1)S(1)}, bf16[128,512]{1,0:T(8,128)(2,1)S(1)}) custom-call(bf16[512,1024]{1,0:T(8,128)(2,1)S(1)} %copy-done.2, bf16[128,512]{1,0:T(8,128)(2,1)} %refs_1_.1), custom_call_target="tpu_custom_call" | custom-call | flops 1 | bytes 1 | tf_op jit(solution)/shard_map/pallas_call | solution.py:332
  10.7 0.0 collective-permute-done.1.refs_1_
  10.7 0.0 copy-start.5
  10.7 0.2 collective-permute-done.2.refs_3_
  10.9 0.4 copy-done.5
  11.3 0.2 copy-done.6
  11.6 2.7 %shard_map.132.refs_0_ = bf16[144,512]{1,0:T(8,128)(2,1)} custom-call(s32[1,2]{1,0:T(1,128)} %ids_ref.1, s32[1]{0:T(128)S(6)} %copy.14.count_ref, f32[1,512]{1,0:T(1,128)} %bitcast.1, bf16[128,512]{1,0:T(8,128)(2,1)} %query_ref, bf16[128,512]{1,0:T(8,128)(2,1)} %refs_0_.4, bf16[128,512]{1,0:T(8,128)(2,1)} %copy-done.5, bf16[128,512]{1,0:T(8,128)(2,1)} %refs_2_.1, ...), custom_call_target="tpu_custom_call" | custom-call | flops 1 | bytes 1 | tf_op jit(solution)/shard_map/pallas_call | solution.py:332
  14.3 0.7 collective-permute-start.3
  14.9 3.7 %collective-permute-start.12 = (bf16[128,1024]{1,0:T(8,128)(2,1)S(1)}, bf16[128,1024]{1,0:T(8,128)(2,1)S(1)}, u32[]{:S(2)}, u32[]{:S(2)}) collective-permute-start(bf16[128,1024]{1,0:T(8,128)(2,1)S(1)} %shard_map.130.refs_3_), channel_id=1, source_target_pairs={{0,12},{1,3},{2,14},{3,1},{4,8},{5,7},{6,10},{7,5},{8,4},{9,11},{1... | collective-permute-start | bytes 786440 | tf_op jit(solution)/shard_map/ppermute | solution.py:352
  18.6 0.0 collective-permute-done.4.refs_2_
  18.6 0.0 collective-permute-done.5.refs_3_
  18.7 0.9 %copy-done.3 = bf16[144,512]{1,0:T(8,128)(2,1)S(1)} copy-done((bf16[144,512]{1,0:T(8,128)(2,1)S(1)}, bf16[144,512]{1,0:T(8,128)(2,1)}, u32[]{:S(2)}) %copy-start.3) | copy-done | bytes 147480
  19.6 0.7 %shard_map.133 = (f32[128,512]{1,0:T(8,128)S(1)}, bf16[128,1024]{1,0:T(8,128)(2,1)S(1)}) custom-call(bf16[144,512]{1,0:T(8,128)(2,1)S(1)} %copy-done.3, bf16[144,512]{1,0:T(8,128)(2,1)S(1)} %collective-permute-done.3.refs_1_, bf16[512,1024]{1,0:T(8,128)(2,1)S(1)} %get-tuple-element.40.refs_2_, bf16[512,1024]{1,0:T(8,128)(2,1)S(1)} %collective-permute-done.5.refs_3_, ...), custom_call_target="tpu_custom_call" | custom-call | flops 1 | bytes 1 | tf_op jit(solution)/shard_map/pallas_call | solution.py:332
  20.3 0.1 collective-permute-start.10
  20.4 1.6 %collective-permute-start.9 = (bf16[128,1024]{1,0:T(8,128)(2,1)S(1)}, bf16[128,1024]{1,0:T(8,128)(2,1)S(1)}, u32[]{:S(2)}, u32[]{:S(2)}) collective-permute-start(bf16[128,1024]{1,0:T(8,128)(2,1)S(1)} %collective-permute-done.4.refs_2_), channel_id=1, source_target_pairs={{0,2},{1,3},{2,0},{3,1},{4,6},{5,7},{6,4},{7,5},{8,10},{9,11},{10,... | collective-permute-start | bytes 786440 | tf_op jit(solution)/shard_map/ppermute | solution.py:352
  21.9 1.5 %collective-permute-start.8 = (bf16[128,1024]{1,0:T(8,128)(2,1)S(1)}, bf16[128,1024]{1,0:T(8,128)(2,1)S(1)}, u32[]{:S(2)}, u32[]{:S(2)}) collective-permute-start(bf16[128,1024]{1,0:T(8,128)(2,1)S(1)} %get-tuple-element.43.refs_0_), channel_id=1, source_target_pairs={{0,12},{1,3},{2,14},{3,1},{4,8},{5,7},{6,10},{7,5},{8,4},{9,11},{1... | collective-permute-start | bytes 786440 | tf_op jit(solution)/shard_map/ppermute | solution.py:352
  23.4 6.1 %collective-permute-done.9.refs_2_ = bf16[128,1024]{1,0:T(8,128)(2,1)S(1)} collective-permute-done((bf16[128,1024]{1,0:T(8,128)(2,1)S(1)}, bf16[128,1024]{1,0:T(8,128)(2,1)S(1)}, u32[]{:S(2)}, u32[]{:S(2)}) %collective-permute-start.9) | collective-permute-done | bytes 262176 | tf_op jit(solution)/shard_map/ppermute | solution.py:352
  29.6 1.1 %collective-permute-done.8.refs_2_.refs_0_ = bf16[128,1024]{1,0:T(8,128)(2,1)S(1)} collective-permute-done((bf16[128,1024]{1,0:T(8,128)(2,1)S(1)}, bf16[128,1024]{1,0:T(8,128)(2,1)S(1)}, u32[]{:S(2)}, u32[]{:S(2)}) %collective-permute-start.8) | collective-permute-done | bytes 262176 | tf_op jit(solution)/shard_map/ppermute | solution.py:352
  30.7 3.9 %collective-permute-done.7.refs_0_ = bf16[128,1024]{1,0:T(8,128)(2,1)S(1)} collective-permute-done((bf16[128,1024]{1,0:T(8,128)(2,1)S(1)}, bf16[128,1024]{1,0:T(8,128)(2,1)S(1)}, u32[]{:S(2)}, u32[]{:S(2)}) %collective-permute-start.7) | collective-permute-done | bytes 262176 | tf_op jit(solution)/shard_map/ppermute | solution.py:352
  34.5 1.5 %collective-permute-start.11 = (bf16[128,1024]{1,0:T(8,128)(2,1)S(1)}, bf16[128,1024]{1,0:T(8,128)(2,1)S(1)}, u32[]{:S(2)}, u32[]{:S(2)}) collective-permute-start(bf16[128,1024]{1,0:T(8,128)(2,1)S(1)} %collective-permute-done.8.refs_2_.refs_0_), channel_id=1, source_target_pairs={{0,1},{1,0},{2,3},{3,2},{4,5},{5,4},{6,7},{7,6},{8,9},{9,8},{10,11... | collective-permute-start | bytes 786440 | tf_op jit(solution)/shard_map/ppermute | solution.py:356
  36.1 3.4 %collective-permute-start.22 = (bf16[128,1024]{1,0:T(8,128)(2,1)S(1)}, bf16[128,1024]{1,0:T(8,128)(2,1)S(1)}, u32[]{:S(2)}, u32[]{:S(2)}) collective-permute-start(bf16[128,1024]{1,0:T(8,128)(2,1)S(1)} %collective-permute-done.12.refs_5_.refs_4_), channel_id=1, source_target_pairs={{0,2},{2,0},{4,6},{6,4},{8,10},{10,8},{12,14},{14,12},{16,18},{18,... | collective-permute-start | bytes 786440 | tf_op jit(solution)/shard_map/ppermute | solution.py:352
  39.5 2.5 %collective-permute-start.20 = (bf16[128,1024]{1,0:T(8,128)(2,1)S(1)}, bf16[128,1024]{1,0:T(8,128)(2,1)S(1)}, u32[]{:S(2)}, u32[]{:S(2)}) collective-permute-start(bf16[128,1024]{1,0:T(8,128)(2,1)S(1)} %collective-permute-done.8.refs_2_.refs_0_), channel_id=1, source_target_pairs={{0,2},{2,0},{4,6},{6,4},{8,10},{10,8},{12,14},{14,12},{16,18},{18,... | collective-permute-start | bytes 786440 | tf_op jit(solution)/shard_map/ppermute | solution.py:352
  41.9 1.5 %collective-permute-start.17 = (bf16[128,1024]{1,0:T(8,128)(2,1)S(1)}, bf16[128,1024]{1,0:T(8,128)(2,1)S(1)}, u32[]{:S(2)}, u32[]{:S(2)}) collective-permute-start(bf16[128,1024]{1,0:T(8,128)(2,1)S(1)} %collective-permute-done.7.refs_0_), channel_id=1, source_target_pairs={{0,2},{1,3},{2,0},{3,1},{4,6},{5,7},{6,4},{7,5},{8,10},{9,11},{10,... | collective-permute-start | bytes 786440 | tf_op jit(solution)/shard_map/ppermute | solution.py:352
  43.5 2.1 %shard_map.134 = (bf16[256,1024]{1,0:T(8,128)(2,1)S(1)}, bf16[256,1024]{1,0:T(8,128)(2,1)S(1)}, bf16[256,1024]{1,0:T(8,128)(2,1)S(1)}, bf16[256,1024]{1,0:T(8,12...) custom-call(bf16[128,1024]{1,0:T(8,128)(2,1)S(1)} %get-tuple-element.43.refs_0_, ...), custom_call_target="tpu_custom_call" | custom-call | flops 1 | bytes 1 | tf_op jit(solution)/shard_map/pallas_call | solution.py:332
  45.6 0.1 collective-permute-start.14
  45.7 0.5 collective-permute-start.16
  46.2 0.1 collective-permute-start.19
  46.3 5.1 %collective-permute-done.17.refs_0_ = bf16[128,1024]{1,0:T(8,128)(2,1)S(1)} collective-permute-done((bf16[128,1024]{1,0:T(8,128)(2,1)S(1)}, bf16[128,1024]{1,0:T(8,128)(2,1)S(1)}, u32[]{:S(2)}, u32[]{:S(2)}) %collective-permute-start.17) | collective-permute-done | bytes 262176 | tf_op jit(solution)/shard_map/ppermute | solution.py:352
  51.3 1.3 %collective-permute-start.23 = (bf16[128,1024]{1,0:T(8,128)(2,1)S(1)}, bf16[128,1024]{1,0:T(8,128)(2,1)S(1)}, u32[]{:S(2)}, u32[]{:S(2)}) collective-permute-start(bf16[128,1024]{1,0:T(8,128)(2,1)S(1)} %collective-permute-done.22.refs_6_), channel_id=1, source_target_pairs={{0,1},{2,3},{4,5},{6,7},{8,9},{10,11},{12,13},{14,15},{16,17},{18,... | collective-permute-start | bytes 786440 | tf_op jit(solution)/shard_map/ppermute | solution.py:360
  52.6 0.1 collective-permute-start.18
  52.7 2.6 %collective-permute-start.21 = (bf16[128,1024]{1,0:T(8,128)(2,1)S(1)}, bf16[128,1024]{1,0:T(8,128)(2,1)S(1)}, u32[]{:S(2)}, u32[]{:S(2)}) collective-permute-start(bf16[128,1024]{1,0:T(8,128)(2,1)S(1)} %collective-permute-done.20.refs_2_), channel_id=1, source_target_pairs={{0,1},{2,3},{4,5},{6,7},{8,9},{10,11},{12,13},{14,15},{16,17},{18,... | collective-permute-start | bytes 786440 | tf_op jit(solution)/shard_map/ppermute | solution.py:360
  55.3 0.1 convert_add_fusion
  55.4 1.5 %collective-permute-start.15 = (bf16[128,512]{1,0:T(8,128)(2,1)S(1)}, bf16[128,512]{1,0:T(8,128)(2,1)S(1)}, u32[]{:S(2)}, u32[]{:S(2)}) collective-permute-start(bf16[128,512]{1,0:T(8,128)(2,1)S(1)} %slice.17), channel_id=1, source_target_pairs={{0,2},{2,0},{1,3},{3,1},{4,6},{6,4},{5,7},{7,5},{8,10},{10,8},{9,1... | collective-permute-start | bytes 393224 | tf_op jit(solution)/shard_map/ppermute | solution.py:448
  57.0 1.5 %shard_map.135 = (bf16[256,1024]{1,0:T(8,128)(2,1)S(1)}, bf16[256,1024]{1,0:T(8,128)(2,1)S(1)}, bf16[256,1024]{1,0:T(8,128)(2,1)S(1)}, bf16[256,1024]{1,0:T(8,128)(2,1)S(1)}) custom-call(bf16[128,1024]{1,0:T(8,128)(2,1)S(1)} %collective-permute-done.7.refs_0_, bf16[128,1024]{1,0:T(8,128)(2,1)S(1)} %collective-permute-done.16.refs_1_, ...), custom_call_target="tpu_custom_call" | custom-call | flops 1 | bytes 1 | tf_op jit(solution)/shard_map/pallas_call | solution.py:332
  58.5 2.4 %shard_map.136 = (f32[1024,1024]{1,0:T(8,128)S(1)}, f32[1024,1024]{1,0:T(8,128)S(1)}) custom-call(bf16[256,1024]{1,0:T(8,128)(2,1)S(1)} %get-tuple-element.49.refs_0_, bf16[256,1024]{1,0:T(8,128)(2,1)S(1)} %get-tuple-element.50.refs_1_, bf16[256,1024]{1,0:T(8,128)(2,1)S(1)} %get-tuple-element.51.refs_2_, bf16[256,1024]{1,0:T(8,128)(2,1)S(1)} %get-tuple-element.52.refs_3_, ...), custom_call_target="tpu_custom_call" | custom-call | flops 1 | bytes 1 | tf_op jit(solution)/shard_map/pallas_call | solution.py:332
  60.9 1.5 %shard_map.137 = (bf16[256,1024]{1,0:T(8,128)(2,1)S(1)}, bf16[256,1024]{1,0:T(8,128)(2,1)S(1)}, bf16[256,1024]{1,0:T(8,128)(2,1)S(1)}, bf16[256,1024]{1,0:T(8,128)(2,1)S(1)}) custom-call(bf16[128,1024]{1,0:T(8,128)(2,1)S(1)} %collective-permute-done.17.refs_0_, bf16[128,1024]{1,0:T(8,128)(2,1)S(1)} %collective-permute-done.18.refs_1_, ...), custom_call_target="tpu_custom_call" | custom-call | flops 1 | bytes 1 | tf_op jit(solution)/shard_map/pallas_call | solution.py:332
  62.5 1.6 %shard_map.138 = (bf16[256,1024]{1,0:T(8,128)(2,1)S(1)}, bf16[256,1024]{1,0:T(8,128)(2,1)S(1)}, bf16[256,1024]{1,0:T(8,128)(2,1)S(1)}, bf16[256,1024]{1,0:T(8,128)(2,1)S(1)}) custom-call(bf16[128,1024]{1,0:T(8,128)(2,1)S(1)} %collective-permute-done.8.refs_2_.refs_0_, bf16[128,1024]{1,0:T(8,128)(2,1)S(1)} %collective-permute-done.11.refs_1_, ...), custom_call_target="tpu_custom_call" | custom-call | flops 1 | bytes 1 | tf_op jit(solution)/shard_map/pallas_call | solution.py:332
  64.1 4.3 %shard_map.139 = (f32[1024,1024]{1,0:T(8,128)}, f32[1024,1024]{1,0:T(8,128)}) custom-call(f32[1024,1024]{1,0:T(8,128)S(1)} %get-tuple-element.58.refs_0_, f32[1024,1024]{1,0:T(8,128)S(1)} %get-tuple-element.59.refs_1_, bf16[256,1024]{1,0:T(8,128)(2,1)S(1)} %get-tuple-element.60.refs_2_, bf16[256,1024]{1,0:T(8,128)(2,1)S(1)} %get-tuple-element.61.refs_3_, ...), custom_call_target="tpu_custom_call" | custom-call | flops 1 | bytes 1 | tf_op jit(solution)/shard_map/pallas_call | solution.py:463
  68.4 0.7 %fusion.1 = bf16[128,512]{1,0:T(8,128)(2,1)} fusion(f32[128,512]{1,0:T(8,128)S(1)} %get-tuple-element.42, f32[256,512]{1,0:T(8,128)S(1)} %convert_add_fusion, bf16[128,512]{1,0:T(8,128)(2,1)S(1)} %collective-permute-done.15), kind=kLoop, calls=%fused_computation.4 | loop fusion | flops 262144 | bytes 786432 | tf_op jit(solution)/shard_map/convert_element_type | solution.py:449
  (27 shorter events, 0.1 us)
Async XLA Ops:
  0.6 42.9 %copy-start.1 = (bf16[1024,1024]{1,0:T(8,128)(2,1)S(1)}, bf16[1024,1024]{1,0:T(8,128)(2,1)}, u32[]{:S(2)}) copy-start(bf16[1024,1024]{1,0:T(8,128)(2,1)} %refs_9_.1) | copy-start | bytes 6291460
  0.6 42.8 %copy-start = (bf16[1024,1024]{1,0:T(8,128)(2,1)S(1)}, bf16[1024,1024]{1,0:T(8,128)(2,1)}, u32[]{:S(2)}) copy-start(bf16[1024,1024]{1,0:T(8,128)(2,1)} %refs_8_.1) | copy-start | bytes 6291460
  0.7 18.0 %collective-permute-start.5 = (bf16[512,1024]{1,0:T(8,128)(2,1)}, bf16[512,1024]{1,0:T(8,128)(2,1)S(1)}, u32[]{:S(2)}, u32[]{:S(2)}) collective-permute-start(bf16[512,1024]{1,0:T(8,128)(2,1)} %refs_0_.3), channel_id=1, source_target_pairs={{0,1},{1,0},{2,3},{3,2},{4,5},{5,4},{6,7},{7,6},{8,9},{9,8},{10,11... | collective-permute-start | bytes 3145736 | tf_op jit(solution)/shard_map/ppermute | solution.py:129
  1.2 3.0 %collective-permute-start = (bf16[128,512]{1,0:T(8,128)(2,1)}, bf16[128,512]{1,0:T(8,128)(2,1)S(1)}, u32[]{:S(2)}, u32[]{:S(2)}) collective-permute-start(bf16[128,512]{1,0:T(8,128)(2,1)} %refs_0_.2), channel_id=1, source_target_pairs={{0,1},{1,0},{2,3},{3,2},{4,5},{5,4},{6,7},{7,6},{8,9},{9,8},{10,11... | collective-permute-start | bytes 393224 | tf_op jit(solution)/shard_map/ppermute | solution.py:129
  1.2 9.4 %collective-permute-start.1 = (bf16[128,512]{1,0:T(8,128)(2,1)}, bf16[128,512]{1,0:T(8,128)(2,1)S(1)}, u32[]{:S(2)}, u32[]{:S(2)}) collective-permute-start(bf16[128,512]{1,0:T(8,128)(2,1)} %refs_0_.4), channel_id=1, source_target_pairs={{0,2},{2,0},{1,3},{3,1},{4,6},{6,4},{5,7},{7,5},{8,10},{10,8},{9,1... | collective-permute-start | bytes 393224 | tf_op jit(solution)/shard_map/ppermute | solution.py:129
  4.2 6.8 %collective-permute-start.2 = (bf16[128,512]{1,0:T(8,128)(2,1)}, bf16[128,512]{1,0:T(8,128)(2,1)S(1)}, u32[]{:S(2)}, u32[]{:S(2)}) collective-permute-start(bf16[128,512]{1,0:T(8,128)(2,1)} %refs_2_.1), channel_id=1, source_target_pairs={{0,2},{2,0},{1,3},{3,1},{4,6},{6,4},{5,7},{7,5},{8,10},{10,8},{9,1... | collective-permute-start | bytes 393224 | tf_op jit(solution)/shard_map/ppermute | solution.py:129
  4.2 0.9 %copy-start.4 = (bf16[128,512]{1,0:T(8,128)(2,1)S(1)}, bf16[128,512]{1,0:T(8,128)(2,1)}, u32[]{:S(2)}) copy-start(bf16[128,512]{1,0:T(8,128)(2,1)} %refs_0_.2) | copy-start | bytes 393220
  5.1 13.5 %collective-permute-start.4 = (bf16[128,1024]{1,0:T(8,128)(2,1)S(1)}, bf16[128,1024]{1,0:T(8,128)(2,1)S(1)}, u32[]{:S(2)}, u32[]{:S(2)}) collective-permute-start(bf16[128,1024]{1,0:T(8,128)(2,1)S(1)} %shard_map.130.refs_3_), channel_id=1, source_target_pairs={{0,4},{1,9},{2,6},{3,11},{4,0},{5,13},{6,2},{7,15},{8,12},{9,1},{1... | collective-permute-start | bytes 786440 | tf_op jit(solution)/shard_map/ppermute | solution.py:352
  8.4 1.2 %copy-start.2 = (bf16[512,1024]{1,0:T(8,128)(2,1)S(1)}, bf16[512,1024]{1,0:T(8,128)(2,1)}, u32[]{:S(2)}) copy-start(bf16[512,1024]{1,0:T(8,128)(2,1)} %refs_0_.3) | copy-start | bytes 3145732
  10.7 0.7 copy-start.5
  10.9 0.7 copy-start.6
  14.3 4.4 %collective-permute-start.3 = (bf16[144,512]{1,0:T(8,128)(2,1)}, bf16[144,512]{1,0:T(8,128)(2,1)S(1)}, u32[]{:S(2)}, u32[]{:S(2)}) collective-permute-start(bf16[144,512]{1,0:T(8,128)(2,1)} %shard_map.132.refs_0_), channel_id=1, source_target_pairs={{0,1},{1,0},{2,3},{3,2},{4,5},{5,4},{6,7},{7,6},{8,9},{9,8},{10,11... | collective-permute-start | bytes 442376 | tf_op jit(solution)/shard_map/ppermute | solution.py:129
  14.9 3.7 %collective-permute-start.6 = (bf16[128,512]{1,0:T(8,128)(2,1)}, bf16[128,512]{1,0:T(8,128)(2,1)S(1)}, u32[]{:S(2)}, u32[]{:S(2)}) collective-permute-start(bf16[128,512]{1,0:T(8,128)(2,1)} %refs_1_.1), channel_id=1, source_target_pairs={{0,1},{1,0},{2,3},{3,2},{4,5},{5,4},{6,7},{7,6},{8,9},{9,8},{10,11... | collective-permute-start | bytes 393224 | tf_op jit(solution)/shard_map/ppermute | solution.py:129
  14.9 8.5 %collective-permute-start.12 = (bf16[128,1024]{1,0:T(8,128)(2,1)S(1)}, bf16[128,1024]{1,0:T(8,128)(2,1)S(1)}, u32[]{:S(2)}, u32[]{:S(2)}) collective-permute-start(bf16[128,1024]{1,0:T(8,128)(2,1)S(1)} %shard_map.130.refs_3_), channel_id=1, source_target_pairs={{0,12},{1,3},{2,14},{3,1},{4,8},{5,7},{6,10},{7,5},{8,4},{9,11},{1... | collective-permute-start | bytes 786440 | tf_op jit(solution)/shard_map/ppermute | solution.py:352
  18.6 0.9 %copy-start.3 = (bf16[144,512]{1,0:T(8,128)(2,1)S(1)}, bf16[144,512]{1,0:T(8,128)(2,1)}, u32[]{:S(2)}) copy-start(bf16[144,512]{1,0:T(8,128)(2,1)} %shard_map.132.refs_0_) | copy-start | bytes 442372
  20.3 3.1 %collective-permute-start.10 = (bf16[128,1024]{1,0:T(8,128)(2,1)S(1)}, bf16[128,1024]{1,0:T(8,128)(2,1)S(1)}, u32[]{:S(2)}, u32[]{:S(2)}) collective-permute-start(bf16[128,1024]{1,0:T(8,128)(2,1)S(1)} %collective-permute-done.4.refs_2_), channel_id=1, source_target_pairs={{0,1},{1,0},{2,3},{3,2},{4,5},{5,4},{6,7},{7,6},{8,9},{9,8},{10,11... | collective-permute-start | bytes 786440 | tf_op jit(solution)/shard_map/ppermute | solution.py:356
  20.4 9.2 %collective-permute-start.9 = (bf16[128,1024]{1,0:T(8,128)(2,1)S(1)}, bf16[128,1024]{1,0:T(8,128)(2,1)S(1)}, u32[]{:S(2)}, u32[]{:S(2)}) collective-permute-start(bf16[128,1024]{1,0:T(8,128)(2,1)S(1)} %collective-permute-done.4.refs_2_), channel_id=1, source_target_pairs={{0,2},{1,3},{2,0},{3,1},{4,6},{5,7},{6,4},{7,5},{8,10},{9,11},{10,... | collective-permute-start | bytes 786440 | tf_op jit(solution)/shard_map/ppermute | solution.py:352
  21.9 8.7 %collective-permute-start.8 = (bf16[128,1024]{1,0:T(8,128)(2,1)S(1)}, bf16[128,1024]{1,0:T(8,128)(2,1)S(1)}, u32[]{:S(2)}, u32[]{:S(2)}) collective-permute-start(bf16[128,1024]{1,0:T(8,128)(2,1)S(1)} %get-tuple-element.43.refs_0_), channel_id=1, source_target_pairs={{0,12},{1,3},{2,14},{3,1},{4,8},{5,7},{6,10},{7,5},{8,4},{9,11},{1... | collective-permute-start | bytes 786440 | tf_op jit(solution)/shard_map/ppermute | solution.py:352
  23.4 11.1 %collective-permute-start.7 = (bf16[128,1024]{1,0:T(8,128)(2,1)S(1)}, bf16[128,1024]{1,0:T(8,128)(2,1)S(1)}, u32[]{:S(2)}, u32[]{:S(2)}) collective-permute-start(bf16[128,1024]{1,0:T(8,128)(2,1)S(1)} %get-tuple-element.43.refs_0_), channel_id=1, source_target_pairs={{0,4},{1,9},{2,6},{3,11},{4,0},{5,13},{6,2},{7,15},{8,12},{9,1},{1... | collective-permute-start | bytes 786440 | tf_op jit(solution)/shard_map/ppermute | solution.py:352
  23.4 20.1 %collective-permute-start.13 = (bf16[128,1024]{1,0:T(8,128)(2,1)S(1)}, bf16[128,1024]{1,0:T(8,128)(2,1)S(1)}, u32[]{:S(2)}, u32[]{:S(2)}) collective-permute-start(bf16[128,1024]{1,0:T(8,128)(2,1)S(1)} %collective-permute-done.12.refs_5_.refs_4_), channel_id=1, source_target_pairs={{0,1},{1,0},{2,3},{3,2},{4,5},{5,4},{6,7},{7,6},{8,9},{9,8},{10,11... | collective-permute-start | bytes 786440 | tf_op jit(solution)/shard_map/ppermute | solution.py:356
  34.5 8.9 %collective-permute-start.11 = (bf16[128,1024]{1,0:T(8,128)(2,1)S(1)}, bf16[128,1024]{1,0:T(8,128)(2,1)S(1)}, u32[]{:S(2)}, u32[]{:S(2)}) collective-permute-start(bf16[128,1024]{1,0:T(8,128)(2,1)S(1)} %collective-permute-done.8.refs_2_.refs_0_), channel_id=1, source_target_pairs={{0,1},{1,0},{2,3},{3,2},{4,5},{5,4},{6,7},{7,6},{8,9},{9,8},{10,11... | collective-permute-start | bytes 786440 | tf_op jit(solution)/shard_map/ppermute | solution.py:356
  36.1 10.1 %collective-permute-start.22 = (bf16[128,1024]{1,0:T(8,128)(2,1)S(1)}, bf16[128,1024]{1,0:T(8,128)(2,1)S(1)}, u32[]{:S(2)}, u32[]{:S(2)}) collective-permute-start(bf16[128,1024]{1,0:T(8,128)(2,1)S(1)} %collective-permute-done.12.refs_5_.refs_4_), channel_id=1, source_target_pairs={{0,2},{2,0},{4,6},{6,4},{8,10},{10,8},{12,14},{14,12},{16,18},{18,... | collective-permute-start | bytes 786440 | tf_op jit(solution)/shard_map/ppermute | solution.py:352
  39.5 13.2 %collective-permute-start.20 = (bf16[128,1024]{1,0:T(8,128)(2,1)S(1)}, bf16[128,1024]{1,0:T(8,128)(2,1)S(1)}, u32[]{:S(2)}, u32[]{:S(2)}) collective-permute-start(bf16[128,1024]{1,0:T(8,128)(2,1)S(1)} %collective-permute-done.8.refs_2_.refs_0_), channel_id=1, source_target_pairs={{0,2},{2,0},{4,6},{6,4},{8,10},{10,8},{12,14},{14,12},{16,18},{18,... | collective-permute-start | bytes 786440 | tf_op jit(solution)/shard_map/ppermute | solution.py:352
  41.9 9.4 %collective-permute-start.17 = (bf16[128,1024]{1,0:T(8,128)(2,1)S(1)}, bf16[128,1024]{1,0:T(8,128)(2,1)S(1)}, u32[]{:S(2)}, u32[]{:S(2)}) collective-permute-start(bf16[128,1024]{1,0:T(8,128)(2,1)S(1)} %collective-permute-done.7.refs_0_), channel_id=1, source_target_pairs={{0,2},{1,3},{2,0},{3,1},{4,6},{5,7},{6,4},{7,5},{8,10},{9,11},{10,... | collective-permute-start | bytes 786440 | tf_op jit(solution)/shard_map/ppermute | solution.py:352
  45.6 7.1 %collective-permute-start.14 = (bf16[256,512]{1,0:T(8,128)(2,1)S(1)}, bf16[256,512]{1,0:T(8,128)(2,1)S(1)}, u32[]{:S(2)}, u32[]{:S(2)}) collective-permute-start(bf16[256,512]{1,0:T(8,128)(2,1)S(1)} %get-tuple-element.48), channel_id=1, source_target_pairs={{0,1},{1,0},{2,3},{3,2},{4,5},{5,4},{6,7},{7,6},{8,9},{9,8},{10,11... | collective-permute-start | bytes 786440 | tf_op jit(solution)/shard_map/ppermute | solution.py:356
  45.7 9.8 %collective-permute-start.16 = (bf16[128,1024]{1,0:T(8,128)(2,1)S(1)}, bf16[128,1024]{1,0:T(8,128)(2,1)S(1)}, u32[]{:S(2)}, u32[]{:S(2)}) collective-permute-start(bf16[128,1024]{1,0:T(8,128)(2,1)S(1)} %collective-permute-done.7.refs_0_), channel_id=1, source_target_pairs={{0,1},{1,0},{2,3},{3,2},{4,5},{5,4},{6,7},{7,6},{8,9},{9,8},{10,11... | collective-permute-start | bytes 786440 | tf_op jit(solution)/shard_map/ppermute | solution.py:356
  46.2 14.7 %collective-permute-start.19 = (bf16[128,1024]{1,0:T(8,128)(2,1)S(1)}, bf16[128,1024]{1,0:T(8,128)(2,1)S(1)}, u32[]{:S(2)}, u32[]{:S(2)}) collective-permute-start(bf16[128,1024]{1,0:T(8,128)(2,1)S(1)} %collective-permute-done.9.refs_2_), channel_id=1, source_target_pairs={{0,1},{1,0},{2,3},{3,2},{4,5},{5,4},{6,7},{7,6},{8,9},{9,8},{10,11... | collective-permute-start | bytes 786440 | tf_op jit(solution)/shard_map/ppermute | solution.py:356
  51.3 11.1 %collective-permute-start.23 = (bf16[128,1024]{1,0:T(8,128)(2,1)S(1)}, bf16[128,1024]{1,0:T(8,128)(2,1)S(1)}, u32[]{:S(2)}, u32[]{:S(2)}) collective-permute-start(bf16[128,1024]{1,0:T(8,128)(2,1)S(1)} %collective-permute-done.22.refs_6_), channel_id=1, source_target_pairs={{0,1},{2,3},{4,5},{6,7},{8,9},{10,11},{12,13},{14,15},{16,17},{18,... | collective-permute-start | bytes 786440 | tf_op jit(solution)/shard_map/ppermute | solution.py:360
  52.6 8.3 %collective-permute-start.18 = (bf16[128,1024]{1,0:T(8,128)(2,1)S(1)}, bf16[128,1024]{1,0:T(8,128)(2,1)S(1)}, u32[]{:S(2)}, u32[]{:S(2)}) collective-permute-start(bf16[128,1024]{1,0:T(8,128)(2,1)S(1)} %collective-permute-done.17.refs_0_), channel_id=1, source_target_pairs={{0,1},{1,0},{2,3},{3,2},{4,5},{5,4},{6,7},{7,6},{8,9},{9,8},{10,11... | collective-permute-start | bytes 786440 | tf_op jit(solution)/shard_map/ppermute | solution.py:356
  52.7 9.7 %collective-permute-start.21 = (bf16[128,1024]{1,0:T(8,128)(2,1)S(1)}, bf16[128,1024]{1,0:T(8,128)(2,1)S(1)}, u32[]{:S(2)}, u32[]{:S(2)}) collective-permute-start(bf16[128,1024]{1,0:T(8,128)(2,1)S(1)} %collective-permute-done.20.refs_2_), channel_id=1, source_target_pairs={{0,1},{2,3},{4,5},{6,7},{8,9},{10,11},{12,13},{14,15},{16,17},{18,... | collective-permute-start | bytes 786440 | tf_op jit(solution)/shard_map/ppermute | solution.py:360
  55.4 12.9 %collective-permute-start.15 = (bf16[128,512]{1,0:T(8,128)(2,1)S(1)}, bf16[128,512]{1,0:T(8,128)(2,1)S(1)}, u32[]{:S(2)}, u32[]{:S(2)}) collective-permute-start(bf16[128,512]{1,0:T(8,128)(2,1)S(1)} %slice.17), channel_id=1, source_target_pairs={{0,2},{2,0},{1,3},{3,1},{4,6},{6,4},{5,7},{7,5},{8,10},{10,8},{9,1... | collective-permute-start | bytes 393224 | tf_op jit(solution)/shard_map/ppermute | solution.py:448

commit v7 on v6

--- a/solution.py
+++ b/solution.py
@@ -297,10 +297,14 @@
 
 
 def finish_products(*refs):
-    up_sum, down_sum = refs[:2]
-    up_ref, down_ref, buffer, sems = refs[-4:]
-    pairs = refs[2:-4]
+    up_sum, down_sum, stream, own_part, other_part = refs[:5]
+    layer_ref, up_ref, down_ref, layer, buffer, sems = refs[-6:]
+    pairs = refs[5:-6]
     count = len(pairs) // 4
+    total = stream[...] + own_part[...] + other_part[...].astype(jnp.float32)
+    layer[...] = total.astype(jnp.bfloat16)
+    layer_copy = pltpu.make_async_copy(layer, layer_ref, sems.at[buffer.shape[0]])
+    layer_copy.start()
     copies = []
     for start in range(0, up_ref.shape[0], TILE):
         tile = pl.ds(start, TILE)
@@ -321,21 +325,22 @@
                 pltpu.make_async_copy(buffer.at[slot], out_ref.at[tile], sems.at[slot])
             )
             copies[-1].start()
-    for copy in copies[-buffer.shape[0] :]:
+    for copy in copies[-buffer.shape[0] :] + [layer_copy]:
         copy.wait()
 
 
 SMALL = pl.CostEstimate(flops=1, bytes_accessed=1, transcendentals=0)
-
-
-def call(kernel, out_shape, smem, args, scratch=(), limit=16 * 2**20):
+LARGE = pl.CostEstimate(flops=8 * 10**9, bytes_accessed=1, transcendentals=0)
+
+
+def call(kernel, out_shape, smem, args, scratch=(), limit=16 * 2**20, cost=SMALL):
     return pl.pallas_call(
         kernel,
         out_shape=out_shape,
         in_specs=[pl.BlockSpec(memory_space=pltpu.SMEM)] * smem
         + [pl.BlockSpec(memory_space=pltpu.VMEM)] * (len(args) - smem),
         scratch_shapes=scratch,
-        cost_estimate=SMALL,
+        cost_estimate=cost,
         compiler_params=pltpu.CompilerParams(vmem_limit_bytes=limit),
     )(*args)
 
@@ -415,21 +420,21 @@
         [pltpu.VMEM((rows, width), jnp.float32), pltpu.VMEM((8, width), jnp.float32)],
     )
 
-    def forward(by12, by3x):
-        return send(by12, [(0, 1), (0, 1)]), send(by3x, [(0, 1), None])
-
     norm12 = send(normed, [(1, 0), (2, 0)])
     norm3x = send(normed, [(3, 0), (0, 1)])
+    first = lax.axis_index("col") == 0
     cot12, cot3x = after(cot12, normed), after(cot3x, normed)
-    cot_over12, cot_over3 = forward(cot12, cot3x)
+    cot_over12 = send(cot12, [(0, 1), (0, 1)])
     cot_swap12, cot_swap3x = swap(cot12), swap(cot3x)
-    cot_swap_over, cot_handed = swap(cot_over12), hand_over(cot_over3)
+    norm12, norm3x = call(
+        keep, [jax.ShapeDtypeStruct((rows, width), bf16)] * 2, 0, [norm12, norm3x], cost=LARGE
+    )
     norm12, norm3x, *_ = lax.optimization_barrier(
-        (norm12, norm3x, cot_over12, cot_swap12)
-    )
-    over12, over3 = forward(norm12, norm3x)
+        (norm12, norm3x, cot_over12, cot_swap12, cot_swap3x)
+    )
+    over12 = send(norm12, [(0, 1), (0, 1)])
+    over3 = send(jnp.where(first, norm3x, cot_swap3x), [(0, 1), (0, 1)])
     swap12, swap3x = swap(norm12), swap(norm3x)
-    swap_over, handed = swap(over12), hand_over(over3)
 
     def pair(choices, blocks, shares=()):
         made = jax.ShapeDtypeStruct((2 * rows, width), bf16)
@@ -446,33 +451,34 @@
     near = pair((1, 1), [norm12, swap12, cot12, cot_swap12])
     both = mine + swap(theirs).astype(jnp.float32)
     rest = lax.ppermute(both[rows:].astype(bf16), "grp", [(0, 1), (1, 0)])
-    layer_out = (stream + both[:rows] + rest.astype(jnp.float32)).astype(bf16)
     panel = up_weight.shape[1]
     grads = (
         jax.ShapeDtypeStruct((width, panel), jnp.float32),
         jax.ShapeDtypeStruct((panel, width), jnp.float32),
     )
     sums = call(add_products, grads, 0, list(group) + list(near))
-    over = pair((1, 1), [over12, swap_over, cot_over12, cot_swap_over])
+    over12, over3 = after(over12, sums[0]), after(over3, sums[0])
+    swap_over, swap_over3 = swap(over12), swap(over3)
+    over = pair((1, 1), [over12, swap_over, cot_over12, swap(cot_over12)])
     third = pair(
         (2, 2),
-        [after(norm3x, sums[0]), swap3x, over3, handed]
-        + [cot3x, cot_swap3x, cot_over3, cot_handed],
+        [norm3x, swap3x, over3, swap_over3, cot3x, cot_swap3x, swap_over3, over3],
     )
     last = list(over) + list(third)
-    up_grad, down_grad = pl.pallas_call(
+    parts = [stream, both[:rows], rest]
+    return pl.pallas_call(
         finish_products,
-        out_shape=grads,
-        in_specs=[pl.BlockSpec(memory_space=pltpu.VMEM)] * (2 + len(last)),
-        out_specs=[pl.BlockSpec(memory_space=pl.ANY)] * 2,
+        out_shape=(jax.ShapeDtypeStruct((rows, half), bf16),) + grads,
+        in_specs=[pl.BlockSpec(memory_space=pltpu.VMEM)] * (5 + len(last)),
+        out_specs=[pl.BlockSpec(memory_space=pl.ANY)] * 3,
         scratch_shapes=[
+            pltpu.VMEM((rows, half), bf16),
             pltpu.VMEM((4, TILE, width), jnp.float32),
-            pltpu.SemaphoreType.DMA((4,)),
+            pltpu.SemaphoreType.DMA((5,)),
         ],
         cost_estimate=SMALL,
         compiler_params=pltpu.CompilerParams(vmem_limit_bytes=16 * 2**20),
-    )(*sums, *last)
-    return (layer_out, up_grad, down_grad)
+    )(*sums, *parts, *last)
 
 
 def layer(*args):

time: 69.4 us -> 62.2 us (0.90)
  starting transfers between devices: 28.7 us -> 20.2 us
  local copies, waits for them, and re-layouts: 3.71 us -> 10.8 us
  waiting for transfers between devices: 16.5 us -> 12.2 us
    unnamed x14 -> x42, local copies, waits for them, and re-layouts: 3.69 us -> 10.7 us
    ppermute x8 -> x7, starting transfers between devices: 16.8 us -> 11 us  [send(): return lax.ppermute(x, ('patch', 'grp', 'col'), pairs)]
    ppermute x8 -> x7, waiting for transfers between devices: 16.2 us -> 10.9 us  [send(): return lax.ppermute(x, ('patch', 'grp', 'col'), pairs)]
    ppermute x2 -> x0, starting transfers between devices: 3.87 us -> none  [hand_over(): return lax.ppermute(x, 'col', [(0, 1)])]
    ppermute x7 -> x8, starting transfers between devices: 2.33 us -> 3.67 us  [swap(): return lax.ppermute(x, 'col', [(0, 1), (1, 0)])]
    ppermute x1, waiting for transfers between devices: 0.01 us -> 1.01 us  [gather_plan(): rest = lax.ppermute(both[rows:].astype(bf16), 'grp', [(0, 1), (1, 0)])]
    pallas_call x9 -> x10, Pallas kernels: 13.5 us -> 12.7 us  [call(): pl.pallas_call(kernel, out_shape=out_shape, in_specs=[pl.BlockSpec(memory...]
    convert_element_type x1 -> x0, other arithmetic: 0.71 us -> none  [gather_plan(): layer_out = (stream + both[:rows] + rest.astype(jnp.float32)).astype(bf16)]
  transfers between devices with their start and end apart: 24 -> 22, of which waited for: 5 -> 5; matrix products, arithmetic and copies ran while one was open for 0% -> 0% of each run, Pallas kernels for 26% -> 20%
where the time goes in v7:
time: 62.2 us; the launch traced here: 61.9 us
  starting transfers between devices  20.2 us (32%)
  Pallas kernels  17.2 us (28%)
  waiting for transfers between devices  12.2 us (20%)
  local copies, waits for them, and re-layouts  10.8 us (17%)
  between operations  1.54 us (2%)
    pallas_call x10, Pallas kernels, call(): pl.pallas_call(kernel, out_shape=out_shape, in_specs=[pl.BlockSpec(memory...  12.7 us
    ppermute x7, starting transfers between devices, send(): return lax.ppermute(x, ('patch', 'grp', 'col'), pairs)  11 us
    ppermute x7, waiting for transfers between devices, send(): return lax.ppermute(x, ('patch', 'grp', 'col'), pairs)  10.9 us
    unnamed x42, local copies, waits for them, and re-layouts  10.7 us
    pallas_call x1, Pallas kernels, gather_plan(): pl.pallas_call(finish_products, out_shape=(jax.ShapeDtypeStruct((rows, ha...  4.48 us
    ppermute x6, starting transfers between devices, others(): lax.ppermute(x, axis, [(i, i ^ k) for i in range(n)])  4.21 us
    ppermute x8, starting transfers between devices, swap(): return lax.ppermute(x, 'col', [(0, 1), (1, 0)])  3.67 us
    ppermute x1, starting transfers between devices, gather_plan(): rest = lax.ppermute(both[rows:].astype(bf16), 'grp', [(0, 1), (1, 0)])  1.25 us
  transfers between devices with their start and end apart: 22, of which 5 were waited for; matrix products, arithmetic and copies ran while one was open for 0% of the time, Pallas kernels for 20%

profile of v7, /device:TPU:0, one launch (start us, length us, event | category | flops | bytes accessed | tf_op | source)
XLA Modules:
  0.0 61.9 jit_solution(9528882759247359826)
XLA Ops:
  0.6 0.5 collective-permute-start.5
  1.1 0.1 collective-permute-start
  1.2 2.9 %collective-permute-start.1 = (bf16[128,512]{1,0:T(8,128)(2,1)}, bf16[128,512]{1,0:T(8,128)(2,1)S(1)}, u32[]{:S(2)}, u32[]{:S(2)}) collective-permute-start(bf16[128,512]{1,0:T(8,128)(2,1)} %refs_0_.4), channel_id=1, source_target_pairs={{0,2},{2,0},{1,3},{3,1},{4,6},{6,4},{5,7},{7,5},{8,10},{10,8},{9,1... | collective-permute-start | bytes 393224 | tf_op jit(solution)/shard_map/ppermute | solution.py:129
  4.1 0.0 collective-permute-start.2
  4.2 0.9 %copy-done.18 = bf16[128,512]{1,0:T(8,128)(2,1)S(1)} copy-done((bf16[128,512]{1,0:T(8,128)(2,1)S(1)}, bf16[128,512]{1,0:T(8,128)(2,1)}, u32[]{:S(2)}) %copy-start.18) | copy-done | bytes 131096
  5.1 2.7 %collective-permute-start.4 = (bf16[128,1024]{1,0:T(8,128)(2,1)S(1)}, bf16[128,1024]{1,0:T(8,128)(2,1)S(1)}, u32[]{:S(2)}, u32[]{:S(2)}) collective-permute-start(bf16[128,1024]{1,0:T(8,128)(2,1)S(1)} %shard_map.130.refs_3_), channel_id=1, source_target_pairs={{0,4},{1,9},{2,6},{3,11},{4,0},{5,13},{6,2},{7,15},{8,12},{9,1},{1... | collective-permute-start | bytes 786440 | tf_op jit(solution)/shard_map/ppermute | solution.py:357
  8.4 1.2 %copy-done.3 = bf16[512,1024]{1,0:T(8,128)(2,1)S(1)} copy-done((bf16[512,1024]{1,0:T(8,128)(2,1)S(1)}, bf16[512,1024]{1,0:T(8,128)(2,1)}, u32[]{:S(2)}) %copy-start.3) | copy-done | bytes 1048600
  9.7 0.9 %copy-done.17 = bf16[128,512]{1,0:T(8,128)(2,1)S(1)} copy-done((bf16[128,512]{1,0:T(8,128)(2,1)S(1)}, bf16[128,512]{1,0:T(8,128)(2,1)}, u32[]{:S(2)}) %copy-start.17) | copy-done | bytes 131096
  10.6 0.1 shard_map.131
  10.7 0.2 collective-permute-done.2.refs_3_
  10.9 0.4 copy-done.19
  11.3 0.2 copy-done.20
  11.6 2.7 %shard_map.132.refs_0_ = bf16[144,512]{1,0:T(8,128)(2,1)} custom-call(s32[1,2]{1,0:T(1,128)} %ids_ref.1, s32[1]{0:T(128)S(6)} %copy.14.count_ref, f32[1,512]{1,0:T(1,128)} %bitcast.1, bf16[128,512]{1,0:T(8,128)(2,1)} %query_ref, bf16[128,512]{1,0:T(8,128)(2,1)} %refs_0_.4, bf16[128,512]{1,0:T(8,128)(2,1)} %copy-done.19, bf16[128,512]{1,0:T(8,128)(2,1)} %refs_2_.1, ...), custom_call_target="tpu_custom_call" | custom-call | flops 1 | bytes 1 | tf_op jit(solution)/shard_map/pallas_call | solution.py:337
  14.2 0.7 %collective-permute-start.3 = (bf16[144,512]{1,0:T(8,128)(2,1)}, bf16[144,512]{1,0:T(8,128)(2,1)S(1)}, u32[]{:S(2)}, u32[]{:S(2)}) collective-permute-start(bf16[144,512]{1,0:T(8,128)(2,1)} %shard_map.132.refs_0_), channel_id=1, source_target_pairs={{0,1},{1,0},{2,3},{3,2},{4,5},{5,4},{6,7},{7,6},{8,9},{9,8},{10,11... | collective-permute-start | bytes 442376 | tf_op jit(solution)/shard_map/ppermute | solution.py:129
  14.9 3.7 %collective-permute-start.11 = (bf16[128,1024]{1,0:T(8,128)(2,1)S(1)}, bf16[128,1024]{1,0:T(8,128)(2,1)S(1)}, u32[]{:S(2)}, u32[]{:S(2)}) collective-permute-start(bf16[128,1024]{1,0:T(8,128)(2,1)S(1)} %shard_map.130.refs_3_), channel_id=1, source_target_pairs={{0,12},{1,3},{2,14},{3,1},{4,8},{5,7},{6,10},{7,5},{8,4},{9,11},{1... | collective-permute-start | bytes 786440 | tf_op jit(solution)/shard_map/ppermute | solution.py:357
  18.6 1.0 %copy-done.4 = bf16[144,512]{1,0:T(8,128)(2,1)S(1)} copy-done((bf16[144,512]{1,0:T(8,128)(2,1)S(1)}, bf16[144,512]{1,0:T(8,128)(2,1)}, u32[]{:S(2)}) %copy-start.4) | copy-done | bytes 147480
  19.6 0.8 %shard_map.133 = (f32[128,512]{1,0:T(8,128)S(1)}, bf16[128,1024]{1,0:T(8,128)(2,1)S(1)}) custom-call(bf16[144,512]{1,0:T(8,128)(2,1)S(1)} %copy-done.4, bf16[144,512]{1,0:T(8,128)(2,1)S(1)} %collective-permute-done.3.refs_1_, bf16[512,1024]{1,0:T(8,128)(2,1)S(1)} %get-tuple-element.41.refs_2_, bf16[512,1024]{1,0:T(8,128)(2,1)S(1)} %collective-permute-done.5.refs_3_, ...), custom_call_target="tpu_custom_call" | custom-call | flops 1 | bytes 1 | tf_op jit(solution)/shard_map/pallas_call | solution.py:337
  20.4 0.7 %copy-done.5 = f32[128,512]{1,0:T(8,128)} copy-done((f32[128,512]{1,0:T(8,128)}, f32[128,512]{1,0:T(8,128)S(1)}, u32[]{:S(2)}) %copy-start.5) | copy-done | bytes 262168
  21.1 1.1 %collective-permute-start.8 = (bf16[128,1024]{1,0:T(8,128)(2,1)S(1)}, bf16[128,1024]{1,0:T(8,128)(2,1)S(1)}, u32[]{:S(2)}, u32[]{:S(2)}) collective-permute-start(bf16[128,1024]{1,0:T(8,128)(2,1)S(1)} %get-tuple-element.43.refs_0_), channel_id=1, source_target_pairs={{0,12},{1,3},{2,14},{3,1},{4,8},{5,7},{6,10},{7,5},{8,4},{9,11},{1... | collective-permute-start | bytes 786440 | tf_op jit(solution)/shard_map/ppermute | solution.py:357
  22.2 0.7 %copy-done.11 = bf16[128,1024]{1,0:T(8,128)(2,1)} copy-done((bf16[128,1024]{1,0:T(8,128)(2,1)}, bf16[128,1024]{1,0:T(8,128)(2,1)S(1)}, u32[]{:S(2)}) %copy-start.11) | copy-done | bytes 262168
  22.9 0.0 collective-permute-start.10
  23.0 1.4 %collective-permute-start.9 = (bf16[128,1024]{1,0:T(8,128)(2,1)S(1)}, bf16[128,1024]{1,0:T(8,128)(2,1)S(1)}, u32[]{:S(2)}, u32[]{:S(2)}) collective-permute-start(bf16[128,1024]{1,0:T(8,128)(2,1)S(1)} %collective-permute-done.4.refs_2_), channel_id=1, source_target_pairs={{0,2},{1,3},{2,0},{3,1},{4,6},{5,7},{6,4},{7,5},{8,10},{9,11},{10,... | collective-permute-start | bytes 786440 | tf_op jit(solution)/shard_map/ppermute | solution.py:357
  24.4 0.2 collective-permute-start.12
  24.7 5.7 %collective-permute-done.8.refs_1_ = bf16[128,1024]{1,0:T(8,128)(2,1)S(1)} collective-permute-done((bf16[128,1024]{1,0:T(8,128)(2,1)S(1)}, bf16[128,1024]{1,0:T(8,128)(2,1)S(1)}, u32[]{:S(2)}, u32[]{:S(2)}) %collective-permute-start.8) | collective-permute-done | bytes 262176 | tf_op jit(solution)/shard_map/ppermute | solution.py:357
  30.4 2.1 %collective-permute-done.7.refs_0_ = bf16[128,1024]{1,0:T(8,128)(2,1)S(1)} collective-permute-done((bf16[128,1024]{1,0:T(8,128)(2,1)S(1)}, bf16[128,1024]{1,0:T(8,128)(2,1)S(1)}, u32[]{:S(2)}, u32[]{:S(2)}) %collective-permute-start.7) | collective-permute-done | bytes 262176 | tf_op jit(solution)/shard_map/ppermute | solution.py:357
  32.5 0.7 %copy-done.15 = bf16[128,1024]{1,0:T(8,128)(2,1)} copy-done((bf16[128,1024]{1,0:T(8,128)(2,1)}, bf16[128,1024]{1,0:T(8,128)(2,1)S(1)}, u32[]{:S(2)}) %copy-start.15) | copy-done | bytes 262168
  33.2 0.7 %copy-done.13 = bf16[128,1024]{1,0:T(8,128)(2,1)} copy-done((bf16[128,1024]{1,0:T(8,128)(2,1)}, bf16[128,1024]{1,0:T(8,128)(2,1)S(1)}, u32[]{:S(2)}) %copy-start.13) | copy-done | bytes 262168
  34.0 0.7 %copy-done.7 = bf16[128,1024]{1,0:T(8,128)(2,1)} copy-done((bf16[128,1024]{1,0:T(8,128)(2,1)}, bf16[128,1024]{1,0:T(8,128)(2,1)S(1)}, u32[]{:S(2)}) %copy-start.7) | copy-done | bytes 262168
  34.7 2.2 %collective-permute-start.13 = (bf16[128,1024]{1,0:T(8,128)(2,1)S(1)}, bf16[128,1024]{1,0:T(8,128)(2,1)S(1)}, u32[]{:S(2)}, u32[]{:S(2)}) collective-permute-start(bf16[128,1024]{1,0:T(8,128)(2,1)S(1)} %get-tuple-element.48.refs_2_.refs_0_), channel_id=1, source_target_pairs={{0,1},{1,0},{2,3},{3,2},{4,5},{5,4},{6,7},{7,6},{8,9},{9,8},{10,11... | collective-permute-start | bytes 786440 | tf_op jit(solution)/shard_map/ppermute | solution.py:361
  36.9 0.1 collective-permute-start.14
  37.0 1.2 %collective-permute-start.20 = (bf16[128,1024]{1,0:T(8,128)(2,1)S(1)}, bf16[128,1024]{1,0:T(8,128)(2,1)S(1)}, u32[]{:S(2)}, u32[]{:S(2)}) collective-permute-start(bf16[128,1024]{1,0:T(8,128)(2,1)S(1)} %broadcast_select_fusion), channel_id=1, source_target_pairs={{0,2},{1,3},{2,0},{3,1},{4,6},{5,7},{6,4},{7,5},{8,10},{9,11},{10,... | collective-permute-start | bytes 786440 | tf_op jit(solution)/shard_map/ppermute | solution.py:357
  38.3 0.8 %collective-permute-start.17 = (bf16[128,1024]{1,0:T(8,128)(2,1)}, bf16[128,1024]{1,0:T(8,128)(2,1)S(1)}, u32[]{:S(2)}, u32[]{:S(2)}) collective-permute-start(bf16[128,1024]{1,0:T(8,128)(2,1)} %copy-done.15), channel_id=1, source_target_pairs={{0,2},{1,3},{2,0},{3,1},{4,6},{5,7},{6,4},{7,5},{8,10},{9,11},{10,... | collective-permute-start | bytes 786440 | tf_op jit(solution)/shard_map/ppermute | solution.py:357
  39.1 1.6 %copy-done.1 = bf16[1024,1024]{1,0:T(8,128)(2,1)S(1)} copy-done((bf16[1024,1024]{1,0:T(8,128)(2,1)S(1)}, bf16[1024,1024]{1,0:T(8,128)(2,1)}, u32[]{:S(2)}) %copy-start.1) | copy-done | bytes 2097176
  40.7 0.9 %copy-done.12 = bf16[128,1024]{1,0:T(8,128)(2,1)S(1)} copy-done((bf16[128,1024]{1,0:T(8,128)(2,1)S(1)}, bf16[128,1024]{1,0:T(8,128)(2,1)}, u32[]{:S(2)}) %copy-start.12) | copy-done | bytes 262168
  41.7 2.1 %shard_map.135 = (bf16[256,1024]{1,0:T(8,128)(2,1)S(1)}, bf16[256,1024]{1,0:T(8,128)(2,1)S(1)}, bf16[256,1024]{1,0:T(8,128)(2,1)S(1)}, bf16[256,1024]{1,0:T(8,12...) custom-call(bf16[128,1024]{1,0:T(8,128)(2,1)S(1)} %copy-done.12, ...), custom_call_target="tpu_custom_call" | custom-call | flops 1 | bytes 1 | tf_op jit(solution)/shard_map/pallas_call | solution.py:337
  43.8 0.1 collective-permute-start.15
  43.8 0.5 collective-permute-start.19
  44.4 1.5 %shard_map.136 = (bf16[256,1024]{1,0:T(8,128)(2,1)S(1)}, bf16[256,1024]{1,0:T(8,128)(2,1)S(1)}, bf16[256,1024]{1,0:T(8,128)(2,1)S(1)}, bf16[256,1024]{1,0:T(8,128)(2,1)S(1)}) custom-call(bf16[128,1024]{1,0:T(8,128)(2,1)S(1)} %copy-done.16, bf16[128,1024]{1,0:T(8,128)(2,1)S(1)} %collective-permute-done.14.refs_1_, bf16[128,1024]{1,0:T(8,128)(2,1)S(1)} %copy-done.10, ...), custom_call_target="tpu_custom_call" | custom-call | flops 1 | bytes 1 | tf_op jit(solution)/shard_map/pallas_call | solution.py:337
  45.9 2.4 %shard_map.137 = (f32[1024,1024]{1,0:T(8,128)S(1)}, f32[1024,1024]{1,0:T(8,128)S(1)}) custom-call(bf16[256,1024]{1,0:T(8,128)(2,1)S(1)} %get-tuple-element.49.refs_0_, bf16[256,1024]{1,0:T(8,128)(2,1)S(1)} %get-tuple-element.50.refs_1_, bf16[256,1024]{1,0:T(8,128)(2,1)S(1)} %get-tuple-element.51.refs_2_, bf16[256,1024]{1,0:T(8,128)(2,1)S(1)} %get-tuple-element.52.refs_3_, ...), custom_call_target="tpu_custom_call" | custom-call | flops 1 | bytes 1 | tf_op jit(solution)/shard_map/pallas_call | solution.py:337
  48.3 3.0 %collective-permute-done.17.refs_0_ = bf16[128,1024]{1,0:T(8,128)(2,1)S(1)} collective-permute-done((bf16[128,1024]{1,0:T(8,128)(2,1)}, bf16[128,1024]{1,0:T(8,128)(2,1)S(1)}, u32[]{:S(2)}, u32[]{:S(2)}) %collective-permute-start.17) | collective-permute-done | bytes 262176 | tf_op jit(solution)/shard_map/ppermute | solution.py:357
  51.4 0.5 collective-permute-start.21
  51.9 0.1 convert_add_fusion
  52.0 1.2 %collective-permute-start.16 = (bf16[128,512]{1,0:T(8,128)(2,1)S(1)}, bf16[128,512]{1,0:T(8,128)(2,1)S(1)}, u32[]{:S(2)}, u32[]{:S(2)}) collective-permute-start(bf16[128,512]{1,0:T(8,128)(2,1)S(1)} %slice.12), channel_id=1, source_target_pairs={{0,2},{2,0},{1,3},{3,1},{4,6},{6,4},{5,7},{7,5},{8,10},{10,8},{9,1... | collective-permute-start | bytes 393224 | tf_op jit(solution)/shard_map/ppermute | solution.py:453
  53.2 0.0 collective-permute-done.21.refs_3_.refs_6_
  53.3 1.6 %shard_map.139 = (bf16[256,1024]{1,0:T(8,128)(2,1)S(1)}, bf16[256,1024]{1,0:T(8,128)(2,1)S(1)}, bf16[256,1024]{1,0:T(8,128)(2,1)S(1)}, bf16[256,1024]{1,0:T(8,128)(2,1)S(1)}) custom-call(bf16[128,1024]{1,0:T(8,128)(2,1)S(1)} %get-tuple-element.48.refs_2_.refs_0_, bf16[128,1024]{1,0:T(8,128)(2,1)S(1)} %collective-permute-done.13.refs_1_, ...), custom_call_target="tpu_custom_call" | custom-call | flops 1 | bytes 1 | tf_op jit(solution)/shard_map/pallas_call | solution.py:337
  54.9 1.5 %shard_map.138 = (bf16[256,1024]{1,0:T(8,128)(2,1)S(1)}, bf16[256,1024]{1,0:T(8,128)(2,1)S(1)}, bf16[256,1024]{1,0:T(8,128)(2,1)S(1)}, bf16[256,1024]{1,0:T(8,128)(2,1)S(1)}) custom-call(bf16[128,1024]{1,0:T(8,128)(2,1)S(1)} %collective-permute-done.17.refs_0_, bf16[128,1024]{1,0:T(8,128)(2,1)S(1)} %collective-permute-done.18.refs_1_, ...), custom_call_target="tpu_custom_call" | custom-call | flops 1 | bytes 1 | tf_op jit(solution)/shard_map/pallas_call | solution.py:337
  56.4 1.0 %collective-permute-done.16.refs_4_ = bf16[128,512]{1,0:T(8,128)(2,1)S(1)} collective-permute-done((bf16[128,512]{1,0:T(8,128)(2,1)S(1)}, bf16[128,512]{1,0:T(8,128)(2,1)S(1)}, u32[]{:S(2)}, u32[]{:S(2)}) %collective-permute-start.16) | collective-permute-done | bytes 131104 | tf_op jit(solution)/shard_map/ppermute | solution.py:453
  57.4 4.5 %shard_map.140 = (bf16[128,512]{1,0:T(8,128)(2,1)}, f32[1024,1024]{1,0:T(8,128)}, f32[1024,1024]{1,0:T(8,128)}) custom-call(f32[1024,1024]{1,0:T(8,128)S(1)} %get-tuple-element.58.refs_0_, f32[1024,1024]{1,0:T(8,128)S(1)} %get-tuple-element.59.refs_1_, f32[128,512]{1,0:T(8,128)S(1)} %copy-done.6, f32[128,512]{1,0:T(8,128)S(1)} %slice.9.refs_3_, ...), custom_call_target="tpu_custom_call" | custom-call | flops 1 | bytes 1 | tf_op jit(solution)/shard_map/pallas_call | solution.py:469
  (53 shorter events, 0.2 us)
Async XLA Ops:
  0.6 18.0 %collective-permute-start.5 = (bf16[512,1024]{1,0:T(8,128)(2,1)}, bf16[512,1024]{1,0:T(8,128)(2,1)S(1)}, u32[]{:S(2)}, u32[]{:S(2)}) collective-permute-start(bf16[512,1024]{1,0:T(8,128)(2,1)} %refs_0_.3), channel_id=1, source_target_pairs={{0,1},{1,0},{2,3},{3,2},{4,5},{5,4},{6,7},{7,6},{8,9},{9,8},{10,11... | collective-permute-start | bytes 3145736 | tf_op jit(solution)/shard_map/ppermute | solution.py:129
  1.1 3.0 %collective-permute-start = (bf16[128,512]{1,0:T(8,128)(2,1)}, bf16[128,512]{1,0:T(8,128)(2,1)S(1)}, u32[]{:S(2)}, u32[]{:S(2)}) collective-permute-start(bf16[128,512]{1,0:T(8,128)(2,1)} %refs_0_.2), channel_id=1, source_target_pairs={{0,1},{1,0},{2,3},{3,2},{4,5},{5,4},{6,7},{7,6},{8,9},{9,8},{10,11... | collective-permute-start | bytes 393224 | tf_op jit(solution)/shard_map/ppermute | solution.py:129
  1.2 9.4 %collective-permute-start.1 = (bf16[128,512]{1,0:T(8,128)(2,1)}, bf16[128,512]{1,0:T(8,128)(2,1)S(1)}, u32[]{:S(2)}, u32[]{:S(2)}) collective-permute-start(bf16[128,512]{1,0:T(8,128)(2,1)} %refs_0_.4), channel_id=1, source_target_pairs={{0,2},{2,0},{1,3},{3,1},{4,6},{6,4},{5,7},{7,5},{8,10},{10,8},{9,1... | collective-permute-start | bytes 393224 | tf_op jit(solution)/shard_map/ppermute | solution.py:129
  4.1 6.8 %collective-permute-start.2 = (bf16[128,512]{1,0:T(8,128)(2,1)}, bf16[128,512]{1,0:T(8,128)(2,1)S(1)}, u32[]{:S(2)}, u32[]{:S(2)}) collective-permute-start(bf16[128,512]{1,0:T(8,128)(2,1)} %refs_2_.1), channel_id=1, source_target_pairs={{0,2},{2,0},{1,3},{3,1},{4,6},{6,4},{5,7},{7,5},{8,10},{10,8},{9,1... | collective-permute-start | bytes 393224 | tf_op jit(solution)/shard_map/ppermute | solution.py:129
  4.2 0.9 %copy-start.18 = (bf16[128,512]{1,0:T(8,128)(2,1)S(1)}, bf16[128,512]{1,0:T(8,128)(2,1)}, u32[]{:S(2)}) copy-start(bf16[128,512]{1,0:T(8,128)(2,1)} %refs_0_.2) | copy-start | bytes 393220
  5.1 13.5 %collective-permute-start.4 = (bf16[128,1024]{1,0:T(8,128)(2,1)S(1)}, bf16[128,1024]{1,0:T(8,128)(2,1)S(1)}, u32[]{:S(2)}, u32[]{:S(2)}) collective-permute-start(bf16[128,1024]{1,0:T(8,128)(2,1)S(1)} %shard_map.130.refs_3_), channel_id=1, source_target_pairs={{0,4},{1,9},{2,6},{3,11},{4,0},{5,13},{6,2},{7,15},{8,12},{9,1},{1... | collective-permute-start | bytes 786440 | tf_op jit(solution)/shard_map/ppermute | solution.py:357
  8.4 1.2 %copy-start.3 = (bf16[512,1024]{1,0:T(8,128)(2,1)S(1)}, bf16[512,1024]{1,0:T(8,128)(2,1)}, u32[]{:S(2)}) copy-start(bf16[512,1024]{1,0:T(8,128)(2,1)} %refs_0_.3) | copy-start | bytes 3145732
  9.7 0.9 %copy-start.17 = (bf16[128,512]{1,0:T(8,128)(2,1)S(1)}, bf16[128,512]{1,0:T(8,128)(2,1)}, u32[]{:S(2)}) copy-start(bf16[128,512]{1,0:T(8,128)(2,1)} %refs_1_.1) | copy-start | bytes 393220
  10.7 0.7 %copy-start.19 = (bf16[128,512]{1,0:T(8,128)(2,1)}, bf16[128,512]{1,0:T(8,128)(2,1)S(1)}, u32[]{:S(2)}) copy-start(bf16[128,512]{1,0:T(8,128)(2,1)S(1)} %collective-permute-done.1.refs_1_) | copy-start | bytes 393220
  10.9 0.7 %copy-start.20 = (bf16[128,512]{1,0:T(8,128)(2,1)}, bf16[128,512]{1,0:T(8,128)(2,1)S(1)}, u32[]{:S(2)}) copy-start(bf16[128,512]{1,0:T(8,128)(2,1)S(1)} %collective-permute-done.2.refs_3_) | copy-start | bytes 393220
  14.2 4.4 %collective-permute-start.3 = (bf16[144,512]{1,0:T(8,128)(2,1)}, bf16[144,512]{1,0:T(8,128)(2,1)S(1)}, u32[]{:S(2)}, u32[]{:S(2)}) collective-permute-start(bf16[144,512]{1,0:T(8,128)(2,1)} %shard_map.132.refs_0_), channel_id=1, source_target_pairs={{0,1},{1,0},{2,3},{3,2},{4,5},{5,4},{6,7},{7,6},{8,9},{9,8},{10,11... | collective-permute-start | bytes 442376 | tf_op jit(solution)/shard_map/ppermute | solution.py:129
  14.9 3.7 %collective-permute-start.6 = (bf16[128,512]{1,0:T(8,128)(2,1)S(1)}, bf16[128,512]{1,0:T(8,128)(2,1)S(1)}, u32[]{:S(2)}, u32[]{:S(2)}) collective-permute-start(bf16[128,512]{1,0:T(8,128)(2,1)S(1)} %copy-done.17), channel_id=1, source_target_pairs={{0,1},{1,0},{2,3},{3,2},{4,5},{5,4},{6,7},{7,6},{8,9},{9,8},{10,11... | collective-permute-start | bytes 393224 | tf_op jit(solution)/shard_map/ppermute | solution.py:129
  14.9 9.5 %collective-permute-start.11 = (bf16[128,1024]{1,0:T(8,128)(2,1)S(1)}, bf16[128,1024]{1,0:T(8,128)(2,1)S(1)}, u32[]{:S(2)}, u32[]{:S(2)}) collective-permute-start(bf16[128,1024]{1,0:T(8,128)(2,1)S(1)} %shard_map.130.refs_3_), channel_id=1, source_target_pairs={{0,12},{1,3},{2,14},{3,1},{4,8},{5,7},{6,10},{7,5},{8,4},{9,11},{1... | collective-permute-start | bytes 786440 | tf_op jit(solution)/shard_map/ppermute | solution.py:357
  18.6 13.9 %copy-start.9 = (bf16[128,1024]{1,0:T(8,128)(2,1)}, bf16[128,1024]{1,0:T(8,128)(2,1)S(1)}, u32[]{:S(2)}) copy-start(bf16[128,1024]{1,0:T(8,128)(2,1)S(1)} %collective-permute-done.4.refs_2_) | copy-start | bytes 786436
  18.6 1.0 %copy-start.4 = (bf16[144,512]{1,0:T(8,128)(2,1)S(1)}, bf16[144,512]{1,0:T(8,128)(2,1)}, u32[]{:S(2)}) copy-start(bf16[144,512]{1,0:T(8,128)(2,1)} %shard_map.132.refs_0_) | copy-start | bytes 442372
  20.4 0.7 %copy-start.5 = (f32[128,512]{1,0:T(8,128)}, f32[128,512]{1,0:T(8,128)S(1)}, u32[]{:S(2)}) copy-start(f32[128,512]{1,0:T(8,128)S(1)} %get-tuple-element.60.refs_2_) | copy-start | bytes 786436
  21.1 18.0 %copy-start = (bf16[1024,1024]{1,0:T(8,128)(2,1)S(1)}, bf16[1024,1024]{1,0:T(8,128)(2,1)}, u32[]{:S(2)}) copy-start(bf16[1024,1024]{1,0:T(8,128)(2,1)} %refs_8_.1) | copy-start | bytes 6291460
  21.1 9.3 %collective-permute-start.8 = (bf16[128,1024]{1,0:T(8,128)(2,1)S(1)}, bf16[128,1024]{1,0:T(8,128)(2,1)S(1)}, u32[]{:S(2)}, u32[]{:S(2)}) collective-permute-start(bf16[128,1024]{1,0:T(8,128)(2,1)S(1)} %get-tuple-element.43.refs_0_), channel_id=1, source_target_pairs={{0,12},{1,3},{2,14},{3,1},{4,8},{5,7},{6,10},{7,5},{8,4},{9,11},{1... | collective-permute-start | bytes 786440 | tf_op jit(solution)/shard_map/ppermute | solution.py:357
  22.2 10.3 %collective-permute-start.7 = (bf16[128,1024]{1,0:T(8,128)(2,1)S(1)}, bf16[128,1024]{1,0:T(8,128)(2,1)S(1)}, u32[]{:S(2)}, u32[]{:S(2)}) collective-permute-start(bf16[128,1024]{1,0:T(8,128)(2,1)S(1)} %get-tuple-element.43.refs_0_), channel_id=1, source_target_pairs={{0,4},{1,9},{2,6},{3,11},{4,0},{5,13},{6,2},{7,15},{8,12},{9,1},{1... | collective-permute-start | bytes 786440 | tf_op jit(solution)/shard_map/ppermute | solution.py:357
  22.2 0.7 %copy-start.11 = (bf16[128,1024]{1,0:T(8,128)(2,1)}, bf16[128,1024]{1,0:T(8,128)(2,1)S(1)}, u32[]{:S(2)}) copy-start(bf16[128,1024]{1,0:T(8,128)(2,1)S(1)} %get-tuple-element.43.refs_0_) | copy-start | bytes 786436
  22.9 10.3 %collective-permute-start.10 = (bf16[128,1024]{1,0:T(8,128)(2,1)S(1)}, bf16[128,1024]{1,0:T(8,128)(2,1)S(1)}, u32[]{:S(2)}, u32[]{:S(2)}) collective-permute-start(bf16[128,1024]{1,0:T(8,128)(2,1)S(1)} %collective-permute-done.4.refs_2_), channel_id=1, source_target_pairs={{0,1},{1,0},{2,3},{3,2},{4,5},{5,4},{6,7},{7,6},{8,9},{9,8},{10,11... | collective-permute-start | bytes 786440 | tf_op jit(solution)/shard_map/ppermute | solution.py:361
  23.0 11.0 %collective-permute-start.9 = (bf16[128,1024]{1,0:T(8,128)(2,1)S(1)}, bf16[128,1024]{1,0:T(8,128)(2,1)S(1)}, u32[]{:S(2)}, u32[]{:S(2)}) collective-permute-start(bf16[128,1024]{1,0:T(8,128)(2,1)S(1)} %collective-permute-done.4.refs_2_), channel_id=1, source_target_pairs={{0,2},{1,3},{2,0},{3,1},{4,6},{5,7},{6,4},{7,5},{8,10},{9,11},{10,... | collective-permute-start | bytes 786440 | tf_op jit(solution)/shard_map/ppermute | solution.py:357
  24.4 9.5 %collective-permute-start.12 = (bf16[128,1024]{1,0:T(8,128)(2,1)S(1)}, bf16[128,1024]{1,0:T(8,128)(2,1)S(1)}, u32[]{:S(2)}, u32[]{:S(2)}) collective-permute-start(bf16[128,1024]{1,0:T(8,128)(2,1)S(1)} %collective-permute-done.11.refs_5_.refs_4_), channel_id=1, source_target_pairs={{0,1},{1,0},{2,3},{3,2},{4,5},{5,4},{6,7},{7,6},{8,9},{9,8},{10,11... | collective-permute-start | bytes 786440 | tf_op jit(solution)/shard_map/ppermute | solution.py:361
  32.5 0.7 %copy-start.15 = (bf16[128,1024]{1,0:T(8,128)(2,1)}, bf16[128,1024]{1,0:T(8,128)(2,1)S(1)}, u32[]{:S(2)}) copy-start(bf16[128,1024]{1,0:T(8,128)(2,1)S(1)} %get-tuple-element.53.refs_0_) | copy-start | bytes 786436
  33.2 0.7 %copy-start.13 = (bf16[128,1024]{1,0:T(8,128)(2,1)}, bf16[128,1024]{1,0:T(8,128)(2,1)S(1)}, u32[]{:S(2)}) copy-start(bf16[128,1024]{1,0:T(8,128)(2,1)S(1)} %collective-permute-done.10.refs_3_) | copy-start | bytes 786436
  34.0 0.7 %copy-start.7 = (bf16[128,1024]{1,0:T(8,128)(2,1)}, bf16[128,1024]{1,0:T(8,128)(2,1)S(1)}, u32[]{:S(2)}) copy-start(bf16[128,1024]{1,0:T(8,128)(2,1)S(1)} %collective-permute-done.9.refs_2_) | copy-start | bytes 786436
  34.7 4.5 %collective-permute-start.13 = (bf16[128,1024]{1,0:T(8,128)(2,1)S(1)}, bf16[128,1024]{1,0:T(8,128)(2,1)S(1)}, u32[]{:S(2)}, u32[]{:S(2)}) collective-permute-start(bf16[128,1024]{1,0:T(8,128)(2,1)S(1)} %get-tuple-element.48.refs_2_.refs_0_), channel_id=1, source_target_pairs={{0,1},{1,0},{2,3},{3,2},{4,5},{5,4},{6,7},{7,6},{8,9},{9,8},{10,11... | collective-permute-start | bytes 786440 | tf_op jit(solution)/shard_map/ppermute | solution.py:361
  36.9 6.9 %copy-start.8 = (bf16[128,1024]{1,0:T(8,128)(2,1)S(1)}, bf16[128,1024]{1,0:T(8,128)(2,1)}, u32[]{:S(2)}) copy-start(bf16[128,1024]{1,0:T(8,128)(2,1)} %copy-done.7) | copy-start | bytes 786436
  36.9 7.4 %copy-start.10 = (bf16[128,1024]{1,0:T(8,128)(2,1)S(1)}, bf16[128,1024]{1,0:T(8,128)(2,1)}, u32[]{:S(2)}) copy-start(bf16[128,1024]{1,0:T(8,128)(2,1)} %copy-done.9) | copy-start | bytes 786436
  36.9 7.4 %copy-start.14 = (bf16[128,1024]{1,0:T(8,128)(2,1)S(1)}, bf16[128,1024]{1,0:T(8,128)(2,1)}, u32[]{:S(2)}) copy-start(bf16[128,1024]{1,0:T(8,128)(2,1)} %copy-done.13) | copy-start | bytes 786436
  36.9 7.4 %collective-permute-start.14 = (bf16[128,1024]{1,0:T(8,128)(2,1)}, bf16[128,1024]{1,0:T(8,128)(2,1)S(1)}, u32[]{:S(2)}, u32[]{:S(2)}) collective-permute-start(bf16[128,1024]{1,0:T(8,128)(2,1)} %copy-done.15), channel_id=1, source_target_pairs={{0,1},{1,0},{2,3},{3,2},{4,5},{5,4},{6,7},{7,6},{8,9},{9,8},{10,11... | collective-permute-start | bytes 786440 | tf_op jit(solution)/shard_map/ppermute | solution.py:361
  37.0 11.3 %collective-permute-start.20 = (bf16[128,1024]{1,0:T(8,128)(2,1)S(1)}, bf16[128,1024]{1,0:T(8,128)(2,1)S(1)}, u32[]{:S(2)}, u32[]{:S(2)}) collective-permute-start(bf16[128,1024]{1,0:T(8,128)(2,1)S(1)} %broadcast_select_fusion), channel_id=1, source_target_pairs={{0,2},{1,3},{2,0},{3,1},{4,6},{5,7},{6,4},{7,5},{8,10},{9,11},{10,... | collective-permute-start | bytes 786440 | tf_op jit(solution)/shard_map/ppermute | solution.py:357
  38.3 13.1 %collective-permute-start.17 = (bf16[128,1024]{1,0:T(8,128)(2,1)}, bf16[128,1024]{1,0:T(8,128)(2,1)S(1)}, u32[]{:S(2)}, u32[]{:S(2)}) collective-permute-start(bf16[128,1024]{1,0:T(8,128)(2,1)} %copy-done.15), channel_id=1, source_target_pairs={{0,2},{1,3},{2,0},{3,1},{4,6},{5,7},{6,4},{7,5},{8,10},{9,11},{10,... | collective-permute-start | bytes 786440 | tf_op jit(solution)/shard_map/ppermute | solution.py:357
  39.1 1.6 %copy-start.1 = (bf16[1024,1024]{1,0:T(8,128)(2,1)S(1)}, bf16[1024,1024]{1,0:T(8,128)(2,1)}, u32[]{:S(2)}) copy-start(bf16[1024,1024]{1,0:T(8,128)(2,1)} %refs_9_.1) | copy-start | bytes 6291460
  40.7 0.9 %copy-start.12 = (bf16[128,1024]{1,0:T(8,128)(2,1)S(1)}, bf16[128,1024]{1,0:T(8,128)(2,1)}, u32[]{:S(2)}) copy-start(bf16[128,1024]{1,0:T(8,128)(2,1)} %copy-done.11) | copy-start | bytes 786436
  41.7 2.7 %copy-start.16 = (bf16[128,1024]{1,0:T(8,128)(2,1)S(1)}, bf16[128,1024]{1,0:T(8,128)(2,1)}, u32[]{:S(2)}) copy-start(bf16[128,1024]{1,0:T(8,128)(2,1)} %copy-done.15) | copy-start | bytes 786436
  43.8 8.1 %collective-permute-start.15 = (bf16[256,512]{1,0:T(8,128)(2,1)S(1)}, bf16[256,512]{1,0:T(8,128)(2,1)S(1)}, u32[]{:S(2)}, u32[]{:S(2)}) collective-permute-start(bf16[256,512]{1,0:T(8,128)(2,1)S(1)} %get-tuple-element.62), channel_id=1, source_target_pairs={{0,1},{1,0},{2,3},{3,2},{4,5},{5,4},{6,7},{7,6},{8,9},{9,8},{10,11... | collective-permute-start | bytes 786440 | tf_op jit(solution)/shard_map/ppermute | solution.py:361
  43.8 11.0 %collective-permute-start.19 = (bf16[128,1024]{1,0:T(8,128)(2,1)S(1)}, bf16[128,1024]{1,0:T(8,128)(2,1)S(1)}, u32[]{:S(2)}, u32[]{:S(2)}) collective-permute-start(bf16[128,1024]{1,0:T(8,128)(2,1)S(1)} %copy-done.8), channel_id=1, source_target_pairs={{0,1},{1,0},{2,3},{3,2},{4,5},{5,4},{6,7},{7,6},{8,9},{9,8},{10,11... | collective-permute-start | bytes 786440 | tf_op jit(solution)/shard_map/ppermute | solution.py:361
  45.9 7.4 %copy-start.2 = (bf16[1024,1024]{1,0:T(8,128)(2,1)S(1)}, bf16[1024,1024]{1,0:T(8,128)(2,1)}, u32[]{:S(2)}) copy-start(bf16[1024,1024]{1,0:T(8,128)(2,1)} %refs_9_.1) | copy-start | bytes 6291460
  51.3 3.5 %collective-permute-start.18 = (bf16[128,1024]{1,0:T(8,128)(2,1)S(1)}, bf16[128,1024]{1,0:T(8,128)(2,1)S(1)}, u32[]{:S(2)}, u32[]{:S(2)}) collective-permute-start(bf16[128,1024]{1,0:T(8,128)(2,1)S(1)} %collective-permute-done.17.refs_0_), channel_id=1, source_target_pairs={{0,1},{1,0},{2,3},{3,2},{4,5},{5,4},{6,7},{7,6},{8,9},{9,8},{10,11... | collective-permute-start | bytes 786440 | tf_op jit(solution)/shard_map/ppermute | solution.py:361
  51.4 1.9 %collective-permute-start.21 = (bf16[128,1024]{1,0:T(8,128)(2,1)S(1)}, bf16[128,1024]{1,0:T(8,128)(2,1)S(1)}, u32[]{:S(2)}, u32[]{:S(2)}) collective-permute-start(bf16[128,1024]{1,0:T(8,128)(2,1)S(1)} %collective-permute-done.20.refs_2_.refs_7_), channel_id=1, source_target_pairs={{0,1},{1,0},{2,3},{3,2},{4,5},{5,4},{6,7},{7,6},{8,9},{9,8},{10,11... | collective-permute-start | bytes 786440 | tf_op jit(solution)/shard_map/ppermute | solution.py:361
  52.0 5.5 %collective-permute-start.16 = (bf16[128,512]{1,0:T(8,128)(2,1)S(1)}, bf16[128,512]{1,0:T(8,128)(2,1)S(1)}, u32[]{:S(2)}, u32[]{:S(2)}) collective-permute-start(bf16[128,512]{1,0:T(8,128)(2,1)S(1)} %slice.12), channel_id=1, source_target_pairs={{0,2},{2,0},{1,3},{3,1},{4,6},{6,4},{5,7},{7,5},{8,10},{10,8},{9,1... | collective-permute-start | bytes 393224 | tf_op jit(solution)/shard_map/ppermute | solution.py:453
  54.8 2.6 %copy-start.6 = (f32[128,512]{1,0:T(8,128)S(1)}, f32[128,512]{1,0:T(8,128)}, u32[]{:S(2)}) copy-start(f32[128,512]{1,0:T(8,128)} %copy-done.5) | copy-start | bytes 786436

commit v8 on v7

--- a/solution.py
+++ b/solution.py
@@ -160,6 +160,17 @@
     count = len(refs) // 2
     for source, target in zip(refs[:count], refs[count:]):
         target[...] = source[...]
+
+
+def pick(first_ref, second_ref, out_ref):
+    out_ref[...] = jnp.where(lax.axis_index("col") == 0, first_ref[...], second_ref[...])
+
+
+def add_halves(mine_ref, other_ref, own_ref, sent_ref):
+    rows = own_ref.shape[0]
+    total = mine_ref[...] + other_ref[...].astype(jnp.float32)
+    own_ref[...] = total[:rows]
+    sent_ref[...] = total[rows:].astype(sent_ref.dtype)
 
 
 def gelu_and_slope(pre):
@@ -330,7 +341,7 @@
 
 
 SMALL = pl.CostEstimate(flops=1, bytes_accessed=1, transcendentals=0)
-LARGE = pl.CostEstimate(flops=8 * 10**9, bytes_accessed=1, transcendentals=0)
+LARGE = pl.CostEstimate(flops=10**8, bytes_accessed=1, transcendentals=0)
 
 
 def call(kernel, out_shape, smem, args, scratch=(), limit=16 * 2**20, cost=SMALL):
@@ -422,7 +433,6 @@
 
     norm12 = send(normed, [(1, 0), (2, 0)])
     norm3x = send(normed, [(3, 0), (0, 1)])
-    first = lax.axis_index("col") == 0
     cot12, cot3x = after(cot12, normed), after(cot3x, normed)
     cot_over12 = send(cot12, [(0, 1), (0, 1)])
     cot_swap12, cot_swap3x = swap(cot12), swap(cot3x)
@@ -433,7 +443,10 @@
         (norm12, norm3x, cot_over12, cot_swap12, cot_swap3x)
     )
     over12 = send(norm12, [(0, 1), (0, 1)])
-    over3 = send(jnp.where(first, norm3x, cot_swap3x), [(0, 1), (0, 1)])
+    third_block = call(
+        pick, jax.ShapeDtypeStruct((rows, width), bf16), 0, [norm3x, cot_swap3x]
+    )
+    over3 = send(third_block, [(0, 1), (0, 1)])
     swap12, swap3x = swap(norm12), swap(norm3x)
 
     def pair(choices, blocks, shares=()):
@@ -449,8 +462,16 @@
         (1, 2), [normed, swap3x, norm3x, cot, cot_swap3x, cot3x], (jnp.float32, bf16)
     )
     near = pair((1, 1), [norm12, swap12, cot12, cot_swap12])
-    both = mine + swap(theirs).astype(jnp.float32)
-    rest = lax.ppermute(both[rows:].astype(bf16), "grp", [(0, 1), (1, 0)])
+    own_part, sent = call(
+        add_halves,
+        (
+            jax.ShapeDtypeStruct((rows, half), jnp.float32),
+            jax.ShapeDtypeStruct((rows, half), bf16),
+        ),
+        0,
+        [mine, swap(theirs)],
+    )
+    rest = lax.ppermute(sent, "grp", [(0, 1), (1, 0)])
     panel = up_weight.shape[1]
     grads = (
         jax.ShapeDtypeStruct((width, panel), jnp.float32),
@@ -465,7 +486,7 @@
         [norm3x, swap3x, over3, swap_over3, cot3x, cot_swap3x, swap_over3, over3],
     )
     last = list(over) + list(third)
-    parts = [stream, both[:rows], rest]
+    parts = [stream, own_part, rest]
     return pl.pallas_call(
         finish_products,
         out_shape=(jax.ShapeDtypeStruct((rows, half), bf16),) + grads,

time: 62.2 us -> 60.2 us (0.968)
  local copies, waits for them, and re-layouts: 10.8 us -> 4.62 us
  waiting for transfers between devices: 12.2 us -> 16.1 us
    unnamed x42 -> x16, local copies, waits for them, and re-layouts: 10.7 us -> 4.62 us
    ppermute x7, waiting for transfers between devices: 10.9 us -> 13.4 us  [send(): return lax.ppermute(x, ('patch', 'grp', 'col'), pairs)]
    ppermute x6, waiting for transfers between devices: 0.25 us -> 1.26 us  [others(): lax.ppermute(x, axis, [(i, i ^ k) for i in range(n)])]
    pallas_call x10 -> x12, Pallas kernels: 12.7 us -> 12.7 us  [call(): pl.pallas_call(kernel, out_shape=out_shape, in_specs=[pl.BlockSpec(memory...]
  transfers between devices with their start and end apart: 22 -> 22, of which waited for: 5 -> 8; matrix products, arithmetic and copies ran while one was open for 0% -> 0% of each run, Pallas kernels for 20% -> 21%
where the time goes in v8:
time: 60.2 us; the launch traced here: 60 us
  starting transfers between devices  20.6 us (34%)
  Pallas kernels  17.2 us (29%)
  waiting for transfers between devices  16.1 us (27%)
  local copies, waits for them, and re-layouts  4.62 us (8%)
  between operations  1.46 us (2%)
    ppermute x7, waiting for transfers between devices, send(): return lax.ppermute(x, ('patch', 'grp', 'col'), pairs)  13.4 us
    pallas_call x12, Pallas kernels, call(): pl.pallas_call(kernel, out_shape=out_shape, in_specs=[pl.BlockSpec(memory...  12.7 us
    ppermute x7, starting transfers between devices, send(): return lax.ppermute(x, ('patch', 'grp', 'col'), pairs)  11 us
    unnamed x16, local copies, waits for them, and re-layouts  4.62 us
    pallas_call x1, Pallas kernels, gather_plan(): pl.pallas_call(finish_products, out_shape=(jax.ShapeDtypeStruct((rows, ha...  4.49 us
    ppermute x8, starting transfers between devices, swap(): return lax.ppermute(x, 'col', [(0, 1), (1, 0)])  4.15 us
    ppermute x6, starting transfers between devices, others(): lax.ppermute(x, axis, [(i, i ^ k) for i in range(n)])  4.06 us
    ppermute x1, starting transfers between devices, gather_plan(): rest = lax.ppermute(sent, 'grp', [(0, 1), (1, 0)])  1.45 us
  transfers between devices with their start and end apart: 22, of which 8 were waited for; matrix products, arithmetic and copies ran while one was open for 0% of the time, Pallas kernels for 21%

profile of v8, /device:TPU:0, one launch (start us, length us, event | category | flops | bytes accessed | tf_op | source)
XLA Modules:
  0.0 60.0 jit_solution(146256689163718646)
XLA Ops:
  0.7 0.5 collective-permute-start.5
  1.2 0.1 collective-permute-start
  1.2 2.9 %collective-permute-start.1 = (bf16[128,512]{1,0:T(8,128)(2,1)}, bf16[128,512]{1,0:T(8,128)(2,1)S(1)}, u32[]{:S(2)}, u32[]{:S(2)}) collective-permute-start(bf16[128,512]{1,0:T(8,128)(2,1)} %refs_0_.4), channel_id=1, source_target_pairs={{0,2},{2,0},{1,3},{3,1},{4,6},{6,4},{5,7},{7,5},{8,10},{10,8},{9,1... | collective-permute-start | bytes 393224 | tf_op jit(solution)/shard_map/ppermute | solution.py:129
  4.2 0.0 collective-permute-start.2
  4.2 0.0 collective-permute-done.refs_1_
  4.2 0.9 %copy-done.5 = bf16[128,512]{1,0:T(8,128)(2,1)S(1)} copy-done((bf16[128,512]{1,0:T(8,128)(2,1)S(1)}, bf16[128,512]{1,0:T(8,128)(2,1)}, u32[]{:S(2)}) %copy-start.5) | copy-done | bytes 131096
  5.1 2.7 %collective-permute-start.4 = (bf16[128,1024]{1,0:T(8,128)(2,1)S(1)}, bf16[128,1024]{1,0:T(8,128)(2,1)S(1)}, u32[]{:S(2)}, u32[]{:S(2)}) collective-permute-start(bf16[128,1024]{1,0:T(8,128)(2,1)S(1)} %shard_map.130.refs_3_), channel_id=1, source_target_pairs={{0,4},{1,9},{2,6},{3,11},{4,0},{5,13},{6,2},{7,15},{8,12},{9,1},{1... | collective-permute-start | bytes 786440 | tf_op jit(solution)/shard_map/ppermute | solution.py:368
  7.8 2.5 %collective-permute-start.11 = (bf16[128,1024]{1,0:T(8,128)(2,1)S(1)}, bf16[128,1024]{1,0:T(8,128)(2,1)S(1)}, u32[]{:S(2)}, u32[]{:S(2)}) collective-permute-start(bf16[128,1024]{1,0:T(8,128)(2,1)S(1)} %shard_map.130.refs_3_), channel_id=1, source_target_pairs={{0,12},{1,3},{2,14},{3,1},{4,8},{5,7},{6,10},{7,5},{8,4},{9,11},{1... | collective-permute-start | bytes 786440 | tf_op jit(solution)/shard_map/ppermute | solution.py:368
  10.9 0.0 copy-start.2
  10.9 1.2 %copy-done.2 = bf16[512,1024]{1,0:T(8,128)(2,1)S(1)} copy-done((bf16[512,1024]{1,0:T(8,128)(2,1)S(1)}, bf16[512,1024]{1,0:T(8,128)(2,1)}, u32[]{:S(2)}) %copy-start.2) | copy-done | bytes 1048600
  12.2 0.9 %copy-done.4 = bf16[128,512]{1,0:T(8,128)(2,1)S(1)} copy-done((bf16[128,512]{1,0:T(8,128)(2,1)S(1)}, bf16[128,512]{1,0:T(8,128)(2,1)}, u32[]{:S(2)}) %copy-start.4) | copy-done | bytes 131096
  13.1 0.1 shard_map.131
  13.1 0.0 copy-start.6
  13.2 0.0 collective-permute-done.2.refs_3_
  13.2 0.0 copy-start.7
  13.2 0.6 %copy-done.6 = bf16[128,512]{1,0:T(8,128)(2,1)} copy-done((bf16[128,512]{1,0:T(8,128)(2,1)}, bf16[128,512]{1,0:T(8,128)(2,1)S(1)}, u32[]{:S(2)}) %copy-start.6) | copy-done | bytes 131096
  13.8 0.0 copy-done.7
  13.8 2.7 %shard_map.132.refs_0_ = bf16[144,512]{1,0:T(8,128)(2,1)} custom-call(s32[1,2]{1,0:T(1,128)} %ids_ref.1, s32[1]{0:T(128)S(6)} %copy.14.count_ref, f32[1,512]{1,0:T(1,128)} %bitcast.1, bf16[128,512]{1,0:T(8,128)(2,1)} %query_ref, bf16[128,512]{1,0:T(8,128)(2,1)} %refs_0_.4, bf16[128,512]{1,0:T(8,128)(2,1)} %copy-done.6, bf16[128,512]{1,0:T(8,128)(2,1)} %refs_2_.1, ...), custom_call_target="tpu_custom_call" | custom-call | flops 1 | bytes 1 | tf_op jit(solution)/shard_map/pallas_call | solution.py:348
  16.5 0.5 collective-permute-start.6
  17.0 0.0 collective-permute-done.4.refs_2_
  17.0 1.0 %collective-permute-done.6.refs_5_ = bf16[128,512]{1,0:T(8,128)(2,1)S(1)} collective-permute-done((bf16[128,512]{1,0:T(8,128)(2,1)S(1)}, bf16[128,512]{1,0:T(8,128)(2,1)S(1)}, u32[]{:S(2)}, u32[]{:S(2)}) %collective-permute-start.6) | collective-permute-done | bytes 131104 | tf_op jit(solution)/shard_map/ppermute | solution.py:129
  18.1 0.2 collective-permute-done.3.refs_1_
  18.3 0.0 collective-permute-done.5.refs_3_
  18.3 0.9 %copy-done.3 = bf16[144,512]{1,0:T(8,128)(2,1)S(1)} copy-done((bf16[144,512]{1,0:T(8,128)(2,1)S(1)}, bf16[144,512]{1,0:T(8,128)(2,1)}, u32[]{:S(2)}) %copy-start.3) | copy-done | bytes 147480
  19.2 0.7 %shard_map.133 = (f32[128,512]{1,0:T(8,128)S(1)}, bf16[128,1024]{1,0:T(8,128)(2,1)S(1)}) custom-call(bf16[144,512]{1,0:T(8,128)(2,1)S(1)} %copy-done.3, bf16[144,512]{1,0:T(8,128)(2,1)S(1)} %collective-permute-done.3.refs_1_, bf16[512,1024]{1,0:T(8,128)(2,1)S(1)} %get-tuple-element.43.refs_2_, bf16[512,1024]{1,0:T(8,128)(2,1)S(1)} %collective-permute-done.5.refs_3_, ...), custom_call_target="tpu_custom_call" | custom-call | flops 1 | bytes 1 | tf_op jit(solution)/shard_map/pallas_call | solution.py:348
  20.0 2.5 %collective-permute-start.8 = (bf16[128,1024]{1,0:T(8,128)(2,1)S(1)}, bf16[128,1024]{1,0:T(8,128)(2,1)S(1)}, u32[]{:S(2)}, u32[]{:S(2)}) collective-permute-start(bf16[128,1024]{1,0:T(8,128)(2,1)S(1)} %get-tuple-element.45.refs_0_), channel_id=1, source_target_pairs={{0,12},{1,3},{2,14},{3,1},{4,8},{5,7},{6,10},{7,5},{8,4},{9,11},{1... | collective-permute-start | bytes 786440 | tf_op jit(solution)/shard_map/ppermute | solution.py:368
  22.5 0.3 collective-permute-start.10
  22.8 1.2 %collective-permute-start.9 = (bf16[128,1024]{1,0:T(8,128)(2,1)S(1)}, bf16[128,1024]{1,0:T(8,128)(2,1)S(1)}, u32[]{:S(2)}, u32[]{:S(2)}) collective-permute-start(bf16[128,1024]{1,0:T(8,128)(2,1)S(1)} %collective-permute-done.4.refs_2_), channel_id=1, source_target_pairs={{0,2},{1,3},{2,0},{3,1},{4,6},{5,7},{6,4},{7,5},{8,10},{9,11},{10,... | collective-permute-start | bytes 786440 | tf_op jit(solution)/shard_map/ppermute | solution.py:368
  24.0 0.2 collective-permute-start.12
  24.2 4.8 %collective-permute-done.8.refs_1_ = bf16[128,1024]{1,0:T(8,128)(2,1)S(1)} collective-permute-done((bf16[128,1024]{1,0:T(8,128)(2,1)S(1)}, bf16[128,1024]{1,0:T(8,128)(2,1)S(1)}, u32[]{:S(2)}, u32[]{:S(2)}) %collective-permute-start.8) | collective-permute-done | bytes 262176 | tf_op jit(solution)/shard_map/ppermute | solution.py:368
  29.0 2.8 %collective-permute-done.7.refs_0_ = bf16[128,1024]{1,0:T(8,128)(2,1)S(1)} collective-permute-done((bf16[128,1024]{1,0:T(8,128)(2,1)S(1)}, bf16[128,1024]{1,0:T(8,128)(2,1)S(1)}, u32[]{:S(2)}, u32[]{:S(2)}) %collective-permute-start.7) | collective-permute-done | bytes 262176 | tf_op jit(solution)/shard_map/ppermute | solution.py:368
  31.8 0.2 collective-permute-done.9.refs_2_
  32.0 3.0 %collective-permute-start.13 = (bf16[128,1024]{1,0:T(8,128)(2,1)S(1)}, bf16[128,1024]{1,0:T(8,128)(2,1)S(1)}, u32[]{:S(2)}, u32[]{:S(2)}) collective-permute-start(bf16[128,1024]{1,0:T(8,128)(2,1)S(1)} %get-tuple-element.50.refs_2_.first_ref.refs_0_), channel_id=1, source_target_pairs={{0,1},{1,0},{2,3},{3,2},{4,5},{5,4},{6,7},{7,6},{8,9},{9,8},{10,11... | collective-permute-start | bytes 786440 | tf_op jit(solution)/shard_map/ppermute | solution.py:372
  35.0 0.1 collective-permute-start.14
  35.1 1.4 %collective-permute-start.20 = (bf16[128,1024]{1,0:T(8,128)(2,1)S(1)}, bf16[128,1024]{1,0:T(8,128)(2,1)S(1)}, u32[]{:S(2)}, u32[]{:S(2)}) collective-permute-start(bf16[128,1024]{1,0:T(8,128)(2,1)S(1)} %shard_map.140), channel_id=1, source_target_pairs={{0,2},{1,3},{2,0},{3,1},{4,6},{5,7},{6,4},{7,5},{8,10},{9,11},{10,... | collective-permute-start | bytes 786440 | tf_op jit(solution)/shard_map/ppermute | solution.py:368
  36.6 0.6 %collective-permute-start.17 = (bf16[128,1024]{1,0:T(8,128)(2,1)S(1)}, bf16[128,1024]{1,0:T(8,128)(2,1)S(1)}, u32[]{:S(2)}, u32[]{:S(2)}) collective-permute-start(bf16[128,1024]{1,0:T(8,128)(2,1)S(1)} %get-tuple-element.55.refs_0_), channel_id=1, source_target_pairs={{0,2},{1,3},{2,0},{3,1},{4,6},{5,7},{6,4},{7,5},{8,10},{9,11},{10,... | collective-permute-start | bytes 786440 | tf_op jit(solution)/shard_map/ppermute | solution.py:368
  37.2 2.1 %shard_map.135 = (bf16[256,1024]{1,0:T(8,128)(2,1)S(1)}, bf16[256,1024]{1,0:T(8,128)(2,1)S(1)}, bf16[256,1024]{1,0:T(8,128)(2,1)S(1)}, bf16[256,1024]{1,0:T(8,12...) custom-call(bf16[128,1024]{1,0:T(8,128)(2,1)S(1)} %get-tuple-element.45.refs_0_, ...), custom_call_target="tpu_custom_call" | custom-call | flops 1 | bytes 1 | tf_op jit(solution)/shard_map/pallas_call | solution.py:348
  39.3 0.1 collective-permute-start.15
  39.4 0.5 collective-permute-start.19
  39.9 1.5 %shard_map.136 = (bf16[256,1024]{1,0:T(8,128)(2,1)S(1)}, bf16[256,1024]{1,0:T(8,128)(2,1)S(1)}, bf16[256,1024]{1,0:T(8,128)(2,1)S(1)}, bf16[256,1024]{1,0:T(8,128)(2,1)S(1)}) custom-call(bf16[128,1024]{1,0:T(8,128)(2,1)S(1)} %get-tuple-element.55.refs_0_, bf16[128,1024]{1,0:T(8,128)(2,1)S(1)} %collective-permute-done.14.refs_1_, ...), custom_call_target="tpu_custom_call" | custom-call | flops 1 | bytes 1 | tf_op jit(solution)/shard_map/pallas_call | solution.py:348
  41.4 2.4 %shard_map.137 = (f32[1024,1024]{1,0:T(8,128)S(1)}, f32[1024,1024]{1,0:T(8,128)S(1)}) custom-call(bf16[256,1024]{1,0:T(8,128)(2,1)S(1)} %get-tuple-element.51.refs_0_, bf16[256,1024]{1,0:T(8,128)(2,1)S(1)} %get-tuple-element.52.refs_1_, bf16[256,1024]{1,0:T(8,128)(2,1)S(1)} %get-tuple-element.53.refs_2_, bf16[256,1024]{1,0:T(8,128)(2,1)S(1)} %get-tuple-element.54.refs_3_, ...), custom_call_target="tpu_custom_call" | custom-call | flops 1 | bytes 1 | tf_op jit(solution)/shard_map/pallas_call | solution.py:348
  43.8 0.5 collective-permute-done.20.refs_2_.refs_7_
  44.3 5.2 %collective-permute-done.17.refs_0_ = bf16[128,1024]{1,0:T(8,128)(2,1)S(1)} collective-permute-done((bf16[128,1024]{1,0:T(8,128)(2,1)S(1)}, bf16[128,1024]{1,0:T(8,128)(2,1)S(1)}, u32[]{:S(2)}, u32[]{:S(2)}) %collective-permute-start.17) | collective-permute-done | bytes 262176 | tf_op jit(solution)/shard_map/ppermute | solution.py:368
  49.5 1.4 %collective-permute-start.16 = (bf16[128,512]{1,0:T(8,128)(2,1)S(1)}, bf16[128,512]{1,0:T(8,128)(2,1)S(1)}, u32[]{:S(2)}, u32[]{:S(2)}) collective-permute-start(bf16[128,512]{1,0:T(8,128)(2,1)S(1)} %get-tuple-element.66), channel_id=1, source_target_pairs={{0,2},{2,0},{1,3},{3,1},{4,6},{6,4},{5,7},{7,5},{8,10},{10,8},{9,1... | collective-permute-start | bytes 393224 | tf_op jit(solution)/shard_map/ppermute | solution.py:474
  51.0 1.5 %shard_map.141 = (bf16[256,1024]{1,0:T(8,128)(2,1)S(1)}, bf16[256,1024]{1,0:T(8,128)(2,1)S(1)}, bf16[256,1024]{1,0:T(8,128)(2,1)S(1)}, bf16[256,1024]{1,0:T(8,128)(2,1)S(1)}) custom-call(bf16[128,1024]{1,0:T(8,128)(2,1)S(1)} %get-tuple-element.50.refs_2_.first_ref.refs_0_, bf16[128,1024]{1,0:T(8,128)(2,1)S(1)} %collective-permute-done.13.refs_1_, ...), custom_call_target="tpu_custom_call" | custom-call | flops 1 | bytes 1 | tf_op jit(solution)/shard_map/pallas_call | solution.py:348
  52.5 1.5 %shard_map.139 = (bf16[256,1024]{1,0:T(8,128)(2,1)S(1)}, bf16[256,1024]{1,0:T(8,128)(2,1)S(1)}, bf16[256,1024]{1,0:T(8,128)(2,1)S(1)}, bf16[256,1024]{1,0:T(8,128)(2,1)S(1)}) custom-call(bf16[128,1024]{1,0:T(8,128)(2,1)S(1)} %collective-permute-done.17.refs_0_, bf16[128,1024]{1,0:T(8,128)(2,1)S(1)} %collective-permute-done.18.refs_1_, ...), custom_call_target="tpu_custom_call" | custom-call | flops 1 | bytes 1 | tf_op jit(solution)/shard_map/pallas_call | solution.py:348
  54.1 1.4 %collective-permute-done.16.refs_4_ = bf16[128,512]{1,0:T(8,128)(2,1)S(1)} collective-permute-done((bf16[128,512]{1,0:T(8,128)(2,1)S(1)}, bf16[128,512]{1,0:T(8,128)(2,1)S(1)}, u32[]{:S(2)}, u32[]{:S(2)}) %collective-permute-start.16) | collective-permute-done | bytes 131104 | tf_op jit(solution)/shard_map/ppermute | solution.py:474
  55.5 4.5 %shard_map.142 = (bf16[128,512]{1,0:T(8,128)(2,1)}, f32[1024,1024]{1,0:T(8,128)}, f32[1024,1024]{1,0:T(8,128)}) custom-call(f32[1024,1024]{1,0:T(8,128)S(1)} %get-tuple-element.60.refs_0_, f32[1024,1024]{1,0:T(8,128)S(1)} %get-tuple-element.61.refs_1_, f32[128,512]{1,0:T(8,128)S(1)} %get-tuple-element.62.refs_2_, f32[128,512]{1,0:T(8,128)S(1)} %get-tuple-element.65.refs_3_, ...), custom_call_target="tpu_custom_call" | custom-call | flops 1 | bytes 1 | tf_op jit(solution)/shard_map/pallas_call | solution.py:490
  (25 shorter events, 0.2 us)
Async XLA Ops:
  0.6 36.6 %copy-start.1 = (bf16[1024,1024]{1,0:T(8,128)(2,1)S(1)}, bf16[1024,1024]{1,0:T(8,128)(2,1)}, u32[]{:S(2)}) copy-start(bf16[1024,1024]{1,0:T(8,128)(2,1)} %refs_9_.1) | copy-start | bytes 6291460
  0.6 36.6 %copy-start = (bf16[1024,1024]{1,0:T(8,128)(2,1)S(1)}, bf16[1024,1024]{1,0:T(8,128)(2,1)}, u32[]{:S(2)}) copy-start(bf16[1024,1024]{1,0:T(8,128)(2,1)} %refs_8_.1) | copy-start | bytes 6291460
  0.7 17.6 %collective-permute-start.5 = (bf16[512,1024]{1,0:T(8,128)(2,1)}, bf16[512,1024]{1,0:T(8,128)(2,1)S(1)}, u32[]{:S(2)}, u32[]{:S(2)}) collective-permute-start(bf16[512,1024]{1,0:T(8,128)(2,1)} %refs_0_.3), channel_id=1, source_target_pairs={{0,1},{1,0},{2,3},{3,2},{4,5},{5,4},{6,7},{7,6},{8,9},{9,8},{10,11... | collective-permute-start | bytes 3145736 | tf_op jit(solution)/shard_map/ppermute | solution.py:129
  1.2 3.0 %collective-permute-start = (bf16[128,512]{1,0:T(8,128)(2,1)}, bf16[128,512]{1,0:T(8,128)(2,1)S(1)}, u32[]{:S(2)}, u32[]{:S(2)}) collective-permute-start(bf16[128,512]{1,0:T(8,128)(2,1)} %refs_0_.2), channel_id=1, source_target_pairs={{0,1},{1,0},{2,3},{3,2},{4,5},{5,4},{6,7},{7,6},{8,9},{9,8},{10,11... | collective-permute-start | bytes 393224 | tf_op jit(solution)/shard_map/ppermute | solution.py:129
  1.2 11.9 %collective-permute-start.1 = (bf16[128,512]{1,0:T(8,128)(2,1)}, bf16[128,512]{1,0:T(8,128)(2,1)S(1)}, u32[]{:S(2)}, u32[]{:S(2)}) collective-permute-start(bf16[128,512]{1,0:T(8,128)(2,1)} %refs_0_.4), channel_id=1, source_target_pairs={{0,2},{2,0},{1,3},{3,1},{4,6},{6,4},{5,7},{7,5},{8,10},{10,8},{9,1... | collective-permute-start | bytes 393224 | tf_op jit(solution)/shard_map/ppermute | solution.py:129
  4.2 9.0 %collective-permute-start.2 = (bf16[128,512]{1,0:T(8,128)(2,1)}, bf16[128,512]{1,0:T(8,128)(2,1)S(1)}, u32[]{:S(2)}, u32[]{:S(2)}) collective-permute-start(bf16[128,512]{1,0:T(8,128)(2,1)} %refs_2_.1), channel_id=1, source_target_pairs={{0,2},{2,0},{1,3},{3,1},{4,6},{6,4},{5,7},{7,5},{8,10},{10,8},{9,1... | collective-permute-start | bytes 393224 | tf_op jit(solution)/shard_map/ppermute | solution.py:129
  4.2 0.9 %copy-start.5 = (bf16[128,512]{1,0:T(8,128)(2,1)S(1)}, bf16[128,512]{1,0:T(8,128)(2,1)}, u32[]{:S(2)}) copy-start(bf16[128,512]{1,0:T(8,128)(2,1)} %refs_0_.2) | copy-start | bytes 393220
  5.1 11.9 %collective-permute-start.4 = (bf16[128,1024]{1,0:T(8,128)(2,1)S(1)}, bf16[128,1024]{1,0:T(8,128)(2,1)S(1)}, u32[]{:S(2)}, u32[]{:S(2)}) collective-permute-start(bf16[128,1024]{1,0:T(8,128)(2,1)S(1)} %shard_map.130.refs_3_), channel_id=1, source_target_pairs={{0,4},{1,9},{2,6},{3,11},{4,0},{5,13},{6,2},{7,15},{8,12},{9,1},{1... | collective-permute-start | bytes 786440 | tf_op jit(solution)/shard_map/ppermute | solution.py:368
  7.8 16.2 %collective-permute-start.11 = (bf16[128,1024]{1,0:T(8,128)(2,1)S(1)}, bf16[128,1024]{1,0:T(8,128)(2,1)S(1)}, u32[]{:S(2)}, u32[]{:S(2)}) collective-permute-start(bf16[128,1024]{1,0:T(8,128)(2,1)S(1)} %shard_map.130.refs_3_), channel_id=1, source_target_pairs={{0,12},{1,3},{2,14},{3,1},{4,8},{5,7},{6,10},{7,5},{8,4},{9,11},{1... | collective-permute-start | bytes 786440 | tf_op jit(solution)/shard_map/ppermute | solution.py:368
  10.9 1.2 %copy-start.2 = (bf16[512,1024]{1,0:T(8,128)(2,1)S(1)}, bf16[512,1024]{1,0:T(8,128)(2,1)}, u32[]{:S(2)}) copy-start(bf16[512,1024]{1,0:T(8,128)(2,1)} %refs_0_.3) | copy-start | bytes 3145732
  12.2 0.9 %copy-start.4 = (bf16[128,512]{1,0:T(8,128)(2,1)S(1)}, bf16[128,512]{1,0:T(8,128)(2,1)}, u32[]{:S(2)}) copy-start(bf16[128,512]{1,0:T(8,128)(2,1)} %refs_1_.1) | copy-start | bytes 393220
  13.1 0.7 %copy-start.6 = (bf16[128,512]{1,0:T(8,128)(2,1)}, bf16[128,512]{1,0:T(8,128)(2,1)S(1)}, u32[]{:S(2)}) copy-start(bf16[128,512]{1,0:T(8,128)(2,1)S(1)} %collective-permute-done.1.refs_1_) | copy-start | bytes 393220
  13.2 0.7 %copy-start.7 = (bf16[128,512]{1,0:T(8,128)(2,1)}, bf16[128,512]{1,0:T(8,128)(2,1)S(1)}, u32[]{:S(2)}) copy-start(bf16[128,512]{1,0:T(8,128)(2,1)S(1)} %collective-permute-done.2.refs_3_) | copy-start | bytes 393220
  16.5 1.8 %collective-permute-start.3 = (bf16[144,512]{1,0:T(8,128)(2,1)}, bf16[144,512]{1,0:T(8,128)(2,1)S(1)}, u32[]{:S(2)}, u32[]{:S(2)}) collective-permute-start(bf16[144,512]{1,0:T(8,128)(2,1)} %shard_map.132.refs_0_), channel_id=1, source_target_pairs={{0,1},{1,0},{2,3},{3,2},{4,5},{5,4},{6,7},{7,6},{8,9},{9,8},{10,11... | collective-permute-start | bytes 442376 | tf_op jit(solution)/shard_map/ppermute | solution.py:129
  16.5 1.6 %collective-permute-start.6 = (bf16[128,512]{1,0:T(8,128)(2,1)S(1)}, bf16[128,512]{1,0:T(8,128)(2,1)S(1)}, u32[]{:S(2)}, u32[]{:S(2)}) collective-permute-start(bf16[128,512]{1,0:T(8,128)(2,1)S(1)} %copy-done.4), channel_id=1, source_target_pairs={{0,1},{1,0},{2,3},{3,2},{4,5},{5,4},{6,7},{7,6},{8,9},{9,8},{10,11... | collective-permute-start | bytes 393224 | tf_op jit(solution)/shard_map/ppermute | solution.py:129
  18.3 0.9 %copy-start.3 = (bf16[144,512]{1,0:T(8,128)(2,1)S(1)}, bf16[144,512]{1,0:T(8,128)(2,1)}, u32[]{:S(2)}) copy-start(bf16[144,512]{1,0:T(8,128)(2,1)} %shard_map.132.refs_0_) | copy-start | bytes 442372
  20.0 9.0 %collective-permute-start.8 = (bf16[128,1024]{1,0:T(8,128)(2,1)S(1)}, bf16[128,1024]{1,0:T(8,128)(2,1)S(1)}, u32[]{:S(2)}, u32[]{:S(2)}) collective-permute-start(bf16[128,1024]{1,0:T(8,128)(2,1)S(1)} %get-tuple-element.45.refs_0_), channel_id=1, source_target_pairs={{0,12},{1,3},{2,14},{3,1},{4,8},{5,7},{6,10},{7,5},{8,4},{9,11},{1... | collective-permute-start | bytes 786440 | tf_op jit(solution)/shard_map/ppermute | solution.py:368
  22.5 9.3 %collective-permute-start.7 = (bf16[128,1024]{1,0:T(8,128)(2,1)S(1)}, bf16[128,1024]{1,0:T(8,128)(2,1)S(1)}, u32[]{:S(2)}, u32[]{:S(2)}) collective-permute-start(bf16[128,1024]{1,0:T(8,128)(2,1)S(1)} %get-tuple-element.45.refs_0_), channel_id=1, source_target_pairs={{0,4},{1,9},{2,6},{3,11},{4,0},{5,13},{6,2},{7,15},{8,12},{9,1},{1... | collective-permute-start | bytes 786440 | tf_op jit(solution)/shard_map/ppermute | solution.py:368
  22.5 9.3 %collective-permute-start.10 = (bf16[128,1024]{1,0:T(8,128)(2,1)S(1)}, bf16[128,1024]{1,0:T(8,128)(2,1)S(1)}, u32[]{:S(2)}, u32[]{:S(2)}) collective-permute-start(bf16[128,1024]{1,0:T(8,128)(2,1)S(1)} %collective-permute-done.4.refs_2_), channel_id=1, source_target_pairs={{0,1},{1,0},{2,3},{3,2},{4,5},{5,4},{6,7},{7,6},{8,9},{9,8},{10,11... | collective-permute-start | bytes 786440 | tf_op jit(solution)/shard_map/ppermute | solution.py:372
  22.8 9.2 %collective-permute-start.9 = (bf16[128,1024]{1,0:T(8,128)(2,1)S(1)}, bf16[128,1024]{1,0:T(8,128)(2,1)S(1)}, u32[]{:S(2)}, u32[]{:S(2)}) collective-permute-start(bf16[128,1024]{1,0:T(8,128)(2,1)S(1)} %collective-permute-done.4.refs_2_), channel_id=1, source_target_pairs={{0,2},{1,3},{2,0},{3,1},{4,6},{5,7},{6,4},{7,5},{8,10},{9,11},{10,... | collective-permute-start | bytes 786440 | tf_op jit(solution)/shard_map/ppermute | solution.py:368
  24.0 8.0 %collective-permute-start.12 = (bf16[128,1024]{1,0:T(8,128)(2,1)S(1)}, bf16[128,1024]{1,0:T(8,128)(2,1)S(1)}, u32[]{:S(2)}, u32[]{:S(2)}) collective-permute-start(bf16[128,1024]{1,0:T(8,128)(2,1)S(1)} %collective-permute-done.11.refs_5_.refs_4_), channel_id=1, source_target_pairs={{0,1},{1,0},{2,3},{3,2},{4,5},{5,4},{6,7},{7,6},{8,9},{9,8},{10,11... | collective-permute-start | bytes 786440 | tf_op jit(solution)/shard_map/ppermute | solution.py:372
  32.0 5.2 %collective-permute-start.13 = (bf16[128,1024]{1,0:T(8,128)(2,1)S(1)}, bf16[128,1024]{1,0:T(8,128)(2,1)S(1)}, u32[]{:S(2)}, u32[]{:S(2)}) collective-permute-start(bf16[128,1024]{1,0:T(8,128)(2,1)S(1)} %get-tuple-element.50.refs_2_.first_ref.refs_0_), channel_id=1, source_target_pairs={{0,1},{1,0},{2,3},{3,2},{4,5},{5,4},{6,7},{7,6},{8,9},{9,8},{10,11... | collective-permute-start | bytes 786440 | tf_op jit(solution)/shard_map/ppermute | solution.py:372
  35.0 4.9 %collective-permute-start.14 = (bf16[128,1024]{1,0:T(8,128)(2,1)S(1)}, bf16[128,1024]{1,0:T(8,128)(2,1)S(1)}, u32[]{:S(2)}, u32[]{:S(2)}) collective-permute-start(bf16[128,1024]{1,0:T(8,128)(2,1)S(1)} %get-tuple-element.55.refs_0_), channel_id=1, source_target_pairs={{0,1},{1,0},{2,3},{3,2},{4,5},{5,4},{6,7},{7,6},{8,9},{9,8},{10,11... | collective-permute-start | bytes 786440 | tf_op jit(solution)/shard_map/ppermute | solution.py:372
  35.1 9.2 %collective-permute-start.20 = (bf16[128,1024]{1,0:T(8,128)(2,1)S(1)}, bf16[128,1024]{1,0:T(8,128)(2,1)S(1)}, u32[]{:S(2)}, u32[]{:S(2)}) collective-permute-start(bf16[128,1024]{1,0:T(8,128)(2,1)S(1)} %shard_map.140), channel_id=1, source_target_pairs={{0,2},{1,3},{2,0},{3,1},{4,6},{5,7},{6,4},{7,5},{8,10},{9,11},{10,... | collective-permute-start | bytes 786440 | tf_op jit(solution)/shard_map/ppermute | solution.py:368
  36.6 12.9 %collective-permute-start.17 = (bf16[128,1024]{1,0:T(8,128)(2,1)S(1)}, bf16[128,1024]{1,0:T(8,128)(2,1)S(1)}, u32[]{:S(2)}, u32[]{:S(2)}) collective-permute-start(bf16[128,1024]{1,0:T(8,128)(2,1)S(1)} %get-tuple-element.55.refs_0_), channel_id=1, source_target_pairs={{0,2},{1,3},{2,0},{3,1},{4,6},{5,7},{6,4},{7,5},{8,10},{9,11},{10,... | collective-permute-start | bytes 786440 | tf_op jit(solution)/shard_map/ppermute | solution.py:368
  39.3 10.1 %collective-permute-start.15 = (bf16[256,512]{1,0:T(8,128)(2,1)S(1)}, bf16[256,512]{1,0:T(8,128)(2,1)S(1)}, u32[]{:S(2)}, u32[]{:S(2)}) collective-permute-start(bf16[256,512]{1,0:T(8,128)(2,1)S(1)} %get-tuple-element.64), channel_id=1, source_target_pairs={{0,1},{1,0},{2,3},{3,2},{4,5},{5,4},{6,7},{7,6},{8,9},{9,8},{10,11... | collective-permute-start | bytes 786440 | tf_op jit(solution)/shard_map/ppermute | solution.py:372
  39.4 13.1 %collective-permute-start.19 = (bf16[128,1024]{1,0:T(8,128)(2,1)S(1)}, bf16[128,1024]{1,0:T(8,128)(2,1)S(1)}, u32[]{:S(2)}, u32[]{:S(2)}) collective-permute-start(bf16[128,1024]{1,0:T(8,128)(2,1)S(1)} %collective-permute-done.9.refs_2_), channel_id=1, source_target_pairs={{0,1},{1,0},{2,3},{3,2},{4,5},{5,4},{6,7},{7,6},{8,9},{9,8},{10,11... | collective-permute-start | bytes 786440 | tf_op jit(solution)/shard_map/ppermute | solution.py:372
  44.3 6.7 %collective-permute-start.21 = (bf16[128,1024]{1,0:T(8,128)(2,1)S(1)}, bf16[128,1024]{1,0:T(8,128)(2,1)S(1)}, u32[]{:S(2)}, u32[]{:S(2)}) collective-permute-start(bf16[128,1024]{1,0:T(8,128)(2,1)S(1)} %collective-permute-done.20.refs_2_.refs_7_), channel_id=1, source_target_pairs={{0,1},{1,0},{2,3},{3,2},{4,5},{5,4},{6,7},{7,6},{8,9},{9,8},{10,11... | collective-permute-start | bytes 786440 | tf_op jit(solution)/shard_map/ppermute | solution.py:372
  49.5 3.1 %collective-permute-start.18 = (bf16[128,1024]{1,0:T(8,128)(2,1)S(1)}, bf16[128,1024]{1,0:T(8,128)(2,1)S(1)}, u32[]{:S(2)}, u32[]{:S(2)}) collective-permute-start(bf16[128,1024]{1,0:T(8,128)(2,1)S(1)} %collective-permute-done.17.refs_0_), channel_id=1, source_target_pairs={{0,1},{1,0},{2,3},{3,2},{4,5},{5,4},{6,7},{7,6},{8,9},{9,8},{10,11... | collective-permute-start | bytes 786440 | tf_op jit(solution)/shard_map/ppermute | solution.py:372
  49.5 6.0 %collective-permute-start.16 = (bf16[128,512]{1,0:T(8,128)(2,1)S(1)}, bf16[128,512]{1,0:T(8,128)(2,1)S(1)}, u32[]{:S(2)}, u32[]{:S(2)}) collective-permute-start(bf16[128,512]{1,0:T(8,128)(2,1)S(1)} %get-tuple-element.66), channel_id=1, source_target_pairs={{0,2},{2,0},{1,3},{3,1},{4,6},{6,4},{5,7},{7,5},{8,10},{10,8},{9,1... | collective-permute-start | bytes 393224 | tf_op jit(solution)/shard_map/ppermute | solution.py:474

commit v9 on v8

--- a/solution.py
+++ b/solution.py
@@ -162,8 +162,10 @@
         target[...] = source[...]
 
 
-def pick(first_ref, second_ref, out_ref):
-    out_ref[...] = jnp.where(lax.axis_index("col") == 0, first_ref[...], second_ref[...])
+def keep_and_pick(one_ref, two_ref, other_ref, kept_one_ref, kept_two_ref, picked_ref):
+    kept_one_ref[...] = one_ref[...]
+    kept_two_ref[...] = two_ref[...]
+    picked_ref[...] = jnp.where(lax.axis_index("col") == 0, other_ref[...], one_ref[...])
 
 
 def add_halves(mine_ref, other_ref, own_ref, sent_ref):
@@ -372,10 +374,6 @@
     return lax.ppermute(x, "col", [(0, 1), (1, 0)])
 
 
-def hand_over(x):
-    return lax.ppermute(x, "col", [(0, 1)])
-
-
 def gather_plan(
     query_vectors,
     key_vectors,
@@ -436,17 +434,18 @@
     cot12, cot3x = after(cot12, normed), after(cot3x, normed)
     cot_over12 = send(cot12, [(0, 1), (0, 1)])
     cot_swap12, cot_swap3x = swap(cot12), swap(cot3x)
-    norm12, norm3x = call(
-        keep, [jax.ShapeDtypeStruct((rows, width), bf16)] * 2, 0, [norm12, norm3x], cost=LARGE
-    )
-    norm12, norm3x, *_ = lax.optimization_barrier(
-        (norm12, norm3x, cot_over12, cot_swap12, cot_swap3x)
-    )
-    over12 = send(norm12, [(0, 1), (0, 1)])
-    third_block = call(
-        pick, jax.ShapeDtypeStruct((rows, width), bf16), 0, [norm3x, cot_swap3x]
-    )
-    over3 = send(third_block, [(0, 1), (0, 1)])
+    norm12, norm3x, picked = call(
+        keep_and_pick,
+        [jax.ShapeDtypeStruct((rows, width), bf16)] * 3,
+        0,
+        [norm12, norm3x, cot3x],
+        cost=LARGE,
+    )
+    norm12, norm3x, picked, *_ = lax.optimization_barrier(
+        (norm12, norm3x, picked, cot_over12, cot_swap12)
+    )
+    far = send(norm3x, [(0, 1), (1, 0)])
+    mixed = send(picked, [(0, 1), (0, 1)])
     swap12, swap3x = swap(norm12), swap(norm3x)
 
     def pair(choices, blocks, shares=()):
@@ -478,12 +477,16 @@
         jax.ShapeDtypeStruct((panel, width), jnp.float32),
     )
     sums = call(add_products, grads, 0, list(group) + list(near))
-    over12, over3 = after(over12, sums[0]), after(over3, sums[0])
-    swap_over, swap_over3 = swap(over12), swap(over3)
-    over = pair((1, 1), [over12, swap_over, cot_over12, swap(cot_over12)])
+    far, mixed = after(far, sums[0]), after(mixed, sums[0])
+    swap_far, swap_mixed = swap(far), swap(mixed)
+    cot_swap_over = swap(cot_over12)
+    over = pair(
+        (2, 2),
+        [swap_far, far, swap_mixed, mixed]
+        + [cot_over12, cot_swap_over, cot_swap_over, cot_over12],
+    )
     third = pair(
-        (2, 2),
-        [norm3x, swap3x, over3, swap_over3, cot3x, cot_swap3x, swap_over3, over3],
+        (2, 2), [norm3x, swap3x, far, swap_far, cot3x, cot_swap3x, mixed, swap_mixed]
     )
     last = list(over) + list(third)
     parts = [stream, own_part, rest]

time: 60.2 us -> 57.3 us (0.952)
  waiting for transfers between devices: 16.1 us -> 11.2 us
  starting transfers between devices: 20.6 us -> 22.6 us
  local copies, waits for them, and re-layouts: 4.62 us -> 3.7 us
  Pallas kernels: 17.2 us -> 18.1 us
    ppermute x7, waiting for transfers between devices: 13.4 us -> 9.66 us  [send(): return lax.ppermute(x, ('patch', 'grp', 'col'), pairs)]
    ppermute x8, starting transfers between devices: 4.15 us -> 5.84 us  [swap(): return lax.ppermute(x, 'col', [(0, 1), (1, 0)])]
    ppermute x6, waiting for transfers between devices: 1.26 us -> 0.25 us  [others(): lax.ppermute(x, axis, [(i, i ^ k) for i in range(n)])]
    pallas_call x12 -> x11, Pallas kernels: 12.7 us -> 13.7 us  [call(): pl.pallas_call(kernel, out_shape=out_shape, in_specs=[pl.BlockSpec(memory...]
    unnamed x16 -> x14, local copies, waits for them, and re-layouts: 4.62 us -> 3.7 us
  transfers between devices with their start and end apart: 22 -> 22, of which waited for: 8 -> 6; matrix products, arithmetic and copies ran while one was open for 0% -> 0% of each run, Pallas kernels for 21% -> 24%
where the time goes in v9:
time: 57.3 us; the launch traced here: 57.1 us
  starting transfers between devices  22.6 us (39%)
  Pallas kernels  18.1 us (32%)
  waiting for transfers between devices  11.2 us (20%)
  local copies, waits for them, and re-layouts  3.7 us (6%)
  between operations  1.46 us (3%)
    pallas_call x11, Pallas kernels, call(): pl.pallas_call(kernel, out_shape=out_shape, in_specs=[pl.BlockSpec(memory...  13.7 us
    ppermute x7, starting transfers between devices, send(): return lax.ppermute(x, ('patch', 'grp', 'col'), pairs)  11 us
    ppermute x7, waiting for transfers between devices, send(): return lax.ppermute(x, ('patch', 'grp', 'col'), pairs)  9.66 us
    ppermute x8, starting transfers between devices, swap(): return lax.ppermute(x, 'col', [(0, 1), (1, 0)])  5.84 us
    pallas_call x1, Pallas kernels, gather_plan(): pl.pallas_call(finish_products, out_shape=(jax.ShapeDtypeStruct((rows, ha...  4.48 us
    ppermute x6, starting transfers between devices, others(): lax.ppermute(x, axis, [(i, i ^ k) for i in range(n)])  4.21 us
    unnamed x14, local copies, waits for them, and re-layouts  3.7 us
    ppermute x1, starting transfers between devices, gather_plan(): rest = lax.ppermute(sent, 'grp', [(0, 1), (1, 0)])  1.61 us
  transfers between devices with their start and end apart: 22, of which 6 were waited for; matrix products, arithmetic and copies ran while one was open for 0% of the time, Pallas kernels for 24%

profile of v9, /device:TPU:0, one launch (start us, length us, event | category | flops | bytes accessed | tf_op | source)
XLA Modules:
  0.0 57.1 jit_solution(13190790764888836433)
XLA Ops:
  0.7 0.5 collective-permute-start.5
  1.2 0.1 collective-permute-start
  1.2 2.9 %collective-permute-start.1 = (bf16[128,512]{1,0:T(8,128)(2,1)}, bf16[128,512]{1,0:T(8,128)(2,1)S(1)}, u32[]{:S(2)}, u32[]{:S(2)}) collective-permute-start(bf16[128,512]{1,0:T(8,128)(2,1)} %refs_0_.4), channel_id=1, source_target_pairs={{0,2},{2,0},{1,3},{3,1},{4,6},{6,4},{5,7},{7,5},{8,10},{10,8},{9,1... | collective-permute-start | bytes 393224 | tf_op jit(solution)/shard_map/ppermute | solution.py:129
  4.2 0.0 collective-permute-start.2
  4.2 0.9 %copy-done.4 = bf16[128,512]{1,0:T(8,128)(2,1)S(1)} copy-done((bf16[128,512]{1,0:T(8,128)(2,1)S(1)}, bf16[128,512]{1,0:T(8,128)(2,1)}, u32[]{:S(2)}) %copy-start.4) | copy-done | bytes 131096
  5.1 2.7 %collective-permute-start.4 = (bf16[128,1024]{1,0:T(8,128)(2,1)S(1)}, bf16[128,1024]{1,0:T(8,128)(2,1)S(1)}, u32[]{:S(2)}, u32[]{:S(2)}) collective-permute-start(bf16[128,1024]{1,0:T(8,128)(2,1)S(1)} %shard_map.130.refs_3_), channel_id=1, source_target_pairs={{0,4},{1,9},{2,6},{3,11},{4,0},{5,13},{6,2},{7,15},{8,12},{9,1},{1... | collective-permute-start | bytes 786440 | tf_op jit(solution)/shard_map/ppermute | solution.py:370
  8.4 0.0 copy-start.2
  8.5 1.2 %copy-done.2 = bf16[512,1024]{1,0:T(8,128)(2,1)S(1)} copy-done((bf16[512,1024]{1,0:T(8,128)(2,1)S(1)}, bf16[512,1024]{1,0:T(8,128)(2,1)}, u32[]{:S(2)}) %copy-start.2) | copy-done | bytes 1048600
  9.7 1.0 %shard_map.131 = (bf16[512,1024]{1,0:T(8,128)(2,1)S(1)}, bf16[128,512]{1,0:T(8,128)(2,1)S(1)}) custom-call(bf16[512,1024]{1,0:T(8,128)(2,1)S(1)} %copy-done.2, bf16[128,512]{1,0:T(8,128)(2,1)} %refs_1_.1), custom_call_target="tpu_custom_call" | custom-call | flops 1 | bytes 1 | tf_op jit(solution)/shard_map/pallas_call | solution.py:350
  10.7 0.0 copy-start.5
  10.7 0.2 collective-permute-done.2.refs_3_
  10.9 0.4 copy-done.5
  11.3 0.2 copy-done.6
  11.6 2.7 %shard_map.132.refs_0_ = bf16[144,512]{1,0:T(8,128)(2,1)} custom-call(s32[1,2]{1,0:T(1,128)} %ids_ref.1, s32[1]{0:T(128)S(6)} %copy.14.count_ref, f32[1,512]{1,0:T(1,128)} %bitcast.1, bf16[128,512]{1,0:T(8,128)(2,1)} %query_ref, bf16[128,512]{1,0:T(8,128)(2,1)} %refs_0_.4, bf16[128,512]{1,0:T(8,128)(2,1)} %copy-done.5, bf16[128,512]{1,0:T(8,128)(2,1)} %refs_2_.1, ...), custom_call_target="tpu_custom_call" | custom-call | flops 1 | bytes 1 | tf_op jit(solution)/shard_map/pallas_call | solution.py:350
  14.3 0.7 %collective-permute-start.3 = (bf16[144,512]{1,0:T(8,128)(2,1)}, bf16[144,512]{1,0:T(8,128)(2,1)S(1)}, u32[]{:S(2)}, u32[]{:S(2)}) collective-permute-start(bf16[144,512]{1,0:T(8,128)(2,1)} %shard_map.132.refs_0_), channel_id=1, source_target_pairs={{0,1},{1,0},{2,3},{3,2},{4,5},{5,4},{6,7},{7,6},{8,9},{9,8},{10,11... | collective-permute-start | bytes 442376 | tf_op jit(solution)/shard_map/ppermute | solution.py:129
  14.9 0.0 collective-permute-start.6
  14.9 3.7 %collective-permute-start.9 = (bf16[128,1024]{1,0:T(8,128)(2,1)S(1)}, bf16[128,1024]{1,0:T(8,128)(2,1)S(1)}, u32[]{:S(2)}, u32[]{:S(2)}) collective-permute-start(bf16[128,1024]{1,0:T(8,128)(2,1)S(1)} %shard_map.130.refs_3_), channel_id=1, source_target_pairs={{0,12},{1,3},{2,14},{3,1},{4,8},{5,7},{6,10},{7,5},{8,4},{9,11},{1... | collective-permute-start | bytes 786440 | tf_op jit(solution)/shard_map/ppermute | solution.py:370
  18.6 0.0 collective-permute-done.5.refs_3_
  18.6 0.0 copy-start.3
  18.7 0.9 %copy-done.3 = bf16[144,512]{1,0:T(8,128)(2,1)S(1)} copy-done((bf16[144,512]{1,0:T(8,128)(2,1)S(1)}, bf16[144,512]{1,0:T(8,128)(2,1)}, u32[]{:S(2)}) %copy-start.3) | copy-done | bytes 147480
  19.6 0.7 %shard_map.133 = (f32[128,512]{1,0:T(8,128)S(1)}, bf16[128,1024]{1,0:T(8,128)(2,1)S(1)}) custom-call(bf16[144,512]{1,0:T(8,128)(2,1)S(1)} %copy-done.3, bf16[144,512]{1,0:T(8,128)(2,1)S(1)} %collective-permute-done.3.refs_1_, bf16[512,1024]{1,0:T(8,128)(2,1)S(1)} %get-tuple-element.45.refs_2_, bf16[512,1024]{1,0:T(8,128)(2,1)S(1)} %collective-permute-done.5.refs_3_, ...), custom_call_target="tpu_custom_call" | custom-call | flops 1 | bytes 1 | tf_op jit(solution)/shard_map/pallas_call | solution.py:350
  20.3 1.3 %collective-permute-start.8 = (bf16[128,1024]{1,0:T(8,128)(2,1)S(1)}, bf16[128,1024]{1,0:T(8,128)(2,1)S(1)}, u32[]{:S(2)}, u32[]{:S(2)}) collective-permute-start(bf16[128,1024]{1,0:T(8,128)(2,1)S(1)} %get-tuple-element.47.refs_0_), channel_id=1, source_target_pairs={{0,12},{1,3},{2,14},{3,1},{4,8},{5,7},{6,10},{7,5},{8,4},{9,11},{1... | collective-permute-start | bytes 786440 | tf_op jit(solution)/shard_map/ppermute | solution.py:370
  21.6 0.2 collective-permute-start.11
  21.8 1.3 %collective-permute-start.10 = (bf16[128,1024]{1,0:T(8,128)(2,1)S(1)}, bf16[128,1024]{1,0:T(8,128)(2,1)S(1)}, u32[]{:S(2)}, u32[]{:S(2)}) collective-permute-start(bf16[128,1024]{1,0:T(8,128)(2,1)S(1)} %collective-permute-done.4.refs_2_), channel_id=1, source_target_pairs={{0,2},{1,3},{2,0},{3,1},{4,6},{5,7},{6,4},{7,5},{8,10},{9,11},{10,... | collective-permute-start | bytes 786440 | tf_op jit(solution)/shard_map/ppermute | solution.py:370
  23.1 0.1 collective-permute-done.9.other_ref.refs_5_.refs_4_
  23.2 0.1 collective-permute-start.13
  23.3 6.6 %collective-permute-done.8.two_ref = bf16[128,1024]{1,0:T(8,128)(2,1)S(1)} collective-permute-done((bf16[128,1024]{1,0:T(8,128)(2,1)S(1)}, bf16[128,1024]{1,0:T(8,128)(2,1)S(1)}, u32[]{:S(2)}, u32[]{:S(2)}) %collective-permute-start.8) | collective-permute-done | bytes 262176 | tf_op jit(solution)/shard_map/ppermute | solution.py:370
  30.0 1.7 %collective-permute-done.7.one_ref = bf16[128,1024]{1,0:T(8,128)(2,1)S(1)} collective-permute-done((bf16[128,1024]{1,0:T(8,128)(2,1)S(1)}, bf16[128,1024]{1,0:T(8,128)(2,1)S(1)}, u32[]{:S(2)}, u32[]{:S(2)}) %collective-permute-start.7) | collective-permute-done | bytes 262176 | tf_op jit(solution)/shard_map/ppermute | solution.py:370
  31.7 0.1 shard_map.134
  31.8 0.0 collective-permute-done.10.refs_4_.refs_7_
  31.8 2.7 %collective-permute-start.12 = (bf16[128,1024]{1,0:T(8,128)(2,1)S(1)}, bf16[128,1024]{1,0:T(8,128)(2,1)S(1)}, u32[]{:S(2)}, u32[]{:S(2)}) collective-permute-start(bf16[128,1024]{1,0:T(8,128)(2,1)S(1)} %get-tuple-element.53.refs_2_.refs_0_), channel_id=1, source_target_pairs={{0,1},{1,0},{2,3},{3,2},{4,5},{5,4},{6,7},{7,6},{8,9},{9,8},{10,11... | collective-permute-start | bytes 786440 | tf_op jit(solution)/shard_map/ppermute | solution.py:374
  34.5 0.1 collective-permute-start.14
  34.6 1.5 %collective-permute-start.19 = (bf16[128,1024]{1,0:T(8,128)(2,1)S(1)}, bf16[128,1024]{1,0:T(8,128)(2,1)S(1)}, u32[]{:S(2)}, u32[]{:S(2)}) collective-permute-start(bf16[128,1024]{1,0:T(8,128)(2,1)S(1)} %get-tuple-element.71), channel_id=1, source_target_pairs={{0,2},{1,3},{2,0},{3,1},{4,6},{5,7},{6,4},{7,5},{8,10},{9,11},{10,... | collective-permute-start | bytes 786440 | tf_op jit(solution)/shard_map/ppermute | solution.py:370
  36.1 0.5 collective-permute-start.17
  36.6 0.0 collective-permute-done.12.refs_1_
  36.6 2.1 %shard_map.135 = (bf16[256,1024]{1,0:T(8,128)(2,1)S(1)}, bf16[256,1024]{1,0:T(8,128)(2,1)S(1)}, bf16[256,1024]{1,0:T(8,128)(2,1)S(1)}, bf16[256,1024]{1,0:T(8,12...) custom-call(bf16[128,1024]{1,0:T(8,128)(2,1)S(1)} %get-tuple-element.47.refs_0_, ...), custom_call_target="tpu_custom_call" | custom-call | flops 1 | bytes 1 | tf_op jit(solution)/shard_map/pallas_call | solution.py:350
  38.7 2.1 %collective-permute-start.15 = (bf16[256,512]{1,0:T(8,128)(2,1)S(1)}, bf16[256,512]{1,0:T(8,128)(2,1)S(1)}, u32[]{:S(2)}, u32[]{:S(2)}) collective-permute-start(bf16[256,512]{1,0:T(8,128)(2,1)S(1)} %get-tuple-element.67), channel_id=1, source_target_pairs={{0,1},{1,0},{2,3},{3,2},{4,5},{5,4},{6,7},{7,6},{8,9},{9,8},{10,11... | collective-permute-start | bytes 786440 | tf_op jit(solution)/shard_map/ppermute | solution.py:374
  40.9 0.0 collective-permute-done.14.refs_1_
  40.9 1.5 %shard_map.136 = (bf16[256,1024]{1,0:T(8,128)(2,1)S(1)}, bf16[256,1024]{1,0:T(8,128)(2,1)S(1)}, bf16[256,1024]{1,0:T(8,128)(2,1)S(1)}, bf16[256,1024]{1,0:T(8,128)(2,1)S(1)}) custom-call(bf16[128,1024]{1,0:T(8,128)(2,1)S(1)} %get-tuple-element.58.refs_0_, bf16[128,1024]{1,0:T(8,128)(2,1)S(1)} %collective-permute-done.14.refs_1_, ...), custom_call_target="tpu_custom_call" | custom-call | flops 1 | bytes 1 | tf_op jit(solution)/shard_map/pallas_call | solution.py:350
  42.4 2.4 %shard_map.137 = (f32[1024,1024]{1,0:T(8,128)S(1)}, f32[1024,1024]{1,0:T(8,128)S(1)}) custom-call(bf16[256,1024]{1,0:T(8,128)(2,1)S(1)} %get-tuple-element.54.refs_0_, bf16[256,1024]{1,0:T(8,128)(2,1)S(1)} %get-tuple-element.55.refs_1_, bf16[256,1024]{1,0:T(8,128)(2,1)S(1)} %get-tuple-element.56.refs_2_, bf16[256,1024]{1,0:T(8,128)(2,1)S(1)} %get-tuple-element.57.refs_3_, ...), custom_call_target="tpu_custom_call" | custom-call | flops 1 | bytes 1 | tf_op jit(solution)/shard_map/pallas_call | solution.py:350
  44.8 1.2 %collective-permute-done.17.refs_1_.refs_2_ = bf16[128,1024]{1,0:T(8,128)(2,1)S(1)} collective-permute-done((bf16[128,1024]{1,0:T(8,128)(2,1)S(1)}, bf16[128,1024]{1,0:T(8,128)(2,1)S(1)}, u32[]{:S(2)}, u32[]{:S(2)}) %collective-permute-start.17) | collective-permute-done | bytes 262176 | tf_op jit(solution)/shard_map/ppermute | solution.py:370
  46.1 0.5 collective-permute-start.20
  46.6 0.0 collective-permute-start.21
  46.6 1.6 %collective-permute-start.16 = (bf16[128,512]{1,0:T(8,128)(2,1)S(1)}, bf16[128,512]{1,0:T(8,128)(2,1)S(1)}, u32[]{:S(2)}, u32[]{:S(2)}) collective-permute-start(bf16[128,512]{1,0:T(8,128)(2,1)S(1)} %get-tuple-element.69), channel_id=1, source_target_pairs={{0,2},{2,0},{1,3},{3,1},{4,6},{6,4},{5,7},{7,5},{8,10},{10,8},{9,1... | collective-permute-start | bytes 393224 | tf_op jit(solution)/shard_map/ppermute | solution.py:473
  48.2 1.6 %shard_map.140 = (bf16[256,1024]{1,0:T(8,128)(2,1)S(1)}, bf16[256,1024]{1,0:T(8,128)(2,1)S(1)}, bf16[256,1024]{1,0:T(8,128)(2,1)S(1)}, bf16[256,1024]{1,0:T(8,128)(2,1)S(1)}) custom-call(bf16[128,1024]{1,0:T(8,128)(2,1)S(1)} %get-tuple-element.53.refs_2_.refs_0_, bf16[128,1024]{1,0:T(8,128)(2,1)S(1)} %collective-permute-done.12.refs_1_, ...), custom_call_target="tpu_custom_call" | custom-call | flops 1 | bytes 1 | tf_op jit(solution)/shard_map/pallas_call | solution.py:350
  49.8 1.6 %shard_map.139 = (bf16[256,1024]{1,0:T(8,128)(2,1)S(1)}, bf16[256,1024]{1,0:T(8,128)(2,1)S(1)}, bf16[256,1024]{1,0:T(8,128)(2,1)S(1)}, bf16[256,1024]{1,0:T(8,128)(2,1)S(1)}) custom-call(bf16[128,1024]{1,0:T(8,128)(2,1)S(1)} %collective-permute-done.18.refs_0_.refs_3_, bf16[128,1024]{1,0:T(8,128)(2,1)S(1)} %collective-permute-done.17.refs_1_.refs_2_, ...), custom_call_target="tpu_custom_call" | custom-call | flops 1 | bytes 1 | tf_op jit(solution)/shard_map/pallas_call | solution.py:350
  51.4 1.2 %collective-permute-done.16.refs_4_ = bf16[128,512]{1,0:T(8,128)(2,1)S(1)} collective-permute-done((bf16[128,512]{1,0:T(8,128)(2,1)S(1)}, bf16[128,512]{1,0:T(8,128)(2,1)S(1)}, u32[]{:S(2)}, u32[]{:S(2)}) %collective-permute-start.16) | collective-permute-done | bytes 131104 | tf_op jit(solution)/shard_map/ppermute | solution.py:473
  52.6 4.5 %shard_map.141 = (bf16[128,512]{1,0:T(8,128)(2,1)}, f32[1024,1024]{1,0:T(8,128)}, f32[1024,1024]{1,0:T(8,128)}) custom-call(f32[1024,1024]{1,0:T(8,128)S(1)} %get-tuple-element.63.refs_0_, f32[1024,1024]{1,0:T(8,128)S(1)} %get-tuple-element.64.refs_1_, f32[128,512]{1,0:T(8,128)S(1)} %get-tuple-element.65.refs_2_, f32[128,512]{1,0:T(8,128)S(1)} %get-tuple-element.68.refs_3_, ...), custom_call_target="tpu_custom_call" | custom-call | flops 1 | bytes 1 | tf_op jit(solution)/shard_map/pallas_call | solution.py:493
  (22 shorter events, 0.1 us)
Async XLA Ops:
  0.6 36.0 %copy-start.1 = (bf16[1024,1024]{1,0:T(8,128)(2,1)S(1)}, bf16[1024,1024]{1,0:T(8,128)(2,1)}, u32[]{:S(2)}) copy-start(bf16[1024,1024]{1,0:T(8,128)(2,1)} %refs_9_.3) | copy-start | bytes 6291460
  0.6 36.0 %copy-start = (bf16[1024,1024]{1,0:T(8,128)(2,1)S(1)}, bf16[1024,1024]{1,0:T(8,128)(2,1)}, u32[]{:S(2)}) copy-start(bf16[1024,1024]{1,0:T(8,128)(2,1)} %refs_8_.3) | copy-start | bytes 6291460
  0.7 18.0 %collective-permute-start.5 = (bf16[512,1024]{1,0:T(8,128)(2,1)}, bf16[512,1024]{1,0:T(8,128)(2,1)S(1)}, u32[]{:S(2)}, u32[]{:S(2)}) collective-permute-start(bf16[512,1024]{1,0:T(8,128)(2,1)} %refs_0_.3), channel_id=1, source_target_pairs={{0,1},{1,0},{2,3},{3,2},{4,5},{5,4},{6,7},{7,6},{8,9},{9,8},{10,11... | collective-permute-start | bytes 3145736 | tf_op jit(solution)/shard_map/ppermute | solution.py:129
  1.2 3.0 %collective-permute-start = (bf16[128,512]{1,0:T(8,128)(2,1)}, bf16[128,512]{1,0:T(8,128)(2,1)S(1)}, u32[]{:S(2)}, u32[]{:S(2)}) collective-permute-start(bf16[128,512]{1,0:T(8,128)(2,1)} %refs_0_.2), channel_id=1, source_target_pairs={{0,1},{1,0},{2,3},{3,2},{4,5},{5,4},{6,7},{7,6},{8,9},{9,8},{10,11... | collective-permute-start | bytes 393224 | tf_op jit(solution)/shard_map/ppermute | solution.py:129
  1.2 9.4 %collective-permute-start.1 = (bf16[128,512]{1,0:T(8,128)(2,1)}, bf16[128,512]{1,0:T(8,128)(2,1)S(1)}, u32[]{:S(2)}, u32[]{:S(2)}) collective-permute-start(bf16[128,512]{1,0:T(8,128)(2,1)} %refs_0_.4), channel_id=1, source_target_pairs={{0,2},{2,0},{1,3},{3,1},{4,6},{6,4},{5,7},{7,5},{8,10},{10,8},{9,1... | collective-permute-start | bytes 393224 | tf_op jit(solution)/shard_map/ppermute | solution.py:129
  4.2 6.8 %collective-permute-start.2 = (bf16[128,512]{1,0:T(8,128)(2,1)}, bf16[128,512]{1,0:T(8,128)(2,1)S(1)}, u32[]{:S(2)}, u32[]{:S(2)}) collective-permute-start(bf16[128,512]{1,0:T(8,128)(2,1)} %refs_2_.1), channel_id=1, source_target_pairs={{0,2},{2,0},{1,3},{3,1},{4,6},{6,4},{5,7},{7,5},{8,10},{10,8},{9,1... | collective-permute-start | bytes 393224 | tf_op jit(solution)/shard_map/ppermute | solution.py:129
  4.2 0.9 %copy-start.4 = (bf16[128,512]{1,0:T(8,128)(2,1)S(1)}, bf16[128,512]{1,0:T(8,128)(2,1)}, u32[]{:S(2)}) copy-start(bf16[128,512]{1,0:T(8,128)(2,1)} %refs_0_.2) | copy-start | bytes 393220
  5.1 13.5 %collective-permute-start.4 = (bf16[128,1024]{1,0:T(8,128)(2,1)S(1)}, bf16[128,1024]{1,0:T(8,128)(2,1)S(1)}, u32[]{:S(2)}, u32[]{:S(2)}) collective-permute-start(bf16[128,1024]{1,0:T(8,128)(2,1)S(1)} %shard_map.130.refs_3_), channel_id=1, source_target_pairs={{0,4},{1,9},{2,6},{3,11},{4,0},{5,13},{6,2},{7,15},{8,12},{9,1},{1... | collective-permute-start | bytes 786440 | tf_op jit(solution)/shard_map/ppermute | solution.py:370
  8.4 1.2 %copy-start.2 = (bf16[512,1024]{1,0:T(8,128)(2,1)S(1)}, bf16[512,1024]{1,0:T(8,128)(2,1)}, u32[]{:S(2)}) copy-start(bf16[512,1024]{1,0:T(8,128)(2,1)} %refs_0_.3) | copy-start | bytes 3145732
  10.7 0.7 %copy-start.5 = (bf16[128,512]{1,0:T(8,128)(2,1)}, bf16[128,512]{1,0:T(8,128)(2,1)S(1)}, u32[]{:S(2)}) copy-start(bf16[128,512]{1,0:T(8,128)(2,1)S(1)} %collective-permute-done.1.refs_1_) | copy-start | bytes 393220
  10.9 0.7 %copy-start.6 = (bf16[128,512]{1,0:T(8,128)(2,1)}, bf16[128,512]{1,0:T(8,128)(2,1)S(1)}, u32[]{:S(2)}) copy-start(bf16[128,512]{1,0:T(8,128)(2,1)S(1)} %collective-permute-done.2.refs_3_) | copy-start | bytes 393220
  14.3 4.4 %collective-permute-start.3 = (bf16[144,512]{1,0:T(8,128)(2,1)}, bf16[144,512]{1,0:T(8,128)(2,1)S(1)}, u32[]{:S(2)}, u32[]{:S(2)}) collective-permute-start(bf16[144,512]{1,0:T(8,128)(2,1)} %shard_map.132.refs_0_), channel_id=1, source_target_pairs={{0,1},{1,0},{2,3},{3,2},{4,5},{5,4},{6,7},{7,6},{8,9},{9,8},{10,11... | collective-permute-start | bytes 442376 | tf_op jit(solution)/shard_map/ppermute | solution.py:129
  14.9 3.7 %collective-permute-start.6 = (bf16[128,512]{1,0:T(8,128)(2,1)}, bf16[128,512]{1,0:T(8,128)(2,1)S(1)}, u32[]{:S(2)}, u32[]{:S(2)}) collective-permute-start(bf16[128,512]{1,0:T(8,128)(2,1)} %refs_1_.1), channel_id=1, source_target_pairs={{0,1},{1,0},{2,3},{3,2},{4,5},{5,4},{6,7},{7,6},{8,9},{9,8},{10,11... | collective-permute-start | bytes 393224 | tf_op jit(solution)/shard_map/ppermute | solution.py:129
  14.9 8.3 %collective-permute-start.9 = (bf16[128,1024]{1,0:T(8,128)(2,1)S(1)}, bf16[128,1024]{1,0:T(8,128)(2,1)S(1)}, u32[]{:S(2)}, u32[]{:S(2)}) collective-permute-start(bf16[128,1024]{1,0:T(8,128)(2,1)S(1)} %shard_map.130.refs_3_), channel_id=1, source_target_pairs={{0,12},{1,3},{2,14},{3,1},{4,8},{5,7},{6,10},{7,5},{8,4},{9,11},{1... | collective-permute-start | bytes 786440 | tf_op jit(solution)/shard_map/ppermute | solution.py:370
  18.6 0.9 %copy-start.3 = (bf16[144,512]{1,0:T(8,128)(2,1)S(1)}, bf16[144,512]{1,0:T(8,128)(2,1)}, u32[]{:S(2)}) copy-start(bf16[144,512]{1,0:T(8,128)(2,1)} %shard_map.132.refs_0_) | copy-start | bytes 442372
  20.3 9.7 %collective-permute-start.8 = (bf16[128,1024]{1,0:T(8,128)(2,1)S(1)}, bf16[128,1024]{1,0:T(8,128)(2,1)S(1)}, u32[]{:S(2)}, u32[]{:S(2)}) collective-permute-start(bf16[128,1024]{1,0:T(8,128)(2,1)S(1)} %get-tuple-element.47.refs_0_), channel_id=1, source_target_pairs={{0,12},{1,3},{2,14},{3,1},{4,8},{5,7},{6,10},{7,5},{8,4},{9,11},{1... | collective-permute-start | bytes 786440 | tf_op jit(solution)/shard_map/ppermute | solution.py:370
  21.6 10.1 %collective-permute-start.7 = (bf16[128,1024]{1,0:T(8,128)(2,1)S(1)}, bf16[128,1024]{1,0:T(8,128)(2,1)S(1)}, u32[]{:S(2)}, u32[]{:S(2)}) collective-permute-start(bf16[128,1024]{1,0:T(8,128)(2,1)S(1)} %get-tuple-element.47.refs_0_), channel_id=1, source_target_pairs={{0,4},{1,9},{2,6},{3,11},{4,0},{5,13},{6,2},{7,15},{8,12},{9,1},{1... | collective-permute-start | bytes 786440 | tf_op jit(solution)/shard_map/ppermute | solution.py:370
  21.6 10.1 %collective-permute-start.11 = (bf16[128,1024]{1,0:T(8,128)(2,1)S(1)}, bf16[128,1024]{1,0:T(8,128)(2,1)S(1)}, u32[]{:S(2)}, u32[]{:S(2)}) collective-permute-start(bf16[128,1024]{1,0:T(8,128)(2,1)S(1)} %collective-permute-done.4.refs_2_), channel_id=1, source_target_pairs={{0,1},{1,0},{2,3},{3,2},{4,5},{5,4},{6,7},{7,6},{8,9},{9,8},{10,11... | collective-permute-start | bytes 786440 | tf_op jit(solution)/shard_map/ppermute | solution.py:374
  21.8 9.9 %collective-permute-start.10 = (bf16[128,1024]{1,0:T(8,128)(2,1)S(1)}, bf16[128,1024]{1,0:T(8,128)(2,1)S(1)}, u32[]{:S(2)}, u32[]{:S(2)}) collective-permute-start(bf16[128,1024]{1,0:T(8,128)(2,1)S(1)} %collective-permute-done.4.refs_2_), channel_id=1, source_target_pairs={{0,2},{1,3},{2,0},{3,1},{4,6},{5,7},{6,4},{7,5},{8,10},{9,11},{10,... | collective-permute-start | bytes 786440 | tf_op jit(solution)/shard_map/ppermute | solution.py:370
  23.2 13.4 %collective-permute-start.13 = (bf16[128,1024]{1,0:T(8,128)(2,1)S(1)}, bf16[128,1024]{1,0:T(8,128)(2,1)S(1)}, u32[]{:S(2)}, u32[]{:S(2)}) collective-permute-start(bf16[128,1024]{1,0:T(8,128)(2,1)S(1)} %collective-permute-done.9.other_ref.refs_5_.refs_4_), channel_id=1, source_target_pairs={{0,1},{1,0},{2,3},{3,2},{4,5},{5,4},{6,7},{7,6},{8,9},{9,8},{10,11... | collective-permute-start | bytes 786440 | tf_op jit(solution)/shard_map/ppermute | solution.py:374
  31.8 4.8 %collective-permute-start.12 = (bf16[128,1024]{1,0:T(8,128)(2,1)S(1)}, bf16[128,1024]{1,0:T(8,128)(2,1)S(1)}, u32[]{:S(2)}, u32[]{:S(2)}) collective-permute-start(bf16[128,1024]{1,0:T(8,128)(2,1)S(1)} %get-tuple-element.53.refs_2_.refs_0_), channel_id=1, source_target_pairs={{0,1},{1,0},{2,3},{3,2},{4,5},{5,4},{6,7},{7,6},{8,9},{9,8},{10,11... | collective-permute-start | bytes 786440 | tf_op jit(solution)/shard_map/ppermute | solution.py:374
  34.5 6.4 %collective-permute-start.14 = (bf16[128,1024]{1,0:T(8,128)(2,1)S(1)}, bf16[128,1024]{1,0:T(8,128)(2,1)S(1)}, u32[]{:S(2)}, u32[]{:S(2)}) collective-permute-start(bf16[128,1024]{1,0:T(8,128)(2,1)S(1)} %get-tuple-element.58.refs_0_), channel_id=1, source_target_pairs={{0,1},{1,0},{2,3},{3,2},{4,5},{5,4},{6,7},{7,6},{8,9},{9,8},{10,11... | collective-permute-start | bytes 786440 | tf_op jit(solution)/shard_map/ppermute | solution.py:374
  34.6 10.2 %collective-permute-start.19 = (bf16[128,1024]{1,0:T(8,128)(2,1)S(1)}, bf16[128,1024]{1,0:T(8,128)(2,1)S(1)}, u32[]{:S(2)}, u32[]{:S(2)}) collective-permute-start(bf16[128,1024]{1,0:T(8,128)(2,1)S(1)} %get-tuple-element.71), channel_id=1, source_target_pairs={{0,2},{1,3},{2,0},{3,1},{4,6},{5,7},{6,4},{7,5},{8,10},{9,11},{10,... | collective-permute-start | bytes 786440 | tf_op jit(solution)/shard_map/ppermute | solution.py:370
  36.1 9.9 %collective-permute-start.17 = (bf16[128,1024]{1,0:T(8,128)(2,1)S(1)}, bf16[128,1024]{1,0:T(8,128)(2,1)S(1)}, u32[]{:S(2)}, u32[]{:S(2)}) collective-permute-start(bf16[128,1024]{1,0:T(8,128)(2,1)S(1)} %get-tuple-element.53.refs_2_.refs_0_), channel_id=1, source_target_pairs={{0,2},{1,5},{2,0},{3,7},{4,6},{5,1},{6,4},{7,3},{8,10},{9,13},{10,... | collective-permute-start | bytes 786440 | tf_op jit(solution)/shard_map/ppermute | solution.py:370
  38.7 7.8 %collective-permute-start.15 = (bf16[256,512]{1,0:T(8,128)(2,1)S(1)}, bf16[256,512]{1,0:T(8,128)(2,1)S(1)}, u32[]{:S(2)}, u32[]{:S(2)}) collective-permute-start(bf16[256,512]{1,0:T(8,128)(2,1)S(1)} %get-tuple-element.67), channel_id=1, source_target_pairs={{0,1},{1,0},{2,3},{3,2},{4,5},{5,4},{6,7},{7,6},{8,9},{9,8},{10,11... | collective-permute-start | bytes 786440 | tf_op jit(solution)/shard_map/ppermute | solution.py:374
  46.0 2.2 %collective-permute-start.18 = (bf16[128,1024]{1,0:T(8,128)(2,1)S(1)}, bf16[128,1024]{1,0:T(8,128)(2,1)S(1)}, u32[]{:S(2)}, u32[]{:S(2)}) collective-permute-start(bf16[128,1024]{1,0:T(8,128)(2,1)S(1)} %collective-permute-done.17.refs_1_.refs_2_), channel_id=1, source_target_pairs={{0,1},{1,0},{2,3},{3,2},{4,5},{5,4},{6,7},{7,6},{8,9},{9,8},{10,11... | collective-permute-start | bytes 786440 | tf_op jit(solution)/shard_map/ppermute | solution.py:374
  46.1 2.2 %collective-permute-start.20 = (bf16[128,1024]{1,0:T(8,128)(2,1)S(1)}, bf16[128,1024]{1,0:T(8,128)(2,1)S(1)}, u32[]{:S(2)}, u32[]{:S(2)}) collective-permute-start(bf16[128,1024]{1,0:T(8,128)(2,1)S(1)} %collective-permute-done.19.refs_3_.refs_6_), channel_id=1, source_target_pairs={{0,1},{1,0},{2,3},{3,2},{4,5},{5,4},{6,7},{7,6},{8,9},{9,8},{10,11... | collective-permute-start | bytes 786440 | tf_op jit(solution)/shard_map/ppermute | solution.py:374
  46.6 3.2 %collective-permute-start.21 = (bf16[128,1024]{1,0:T(8,128)(2,1)S(1)}, bf16[128,1024]{1,0:T(8,128)(2,1)S(1)}, u32[]{:S(2)}, u32[]{:S(2)}) collective-permute-start(bf16[128,1024]{1,0:T(8,128)(2,1)S(1)} %collective-permute-done.10.refs_4_.refs_7_), channel_id=1, source_target_pairs={{0,1},{1,0},{2,3},{3,2},{4,5},{5,4},{6,7},{7,6},{8,9},{9,8},{10,11... | collective-permute-start | bytes 786440 | tf_op jit(solution)/shard_map/ppermute | solution.py:374
  46.6 6.0 %collective-permute-start.16 = (bf16[128,512]{1,0:T(8,128)(2,1)S(1)}, bf16[128,512]{1,0:T(8,128)(2,1)S(1)}, u32[]{:S(2)}, u32[]{:S(2)}) collective-permute-start(bf16[128,512]{1,0:T(8,128)(2,1)S(1)} %get-tuple-element.69), channel_id=1, source_target_pairs={{0,2},{2,0},{1,3},{3,1},{4,6},{6,4},{5,7},{7,5},{8,10},{10,8},{9,1... | collective-permute-start | bytes 393224 | tf_op jit(solution)/shard_map/ppermute | solution.py:473

commit v10 on v9

--- a/solution.py
+++ b/solution.py
@@ -181,6 +181,11 @@
     half = 0.5 * (1.0 + curve)
     slope = half + 0.5 * pre * (1.0 - curve * curve) * (ROOT * (1.0 + 3.0 * CUBIC * square))
     return pre * half, slope
+
+
+def add_layer(stream_ref, own_ref, other_ref, out_ref):
+    total = stream_ref[...] + own_ref[...] + other_ref[...].astype(jnp.float32)
+    out_ref[...] = total.astype(out_ref.dtype)
 
 
 def feed_forward(choices, share, *refs):
@@ -310,14 +315,10 @@
 
 
 def finish_products(*refs):
-    up_sum, down_sum, stream, own_part, other_part = refs[:5]
-    layer_ref, up_ref, down_ref, layer, buffer, sems = refs[-6:]
-    pairs = refs[5:-6]
+    up_sum, down_sum = refs[:2]
+    up_ref, down_ref, buffer, sems = refs[-4:]
+    pairs = refs[2:-4]
     count = len(pairs) // 4
-    total = stream[...] + own_part[...] + other_part[...].astype(jnp.float32)
-    layer[...] = total.astype(jnp.bfloat16)
-    layer_copy = pltpu.make_async_copy(layer, layer_ref, sems.at[buffer.shape[0]])
-    layer_copy.start()
     copies = []
     for start in range(0, up_ref.shape[0], TILE):
         tile = pl.ds(start, TILE)
@@ -338,7 +339,7 @@
                 pltpu.make_async_copy(buffer.at[slot], out_ref.at[tile], sems.at[slot])
             )
             copies[-1].start()
-    for copy in copies[-buffer.shape[0] :] + [layer_copy]:
+    for copy in copies[-buffer.shape[0] :]:
         copy.wait()
 
 
@@ -449,7 +450,7 @@
     swap12, swap3x = swap(norm12), swap(norm3x)
 
     def pair(choices, blocks, shares=()):
-        made = jax.ShapeDtypeStruct((2 * rows, width), bf16)
+        made = jax.ShapeDtypeStruct((len(choices) * rows, width), bf16)
         return call(
             functools.partial(feed_forward, choices, bool(shares)),
             [made] * 4 + [jax.ShapeDtypeStruct((2 * rows, half), t) for t in shares],
@@ -480,29 +481,31 @@
     far, mixed = after(far, sums[0]), after(mixed, sums[0])
     swap_far, swap_mixed = swap(far), swap(mixed)
     cot_swap_over = swap(cot_over12)
-    over = pair(
-        (2, 2),
-        [swap_far, far, swap_mixed, mixed]
-        + [cot_over12, cot_swap_over, cot_swap_over, cot_over12],
-    )
-    third = pair(
-        (2, 2), [norm3x, swap3x, far, swap_far, cot3x, cot_swap3x, mixed, swap_mixed]
-    )
-    last = list(over) + list(third)
-    parts = [stream, own_part, rest]
-    return pl.pallas_call(
+    last = pair(
+        (2, 2, 2, 2),
+        [swap_far, far, swap_mixed, mixed, norm3x, swap3x, far, swap_far]
+        + [cot_over12, cot_swap_over, cot_swap_over, cot_over12]
+        + [cot3x, cot_swap3x, mixed, swap_mixed],
+    )
+    up_grad, down_grad = pl.pallas_call(
         finish_products,
-        out_shape=(jax.ShapeDtypeStruct((rows, half), bf16),) + grads,
-        in_specs=[pl.BlockSpec(memory_space=pltpu.VMEM)] * (5 + len(last)),
-        out_specs=[pl.BlockSpec(memory_space=pl.ANY)] * 3,
+        out_shape=grads,
+        in_specs=[pl.BlockSpec(memory_space=pltpu.VMEM)] * (2 + len(last)),
+        out_specs=[pl.BlockSpec(memory_space=pl.ANY)] * 2,
         scratch_shapes=[
-            pltpu.VMEM((rows, half), bf16),
-            pltpu.VMEM((4, TILE, width), jnp.float32),
-            pltpu.SemaphoreType.DMA((5,)),
+            pltpu.VMEM((8, TILE, width), jnp.float32),
+            pltpu.SemaphoreType.DMA((8,)),
         ],
         cost_estimate=SMALL,
         compiler_params=pltpu.CompilerParams(vmem_limit_bytes=16 * 2**20),
-    )(*sums, *parts, *last)
+    )(*sums, *last)
+    layer_out = call(
+        add_layer,
+        jax.ShapeDtypeStruct((rows, half), bf16),
+        0,
+        [stream, own_part, after(rest, up_grad)],
+    )
+    return (layer_out, up_grad, down_grad)
 
 
 def layer(*args):

time: 57.3 us -> 55.8 us (0.974)
  waiting for transfers between devices: 11.2 us -> 9.85 us
  Pallas kernels: 18.1 us -> 16.9 us
  local copies, waits for them, and re-layouts: 3.7 us -> 4.6 us
    ppermute x1, waiting for transfers between devices: 1.22 us -> 0.01 us  [gather_plan(): rest = lax.ppermute(sent, 'grp', [(0, 1), (1, 0)])]
    unnamed x14 -> x16, local copies, waits for them, and re-layouts: 3.7 us -> 4.6 us
    pallas_call x1, Pallas kernels: 4.48 us -> 3.84 us  [gather_plan(): pl.pallas_call(finish_products, out_shape=grads, in_specs=[pl.BlockSpec(m...]
  transfers between devices with their start and end apart: 22 -> 22, of which waited for: 6 -> 5; matrix products, arithmetic and copies ran while one was open for 0% -> 0% of each run, Pallas kernels for 24% -> 29%
where the time goes in v10:
time: 55.8 us; the launch traced here: 55.6 us
  starting transfers between devices  22.7 us (41%)
  Pallas kernels  16.9 us (30%)
  waiting for transfers between devices  9.85 us (18%)
  local copies, waits for them, and re-layouts  4.6 us (8%)
  between operations  1.47 us (3%)
    pallas_call x11, Pallas kernels, call(): pl.pallas_call(kernel, out_shape=out_shape, in_specs=[pl.BlockSpec(memory...  13.1 us
    ppermute x7, starting transfers between devices, send(): return lax.ppermute(x, ('patch', 'grp', 'col'), pairs)  11 us
    ppermute x7, waiting for transfers between devices, send(): return lax.ppermute(x, ('patch', 'grp', 'col'), pairs)  9.58 us
    ppermute x8, starting transfers between devices, swap(): return lax.ppermute(x, 'col', [(0, 1), (1, 0)])  5.92 us
    unnamed x16, local copies, waits for them, and re-layouts  4.6 us
    ppermute x6, starting transfers between devices, others(): lax.ppermute(x, axis, [(i, i ^ k) for i in range(n)])  4.21 us
    pallas_call x1, Pallas kernels, gather_plan(): pl.pallas_call(finish_products, out_shape=grads, in_specs=[pl.BlockSpec(m...  3.84 us
    ppermute x1, starting transfers between devices, gather_plan(): rest = lax.ppermute(sent, 'grp', [(0, 1), (1, 0)])  1.61 us
  transfers between devices with their start and end apart: 22, of which 5 were waited for; matrix products, arithmetic and copies ran while one was open for 0% of the time, Pallas kernels for 29%

profile of v10, /device:TPU:0, one launch (start us, length us, event | category | flops | bytes accessed | tf_op | source)
XLA Modules:
  0.0 55.6 jit_solution(9296165371480128920)
XLA Ops:
  0.7 0.5 collective-permute-start.5
  1.2 0.1 collective-permute-start
  1.2 2.9 %collective-permute-start.1 = (bf16[128,512]{1,0:T(8,128)(2,1)}, bf16[128,512]{1,0:T(8,128)(2,1)S(1)}, u32[]{:S(2)}, u32[]{:S(2)}) collective-permute-start(bf16[128,512]{1,0:T(8,128)(2,1)} %refs_0_.4), channel_id=1, source_target_pairs={{0,2},{2,0},{1,3},{3,1},{4,6},{6,4},{5,7},{7,5},{8,10},{10,8},{9,1... | collective-permute-start | bytes 393224 | tf_op jit(solution)/shard_map/ppermute | solution.py:129
  4.2 0.0 collective-permute-start.2
  4.2 0.0 collective-permute-done.refs_1_
  4.2 0.9 %copy-done.5 = bf16[128,512]{1,0:T(8,128)(2,1)S(1)} copy-done((bf16[128,512]{1,0:T(8,128)(2,1)S(1)}, bf16[128,512]{1,0:T(8,128)(2,1)}, u32[]{:S(2)}) %copy-start.5) | copy-done | bytes 131096
  5.1 2.7 %collective-permute-start.4 = (bf16[128,1024]{1,0:T(8,128)(2,1)S(1)}, bf16[128,1024]{1,0:T(8,128)(2,1)S(1)}, u32[]{:S(2)}, u32[]{:S(2)}) collective-permute-start(bf16[128,1024]{1,0:T(8,128)(2,1)S(1)} %shard_map.130.refs_3_), channel_id=1, source_target_pairs={{0,4},{1,9},{2,6},{3,11},{4,0},{5,13},{6,2},{7,15},{8,12},{9,1},{1... | collective-permute-start | bytes 786440 | tf_op jit(solution)/shard_map/ppermute | solution.py:371
  8.4 0.0 copy-start.2
  8.5 1.2 %copy-done.2 = bf16[512,1024]{1,0:T(8,128)(2,1)S(1)} copy-done((bf16[512,1024]{1,0:T(8,128)(2,1)S(1)}, bf16[512,1024]{1,0:T(8,128)(2,1)}, u32[]{:S(2)}) %copy-start.2) | copy-done | bytes 1048600
  9.7 0.9 %copy-done.4 = bf16[128,512]{1,0:T(8,128)(2,1)S(1)} copy-done((bf16[128,512]{1,0:T(8,128)(2,1)S(1)}, bf16[128,512]{1,0:T(8,128)(2,1)}, u32[]{:S(2)}) %copy-start.4) | copy-done | bytes 131096
  10.6 0.1 shard_map.131
  10.7 0.0 copy-start.6
  10.7 0.2 collective-permute-done.2.refs_3_
  10.9 0.4 copy-done.6
  11.3 0.2 copy-done.7
  11.6 2.7 %shard_map.132.refs_0_ = bf16[144,512]{1,0:T(8,128)(2,1)} custom-call(s32[1,2]{1,0:T(1,128)} %ids_ref.1, s32[1]{0:T(128)S(6)} %copy.14.count_ref, f32[1,512]{1,0:T(1,128)} %bitcast.1, bf16[128,512]{1,0:T(8,128)(2,1)} %query_ref, bf16[128,512]{1,0:T(8,128)(2,1)} %refs_0_.4, bf16[128,512]{1,0:T(8,128)(2,1)} %copy-done.6, bf16[128,512]{1,0:T(8,128)(2,1)} %refs_2_.1, ...), custom_call_target="tpu_custom_call" | custom-call | flops 1 | bytes 1 | tf_op jit(solution)/shard_map/pallas_call | solution.py:351
  14.3 0.7 %collective-permute-start.3 = (bf16[144,512]{1,0:T(8,128)(2,1)}, bf16[144,512]{1,0:T(8,128)(2,1)S(1)}, u32[]{:S(2)}, u32[]{:S(2)}) collective-permute-start(bf16[144,512]{1,0:T(8,128)(2,1)} %shard_map.132.refs_0_), channel_id=1, source_target_pairs={{0,1},{1,0},{2,3},{3,2},{4,5},{5,4},{6,7},{7,6},{8,9},{9,8},{10,11... | collective-permute-start | bytes 442376 | tf_op jit(solution)/shard_map/ppermute | solution.py:129
  14.9 0.0 collective-permute-start.6
  14.9 3.7 %collective-permute-start.9 = (bf16[128,1024]{1,0:T(8,128)(2,1)S(1)}, bf16[128,1024]{1,0:T(8,128)(2,1)S(1)}, u32[]{:S(2)}, u32[]{:S(2)}) collective-permute-start(bf16[128,1024]{1,0:T(8,128)(2,1)S(1)} %shard_map.130.refs_3_), channel_id=1, source_target_pairs={{0,12},{1,3},{2,14},{3,1},{4,8},{5,7},{6,10},{7,5},{8,4},{9,11},{1... | collective-permute-start | bytes 786440 | tf_op jit(solution)/shard_map/ppermute | solution.py:371
  18.6 0.0 collective-permute-done.6.refs_5_
  18.6 0.0 collective-permute-done.3.refs_1_
  18.6 0.0 copy-start.3
  18.7 0.9 %copy-done.3 = bf16[144,512]{1,0:T(8,128)(2,1)S(1)} copy-done((bf16[144,512]{1,0:T(8,128)(2,1)S(1)}, bf16[144,512]{1,0:T(8,128)(2,1)}, u32[]{:S(2)}) %copy-start.3) | copy-done | bytes 147480
  19.6 0.7 %shard_map.133 = (f32[128,512]{1,0:T(8,128)S(1)}, bf16[128,1024]{1,0:T(8,128)(2,1)S(1)}) custom-call(bf16[144,512]{1,0:T(8,128)(2,1)S(1)} %copy-done.3, bf16[144,512]{1,0:T(8,128)(2,1)S(1)} %collective-permute-done.3.refs_1_, bf16[512,1024]{1,0:T(8,128)(2,1)S(1)} %get-tuple-element.44.refs_2_, bf16[512,1024]{1,0:T(8,128)(2,1)S(1)} %collective-permute-done.5.refs_3_, ...), custom_call_target="tpu_custom_call" | custom-call | flops 1 | bytes 1 | tf_op jit(solution)/shard_map/pallas_call | solution.py:351
  20.3 1.3 %collective-permute-start.8 = (bf16[128,1024]{1,0:T(8,128)(2,1)S(1)}, bf16[128,1024]{1,0:T(8,128)(2,1)S(1)}, u32[]{:S(2)}, u32[]{:S(2)}) collective-permute-start(bf16[128,1024]{1,0:T(8,128)(2,1)S(1)} %get-tuple-element.47.refs_0_), channel_id=1, source_target_pairs={{0,12},{1,3},{2,14},{3,1},{4,8},{5,7},{6,10},{7,5},{8,4},{9,11},{1... | collective-permute-start | bytes 786440 | tf_op jit(solution)/shard_map/ppermute | solution.py:371
  21.6 0.0 collective-permute-start.7
  21.6 0.2 collective-permute-start.11
  21.8 1.3 %collective-permute-start.10 = (bf16[128,1024]{1,0:T(8,128)(2,1)S(1)}, bf16[128,1024]{1,0:T(8,128)(2,1)S(1)}, u32[]{:S(2)}, u32[]{:S(2)}) collective-permute-start(bf16[128,1024]{1,0:T(8,128)(2,1)S(1)} %collective-permute-done.4.refs_2_), channel_id=1, source_target_pairs={{0,2},{1,3},{2,0},{3,1},{4,6},{5,7},{6,4},{7,5},{8,10},{9,11},{10,... | collective-permute-start | bytes 786440 | tf_op jit(solution)/shard_map/ppermute | solution.py:371
  23.1 0.1 collective-permute-done.9.other_ref.refs_5_.refs_12_
  23.2 0.1 collective-permute-start.13
  23.3 6.6 %collective-permute-done.8.two_ref = bf16[128,1024]{1,0:T(8,128)(2,1)S(1)} collective-permute-done((bf16[128,1024]{1,0:T(8,128)(2,1)S(1)}, bf16[128,1024]{1,0:T(8,128)(2,1)S(1)}, u32[]{:S(2)}, u32[]{:S(2)}) %collective-permute-start.8) | collective-permute-done | bytes 262176 | tf_op jit(solution)/shard_map/ppermute | solution.py:371
  30.0 1.7 %collective-permute-done.7.one_ref = bf16[128,1024]{1,0:T(8,128)(2,1)S(1)} collective-permute-done((bf16[128,1024]{1,0:T(8,128)(2,1)S(1)}, bf16[128,1024]{1,0:T(8,128)(2,1)S(1)}, u32[]{:S(2)}, u32[]{:S(2)}) %collective-permute-start.7) | collective-permute-done | bytes 262176 | tf_op jit(solution)/shard_map/ppermute | solution.py:371
  31.7 0.1 shard_map.134
  31.8 2.7 %collective-permute-start.12 = (bf16[128,1024]{1,0:T(8,128)(2,1)S(1)}, bf16[128,1024]{1,0:T(8,128)(2,1)S(1)}, u32[]{:S(2)}, u32[]{:S(2)}) collective-permute-start(bf16[128,1024]{1,0:T(8,128)(2,1)S(1)} %get-tuple-element.53.refs_2_.refs_4_), channel_id=1, source_target_pairs={{0,1},{1,0},{2,3},{3,2},{4,5},{5,4},{6,7},{7,6},{8,9},{9,8},{10,11... | collective-permute-start | bytes 786440 | tf_op jit(solution)/shard_map/ppermute | solution.py:375
  34.5 0.1 collective-permute-start.16
  34.6 1.5 %collective-permute-start.19 = (bf16[128,1024]{1,0:T(8,128)(2,1)S(1)}, bf16[128,1024]{1,0:T(8,128)(2,1)S(1)}, u32[]{:S(2)}, u32[]{:S(2)}) collective-permute-start(bf16[128,1024]{1,0:T(8,128)(2,1)S(1)} %get-tuple-element.70), channel_id=1, source_target_pairs={{0,2},{1,3},{2,0},{3,1},{4,6},{5,7},{6,4},{7,5},{8,10},{9,11},{10,... | collective-permute-start | bytes 786440 | tf_op jit(solution)/shard_map/ppermute | solution.py:371
  36.1 0.5 collective-permute-start.17
  36.6 2.1 %shard_map.135 = (bf16[256,1024]{1,0:T(8,128)(2,1)S(1)}, bf16[256,1024]{1,0:T(8,128)(2,1)S(1)}, bf16[256,1024]{1,0:T(8,128)(2,1)S(1)}, bf16[256,1024]{1,0:T(8,12...) custom-call(bf16[128,1024]{1,0:T(8,128)(2,1)S(1)} %get-tuple-element.47.refs_0_, ...), custom_call_target="tpu_custom_call" | custom-call | flops 1 | bytes 1 | tf_op jit(solution)/shard_map/pallas_call | solution.py:351
  38.7 2.1 %collective-permute-start.14 = (bf16[256,512]{1,0:T(8,128)(2,1)S(1)}, bf16[256,512]{1,0:T(8,128)(2,1)S(1)}, u32[]{:S(2)}, u32[]{:S(2)}) collective-permute-start(bf16[256,512]{1,0:T(8,128)(2,1)S(1)} %get-tuple-element.55), channel_id=1, source_target_pairs={{0,1},{1,0},{2,3},{3,2},{4,5},{5,4},{6,7},{7,6},{8,9},{9,8},{10,11... | collective-permute-start | bytes 786440 | tf_op jit(solution)/shard_map/ppermute | solution.py:375
  40.9 0.1 collective-permute-start.21
  41.0 1.5 %shard_map.137 = (bf16[256,1024]{1,0:T(8,128)(2,1)S(1)}, bf16[256,1024]{1,0:T(8,128)(2,1)S(1)}, bf16[256,1024]{1,0:T(8,128)(2,1)S(1)}, bf16[256,1024]{1,0:T(8,128)(2,1)S(1)}) custom-call(bf16[128,1024]{1,0:T(8,128)(2,1)S(1)} %get-tuple-element.62.refs_0_, bf16[128,1024]{1,0:T(8,128)(2,1)S(1)} %collective-permute-done.16.refs_1_, ...), custom_call_target="tpu_custom_call" | custom-call | flops 1 | bytes 1 | tf_op jit(solution)/shard_map/pallas_call | solution.py:351
  42.5 2.4 %shard_map.138 = (f32[1024,1024]{1,0:T(8,128)S(1)}, f32[1024,1024]{1,0:T(8,128)S(1)}) custom-call(bf16[256,1024]{1,0:T(8,128)(2,1)S(1)} %get-tuple-element.58.refs_0_, bf16[256,1024]{1,0:T(8,128)(2,1)S(1)} %get-tuple-element.59.refs_1_, bf16[256,1024]{1,0:T(8,128)(2,1)S(1)} %get-tuple-element.60.refs_2_, bf16[256,1024]{1,0:T(8,128)(2,1)S(1)} %get-tuple-element.61.refs_3_, ...), custom_call_target="tpu_custom_call" | custom-call | flops 1 | bytes 1 | tf_op jit(solution)/shard_map/pallas_call | solution.py:351
  44.9 1.1 %collective-permute-done.17.refs_1_.refs_6_ = bf16[128,1024]{1,0:T(8,128)(2,1)S(1)} collective-permute-done((bf16[128,1024]{1,0:T(8,128)(2,1)S(1)}, bf16[128,1024]{1,0:T(8,128)(2,1)S(1)}, u32[]{:S(2)}, u32[]{:S(2)}) %collective-permute-start.17) | collective-permute-done | bytes 262176 | tf_op jit(solution)/shard_map/ppermute | solution.py:371
  46.1 0.5 collective-permute-start.20
  46.6 1.6 %collective-permute-start.15 = (bf16[128,512]{1,0:T(8,128)(2,1)S(1)}, bf16[128,512]{1,0:T(8,128)(2,1)S(1)}, u32[]{:S(2)}, u32[]{:S(2)}) collective-permute-start(bf16[128,512]{1,0:T(8,128)(2,1)S(1)} %get-tuple-element.57), channel_id=1, source_target_pairs={{0,2},{2,0},{1,3},{3,1},{4,6},{6,4},{5,7},{7,5},{8,10},{10,8},{9,1... | collective-permute-start | bytes 393224 | tf_op jit(solution)/shard_map/ppermute | solution.py:474
  48.2 2.8 %shard_map.139 = (bf16[512,1024]{1,0:T(8,128)(2,1)S(1)}, bf16[512,1024]{1,0:T(8,128)(2,1)S(1)}, bf16[512,1024]{1,0:T(8,128)(2,1)S(1)}, bf16[512,1024]{1,0:T(8,128)(2,1)S(1)}) custom-call(bf16[128,1024]{1,0:T(8,128)(2,1)S(1)} %collective-permute-done.18.refs_0_.refs_7_, bf16[128,1024]{1,0:T(8,128)(2,1)S(1)} %collective-permute-done.17.refs_1_.refs_6_, ...), custom_call_target="tpu_custom_call" | custom-call | flops 1 | bytes 1 | tf_op jit(solution)/shard_map/pallas_call | solution.py:351
  51.0 3.8 %shard_map.140 = (f32[1024,1024]{1,0:T(8,128)}, f32[1024,1024]{1,0:T(8,128)}) custom-call(f32[1024,1024]{1,0:T(8,128)S(1)} %get-tuple-element.67.refs_0_, f32[1024,1024]{1,0:T(8,128)S(1)} %get-tuple-element.68.refs_1_, bf16[512,1024]{1,0:T(8,128)(2,1)S(1)} %get-tuple-element.72.refs_2_, bf16[512,1024]{1,0:T(8,128)(2,1)S(1)} %get-tuple-element.73.refs_3_, ...), custom_call_target="tpu_custom_call" | custom-call | flops 1 | bytes 1 | tf_op jit(solution)/shard_map/pallas_call | solution.py:490
  54.9 0.7 %shard_map.141 = bf16[128,512]{1,0:T(8,128)(2,1)} custom-call(f32[128,512]{1,0:T(8,128)S(1)} %get-tuple-element.46.stream_ref, f32[128,512]{1,0:T(8,128)S(1)} %get-tuple-element.56.own_ref, bf16[128,512]{1,0:T(8,128)(2,1)S(1)} %collective-permute-done.15.other_ref), custom_call_target="tpu_custom_call" | custom-call | flops 1 | bytes 1 | tf_op jit(solution)/shard_map/pallas_call | solution.py:351
  (24 shorter events, 0.1 us)
Async XLA Ops:
  0.6 36.0 %copy-start.1 = (bf16[1024,1024]{1,0:T(8,128)(2,1)S(1)}, bf16[1024,1024]{1,0:T(8,128)(2,1)}, u32[]{:S(2)}) copy-start(bf16[1024,1024]{1,0:T(8,128)(2,1)} %refs_17_.1) | copy-start | bytes 6291460
  0.6 36.0 %copy-start = (bf16[1024,1024]{1,0:T(8,128)(2,1)S(1)}, bf16[1024,1024]{1,0:T(8,128)(2,1)}, u32[]{:S(2)}) copy-start(bf16[1024,1024]{1,0:T(8,128)(2,1)} %refs_16_.1) | copy-start | bytes 6291460
  0.7 18.0 %collective-permute-start.5 = (bf16[512,1024]{1,0:T(8,128)(2,1)}, bf16[512,1024]{1,0:T(8,128)(2,1)S(1)}, u32[]{:S(2)}, u32[]{:S(2)}) collective-permute-start(bf16[512,1024]{1,0:T(8,128)(2,1)} %refs_0_.3), channel_id=1, source_target_pairs={{0,1},{1,0},{2,3},{3,2},{4,5},{5,4},{6,7},{7,6},{8,9},{9,8},{10,11... | collective-permute-start | bytes 3145736 | tf_op jit(solution)/shard_map/ppermute | solution.py:129
  1.2 3.0 %collective-permute-start = (bf16[128,512]{1,0:T(8,128)(2,1)}, bf16[128,512]{1,0:T(8,128)(2,1)S(1)}, u32[]{:S(2)}, u32[]{:S(2)}) collective-permute-start(bf16[128,512]{1,0:T(8,128)(2,1)} %refs_0_.2), channel_id=1, source_target_pairs={{0,1},{1,0},{2,3},{3,2},{4,5},{5,4},{6,7},{7,6},{8,9},{9,8},{10,11... | collective-permute-start | bytes 393224 | tf_op jit(solution)/shard_map/ppermute | solution.py:129
  1.2 9.4 %collective-permute-start.1 = (bf16[128,512]{1,0:T(8,128)(2,1)}, bf16[128,512]{1,0:T(8,128)(2,1)S(1)}, u32[]{:S(2)}, u32[]{:S(2)}) collective-permute-start(bf16[128,512]{1,0:T(8,128)(2,1)} %refs_0_.4), channel_id=1, source_target_pairs={{0,2},{2,0},{1,3},{3,1},{4,6},{6,4},{5,7},{7,5},{8,10},{10,8},{9,1... | collective-permute-start | bytes 393224 | tf_op jit(solution)/shard_map/ppermute | solution.py:129
  4.2 6.8 %collective-permute-start.2 = (bf16[128,512]{1,0:T(8,128)(2,1)}, bf16[128,512]{1,0:T(8,128)(2,1)S(1)}, u32[]{:S(2)}, u32[]{:S(2)}) collective-permute-start(bf16[128,512]{1,0:T(8,128)(2,1)} %refs_2_.1), channel_id=1, source_target_pairs={{0,2},{2,0},{1,3},{3,1},{4,6},{6,4},{5,7},{7,5},{8,10},{10,8},{9,1... | collective-permute-start | bytes 393224 | tf_op jit(solution)/shard_map/ppermute | solution.py:129
  4.2 0.9 %copy-start.5 = (bf16[128,512]{1,0:T(8,128)(2,1)S(1)}, bf16[128,512]{1,0:T(8,128)(2,1)}, u32[]{:S(2)}) copy-start(bf16[128,512]{1,0:T(8,128)(2,1)} %refs_0_.2) | copy-start | bytes 393220
  5.1 13.5 %collective-permute-start.4 = (bf16[128,1024]{1,0:T(8,128)(2,1)S(1)}, bf16[128,1024]{1,0:T(8,128)(2,1)S(1)}, u32[]{:S(2)}, u32[]{:S(2)}) collective-permute-start(bf16[128,1024]{1,0:T(8,128)(2,1)S(1)} %shard_map.130.refs_3_), channel_id=1, source_target_pairs={{0,4},{1,9},{2,6},{3,11},{4,0},{5,13},{6,2},{7,15},{8,12},{9,1},{1... | collective-permute-start | bytes 786440 | tf_op jit(solution)/shard_map/ppermute | solution.py:371
  8.4 1.2 %copy-start.2 = (bf16[512,1024]{1,0:T(8,128)(2,1)S(1)}, bf16[512,1024]{1,0:T(8,128)(2,1)}, u32[]{:S(2)}) copy-start(bf16[512,1024]{1,0:T(8,128)(2,1)} %refs_0_.3) | copy-start | bytes 3145732
  9.7 0.9 %copy-start.4 = (bf16[128,512]{1,0:T(8,128)(2,1)S(1)}, bf16[128,512]{1,0:T(8,128)(2,1)}, u32[]{:S(2)}) copy-start(bf16[128,512]{1,0:T(8,128)(2,1)} %refs_1_.1) | copy-start | bytes 393220
  10.7 0.7 %copy-start.6 = (bf16[128,512]{1,0:T(8,128)(2,1)}, bf16[128,512]{1,0:T(8,128)(2,1)S(1)}, u32[]{:S(2)}) copy-start(bf16[128,512]{1,0:T(8,128)(2,1)S(1)} %collective-permute-done.1.refs_1_) | copy-start | bytes 393220
  10.9 0.7 %copy-start.7 = (bf16[128,512]{1,0:T(8,128)(2,1)}, bf16[128,512]{1,0:T(8,128)(2,1)S(1)}, u32[]{:S(2)}) copy-start(bf16[128,512]{1,0:T(8,128)(2,1)S(1)} %collective-permute-done.2.refs_3_) | copy-start | bytes 393220
  14.3 4.4 %collective-permute-start.3 = (bf16[144,512]{1,0:T(8,128)(2,1)}, bf16[144,512]{1,0:T(8,128)(2,1)S(1)}, u32[]{:S(2)}, u32[]{:S(2)}) collective-permute-start(bf16[144,512]{1,0:T(8,128)(2,1)} %shard_map.132.refs_0_), channel_id=1, source_target_pairs={{0,1},{1,0},{2,3},{3,2},{4,5},{5,4},{6,7},{7,6},{8,9},{9,8},{10,11... | collective-permute-start | bytes 442376 | tf_op jit(solution)/shard_map/ppermute | solution.py:129
  14.9 3.7 %collective-permute-start.6 = (bf16[128,512]{1,0:T(8,128)(2,1)}, bf16[128,512]{1,0:T(8,128)(2,1)S(1)}, u32[]{:S(2)}, u32[]{:S(2)}) collective-permute-start(bf16[128,512]{1,0:T(8,128)(2,1)} %refs_1_.1), channel_id=1, source_target_pairs={{0,1},{1,0},{2,3},{3,2},{4,5},{5,4},{6,7},{7,6},{8,9},{9,8},{10,11... | collective-permute-start | bytes 393224 | tf_op jit(solution)/shard_map/ppermute | solution.py:129
  14.9 8.3 %collective-permute-start.9 = (bf16[128,1024]{1,0:T(8,128)(2,1)S(1)}, bf16[128,1024]{1,0:T(8,128)(2,1)S(1)}, u32[]{:S(2)}, u32[]{:S(2)}) collective-permute-start(bf16[128,1024]{1,0:T(8,128)(2,1)S(1)} %shard_map.130.refs_3_), channel_id=1, source_target_pairs={{0,12},{1,3},{2,14},{3,1},{4,8},{5,7},{6,10},{7,5},{8,4},{9,11},{1... | collective-permute-start | bytes 786440 | tf_op jit(solution)/shard_map/ppermute | solution.py:371
  18.6 0.9 %copy-start.3 = (bf16[144,512]{1,0:T(8,128)(2,1)S(1)}, bf16[144,512]{1,0:T(8,128)(2,1)}, u32[]{:S(2)}) copy-start(bf16[144,512]{1,0:T(8,128)(2,1)} %shard_map.132.refs_0_) | copy-start | bytes 442372
  20.3 9.7 %collective-permute-start.8 = (bf16[128,1024]{1,0:T(8,128)(2,1)S(1)}, bf16[128,1024]{1,0:T(8,128)(2,1)S(1)}, u32[]{:S(2)}, u32[]{:S(2)}) collective-permute-start(bf16[128,1024]{1,0:T(8,128)(2,1)S(1)} %get-tuple-element.47.refs_0_), channel_id=1, source_target_pairs={{0,12},{1,3},{2,14},{3,1},{4,8},{5,7},{6,10},{7,5},{8,4},{9,11},{1... | collective-permute-start | bytes 786440 | tf_op jit(solution)/shard_map/ppermute | solution.py:371
  21.6 10.1 %collective-permute-start.7 = (bf16[128,1024]{1,0:T(8,128)(2,1)S(1)}, bf16[128,1024]{1,0:T(8,128)(2,1)S(1)}, u32[]{:S(2)}, u32[]{:S(2)}) collective-permute-start(bf16[128,1024]{1,0:T(8,128)(2,1)S(1)} %get-tuple-element.47.refs_0_), channel_id=1, source_target_pairs={{0,4},{1,9},{2,6},{3,11},{4,0},{5,13},{6,2},{7,15},{8,12},{9,1},{1... | collective-permute-start | bytes 786440 | tf_op jit(solution)/shard_map/ppermute | solution.py:371
  21.6 10.1 %collective-permute-start.11 = (bf16[128,1024]{1,0:T(8,128)(2,1)S(1)}, bf16[128,1024]{1,0:T(8,128)(2,1)S(1)}, u32[]{:S(2)}, u32[]{:S(2)}) collective-permute-start(bf16[128,1024]{1,0:T(8,128)(2,1)S(1)} %collective-permute-done.4.refs_2_), channel_id=1, source_target_pairs={{0,1},{1,0},{2,3},{3,2},{4,5},{5,4},{6,7},{7,6},{8,9},{9,8},{10,11... | collective-permute-start | bytes 786440 | tf_op jit(solution)/shard_map/ppermute | solution.py:375
  21.8 9.9 %collective-permute-start.10 = (bf16[128,1024]{1,0:T(8,128)(2,1)S(1)}, bf16[128,1024]{1,0:T(8,128)(2,1)S(1)}, u32[]{:S(2)}, u32[]{:S(2)}) collective-permute-start(bf16[128,1024]{1,0:T(8,128)(2,1)S(1)} %collective-permute-done.4.refs_2_), channel_id=1, source_target_pairs={{0,2},{1,3},{2,0},{3,1},{4,6},{5,7},{6,4},{7,5},{8,10},{9,11},{10,... | collective-permute-start | bytes 786440 | tf_op jit(solution)/shard_map/ppermute | solution.py:371
  23.2 13.4 %collective-permute-start.13 = (bf16[128,1024]{1,0:T(8,128)(2,1)S(1)}, bf16[128,1024]{1,0:T(8,128)(2,1)S(1)}, u32[]{:S(2)}, u32[]{:S(2)}) collective-permute-start(bf16[128,1024]{1,0:T(8,128)(2,1)S(1)} %collective-permute-done.9.other_ref.refs_5_.refs_12_), channel_id=1, source_target_pairs={{0,1},{1,0},{2,3},{3,2},{4,5},{5,4},{6,7},{7,6},{8,9},{9,8},{10,11... | collective-permute-start | bytes 786440 | tf_op jit(solution)/shard_map/ppermute | solution.py:375
  31.8 4.8 %collective-permute-start.12 = (bf16[128,1024]{1,0:T(8,128)(2,1)S(1)}, bf16[128,1024]{1,0:T(8,128)(2,1)S(1)}, u32[]{:S(2)}, u32[]{:S(2)}) collective-permute-start(bf16[128,1024]{1,0:T(8,128)(2,1)S(1)} %get-tuple-element.53.refs_2_.refs_4_), channel_id=1, source_target_pairs={{0,1},{1,0},{2,3},{3,2},{4,5},{5,4},{6,7},{7,6},{8,9},{9,8},{10,11... | collective-permute-start | bytes 786440 | tf_op jit(solution)/shard_map/ppermute | solution.py:375
  34.5 6.5 %collective-permute-start.16 = (bf16[128,1024]{1,0:T(8,128)(2,1)S(1)}, bf16[128,1024]{1,0:T(8,128)(2,1)S(1)}, u32[]{:S(2)}, u32[]{:S(2)}) collective-permute-start(bf16[128,1024]{1,0:T(8,128)(2,1)S(1)} %get-tuple-element.62.refs_0_), channel_id=1, source_target_pairs={{0,1},{1,0},{2,3},{3,2},{4,5},{5,4},{6,7},{7,6},{8,9},{9,8},{10,11... | collective-permute-start | bytes 786440 | tf_op jit(solution)/shard_map/ppermute | solution.py:375
  34.6 10.3 %collective-permute-start.19 = (bf16[128,1024]{1,0:T(8,128)(2,1)S(1)}, bf16[128,1024]{1,0:T(8,128)(2,1)S(1)}, u32[]{:S(2)}, u32[]{:S(2)}) collective-permute-start(bf16[128,1024]{1,0:T(8,128)(2,1)S(1)} %get-tuple-element.70), channel_id=1, source_target_pairs={{0,2},{1,3},{2,0},{3,1},{4,6},{5,7},{6,4},{7,5},{8,10},{9,11},{10,... | collective-permute-start | bytes 786440 | tf_op jit(solution)/shard_map/ppermute | solution.py:371
  36.1 9.9 %collective-permute-start.17 = (bf16[128,1024]{1,0:T(8,128)(2,1)S(1)}, bf16[128,1024]{1,0:T(8,128)(2,1)S(1)}, u32[]{:S(2)}, u32[]{:S(2)}) collective-permute-start(bf16[128,1024]{1,0:T(8,128)(2,1)S(1)} %get-tuple-element.53.refs_2_.refs_4_), channel_id=1, source_target_pairs={{0,2},{1,5},{2,0},{3,7},{4,6},{5,1},{6,4},{7,3},{8,10},{9,13},{10,... | collective-permute-start | bytes 786440 | tf_op jit(solution)/shard_map/ppermute | solution.py:371
  38.7 7.8 %collective-permute-start.14 = (bf16[256,512]{1,0:T(8,128)(2,1)S(1)}, bf16[256,512]{1,0:T(8,128)(2,1)S(1)}, u32[]{:S(2)}, u32[]{:S(2)}) collective-permute-start(bf16[256,512]{1,0:T(8,128)(2,1)S(1)} %get-tuple-element.55), channel_id=1, source_target_pairs={{0,1},{1,0},{2,3},{3,2},{4,5},{5,4},{6,7},{7,6},{8,9},{9,8},{10,11... | collective-permute-start | bytes 786440 | tf_op jit(solution)/shard_map/ppermute | solution.py:375
  40.9 7.3 %collective-permute-start.21 = (bf16[128,1024]{1,0:T(8,128)(2,1)S(1)}, bf16[128,1024]{1,0:T(8,128)(2,1)S(1)}, u32[]{:S(2)}, u32[]{:S(2)}) collective-permute-start(bf16[128,1024]{1,0:T(8,128)(2,1)S(1)} %collective-permute-done.10.refs_8_.refs_11_), channel_id=1, source_target_pairs={{0,1},{1,0},{2,3},{3,2},{4,5},{5,4},{6,7},{7,6},{8,9},{9,8},{10,11... | collective-permute-start | bytes 786440 | tf_op jit(solution)/shard_map/ppermute | solution.py:375
  46.0 2.2 %collective-permute-start.18 = (bf16[128,1024]{1,0:T(8,128)(2,1)S(1)}, bf16[128,1024]{1,0:T(8,128)(2,1)S(1)}, u32[]{:S(2)}, u32[]{:S(2)}) collective-permute-start(bf16[128,1024]{1,0:T(8,128)(2,1)S(1)} %collective-permute-done.17.refs_1_.refs_6_), channel_id=1, source_target_pairs={{0,1},{1,0},{2,3},{3,2},{4,5},{5,4},{6,7},{7,6},{8,9},{9,8},{10,11... | collective-permute-start | bytes 786440 | tf_op jit(solution)/shard_map/ppermute | solution.py:375
  46.1 2.2 %collective-permute-start.20 = (bf16[128,1024]{1,0:T(8,128)(2,1)S(1)}, bf16[128,1024]{1,0:T(8,128)(2,1)S(1)}, u32[]{:S(2)}, u32[]{:S(2)}) collective-permute-start(bf16[128,1024]{1,0:T(8,128)(2,1)S(1)} %collective-permute-done.19.refs_3_.refs_14_), channel_id=1, source_target_pairs={{0,1},{1,0},{2,3},{3,2},{4,5},{5,4},{6,7},{7,6},{8,9},{9,8},{10,11... | collective-permute-start | bytes 786440 | tf_op jit(solution)/shard_map/ppermute | solution.py:375
  46.6 8.3 %collective-permute-start.15 = (bf16[128,512]{1,0:T(8,128)(2,1)S(1)}, bf16[128,512]{1,0:T(8,128)(2,1)S(1)}, u32[]{:S(2)}, u32[]{:S(2)}) collective-permute-start(bf16[128,512]{1,0:T(8,128)(2,1)S(1)} %get-tuple-element.57), channel_id=1, source_target_pairs={{0,2},{2,0},{1,3},{3,1},{4,6},{6,4},{5,7},{7,5},{8,10},{10,8},{9,1... | collective-permute-start | bytes 393224 | tf_op jit(solution)/shard_map/ppermute | solution.py:474

commit v11 on v10

--- a/solution.py
+++ b/solution.py
@@ -110,7 +110,7 @@
 TILE = 256
 PANEL_TILE = 512
 ROOT, CUBIC = 0.7978845608028654, 0.044715
-OWN_LIMIT = 56 * 2**20
+OWN_LIMIT = 54 * 2**20
 
 
 def shift(x, axis, k):
@@ -344,7 +344,7 @@
 
 
 SMALL = pl.CostEstimate(flops=1, bytes_accessed=1, transcendentals=0)
-LARGE = pl.CostEstimate(flops=10**8, bytes_accessed=1, transcendentals=0)
+LARGE = pl.CostEstimate(flops=10**9, bytes_accessed=1, transcendentals=0)
 
 
 def call(kernel, out_shape, smem, args, scratch=(), limit=16 * 2**20, cost=SMALL):

time: 55.8 us -> 55.8 us (level)
  no operation moved by 1% of the time
where the time goes in v11:
time: 55.8 us; the launch traced here: 55.5 us
  starting transfers between devices  22.7 us (41%)
  Pallas kernels  16.9 us (30%)
  waiting for transfers between devices  9.84 us (18%)
  local copies, waits for them, and re-layouts  4.6 us (8%)
  between operations  1.46 us (3%)
    pallas_call x11, Pallas kernels, call(): pl.pallas_call(kernel, out_shape=out_shape, in_specs=[pl.BlockSpec(memory...  13.1 us
    ppermute x7, starting transfers between devices, send(): return lax.ppermute(x, ('patch', 'grp', 'col'), pairs)  10.9 us
    ppermute x7, waiting for transfers between devices, send(): return lax.ppermute(x, ('patch', 'grp', 'col'), pairs)  9.59 us
    ppermute x8, starting transfers between devices, swap(): return lax.ppermute(x, 'col', [(0, 1), (1, 0)])  5.93 us
    unnamed x16, local copies, waits for them, and re-layouts  4.6 us
    ppermute x6, starting transfers between devices, others(): lax.ppermute(x, axis, [(i, i ^ k) for i in range(n)])  4.24 us
    pallas_call x1, Pallas kernels, gather_plan(): pl.pallas_call(finish_products, out_shape=grads, in_specs=[pl.BlockSpec(m...  3.84 us
    ppermute x1, starting transfers between devices, gather_plan(): rest = lax.ppermute(sent, 'grp', [(0, 1), (1, 0)])  1.58 us
  transfers between devices with their start and end apart: 22, of which 5 were waited for; matrix products, arithmetic and copies ran while one was open for 0% of the time, Pallas kernels for 29%

profile of v11, /device:TPU:0, one launch (start us, length us, event | category | flops | bytes accessed | tf_op | source)
XLA Modules:
  0.0 55.5 jit_solution(2042356974827931426)
XLA Ops:
  0.6 0.5 collective-permute-start.5
  1.1 0.1 collective-permute-start
  1.2 2.9 %collective-permute-start.1 = (bf16[128,512]{1,0:T(8,128)(2,1)}, bf16[128,512]{1,0:T(8,128)(2,1)S(1)}, u32[]{:S(2)}, u32[]{:S(2)}) collective-permute-start(bf16[128,512]{1,0:T(8,128)(2,1)} %refs_0_.4), channel_id=1, source_target_pairs={{0,2},{2,0},{1,3},{3,1},{4,6},{6,4},{5,7},{7,5},{8,10},{10,8},{9,1... | collective-permute-start | bytes 393224 | tf_op jit(solution)/shard_map/ppermute | solution.py:129
  4.1 0.0 collective-permute-start.2
  4.2 0.0 collective-permute-done.refs_1_
  4.2 0.9 %copy-done.5 = bf16[128,512]{1,0:T(8,128)(2,1)S(1)} copy-done((bf16[128,512]{1,0:T(8,128)(2,1)S(1)}, bf16[128,512]{1,0:T(8,128)(2,1)}, u32[]{:S(2)}) %copy-start.5) | copy-done | bytes 131096
  5.1 0.0 copy-start
  5.1 0.0 copy-start.1
  5.1 2.7 %collective-permute-start.4 = (bf16[128,1024]{1,0:T(8,128)(2,1)S(1)}, bf16[128,1024]{1,0:T(8,128)(2,1)S(1)}, u32[]{:S(2)}, u32[]{:S(2)}) collective-permute-start(bf16[128,1024]{1,0:T(8,128)(2,1)S(1)} %shard_map.130.refs_3_), channel_id=1, source_target_pairs={{0,4},{1,9},{2,6},{3,11},{4,0},{5,13},{6,2},{7,15},{8,12},{9,1},{1... | collective-permute-start | bytes 786440 | tf_op jit(solution)/shard_map/ppermute | solution.py:371
  8.5 0.0 copy-start.2
  8.5 1.2 %copy-done.2 = bf16[512,1024]{1,0:T(8,128)(2,1)S(1)} copy-done((bf16[512,1024]{1,0:T(8,128)(2,1)S(1)}, bf16[512,1024]{1,0:T(8,128)(2,1)}, u32[]{:S(2)}) %copy-start.2) | copy-done | bytes 1048600
  9.7 0.9 %copy-done.4 = bf16[128,512]{1,0:T(8,128)(2,1)S(1)} copy-done((bf16[128,512]{1,0:T(8,128)(2,1)S(1)}, bf16[128,512]{1,0:T(8,128)(2,1)}, u32[]{:S(2)}) %copy-start.4) | copy-done | bytes 131096
  10.6 0.1 shard_map.131
  10.7 0.0 collective-permute-done.1.refs_1_
  10.7 0.0 copy-start.6
  10.7 0.2 collective-permute-done.2.refs_3_
  10.9 0.4 copy-done.6
  11.3 0.2 copy-done.7
  11.6 2.7 %shard_map.132.refs_0_ = bf16[144,512]{1,0:T(8,128)(2,1)} custom-call(s32[1,2]{1,0:T(1,128)} %ids_ref.1, s32[1]{0:T(128)S(6)} %copy.14.count_ref, f32[1,512]{1,0:T(1,128)} %bitcast.1, bf16[128,512]{1,0:T(8,128)(2,1)} %query_ref, bf16[128,512]{1,0:T(8,128)(2,1)} %refs_0_.4, bf16[128,512]{1,0:T(8,128)(2,1)} %copy-done.6, bf16[128,512]{1,0:T(8,128)(2,1)} %refs_2_.1, ...), custom_call_target="tpu_custom_call" | custom-call | flops 1 | bytes 1 | tf_op jit(solution)/shard_map/pallas_call | solution.py:351
  14.2 0.7 %collective-permute-start.3 = (bf16[144,512]{1,0:T(8,128)(2,1)}, bf16[144,512]{1,0:T(8,128)(2,1)S(1)}, u32[]{:S(2)}, u32[]{:S(2)}) collective-permute-start(bf16[144,512]{1,0:T(8,128)(2,1)} %shard_map.132.refs_0_), channel_id=1, source_target_pairs={{0,1},{1,0},{2,3},{3,2},{4,5},{5,4},{6,7},{7,6},{8,9},{9,8},{10,11... | collective-permute-start | bytes 442376 | tf_op jit(solution)/shard_map/ppermute | solution.py:129
  14.9 0.0 collective-permute-start.6
  14.9 3.7 %collective-permute-start.9 = (bf16[128,1024]{1,0:T(8,128)(2,1)S(1)}, bf16[128,1024]{1,0:T(8,128)(2,1)S(1)}, u32[]{:S(2)}, u32[]{:S(2)}) collective-permute-start(bf16[128,1024]{1,0:T(8,128)(2,1)S(1)} %shard_map.130.refs_3_), channel_id=1, source_target_pairs={{0,12},{1,3},{2,14},{3,1},{4,8},{5,7},{6,10},{7,5},{8,4},{9,11},{1... | collective-permute-start | bytes 786440 | tf_op jit(solution)/shard_map/ppermute | solution.py:371
  18.6 0.0 copy-start.3
  18.6 0.9 %copy-done.3 = bf16[144,512]{1,0:T(8,128)(2,1)S(1)} copy-done((bf16[144,512]{1,0:T(8,128)(2,1)S(1)}, bf16[144,512]{1,0:T(8,128)(2,1)}, u32[]{:S(2)}) %copy-start.3) | copy-done | bytes 147480
  19.5 0.8 %shard_map.133 = (f32[128,512]{1,0:T(8,128)S(1)}, bf16[128,1024]{1,0:T(8,128)(2,1)S(1)}) custom-call(bf16[144,512]{1,0:T(8,128)(2,1)S(1)} %copy-done.3, bf16[144,512]{1,0:T(8,128)(2,1)S(1)} %collective-permute-done.3.refs_1_, bf16[512,1024]{1,0:T(8,128)(2,1)S(1)} %get-tuple-element.44.refs_2_, bf16[512,1024]{1,0:T(8,128)(2,1)S(1)} %collective-permute-done.5.refs_3_, ...), custom_call_target="tpu_custom_call" | custom-call | flops 1 | bytes 1 | tf_op jit(solution)/shard_map/pallas_call | solution.py:351
  20.3 1.3 %collective-permute-start.8 = (bf16[128,1024]{1,0:T(8,128)(2,1)S(1)}, bf16[128,1024]{1,0:T(8,128)(2,1)S(1)}, u32[]{:S(2)}, u32[]{:S(2)}) collective-permute-start(bf16[128,1024]{1,0:T(8,128)(2,1)S(1)} %get-tuple-element.47.refs_0_), channel_id=1, source_target_pairs={{0,12},{1,3},{2,14},{3,1},{4,8},{5,7},{6,10},{7,5},{8,4},{9,11},{1... | collective-permute-start | bytes 786440 | tf_op jit(solution)/shard_map/ppermute | solution.py:371
  21.6 0.2 collective-permute-start.11
  21.8 1.3 %collective-permute-start.10 = (bf16[128,1024]{1,0:T(8,128)(2,1)S(1)}, bf16[128,1024]{1,0:T(8,128)(2,1)S(1)}, u32[]{:S(2)}, u32[]{:S(2)}) collective-permute-start(bf16[128,1024]{1,0:T(8,128)(2,1)S(1)} %collective-permute-done.4.refs_2_), channel_id=1, source_target_pairs={{0,2},{1,3},{2,0},{3,1},{4,6},{5,7},{6,4},{7,5},{8,10},{9,11},{10,... | collective-permute-start | bytes 786440 | tf_op jit(solution)/shard_map/ppermute | solution.py:371
  23.1 0.1 collective-permute-done.9.other_ref.refs_5_.refs_12_
  23.2 0.1 collective-permute-start.13
  23.3 6.7 %collective-permute-done.8.two_ref = bf16[128,1024]{1,0:T(8,128)(2,1)S(1)} collective-permute-done((bf16[128,1024]{1,0:T(8,128)(2,1)S(1)}, bf16[128,1024]{1,0:T(8,128)(2,1)S(1)}, u32[]{:S(2)}, u32[]{:S(2)}) %collective-permute-start.8) | collective-permute-done | bytes 262176 | tf_op jit(solution)/shard_map/ppermute | solution.py:371
  30.0 1.7 %collective-permute-done.7.one_ref = bf16[128,1024]{1,0:T(8,128)(2,1)S(1)} collective-permute-done((bf16[128,1024]{1,0:T(8,128)(2,1)S(1)}, bf16[128,1024]{1,0:T(8,128)(2,1)S(1)}, u32[]{:S(2)}, u32[]{:S(2)}) %collective-permute-start.7) | collective-permute-done | bytes 262176 | tf_op jit(solution)/shard_map/ppermute | solution.py:371
  31.6 0.1 shard_map.134
  31.7 2.8 %collective-permute-start.12 = (bf16[128,1024]{1,0:T(8,128)(2,1)S(1)}, bf16[128,1024]{1,0:T(8,128)(2,1)S(1)}, u32[]{:S(2)}, u32[]{:S(2)}) collective-permute-start(bf16[128,1024]{1,0:T(8,128)(2,1)S(1)} %get-tuple-element.53.refs_2_.refs_4_), channel_id=1, source_target_pairs={{0,1},{1,0},{2,3},{3,2},{4,5},{5,4},{6,7},{7,6},{8,9},{9,8},{10,11... | collective-permute-start | bytes 786440 | tf_op jit(solution)/shard_map/ppermute | solution.py:375
  34.5 0.1 collective-permute-start.16
  34.6 1.5 %collective-permute-start.19 = (bf16[128,1024]{1,0:T(8,128)(2,1)S(1)}, bf16[128,1024]{1,0:T(8,128)(2,1)S(1)}, u32[]{:S(2)}, u32[]{:S(2)}) collective-permute-start(bf16[128,1024]{1,0:T(8,128)(2,1)S(1)} %get-tuple-element.70), channel_id=1, source_target_pairs={{0,2},{1,3},{2,0},{3,1},{4,6},{5,7},{6,4},{7,5},{8,10},{9,11},{10,... | collective-permute-start | bytes 786440 | tf_op jit(solution)/shard_map/ppermute | solution.py:371
  36.1 0.5 collective-permute-start.17
  36.6 2.1 %shard_map.135 = (bf16[256,1024]{1,0:T(8,128)(2,1)S(1)}, bf16[256,1024]{1,0:T(8,128)(2,1)S(1)}, bf16[256,1024]{1,0:T(8,128)(2,1)S(1)}, bf16[256,1024]{1,0:T(8,12...) custom-call(bf16[128,1024]{1,0:T(8,128)(2,1)S(1)} %get-tuple-element.47.refs_0_, ...), custom_call_target="tpu_custom_call" | custom-call | flops 1 | bytes 1 | tf_op jit(solution)/shard_map/pallas_call | solution.py:351
  38.7 2.1 %collective-permute-start.14 = (bf16[256,512]{1,0:T(8,128)(2,1)S(1)}, bf16[256,512]{1,0:T(8,128)(2,1)S(1)}, u32[]{:S(2)}, u32[]{:S(2)}) collective-permute-start(bf16[256,512]{1,0:T(8,128)(2,1)S(1)} %get-tuple-element.55), channel_id=1, source_target_pairs={{0,1},{1,0},{2,3},{3,2},{4,5},{5,4},{6,7},{7,6},{8,9},{9,8},{10,11... | collective-permute-start | bytes 786440 | tf_op jit(solution)/shard_map/ppermute | solution.py:375
  40.9 0.1 collective-permute-start.21
  40.9 1.5 %shard_map.137 = (bf16[256,1024]{1,0:T(8,128)(2,1)S(1)}, bf16[256,1024]{1,0:T(8,128)(2,1)S(1)}, bf16[256,1024]{1,0:T(8,128)(2,1)S(1)}, bf16[256,1024]{1,0:T(8,128)(2,1)S(1)}) custom-call(bf16[128,1024]{1,0:T(8,128)(2,1)S(1)} %get-tuple-element.62.refs_0_, bf16[128,1024]{1,0:T(8,128)(2,1)S(1)} %collective-permute-done.16.refs_1_, ...), custom_call_target="tpu_custom_call" | custom-call | flops 1 | bytes 1 | tf_op jit(solution)/shard_map/pallas_call | solution.py:351
  42.5 2.4 %shard_map.138 = (f32[1024,1024]{1,0:T(8,128)S(1)}, f32[1024,1024]{1,0:T(8,128)S(1)}) custom-call(bf16[256,1024]{1,0:T(8,128)(2,1)S(1)} %get-tuple-element.58.refs_0_, bf16[256,1024]{1,0:T(8,128)(2,1)S(1)} %get-tuple-element.59.refs_1_, bf16[256,1024]{1,0:T(8,128)(2,1)S(1)} %get-tuple-element.60.refs_2_, bf16[256,1024]{1,0:T(8,128)(2,1)S(1)} %get-tuple-element.61.refs_3_, ...), custom_call_target="tpu_custom_call" | custom-call | flops 1 | bytes 1 | tf_op jit(solution)/shard_map/pallas_call | solution.py:351
  44.9 1.2 %collective-permute-done.17.refs_1_.refs_6_ = bf16[128,1024]{1,0:T(8,128)(2,1)S(1)} collective-permute-done((bf16[128,1024]{1,0:T(8,128)(2,1)S(1)}, bf16[128,1024]{1,0:T(8,128)(2,1)S(1)}, u32[]{:S(2)}, u32[]{:S(2)}) %collective-permute-start.17) | collective-permute-done | bytes 262176 | tf_op jit(solution)/shard_map/ppermute | solution.py:371
  46.1 0.5 collective-permute-start.20
  46.6 1.6 %collective-permute-start.15 = (bf16[128,512]{1,0:T(8,128)(2,1)S(1)}, bf16[128,512]{1,0:T(8,128)(2,1)S(1)}, u32[]{:S(2)}, u32[]{:S(2)}) collective-permute-start(bf16[128,512]{1,0:T(8,128)(2,1)S(1)} %get-tuple-element.57), channel_id=1, source_target_pairs={{0,2},{2,0},{1,3},{3,1},{4,6},{6,4},{5,7},{7,5},{8,10},{10,8},{9,1... | collective-permute-start | bytes 393224 | tf_op jit(solution)/shard_map/ppermute | solution.py:474
  48.2 2.8 %shard_map.139 = (bf16[512,1024]{1,0:T(8,128)(2,1)S(1)}, bf16[512,1024]{1,0:T(8,128)(2,1)S(1)}, bf16[512,1024]{1,0:T(8,128)(2,1)S(1)}, bf16[512,1024]{1,0:T(8,128)(2,1)S(1)}) custom-call(bf16[128,1024]{1,0:T(8,128)(2,1)S(1)} %collective-permute-done.18.refs_0_.refs_7_, bf16[128,1024]{1,0:T(8,128)(2,1)S(1)} %collective-permute-done.17.refs_1_.refs_6_, ...), custom_call_target="tpu_custom_call" | custom-call | flops 1 | bytes 1 | tf_op jit(solution)/shard_map/pallas_call | solution.py:351
  51.0 3.8 %shard_map.140 = (f32[1024,1024]{1,0:T(8,128)}, f32[1024,1024]{1,0:T(8,128)}) custom-call(f32[1024,1024]{1,0:T(8,128)S(1)} %get-tuple-element.67.refs_0_, f32[1024,1024]{1,0:T(8,128)S(1)} %get-tuple-element.68.refs_1_, bf16[512,1024]{1,0:T(8,128)(2,1)S(1)} %get-tuple-element.72.refs_2_, bf16[512,1024]{1,0:T(8,128)(2,1)S(1)} %get-tuple-element.73.refs_3_, ...), custom_call_target="tpu_custom_call" | custom-call | flops 1 | bytes 1 | tf_op jit(solution)/shard_map/pallas_call | solution.py:490
  54.9 0.7 %shard_map.141 = bf16[128,512]{1,0:T(8,128)(2,1)} custom-call(f32[128,512]{1,0:T(8,128)S(1)} %get-tuple-element.46.stream_ref, f32[128,512]{1,0:T(8,128)S(1)} %get-tuple-element.56.own_ref, bf16[128,512]{1,0:T(8,128)(2,1)S(1)} %collective-permute-done.15.other_ref), custom_call_target="tpu_custom_call" | custom-call | flops 1 | bytes 1 | tf_op jit(solution)/shard_map/pallas_call | solution.py:351
  (24 shorter events, 0.1 us)
Async XLA Ops:
  0.6 18.0 %collective-permute-start.5 = (bf16[512,1024]{1,0:T(8,128)(2,1)}, bf16[512,1024]{1,0:T(8,128)(2,1)S(1)}, u32[]{:S(2)}, u32[]{:S(2)}) collective-permute-start(bf16[512,1024]{1,0:T(8,128)(2,1)} %refs_0_.3), channel_id=1, source_target_pairs={{0,1},{1,0},{2,3},{3,2},{4,5},{5,4},{6,7},{7,6},{8,9},{9,8},{10,11... | collective-permute-start | bytes 3145736 | tf_op jit(solution)/shard_map/ppermute | solution.py:129
  1.1 3.0 %collective-permute-start = (bf16[128,512]{1,0:T(8,128)(2,1)}, bf16[128,512]{1,0:T(8,128)(2,1)S(1)}, u32[]{:S(2)}, u32[]{:S(2)}) collective-permute-start(bf16[128,512]{1,0:T(8,128)(2,1)} %refs_0_.2), channel_id=1, source_target_pairs={{0,1},{1,0},{2,3},{3,2},{4,5},{5,4},{6,7},{7,6},{8,9},{9,8},{10,11... | collective-permute-start | bytes 393224 | tf_op jit(solution)/shard_map/ppermute | solution.py:129
  1.2 9.4 %collective-permute-start.1 = (bf16[128,512]{1,0:T(8,128)(2,1)}, bf16[128,512]{1,0:T(8,128)(2,1)S(1)}, u32[]{:S(2)}, u32[]{:S(2)}) collective-permute-start(bf16[128,512]{1,0:T(8,128)(2,1)} %refs_0_.4), channel_id=1, source_target_pairs={{0,2},{2,0},{1,3},{3,1},{4,6},{6,4},{5,7},{7,5},{8,10},{10,8},{9,1... | collective-permute-start | bytes 393224 | tf_op jit(solution)/shard_map/ppermute | solution.py:129
  4.1 6.8 %collective-permute-start.2 = (bf16[128,512]{1,0:T(8,128)(2,1)}, bf16[128,512]{1,0:T(8,128)(2,1)S(1)}, u32[]{:S(2)}, u32[]{:S(2)}) collective-permute-start(bf16[128,512]{1,0:T(8,128)(2,1)} %refs_2_.1), channel_id=1, source_target_pairs={{0,2},{2,0},{1,3},{3,1},{4,6},{6,4},{5,7},{7,5},{8,10},{10,8},{9,1... | collective-permute-start | bytes 393224 | tf_op jit(solution)/shard_map/ppermute | solution.py:129
  4.2 0.9 %copy-start.5 = (bf16[128,512]{1,0:T(8,128)(2,1)S(1)}, bf16[128,512]{1,0:T(8,128)(2,1)}, u32[]{:S(2)}) copy-start(bf16[128,512]{1,0:T(8,128)(2,1)} %refs_0_.2) | copy-start | bytes 393220
  5.1 31.5 %copy-start = (bf16[1024,1024]{1,0:T(8,128)(2,1)S(1)}, bf16[1024,1024]{1,0:T(8,128)(2,1)}, u32[]{:S(2)}) copy-start(bf16[1024,1024]{1,0:T(8,128)(2,1)} %refs_16_.1) | copy-start | bytes 6291460
  5.1 31.5 %copy-start.1 = (bf16[1024,1024]{1,0:T(8,128)(2,1)S(1)}, bf16[1024,1024]{1,0:T(8,128)(2,1)}, u32[]{:S(2)}) copy-start(bf16[1024,1024]{1,0:T(8,128)(2,1)} %refs_17_.1) | copy-start | bytes 6291460
  5.1 13.5 %collective-permute-start.4 = (bf16[128,1024]{1,0:T(8,128)(2,1)S(1)}, bf16[128,1024]{1,0:T(8,128)(2,1)S(1)}, u32[]{:S(2)}, u32[]{:S(2)}) collective-permute-start(bf16[128,1024]{1,0:T(8,128)(2,1)S(1)} %shard_map.130.refs_3_), channel_id=1, source_target_pairs={{0,4},{1,9},{2,6},{3,11},{4,0},{5,13},{6,2},{7,15},{8,12},{9,1},{1... | collective-permute-start | bytes 786440 | tf_op jit(solution)/shard_map/ppermute | solution.py:371
  8.5 1.2 %copy-start.2 = (bf16[512,1024]{1,0:T(8,128)(2,1)S(1)}, bf16[512,1024]{1,0:T(8,128)(2,1)}, u32[]{:S(2)}) copy-start(bf16[512,1024]{1,0:T(8,128)(2,1)} %refs_0_.3) | copy-start | bytes 3145732
  9.7 0.9 %copy-start.4 = (bf16[128,512]{1,0:T(8,128)(2,1)S(1)}, bf16[128,512]{1,0:T(8,128)(2,1)}, u32[]{:S(2)}) copy-start(bf16[128,512]{1,0:T(8,128)(2,1)} %refs_1_.1) | copy-start | bytes 393220
  10.7 0.7 %copy-start.6 = (bf16[128,512]{1,0:T(8,128)(2,1)}, bf16[128,512]{1,0:T(8,128)(2,1)S(1)}, u32[]{:S(2)}) copy-start(bf16[128,512]{1,0:T(8,128)(2,1)S(1)} %collective-permute-done.1.refs_1_) | copy-start | bytes 393220
  10.9 0.7 %copy-start.7 = (bf16[128,512]{1,0:T(8,128)(2,1)}, bf16[128,512]{1,0:T(8,128)(2,1)S(1)}, u32[]{:S(2)}) copy-start(bf16[128,512]{1,0:T(8,128)(2,1)S(1)} %collective-permute-done.2.refs_3_) | copy-start | bytes 393220
  14.2 4.4 %collective-permute-start.3 = (bf16[144,512]{1,0:T(8,128)(2,1)}, bf16[144,512]{1,0:T(8,128)(2,1)S(1)}, u32[]{:S(2)}, u32[]{:S(2)}) collective-permute-start(bf16[144,512]{1,0:T(8,128)(2,1)} %shard_map.132.refs_0_), channel_id=1, source_target_pairs={{0,1},{1,0},{2,3},{3,2},{4,5},{5,4},{6,7},{7,6},{8,9},{9,8},{10,11... | collective-permute-start | bytes 442376 | tf_op jit(solution)/shard_map/ppermute | solution.py:129
  14.9 3.7 %collective-permute-start.6 = (bf16[128,512]{1,0:T(8,128)(2,1)}, bf16[128,512]{1,0:T(8,128)(2,1)S(1)}, u32[]{:S(2)}, u32[]{:S(2)}) collective-permute-start(bf16[128,512]{1,0:T(8,128)(2,1)} %refs_1_.1), channel_id=1, source_target_pairs={{0,1},{1,0},{2,3},{3,2},{4,5},{5,4},{6,7},{7,6},{8,9},{9,8},{10,11... | collective-permute-start | bytes 393224 | tf_op jit(solution)/shard_map/ppermute | solution.py:129
  14.9 8.3 %collective-permute-start.9 = (bf16[128,1024]{1,0:T(8,128)(2,1)S(1)}, bf16[128,1024]{1,0:T(8,128)(2,1)S(1)}, u32[]{:S(2)}, u32[]{:S(2)}) collective-permute-start(bf16[128,1024]{1,0:T(8,128)(2,1)S(1)} %shard_map.130.refs_3_), channel_id=1, source_target_pairs={{0,12},{1,3},{2,14},{3,1},{4,8},{5,7},{6,10},{7,5},{8,4},{9,11},{1... | collective-permute-start | bytes 786440 | tf_op jit(solution)/shard_map/ppermute | solution.py:371
  18.6 0.9 %copy-start.3 = (bf16[144,512]{1,0:T(8,128)(2,1)S(1)}, bf16[144,512]{1,0:T(8,128)(2,1)}, u32[]{:S(2)}) copy-start(bf16[144,512]{1,0:T(8,128)(2,1)} %shard_map.132.refs_0_) | copy-start | bytes 442372
  20.3 9.7 %collective-permute-start.8 = (bf16[128,1024]{1,0:T(8,128)(2,1)S(1)}, bf16[128,1024]{1,0:T(8,128)(2,1)S(1)}, u32[]{:S(2)}, u32[]{:S(2)}) collective-permute-start(bf16[128,1024]{1,0:T(8,128)(2,1)S(1)} %get-tuple-element.47.refs_0_), channel_id=1, source_target_pairs={{0,12},{1,3},{2,14},{3,1},{4,8},{5,7},{6,10},{7,5},{8,4},{9,11},{1... | collective-permute-start | bytes 786440 | tf_op jit(solution)/shard_map/ppermute | solution.py:371
  21.6 10.0 %collective-permute-start.7 = (bf16[128,1024]{1,0:T(8,128)(2,1)S(1)}, bf16[128,1024]{1,0:T(8,128)(2,1)S(1)}, u32[]{:S(2)}, u32[]{:S(2)}) collective-permute-start(bf16[128,1024]{1,0:T(8,128)(2,1)S(1)} %get-tuple-element.47.refs_0_), channel_id=1, source_target_pairs={{0,4},{1,9},{2,6},{3,11},{4,0},{5,13},{6,2},{7,15},{8,12},{9,1},{1... | collective-permute-start | bytes 786440 | tf_op jit(solution)/shard_map/ppermute | solution.py:371
  21.6 10.1 %collective-permute-start.11 = (bf16[128,1024]{1,0:T(8,128)(2,1)S(1)}, bf16[128,1024]{1,0:T(8,128)(2,1)S(1)}, u32[]{:S(2)}, u32[]{:S(2)}) collective-permute-start(bf16[128,1024]{1,0:T(8,128)(2,1)S(1)} %collective-permute-done.4.refs_2_), channel_id=1, source_target_pairs={{0,1},{1,0},{2,3},{3,2},{4,5},{5,4},{6,7},{7,6},{8,9},{9,8},{10,11... | collective-permute-start | bytes 786440 | tf_op jit(solution)/shard_map/ppermute | solution.py:375
  21.8 9.9 %collective-permute-start.10 = (bf16[128,1024]{1,0:T(8,128)(2,1)S(1)}, bf16[128,1024]{1,0:T(8,128)(2,1)S(1)}, u32[]{:S(2)}, u32[]{:S(2)}) collective-permute-start(bf16[128,1024]{1,0:T(8,128)(2,1)S(1)} %collective-permute-done.4.refs_2_), channel_id=1, source_target_pairs={{0,2},{1,3},{2,0},{3,1},{4,6},{5,7},{6,4},{7,5},{8,10},{9,11},{10,... | collective-permute-start | bytes 786440 | tf_op jit(solution)/shard_map/ppermute | solution.py:371
  23.2 13.4 %collective-permute-start.13 = (bf16[128,1024]{1,0:T(8,128)(2,1)S(1)}, bf16[128,1024]{1,0:T(8,128)(2,1)S(1)}, u32[]{:S(2)}, u32[]{:S(2)}) collective-permute-start(bf16[128,1024]{1,0:T(8,128)(2,1)S(1)} %collective-permute-done.9.other_ref.refs_5_.refs_12_), channel_id=1, source_target_pairs={{0,1},{1,0},{2,3},{3,2},{4,5},{5,4},{6,7},{7,6},{8,9},{9,8},{10,11... | collective-permute-start | bytes 786440 | tf_op jit(solution)/shard_map/ppermute | solution.py:375
  31.7 4.9 %collective-permute-start.12 = (bf16[128,1024]{1,0:T(8,128)(2,1)S(1)}, bf16[128,1024]{1,0:T(8,128)(2,1)S(1)}, u32[]{:S(2)}, u32[]{:S(2)}) collective-permute-start(bf16[128,1024]{1,0:T(8,128)(2,1)S(1)} %get-tuple-element.53.refs_2_.refs_4_), channel_id=1, source_target_pairs={{0,1},{1,0},{2,3},{3,2},{4,5},{5,4},{6,7},{7,6},{8,9},{9,8},{10,11... | collective-permute-start | bytes 786440 | tf_op jit(solution)/shard_map/ppermute | solution.py:375
  34.5 6.4 %collective-permute-start.16 = (bf16[128,1024]{1,0:T(8,128)(2,1)S(1)}, bf16[128,1024]{1,0:T(8,128)(2,1)S(1)}, u32[]{:S(2)}, u32[]{:S(2)}) collective-permute-start(bf16[128,1024]{1,0:T(8,128)(2,1)S(1)} %get-tuple-element.62.refs_0_), channel_id=1, source_target_pairs={{0,1},{1,0},{2,3},{3,2},{4,5},{5,4},{6,7},{7,6},{8,9},{9,8},{10,11... | collective-permute-start | bytes 786440 | tf_op jit(solution)/shard_map/ppermute | solution.py:375
  34.6 10.3 %collective-permute-start.19 = (bf16[128,1024]{1,0:T(8,128)(2,1)S(1)}, bf16[128,1024]{1,0:T(8,128)(2,1)S(1)}, u32[]{:S(2)}, u32[]{:S(2)}) collective-permute-start(bf16[128,1024]{1,0:T(8,128)(2,1)S(1)} %get-tuple-element.70), channel_id=1, source_target_pairs={{0,2},{1,3},{2,0},{3,1},{4,6},{5,7},{6,4},{7,5},{8,10},{9,11},{10,... | collective-permute-start | bytes 786440 | tf_op jit(solution)/shard_map/ppermute | solution.py:371
  36.1 9.9 %collective-permute-start.17 = (bf16[128,1024]{1,0:T(8,128)(2,1)S(1)}, bf16[128,1024]{1,0:T(8,128)(2,1)S(1)}, u32[]{:S(2)}, u32[]{:S(2)}) collective-permute-start(bf16[128,1024]{1,0:T(8,128)(2,1)S(1)} %get-tuple-element.53.refs_2_.refs_4_), channel_id=1, source_target_pairs={{0,2},{1,5},{2,0},{3,7},{4,6},{5,1},{6,4},{7,3},{8,10},{9,13},{10,... | collective-permute-start | bytes 786440 | tf_op jit(solution)/shard_map/ppermute | solution.py:371
  38.7 7.8 %collective-permute-start.14 = (bf16[256,512]{1,0:T(8,128)(2,1)S(1)}, bf16[256,512]{1,0:T(8,128)(2,1)S(1)}, u32[]{:S(2)}, u32[]{:S(2)}) collective-permute-start(bf16[256,512]{1,0:T(8,128)(2,1)S(1)} %get-tuple-element.55), channel_id=1, source_target_pairs={{0,1},{1,0},{2,3},{3,2},{4,5},{5,4},{6,7},{7,6},{8,9},{9,8},{10,11... | collective-permute-start | bytes 786440 | tf_op jit(solution)/shard_map/ppermute | solution.py:375
  40.9 7.3 %collective-permute-start.21 = (bf16[128,1024]{1,0:T(8,128)(2,1)S(1)}, bf16[128,1024]{1,0:T(8,128)(2,1)S(1)}, u32[]{:S(2)}, u32[]{:S(2)}) collective-permute-start(bf16[128,1024]{1,0:T(8,128)(2,1)S(1)} %collective-permute-done.10.refs_8_.refs_11_), channel_id=1, source_target_pairs={{0,1},{1,0},{2,3},{3,2},{4,5},{5,4},{6,7},{7,6},{8,9},{9,8},{10,11... | collective-permute-start | bytes 786440 | tf_op jit(solution)/shard_map/ppermute | solution.py:375
  46.1 2.2 %collective-permute-start.18 = (bf16[128,1024]{1,0:T(8,128)(2,1)S(1)}, bf16[128,1024]{1,0:T(8,128)(2,1)S(1)}, u32[]{:S(2)}, u32[]{:S(2)}) collective-permute-start(bf16[128,1024]{1,0:T(8,128)(2,1)S(1)} %collective-permute-done.17.refs_1_.refs_6_), channel_id=1, source_target_pairs={{0,1},{1,0},{2,3},{3,2},{4,5},{5,4},{6,7},{7,6},{8,9},{9,8},{10,11... | collective-permute-start | bytes 786440 | tf_op jit(solution)/shard_map/ppermute | solution.py:375
  46.1 2.2 %collective-permute-start.20 = (bf16[128,1024]{1,0:T(8,128)(2,1)S(1)}, bf16[128,1024]{1,0:T(8,128)(2,1)S(1)}, u32[]{:S(2)}, u32[]{:S(2)}) collective-permute-start(bf16[128,1024]{1,0:T(8,128)(2,1)S(1)} %collective-permute-done.19.refs_3_.refs_14_), channel_id=1, source_target_pairs={{0,1},{1,0},{2,3},{3,2},{4,5},{5,4},{6,7},{7,6},{8,9},{9,8},{10,11... | collective-permute-start | bytes 786440 | tf_op jit(solution)/shard_map/ppermute | solution.py:375
  46.6 8.2 %collective-permute-start.15 = (bf16[128,512]{1,0:T(8,128)(2,1)S(1)}, bf16[128,512]{1,0:T(8,128)(2,1)S(1)}, u32[]{:S(2)}, u32[]{:S(2)}) collective-permute-start(bf16[128,512]{1,0:T(8,128)(2,1)S(1)} %get-tuple-element.57), channel_id=1, source_target_pairs={{0,2},{2,0},{1,3},{3,1},{4,6},{6,4},{5,7},{7,5},{8,10},{10,8},{9,1... | collective-permute-start | bytes 393224 | tf_op jit(solution)/shard_map/ppermute | solution.py:474
